TPU v7x, 256 devices: a whole 4x4x8 slice. The times are simulated.
256 devices in a mesh: slab: 32 (over z, x), pencil: 8 (over y, core).
Axes of the slice: x: 4, y: 4, z: 8, core: 2. Of those that a mesh axis runs over, the one named last changes fastest.
Arguments:
- strength: float32 [65536], P(('slab', 'pencil')), may hold values from -6 to 6
- stencil_weight: float32 [64, 65536], P(None, ('slab', 'pencil')), may hold values from -1.5 to 1.5
- slot_panel: int32 [32, 8, 768], P('slab', 'pencil'), may hold values from 0 to 256, as said below
- slot_anchor: int32 [32, 8, 768], P('slab', 'pencil'), may hold values from 0 to 105724, as said below
- green_spectrum: float32 [256, 256, 512], P('slab', 'pencil'), may hold values from 0.1 to 10, as said below
- near_index: int32 [32, 65536], P(None, ('slab', 'pencil')), may hold values from 0 to 767
- near_factor: float32 [32, 65536], P(None, ('slab', 'pencil')), may hold values from -1.2 to 1.2
Outputs:
- applied: float32 [65536], P(('slab', 'pencil'))
Inputs may be any that keep to these rules, and one draw needn't show every extreme that they name: `slot_panel`: on each sending device every one of its 256 panels stands in exactly one slot; the value 256 marks an empty slot. On each sending device the 24 slots of some destination slab are all occupied, and for each pencil index some destination slab receives full blocks of 24 from every sending slab. `slot_anchor`: each entry is (ox * 32 + oy) * 256 + oz with ox <= 12, oy <= 28, oz <= 252, so that every stencil lies inside the receiving device's cells. green_spectrum[y, z, x] equals green_spectrum[(-y) mod 256, (-z) mod 256, (-x) mod 512]: the spectrum of a real even Green's function.
All inputs are finite; a program needn't handle non-finite values.
Results may differ from a plain program's by a relative error of at most 0.0003.
Values sent between devices are 32-bit elements; how exact they have to be, the bound alone decides.
No kernel may reach another device: no remote copies, remote signals or barrier semaphores. Data moves between devices by JAX's collectives and lax.ppermute only.
A program may use at most 128 MiB of HBM per device.

v0:
```python
import math

import jax
import jax.numpy as jnp
from jax import lax
from jax.sharding import PartitionSpec as P

GX = 512
GY = 256
GZ = 256
EDGE = 4
PAN_DEV = 256
STENCIL = 64


def extended_2(block, sides, width):
    for axis, dim in sides:
        count = lax.axis_size(axis)
        forward = [(i, i + 1) for i in range(count - 1)]
        forward.append((count - 1, 0))
        backward = [(target, source) for source, target in forward]
        low = lax.ppermute(
            lax.slice_in_dim(block, block.shape[dim] - width, None, axis=dim), axis, forward
        )
        high = lax.ppermute(lax.slice_in_dim(block, 0, width, axis=dim), axis, backward)
        block = jnp.concatenate([low, block, high], axis=dim)
    return block


def fourier_tables(length):
    counter = lax.iota(jnp.int32, length)
    product = counter[:, None] * counter[None, :] % length
    angles = product.astype(jnp.float32) * (2.0 * math.pi / length)
    return (jnp.cos(angles), jnp.sin(angles))


def forward_block(length):
    cosine, sine = fourier_tables(length)
    return jnp.stack(
        [jnp.stack([cosine, sine], axis=-1), jnp.stack([-sine, cosine], axis=-1)], axis=1
    )


def inverse_block(length):
    cosine, sine = fourier_tables(length)
    block = jnp.stack(
        [jnp.stack([cosine, -sine], axis=-1), jnp.stack([sine, cosine], axis=-1)], axis=1
    )
    return block / length


def contract(form, left, right):
    return jnp.einsum(form, left, right, precision=lax.Precision.HIGHEST)


def convolve(charge, green_spectrum, pencil_count):
    slab_rows, pencil_rows, _ = charge.shape
    slab_share, pencil_share, _ = green_spectrum.shape
    cosine_z, sine_z = fourier_tables(GZ)
    split_cosine = cosine_z.reshape(GZ, pencil_count, 1, pencil_share)
    split_sine = sine_z.reshape(GZ, pencil_count, 1, pencil_share)
    z_table = jnp.concatenate([split_cosine, -split_sine], axis=2).reshape(GZ, -1)
    after_z = contract("mz,zc->mc", charge.reshape(-1, GZ), z_table).reshape(
        slab_rows, pencil_rows, pencil_count, 2 * pencil_share
    )
    pencil_data = lax.all_to_all(
        after_z, "pencil", split_axis=2, concat_axis=1, tiled=True
    ).reshape(slab_rows, GY, 2, pencil_share)
    after_y = contract("bsyr,xyrk->xbsk", forward_block(GY), pencil_data)
    slab_data = lax.all_to_all(after_y, "slab", split_axis=1, concat_axis=0, tiled=True)
    after_x = contract("asxr,xmrk->mkas", forward_block(GX), slab_data)
    product = after_x * green_spectrum[:, :, :, None]
    back_x = contract("xras,mkas->xmrk", inverse_block(GX), product)
    returned_slab = lax.all_to_all(back_x, "slab", split_axis=0, concat_axis=1, tiled=True)
    back_y = contract("yrbs,xbsk->xyrk", inverse_block(GY), returned_slab)
    returned_pencil = lax.all_to_all(back_y, "pencil", split_axis=1, concat_axis=2, tiled=True)
    inverse_cosine = cosine_z.reshape(pencil_count, 1, pencil_share, GZ)
    inverse_sine = sine_z.reshape(pencil_count, 1, pencil_share, GZ)
    back_table = (jnp.concatenate([inverse_cosine, -inverse_sine], axis=1) / GZ).reshape(-1, GZ)
    flat_back = returned_pencil.reshape(slab_rows * pencil_rows, -1)
    return contract("mc,cz->mz", flat_back, back_table).reshape(slab_rows, pencil_rows, GZ)


def per_device(
    strength, stencil_weight, slot_panel, slot_anchor, green_spectrum, near_index, near_factor
):
    slab_count = lax.axis_size("slab")
    pencil_count = lax.axis_size("pencil")
    slab_rows = GX // slab_count
    pencil_rows = GY // pencil_count
    slot_list = slot_panel.reshape(-1)
    occupied = slot_list < PAN_DEV
    panel_of = jnp.minimum(slot_list, PAN_DEV - 1)
    chosen_weight = jnp.take(stencil_weight, panel_of, axis=1)
    chosen_strength = jnp.where(occupied, strength[panel_of], 0.0)
    corner = lax.iota(jnp.int32, STENCIL)
    offsets = (corner // (EDGE * EDGE) * pencil_rows + corner // EDGE % EDGE) * GZ + corner % EDGE
    grid_cells = slot_anchor.reshape(-1)[None, :] + offsets[:, None]
    blocks = chosen_weight * chosen_strength[None, :]
    arrived = lax.all_to_all(blocks, "slab", split_axis=1, concat_axis=1, tiled=True)
    charge = (
        jnp.zeros((slab_rows * pencil_rows * GZ,), jnp.float32)
        .at[grid_cells.reshape(-1)]
        .add(arrived.reshape(-1))
    )
    potential = convolve(
        charge.reshape(slab_rows, pencil_rows, GZ), green_spectrum, pencil_count
    ).reshape(-1)
    sampled = potential[grid_cells]
    returned = lax.all_to_all(sampled, "slab", split_axis=1, concat_axis=1, tiled=True)
    far_slot = jnp.sum(chosen_weight * returned, axis=0)
    far_field = jnp.zeros((PAN_DEV,), jnp.float32).at[slot_list].add(far_slot, mode="drop")
    extended = extended_2(strength, (("slab", 0),), PAN_DEV)
    near_field = jnp.sum(near_factor * extended[near_index], axis=0)
    return far_field + near_field


def solution(mesh):
    in_specs = (
        P(("slab", "pencil")),
        P(None, ("slab", "pencil")),
        P("slab", "pencil", None),
        P("slab", "pencil", None),
        P("slab", "pencil", None),
        P(None, ("slab", "pencil")),
        P(None, ("slab", "pencil")),
    )
    out_specs = P(("slab", "pencil"))
    return jax.shard_map(
        per_device, mesh=mesh, in_specs=in_specs, out_specs=out_specs, check_vma=False
    )
```

profile of v0, /device:TPU:2, one launch (start us, length us, event | category | flops | bytes accessed | tf_op | source)
XLA Modules:
  0.0 869.3 jit_solution(501348580995430943)
XLA Ops:
  0.0 1.3 fusion.80
  1.3 0.7 compare_reduce_fusion
  2.0 0.7 minimum_reduce_fusion
  2.8 0.9 copy.20
  3.7 1.6 gather_fusion.1
  5.3 5.0 gather_fusion.2
  10.9 0.9 reshape.690
  11.8 11.6 %all-to-all-start = ((f32[32,1,1536]{2,1,0:T(1,128)}), f32[32,1,1536]{2,1,0:T(1,128)S(1)}, u32[]{:S(2)}, u32[]{:S(2)}) async-start(f32[32,1,1536]{2,1,0:T(1,128)} %reshape.690), calls=%async_computation | async-start | bytes 393216 | tf_op jit(solution)/shard_map/all_to_all | solution.py:100
  24.5 1.1 fusion.76
  25.6 7.6 all-to-all-done
  33.7 1.0 reduce.10
  34.9 0.9 copy.21
  36.4 256.4 %scatter_custom_fusion = f32[131072]{0:T(1024)S(1)} fusion(s32[49152]{0:T(1024)S(1)} %bitcast.166, f32[49152]{0:T(1024)S(1)} %reshape.651, f32[]{:T(128)} %constant.126.clone.1), kind=kCustom, calls=%fused_computation.97 | custom fusion | flops 49152 | bytes 524292 | tf_op jit(solution)/shard_map/scatter-add | solution.py:104
  293.0 1.8 convolution_bitcast_fusion.2
  294.8 2.1 reshape.692
  297.0 4.7 all-to-all-start.1
  301.6 1.0 fusion.77
  302.6 1.0 fusion.74
  303.7 1.2 fusion.48
  304.8 12.7 %all-to-all-done.1 = f32[8,1,32768]{2,1,0:T(1,128)S(1)} async-done(((f32[8,1,32768]{2,1,0:T(1,128)}), f32[8,1,32768]{2,1,0:T(1,128)S(1)}, u32[]{:S(2)}, u32[]{:S(2)}) %all-to-all-start.1) | async-done | bytes 1048608 | tf_op jit(solution)/shard_map/all_to_all | solution.py:66
  317.6 3.2 reduce.11
  320.7 2.2 reshape.693
  322.9 1.9 bitcast_bitcast_fusion
  324.8 2.8 copy.23
  327.6 3.3 reshape.669
  330.9 1.9 convolution_bitcast_fusion
  332.8 4.5 copy.24
  337.3 6.5 reshape.694
  343.8 7.0 all-to-all-start.2
  350.8 3.9 fusion.52
  354.6 4.1 fusion.50
  358.7 3.3 fusion.15
  362.0 16.9 %all-to-all-done.2 = f32[32,1,8192]{2,1,0:T(1,128)} async-done(((f32[32,1,8192]{2,1,0:T(1,128)}), f32[32,1,8192]{2,1,0:T(1,128)}, u32[]{:S(2)}, u32[]{:S(2)}) %all-to-all-start.2) | async-done | bytes 1048608 | tf_op jit(solution)/shard_map/all_to_all | solution.py:70
  378.9 4.4 reduce.12
  383.3 5.0 reshape.695
  388.4 4.6 copy.67
  393.5 1.0 copy-done.2
  395.3 26.7 %fusion.29 = f32[8,32,512,2,1]{2,1,3,4,0:T(8,128)S(1)} fusion(f32[512,1,512,2]{2,0,3,1:T(8,128)S(1)} %copy-done.2, f32[512,1,512,2]{2,0,3,1:T(8,128)S(1)} %copy-done.3, f32[512,8,2,32,1]{3,1,2,0,4:T(8,128)S(1)} %bitcast.157, f32[8,32,512]{2,1,0:T(8,128)S(1)} %copy-done.4), kind=kOutput, calls=%fused_computation.37 | convolution fusion | flops 3222536192 | bytes 6815744 | tf_op jit(solution)/shard_map/asxr,xmrk->mkas/dot_general | solution.py:53
  422.0 4.1 fusion.20
  426.1 4.5 copy.28
  430.6 6.6 reshape.696
  437.2 5.6 all-to-all-start.3
  442.8 1.5 collective-permute-start
  446.3 1.1 fusion.73
  447.5 22.8 %all-to-all-done.3 = f32[32,1,8192]{2,1,0:T(1,128)S(1)} async-done(((f32[32,1,8192]{2,1,0:T(1,128)}), f32[32,1,8192]{2,1,0:T(1,128)S(1)}, u32[]{:S(2)}, u32[]{:S(2)}) %all-to-all-start.3) | async-done | bytes 1048608 | tf_op jit(solution)/shard_map/all_to_all | solution.py:74
  470.3 3.2 reduce.13
  473.5 5.1 reshape.697
  478.6 2.5 copy.29
  481.1 13.4 %fusion.17 = f32[16,256,2,32]{1,3,2,0:T(8,128)S(1)} fusion(f32[16,32,8,2,32]{4,2,3,0,1:T(8,128)S(1)} %bitcast.156, f32[256,1,256,2]{2,0,3,1:T(8,128)S(1)} %copy-done.6, f32[256,1,256,2]{2,0,3,1:T(8,128)S(1)} %copy-done.5), kind=kOutput, calls=%fused_computation.32 | convolution fusion | flops 1611137024 | bytes 3145728 | tf_op jit(solution)/shard_map/yrbs,xbsk->xyrk/dot_general | solution.py:53
  494.6 4.5 copy.32
  499.1 6.7 reshape.698
  505.8 3.6 all-to-all-start.4
  510.1 15.2 %all-to-all-done.4 = f32[8,1,32768]{2,1,0:T(1,128)S(1)} async-done(((f32[8,1,32768]{2,1,0:T(1,128)}), f32[8,1,32768]{2,1,0:T(1,128)S(1)}, u32[]{:S(2)}, u32[]{:S(2)}) %all-to-all-start.4) | async-done | bytes 1048608 | tf_op jit(solution)/shard_map/all_to_all | solution.py:76
  525.3 3.2 reduce.14
  528.4 5.5 reshape.699
  533.9 7.8 copy.33
  541.8 3.6 reshape.614
  545.4 1.9 convolution_bitcast_fusion.1
  547.5 270.5 %gather_fusion.3 = f32[49152]{0:T(1024)S(1)} fusion(f32[131072]{0:T(1024)S(1)} %bitcast.150, s32[49152]{0:T(1024)S(1)} %copy-done.8), kind=kCustom, calls=%fused_computation.3 | custom fusion | bytes 589824 | tf_op jit(solution)/shard_map/gather | solution.py:109
  819.4 0.9 reshape.700
  820.3 5.8 all-to-all-start.5
  826.9 32.9 %gather_fusion = f32[8192]{0:T(1024)S(1)} fusion(f32[768]{0:T(1024)S(1)} %pad_maximum_fusion.9, s32[8192]{0:T(1024)S(1)} %broadcast_clamp_fusion.1), kind=kCustom, calls=%fused_computation | custom fusion | bytes 98304 | tf_op jit(solution)/shard_map/gather | solution.py:114
  860.4 1.0 reduce.15
  862.0 7.1 scatter_fusion
  (70 shorter events, 10.4 us)
Async XLA Ops:
  0.0 5.3 copy-start
  0.0 23.4 %copy-start.13 = (s32[1,1,768]{2,1,0:T(1,128)S(1)}, s32[1,1,768]{2,1,0:T(1,128)}, u32[]{:S(2)}) copy-start(s32[1,1,768]{2,1,0:T(1,128)} %param.10) | copy-start | bytes 9220
  11.8 21.4 %all-to-all-start = ((f32[32,1,1536]{2,1,0:T(1,128)}), f32[32,1,1536]{2,1,0:T(1,128)S(1)}, u32[]{:S(2)}, u32[]{:S(2)}) async-start(f32[32,1,1536]{2,1,0:T(1,128)} %reshape.690), calls=%async_computation | async-start | bytes 393216 | tf_op jit(solution)/shard_map/all_to_all | solution.py:100
  23.4 0.5 copy-start.14
  297.0 20.6 %all-to-all-start.1 = ((f32[8,1,32768]{2,1,0:T(1,128)}), f32[8,1,32768]{2,1,0:T(1,128)S(1)}, u32[]{:S(2)}, u32[]{:S(2)}) async-start(f32[8,1,32768]{2,1,0:T(1,128)} %reshape.692), calls=%async_computation.1 | async-start | bytes 2097152 | tf_op jit(solution)/shard_map/all_to_all | solution.py:66
  343.8 35.1 %all-to-all-start.2 = ((f32[32,1,8192]{2,1,0:T(1,128)}), f32[32,1,8192]{2,1,0:T(1,128)}, u32[]{:S(2)}, u32[]{:S(2)}) async-start(f32[32,1,8192]{2,1,0:T(1,128)} %reshape.694), calls=%async_computation.2 | async-start | bytes 2097152 | tf_op jit(solution)/shard_map/all_to_all | solution.py:70
  393.0 1.6 copy-start.2
  393.0 2.2 copy-start.3
  393.0 2.3 copy-start.4
  395.3 26.7 %copy-start.1 = (f32[512,1,512,2]{2,0,3,1:T(8,128)S(1)}, f32[512,1,512,2]{2,0,3,1:T(8,128)}, u32[]{:S(2)}) copy-start(f32[512,1,512,2]{2,0,3,1:T(8,128)} %get-tuple-element.12) | copy-start | bytes 6291460
  430.6 14.2 %copy-start.15 = (s32[64]{0:T(128)S(1)}, s32[64]{0:T(128)}, u32[]{:S(2)}) copy-start(s32[64]{0:T(128)} %copy-done.14) | copy-start | bytes 772
  430.6 15.0 %copy-start.10 = (s32[32,256]{1,0:T(8,128)S(1)}, s32[32,256]{1,0:T(8,128)}, u32[]{:S(2)}) copy-start(s32[32,256]{1,0:T(8,128)} %param.12) | copy-start | bytes 98308
  437.2 33.1 %all-to-all-start.3 = ((f32[32,1,8192]{2,1,0:T(1,128)}), f32[32,1,8192]{2,1,0:T(1,128)S(1)}, u32[]{:S(2)}, u32[]{:S(2)}) async-start(f32[32,1,8192]{2,1,0:T(1,128)} %reshape.696), calls=%async_computation.3 | async-start | bytes 2097152 | tf_op jit(solution)/shard_map/all_to_all | solution.py:74
  442.8 383.4 %collective-permute-start = (f32[256]{0:T(256)S(1)}, f32[256]{0:T(256)}, u32[]{:S(2)}, u32[]{:S(2)}) collective-permute-start(f32[256]{0:T(256)S(1)} %copy-done), channel_id=1, source_target_pairs={{0,8},{8,16},{16,24},{24,32},{32,40},{40,48},{48,56},{56,64},{64,7... | collective-permute-start | bytes 3080 | tf_op jit(solution)/shard_map/ppermute | solution.py:22
  444.3 381.9 %collective-permute-start.1 = (f32[256]{0:T(256)S(1)}, f32[256]{0:T(256)}, u32[]{:S(2)}, u32[]{:S(2)}) collective-permute-start(f32[256]{0:T(256)S(1)} %copy-done), channel_id=1, source_target_pairs={{8,0},{16,8},{24,16},{32,24},{40,32},{48,40},{56,48},{64,56},{72,6... | collective-permute-start | bytes 3080 | tf_op jit(solution)/shard_map/ppermute | solution.py:25
  478.6 2.6 copy-start.5
  478.6 2.6 copy-start.6
  499.1 10.3 %copy-start.7 = (s32[49152]{0:T(1024)S(1)}, s32[49152]{0:T(1024)}, u32[]{:S(2)}) copy-start(s32[49152]{0:T(1024)} %reshape.641) | copy-start | bytes 589828
  505.8 19.4 %all-to-all-start.4 = ((f32[8,1,32768]{2,1,0:T(1,128)}), f32[8,1,32768]{2,1,0:T(1,128)S(1)}, u32[]{:S(2)}, u32[]{:S(2)}) async-start(f32[8,1,32768]{2,1,0:T(1,128)} %reshape.698), calls=%async_computation.4 | async-start | bytes 2097152 | tf_op jit(solution)/shard_map/all_to_all | solution.py:76
  541.8 5.7 copy-start.8
  547.5 278.6 %copy-start.9 = (s32[4,2,8,128]{3,1,2,0:T(2,128)S(1)}, s32[4,2,8,128]{3,1,2,0:T(2,128)}, u32[]{:S(2)}) copy-start(s32[4,2,8,128]{3,1,2,0:T(2,128)} %copy.49) | copy-start | bytes 98308
  820.3 40.1 %all-to-all-start.5 = ((f32[32,1,1536]{2,1,0:T(1,128)}), f32[32,1,1536]{2,1,0:T(1,128)S(1)}, u32[]{:S(2)}, u32[]{:S(2)}) async-start(f32[32,1,1536]{2,1,0:T(1,128)} %reshape.700), calls=%async_computation.5 | async-start | bytes 393216 | tf_op jit(solution)/shard_map/all_to_all | solution.py:110
  826.9 32.9 %copy-start.11 = (f32[32,256]{1,0:T(8,128)S(1)}, f32[32,256]{1,0:T(8,128)}, u32[]{:S(2)}) copy-start(f32[32,256]{1,0:T(8,128)} %param.13) | copy-start | bytes 98308
  826.9 35.1 %copy-start.12 = (s32[768]{0:T(1024)S(1)}, s32[768]{0:T(1024)}, u32[]{:S(2)}) copy-start(s32[768]{0:T(1024)} %get-tuple-element.6) | copy-start | bytes 9220
where the time goes:
time: 877 us; the launch traced here: 869 us
  local copies, waits for them, and re-layouts  401 us (46%)
  other arithmetic  302 us (34%)
  waiting for transfers between devices  75.2 us (9%)
  matrix products  49.8 us (6%)
  starting transfers between devices  40.3 us (5%)
    gather x1, local copies, waits for them, and re-layouts, per_device(): sampled = potential[grid_cells]  271 us
    scatter-add x1, other arithmetic, per_device(): charge = jnp.zeros((slab_rows * pencil_rows * GZ,), jnp.float32).at[grid_...  256 us
    dot_general x6, matrix products, contract(): return jnp.einsum(form, left, right, precision=lax.Precision.HIGHEST)  49.8 us
    unnamed x48, local copies, waits for them, and re-layouts  46.1 us
    gather x2, local copies, waits for them, and re-layouts, per_device(): near_field = jnp.sum(near_factor * extended[near_index], axis=0)  32.9 us
    all_to_all x1, waiting for transfers between devices, convolve(): lax.all_to_all(back_x, 'slab', split_axis=0, concat_axis=1, tiled=True)  22.8 us
  transfers between devices with their start and end apart: 8, of which 5 were waited for; matrix products, arithmetic and copies ran while one was open for 44% of the time, Pallas kernels for 0%

commit v1 on v0

v1 whole, which is shorter than its diff:
```python
import math

import jax
import jax.numpy as jnp
import numpy as np
from jax import lax
from jax.experimental import pallas as pl
from jax.experimental.pallas import tpu as pltpu
from jax.sharding import PartitionSpec as P

GX = 512
GY = 256
GZ = 256
EDGE = 4
PAN_DEV = 256
CAP = 24
N_SLAB = 32
N_PENCIL = 8
SLOTS = N_SLAB * CAP
SLAB_ROWS = 16
PENCIL_ROWS = 32
KZ = 16
VMEM_LIMIT = 40 * 2**20
F32 = jnp.float32
BF16 = jnp.bfloat16


def kz_of(pencil, place):
    return np.where(
        pencil < 4, 32 * pencil + place, -(32 * (7 - pencil) + 16 + place)
    )


def z_tables():
    pencil, ri, place = np.meshgrid(np.arange(8), np.arange(2), np.arange(KZ), indexing="ij")
    kz = kz_of(pencil, place).reshape(-1)
    ri = ri.reshape(-1)
    shared = (pencil.reshape(-1) == 0) & (place.reshape(-1) == 0)
    z = np.arange(GZ)
    theta = 2 * np.pi * ((z[:, None] * kz[None, :]) % GZ) / GZ
    sign = 1.0 - 2.0 * (z % 2)
    forward = np.where(ri == 0, np.cos(theta), -np.sin(theta))
    forward = np.where(shared & (ri == 1), sign[:, None], forward)
    scale = np.where(shared, 1.0, 2.0) / GZ
    backward = (forward * scale).T
    return forward, backward


def y_tables():
    slab, ro, k8 = (a.reshape(-1) for a in np.meshgrid(np.arange(32), np.arange(2), np.arange(8), indexing="ij"))
    pencil, ri, y32 = (a.reshape(-1) for a in np.meshgrid(np.arange(8), np.arange(2), np.arange(32), indexing="ij"))
    ky = (8 * slab + k8)[:, None]
    ro = ro[:, None]
    y = (32 * pencil + y32)[None, :]
    ri = ri[None, :]
    theta = 2 * np.pi * ((ky * y) % GY) / GY
    cosine, sine = np.cos(theta), np.sin(theta)
    forward = np.where(ro == ri, cosine, np.where(ro == 0, sine, -sine))
    backward = forward.T / GY
    low = (ky > 0) & (ky < 128)
    high = ky > 128
    ends = (ky == 0) | (ky == 128)
    part = np.where(ro == 0, cosine, -sine)
    shared = np.where(low & (ri == 0), part, 0.0)
    shared = np.where(high & (ri == 1), part, shared)
    shared = np.where(ends & (ro == ri), cosine, shared)
    shared_back = (shared * np.where(ends, 1.0, 2.0)).T / GY
    return forward, shared, backward, shared_back


def x_tables():
    k1, ro, ko = (a.reshape(-1)[:, None] for a in np.meshgrid(np.arange(32), np.arange(2), np.arange(8), indexing="ij"))
    slab, ri, ki = (a.reshape(-1)[None, :] for a in np.meshgrid(np.arange(32), np.arange(2), np.arange(8), indexing="ij"))
    theta = 2 * np.pi * ((k1 * slab) % 32) / 32
    rows = np.where(ro == ri, np.cos(theta), np.where(ro == 0, np.sin(theta), -np.sin(theta)))
    rows = rows * (ko == ki)
    rows_back = rows.T / GX
    x16 = np.arange(16)
    twist = 2 * np.pi * np.arange(32)[:, None] * x16[None, :] / GX
    twist = np.repeat(np.repeat(twist, 8, axis=0), KZ, axis=1)
    inner = 2 * np.pi * ((x16[:, None] * x16[None, :]) % 16) / 16
    eye = np.eye(KZ)
    cosine, sine = np.kron(np.cos(inner), eye), np.kron(np.sin(inner), eye)
    lanes = np.block([[cosine, -sine], [sine, cosine]])
    lanes_back = lanes.T
    return rows, rows_back, np.cos(twist), np.sin(twist), lanes, lanes_back


def pair(table):
    high = np.asarray(table, np.float32).astype(jnp.bfloat16)
    low = (np.asarray(table, np.float64) - high.astype(np.float64)).astype(jnp.bfloat16)
    return jnp.asarray(high), jnp.asarray(low)


def split(value):
    high = value.astype(BF16)
    return high, (value - high.astype(F32)).astype(BF16)


def mm(left, right):
    return jnp.dot(left, right, preferred_element_type=F32)


def mm_nt(left, right):
    return lax.dot_general(left, right, (((1,), (1,)), ((), ())), preferred_element_type=F32)


def mm3(left, right):
    return mm(left[0], right[0]) + (mm(left[0], right[1]) + mm(left[1], right[0]))


def call(kernel, out_shape, *args, scratch=(), smem=()):
    specs = [
        pl.BlockSpec(memory_space=pltpu.SMEM) if i in smem else pl.BlockSpec(memory_space=pltpu.VMEM)
        for i in range(len(args))
    ]
    multi = isinstance(out_shape, (list, tuple)) and not isinstance(out_shape, jax.ShapeDtypeStruct)
    out_spec = pl.BlockSpec(memory_space=pltpu.VMEM)
    return pl.pallas_call(
        kernel,
        out_shape=out_shape,
        in_specs=specs,
        out_specs=[out_spec] * len(out_shape) if multi else out_spec,
        scratch_shapes=list(scratch),
        compiler_params=pltpu.CompilerParams(vmem_limit_bytes=VMEM_LIMIT),
        name=kernel.__name__,
    )(*args)


def swap_groups(tiles):
    tiles = list(tiles)
    group = lax.broadcasted_iota(jnp.int32, tiles[0].shape, 1) // 16
    for bit in range(3):
        step = 1 << bit
        upper = (group & step) != 0
        for i in range(8):
            if i & step:
                continue
            low, high = tiles[i], tiles[i + step]
            tiles[i] = jnp.where(upper, pltpu.roll(high, 16 * step, 1), low)
            tiles[i + step] = jnp.where(upper, high, pltpu.roll(low, 128 - 16 * step, 1))
    return tiles


def pack(weight_ref, strength_ref, slot_ref, out_ref):
    slots = jnp.transpose(jnp.broadcast_to(slot_ref[0], (128, SLOTS)))
    panel = lax.broadcasted_iota(jnp.int32, (SLOTS, 128), 1)
    hot = jnp.concatenate([(slots == panel), (slots == panel + 128)], axis=1)
    hot = jnp.where(hot, 1.0, 0.0).astype(BF16)
    row = lax.broadcasted_iota(jnp.int32, (64, PAN_DEV), 0)
    extra = jnp.where(row == 0, jnp.broadcast_to(strength_ref[...], (64, PAN_DEV)), 0.0)
    values = jnp.concatenate([weight_ref[...], extra], axis=0)
    high, low = split(values)
    out_ref[...] = mm_nt(hot, high) + mm_nt(hot, low)


def anchor_parts(anchor):
    return anchor >> 13, (anchor >> 8) & 31, anchor & 255


def weights_by_slot(arrived_ref, order_ref):
    high, low = split(arrived_ref[...])
    return mm_nt(order_ref[...], high) + mm_nt(order_ref[...], low)


def z_hot(third, dz):
    z = lax.broadcasted_iota(jnp.int32, (GZ, SLOTS), 0)
    return jnp.where(z - dz == third, 1.0, 0.0).astype(BF16)


def y_place(second, y_ref, inside_ref):
    rel = lax.broadcasted_iota(jnp.int32, (PENCIL_ROWS, SLOTS), 0) - second
    inside = (rel >= 0) & (rel < EDGE)
    y_ref[...] = jnp.where(inside, rel, 0)
    inside_ref[...] = jnp.where(inside, 1.0, 0.0)


def stencil_row(x, first, weight_ref):
    total = jnp.zeros((16, SLOTS), F32)
    for dx in range(EDGE):
        total = jnp.where(first == x - dx, weight_ref[dx * 16 : (dx + 1) * 16, :], total)
    return total


def place_rows(rows, dz, y_ref, inside_ref):
    half = rows[(dz // 2) * 8 : (dz // 2) * 8 + 8]
    out = []
    for block in range(PENCIL_ROWS // 8):
        pieces = []
        for lane in range(SLOTS // 128):
            index = y_ref[block * 8 : block * 8 + 8, lane * 128 : (lane + 1) * 128] + (dz % 2) * 4
            pieces.append(
                jnp.take_along_axis(half[:, lane * 128 : (lane + 1) * 128], index, axis=0, mode="promise_in_bounds")
            )
        out.append(jnp.concatenate(pieces, axis=1) * inside_ref[block * 8 : block * 8 + 8, :])
    return jnp.concatenate(out, axis=0)


def project(arrived_ref, anchor_ref, order_ref, zh_ref, zl_ref, out_ref, weight_ref, y_ref, inside_ref, high_ref, low_ref, hot_ref):
    first, second, third = anchor_parts(anchor_ref[0])
    weights = weights_by_slot(arrived_ref, order_ref)
    weight_ref[...] = weights[:64] * weights[64:65]
    y_place(second, y_ref, inside_ref)
    for dz in range(EDGE):
        hot_ref[:, dz * SLOTS : (dz + 1) * SLOTS] = z_hot(third, dz)

    def step(x, carry):
        rows = stencil_row(x, first, weight_ref)
        at = pl.ds(pl.multiple_of(x * PENCIL_ROWS, PENCIL_ROWS), PENCIL_ROWS)
        for dz in range(EDGE):
            high, low = split(place_rows(rows, dz, y_ref, inside_ref))
            high_ref[at, dz * SLOTS : (dz + 1) * SLOTS] = high
            low_ref[at, dz * SLOTS : (dz + 1) * SLOTS] = low
        return carry

    lax.fori_loop(0, SLAB_ROWS, step, 0)
    hot = hot_ref[...]
    charge = mm_nt(high_ref[...], hot) + mm_nt(low_ref[...], hot)
    after = mm3(split(charge), (zh_ref[...], zl_ref[...]))
    for half in range(2):
        for quarter in range(2):
            tiles = [
                after[x * 32 : x * 32 + 32, quarter * 128 : quarter * 128 + 128]
                for x in range(half * 8, half * 8 + 8)
            ]
            for g, tile in enumerate(swap_groups(tiles)):
                pencil, ri = quarter * 4 + g // 2, g % 2
                start = pencil * 128 + half * 64 + ri * 32
                out_ref[start : start + 32, :] = tile


def gathered(ref, count, rows):
    block = ref[...].reshape(count, 2, rows, 128)
    return jnp.concatenate([block[:, half].reshape(count * rows, 128) for half in range(2)], axis=1)


def scattered(value, ref, count, rows):
    for half in range(2):
        part = value[:, half * 128 : half * 128 + 128].reshape(count, rows, 128)
        for i in range(count):
            ref[(i * 2 + half) * rows : (i * 2 + half + 1) * rows, :] = part[i]


def shared_lane(shape):
    return lax.broadcasted_iota(jnp.int32, shape, 1) % KZ == 0


def y_stage(source, target):
    def kernel(flag_ref, in_ref, th_ref, tl_ref, sh_ref, sl_ref, out_ref, work_ref):
        data = split(gathered(in_ref, *source))
        work_ref[...] = mm3((th_ref[...], tl_ref[...]), data)

        @pl.when(flag_ref[0] == 1)
        def _():
            other = mm3((sh_ref[...], sl_ref[...]), data)
            work_ref[...] = jnp.where(shared_lane(other.shape), other, work_ref[...])

        scattered(work_ref[...], out_ref, *target)

    return kernel


def y_forward(*refs):
    y_stage((8, 64), (32, 16))(*refs)


def y_backward(*refs):
    y_stage((32, 16), (8, 64))(*refs)


def x_stage(flag_ref, in_ref, rh, rl, rbh, rbl, cos_ref, sin_ref, lh, ll, lbh, lbl, green_ref, other_ref, out_ref, re_ref, im_ref):
    cosine, sine = cos_ref[...], sin_ref[...]
    data = gathered(in_ref, 32, 16)

    def spectrum(value):
        rows = mm3((rh[...], rl[...]), split(value)).reshape(32, 2, 8, 256)
        re, im = rows[:, 0].reshape(256, 256), rows[:, 1].reshape(256, 256)
        turned = jnp.concatenate([re * cosine + im * sine, im * cosine - re * sine], axis=1)
        return mm3(split(turned), (lh[...], ll[...]))

    full = spectrum(data)
    re_ref[...] = full[:, :256] * green_ref[...]
    im_ref[...] = full[:, 256:] * green_ref[...]

    @pl.when(flag_ref[1] == 1)
    def _():
        row = lax.broadcasted_iota(jnp.int32, data.shape, 0)
        mirror = spectrum(jnp.where((row // 8) % 2 == 1, -data, data))
        re_ref[...] += mirror[:, :256] * other_ref[...]
        im_ref[...] += mirror[:, 256:] * other_ref[...]

    product = jnp.concatenate([re_ref[...], im_ref[...]], axis=1)
    back = mm3(split(product), (lbh[...], lbl[...]))
    re, im = back[:, :256], back[:, 256:]
    re, im = re * cosine - im * sine, im * cosine + re * sine
    rows = jnp.stack([re.reshape(32, 8, 256), im.reshape(32, 8, 256)], axis=1).reshape(512, 256)
    scattered(mm3((rbh[...], rbl[...]), split(rows)), out_ref, 32, 16)


def sample(in_ref, arrived_ref, anchor_ref, order_ref, zh_ref, zl_ref, spread_ref, out_ref, weight_ref, y_ref, inside_ref, after_ref, ph_ref, pl_ref, hot_ref, sum_ref):
    for half in range(2):
        for quarter in range(2):
            tiles = []
            for g in range(8):
                pencil, ri = quarter * 4 + g // 2, g % 2
                start = pencil * 128 + half * 64 + ri * 32
                tiles.append(in_ref[start : start + 32, :])
            for i, tile in enumerate(swap_groups(tiles)):
                x = half * 8 + i
                after_ref[x * 32 : x * 32 + 32, quarter * 128 : quarter * 128 + 128] = tile
    potential = mm3(split(after_ref[...]), (zh_ref[...], zl_ref[...]))
    ph_ref[...], pl_ref[...] = split(potential)
    first, second, third = anchor_parts(anchor_ref[0])
    weights = weights_by_slot(arrived_ref, order_ref)
    weight_ref[...] = weights[:64]
    y_place(second, y_ref, inside_ref)
    for dz in range(EDGE):
        hot_ref[:, dz * SLOTS : (dz + 1) * SLOTS] = z_hot(third, dz)
    sum_ref[...] = jnp.zeros((PENCIL_ROWS, SLOTS), F32)

    def step(x, carry):
        rows = stencil_row(x, first, weight_ref)
        at = pl.ds(pl.multiple_of(x * PENCIL_ROWS, PENCIL_ROWS), PENCIL_ROWS)
        high, low = ph_ref[at, :], pl_ref[at, :]
        total = sum_ref[...]
        for dz in range(EDGE):
            hot = hot_ref[:, dz * SLOTS : (dz + 1) * SLOTS]
            total += (mm(high, hot) + mm(low, hot)) * place_rows(rows, dz, y_ref, inside_ref)
        sum_ref[...] = total
        return carry

    lax.fori_loop(0, SLAB_ROWS, step, 0)
    far = jnp.sum(sum_ref[...], axis=0, keepdims=True)
    slab = lax.broadcasted_iota(jnp.int32, (N_SLAB, SLOTS), 0)
    slot = lax.broadcasted_iota(jnp.int32, (N_SLAB, SLOTS), 1)
    own = (slot >= slab * CAP) & (slot < slab * CAP + CAP)
    high, low = split(jnp.where(own, jnp.broadcast_to(far, own.shape), 0.0))
    out_ref[...] = mm(high, spread_ref[...]) + mm(low, spread_ref[...])


def near(low_ref, own_ref, high_ref, index_ref, factor_ref, out_ref):
    table = jnp.concatenate([low_ref[...], own_ref[...], high_ref[...]], axis=1)
    for lane in range(2):
        total = jnp.zeros((8, 128), F32)
        for block in range(4):
            at = (slice(block * 8, block * 8 + 8), slice(lane * 128, lane * 128 + 128))
            index = index_ref[at]
            inner, outer = index & 127, index >> 7
            found = jnp.zeros((8, 128), F32)
            for part in range(6):
                row = jnp.broadcast_to(table[:, part * 128 : part * 128 + 128], (8, 128))
                value = jnp.take_along_axis(row, inner, axis=1, mode="promise_in_bounds")
                found = jnp.where(outer == part, value, found)
            total += found * factor_ref[at]
        out_ref[:, lane * 128 : lane * 128 + 128] = jnp.sum(total, axis=0, keepdims=True)


def finish(far_ref, spread_ref, own_ref, slot_ref, near_ref, out_ref):
    high, low = split(far_ref[...])
    own = own_ref[...]
    rows = (mm(own, high) + mm(own, low)) * spread_ref[...].astype(F32)
    column = jnp.sum(rows, axis=1, keepdims=True)
    slots = jnp.transpose(jnp.broadcast_to(slot_ref[0], (128, SLOTS)))
    panel = lax.broadcasted_iota(jnp.int32, (SLOTS, 128), 1)
    for lane in range(2):
        part = jnp.where(slots == panel + lane * 128, column, 0.0)
        at = slice(lane * 128, lane * 128 + 128)
        out_ref[:, at] = jnp.sum(part, axis=0, keepdims=True) + near_ref[:, at]


def swap(value, axis, count):
    rows = value.shape[0]
    return lax.all_to_all(value.reshape(count, rows // count, 128), axis, 0, 0, tiled=True).reshape(rows, 128)


def arrange_green(green, slab, pencil):
    plane = lax.ppermute(green[:, 0, :], "pencil", [(4, 0)])
    chosen = jnp.where(pencil < 4, green[:, :KZ], jnp.flip(green[:, 1 : KZ + 1], axis=1))
    zero = chosen[:, 0, :]
    line = lax.broadcasted_iota(jnp.int32, zero.shape, 0) == 0
    ends = line & ((slab == 0) | (slab == 16))
    both = jnp.where(ends, 0.5 * (zero + plane), jnp.where(slab >= 16, plane, zero))
    both = jnp.where(pencil == 0, both, zero)
    differ = jnp.where(ends & (pencil == 0), 0.5 * (zero - plane), 0.0)
    place = lax.broadcasted_iota(jnp.int32, chosen.shape, 1) == 0
    chosen = jnp.where(place, both[:, None, :], chosen)
    other = jnp.where(place, differ[:, None, :], 0.0)

    def order(value):
        return value.reshape(8, KZ, 16, 32).transpose(3, 0, 2, 1).reshape(256, 256)

    return order(chosen), order(other)


def per_device(strength, stencil_weight, slot_panel, slot_anchor, green_spectrum, near_index, near_factor):
    slab = lax.axis_index("slab")
    pencil = lax.axis_index("pencil")
    flags = jnp.stack([pencil == 0, (pencil == 0) & ((slab == 0) | (slab == 16))]).astype(jnp.int32)
    row = strength.reshape(1, PAN_DEV)

    z_fwd, z_bwd = (pair(t) for t in z_tables())
    y_fwd, y_fwd_shared, y_bwd, y_bwd_shared = (pair(t) for t in y_tables())
    rows, rows_back, cosine, sine, lanes, lanes_back = x_tables()
    rows, rows_back, lanes, lanes_back = (pair(t) for t in (rows, rows_back, lanes, lanes_back))
    cosine, sine = jnp.asarray(cosine, F32), jnp.asarray(sine, F32)
    order = np.zeros((128, 128))
    for dx in range(4):
        for dy in range(4):
            for dz in range(4):
                order[dx * 16 + dz * 4 + dy, dx * 16 + dy * 4 + dz] = 1.0
    order[64, 64] = 1.0
    order = jnp.asarray(order, BF16)
    index = np.arange(SLOTS)
    spread = jnp.asarray((index % CAP)[:, None] == np.arange(128)[None, :], BF16)
    own = jnp.asarray((index // CAP)[:, None] == np.arange(N_SLAB)[None, :], BF16)

    shape = jax.ShapeDtypeStruct
    payload = call(pack, shape((SLOTS, 128), F32), stencil_weight, row, slot_panel)
    arrived = swap(payload, "slab", N_SLAB)
    common = [
        pltpu.VMEM((64, SLOTS), F32),
        pltpu.VMEM((PENCIL_ROWS, SLOTS), jnp.int32),
        pltpu.VMEM((PENCIL_ROWS, SLOTS), F32),
    ]
    after_z = call(
        project, shape((1024, 128), F32), arrived, slot_anchor, order, *z_fwd,
        scratch=common + [pltpu.VMEM((512, EDGE * SLOTS), BF16)] * 2 + [pltpu.VMEM((GZ, EDGE * SLOTS), BF16)],
    )
    by_y = swap(after_z, "pencil", N_PENCIL)
    after_y = call(
        y_forward, shape((1024, 128), F32), flags, by_y, *y_fwd, *y_fwd_shared,
        scratch=[pltpu.VMEM((512, 256), F32)], smem=(0,),
    )
    by_x = swap(after_y, "slab", N_SLAB)
    green, other = arrange_green(green_spectrum, slab, pencil)
    after_x = call(
        x_stage, shape((1024, 128), F32), flags, by_x, *rows, *rows_back, cosine, sine, *lanes, *lanes_back, green, other,
        scratch=[pltpu.VMEM((256, 256), F32)] * 2, smem=(0,),
    )
    back_x = swap(after_x, "slab", N_SLAB)
    back_y = call(
        y_backward, shape((1024, 128), F32), flags, back_x, *y_bwd, *y_bwd_shared,
        scratch=[pltpu.VMEM((512, 256), F32)], smem=(0,),
    )
    by_z = swap(back_y, "pencil", N_PENCIL)
    sampled = call(
        sample, shape((N_SLAB, 128), F32), by_z, arrived, slot_anchor, order, *z_bwd, spread,
        scratch=common
        + [pltpu.VMEM((512, 256), F32)]
        + [pltpu.VMEM((512, 256), BF16)] * 2
        + [pltpu.VMEM((GZ, EDGE * SLOTS), BF16), pltpu.VMEM((PENCIL_ROWS, SLOTS), F32)],
    )
    far = lax.all_to_all(sampled, "slab", 0, 0, tiled=True)
    forward = [(i, (i + 1) % N_SLAB) for i in range(N_SLAB)]
    backward = [(target, source) for source, target in forward]
    low = lax.ppermute(row, "slab", forward)
    high = lax.ppermute(row, "slab", backward)
    near_field = call(near, shape((1, PAN_DEV), F32), low, row, high, near_index, near_factor)
    return call(finish, shape((1, PAN_DEV), F32), far, spread, own, slot_panel, near_field).reshape(PAN_DEV)


def solution(mesh):
    in_specs = (
        P(("slab", "pencil")),
        P(None, ("slab", "pencil")),
        P("slab", "pencil", None),
        P("slab", "pencil", None),
        P("slab", "pencil", None),
        P(None, ("slab", "pencil")),
        P(None, ("slab", "pencil")),
    )
    out_specs = P(("slab", "pencil"))
    return jax.shard_map(
        per_device, mesh=mesh, in_specs=in_specs, out_specs=out_specs, check_vma=False
    )
```

time: 877 us -> 153 us (0.17)
  local copies, waits for them, and re-layouts: 401 us -> 25.1 us
  other arithmetic: 302 us -> 2.11 us
  matrix products: 49.8 us -> 0 us
  waiting for transfers between devices: 75.2 us -> 29.6 us
  blocking collectives: 0 us -> 34.5 us
  Pallas kernels: 0 us -> 29.6 us
  starting transfers between devices: 40.3 us -> 30.6 us
    gather x6 -> x0, local copies, waits for them, and re-layouts: 310 us -> none  [the longest x1 271 us: per_device(): sampled = potential[grid_cells]]
    scatter-add x2 -> x0, other arithmetic: 263 us -> none  [the longest x1 256 us: per_device(): charge = jnp.zeros((slab_rows * pencil_rows * GZ,), jnp.float32).at[grid_...]
    dot_general x6 -> x0, matrix products: 49.8 us -> none  [contract(): return jnp.einsum(form, left, right, precision=lax.Precision.HIGHEST)]
    all_to_all x6 -> x4, waiting for transfers between devices: 75.2 us -> 26.6 us  [the longest x3 23.4 us: swap(): lax.all_to_all(value.reshape(count, rows // count, 128), axis, 0, 0, tile...]
    all_to_all x0 -> x2, blocking collectives: none -> 34.5 us  [swap(): lax.all_to_all(value.reshape(count, rows // count, 128), axis, 0, 0, tile...]
    unnamed x48 -> x72, local copies, waits for them, and re-layouts: 46.1 us -> 12.4 us
    pallas_call x0 -> x8, Pallas kernels: none -> 29.6 us  [call(): pl.pallas_call(kernel, out_shape=out_shape, in_specs=specs, out_specs=[ou...]
    all_to_all x10 -> x0, local copies, waits for them, and re-layouts: 22.9 us -> none  [the longest x1 7.84 us: convolve(): lax.all_to_all(back_y, 'pencil', split_axis=1, concat_axis=2, tiled=True)]
  transfers between devices with their start and end apart: 8 -> 7, of which waited for: 5 -> 6; matrix products, arithmetic and copies ran while one was open for 44% -> 10% of each run, Pallas kernels for 0% -> 6%
where the time goes in v1:
time: 153 us; the launch traced here: 152 us
  blocking collectives  34.5 us (23%)
  starting transfers between devices  30.6 us (20%)
  Pallas kernels  29.6 us (19%)
  waiting for transfers between devices  29.6 us (19%)
  local copies, waits for them, and re-layouts  25.1 us (16%)
  other arithmetic  2.11 us (1%)
    all_to_all x2, blocking collectives, swap(): lax.all_to_all(value.reshape(count, rows // count, 128), axis, 0, 0, tile...  34.5 us
    pallas_call x8, Pallas kernels, call(): pl.pallas_call(kernel, out_shape=out_shape, in_specs=specs, out_specs=[ou...  29.6 us
    all_to_all x3, waiting for transfers between devices, swap(): lax.all_to_all(value.reshape(count, rows // count, 128), axis, 0, 0, tile...  23.4 us
    all_to_all x3, starting transfers between devices, swap(): lax.all_to_all(value.reshape(count, rows // count, 128), axis, 0, 0, tile...  21.6 us
    unnamed x72, local copies, waits for them, and re-layouts  12.4 us
    all_to_all x1, starting transfers between devices, per_device(): far = lax.all_to_all(sampled, 'slab', 0, 0, tiled=True)  5.57 us
    reshape x3, local copies, waits for them, and re-layouts, order(): return value.reshape(8, KZ, 16, 32).transpose(3, 0, 2, 1).reshape(256, 256)  5.23 us
    broadcast_in_dim x4, local copies, waits for them, and re-layouts, arrange_green(): other = jnp.where(place, differ[:, None, :], 0.0)  5.19 us
  transfers between devices with their start and end apart: 7, of which 6 were waited for; matrix products, arithmetic and copies ran while one was open for 10% of the time, Pallas kernels for 6%

profile of v1, /device:TPU:2, one launch (start us, length us, event | category | flops | bytes accessed | tf_op | source)
XLA Modules:
  0.0 151.9 jit_solution(18207693528158618792)
XLA Ops:
  0.0 0.8 copy-done.26
  0.8 0.7 copy-done.29
  1.5 0.7 copy-done.33
  2.2 1.2 pack.1
  3.4 11.6 %all-to-all-start = ((f32[32,24,128]{2,1,0:T(8,128)}), f32[32,24,128]{2,1,0:T(8,128)S(1)}, u32[]{:S(2)}, u32[]{:S(2)}) async-start(f32[32,24,128]{2,1,0:T(8,128)} %bitcast.3), calls=%async_computation | async-start | bytes 786432 | tf_op jit(solution)/shard_map/all_to_all | solution.py:373
  15.0 0.0 copy-start.14
  15.0 0.0 copy-start.15
  15.0 0.0 copy-start.16
  15.0 1.1 slice.15
  16.1 0.6 copy.52
  16.7 1.3 collective-permute-start
  18.0 11.0 %all-to-all-done = f32[32,24,128]{2,1,0:T(8,128)S(1)} async-done(((f32[32,24,128]{2,1,0:T(8,128)}), f32[32,24,128]{2,1,0:T(8,128)S(1)}, u32[]{:S(2)}, u32[]{:S(2)}) %all-to-all-start) | async-done | bytes 393248 | tf_op jit(solution)/shard_map/all_to_all | solution.py:373
  29.0 0.8 copy-done.22
  29.8 0.9 copy-done.24
  30.7 0.9 copy-done.25
  31.6 0.7 copy-done.31
  32.3 6.8 %project.1 = f32[1024,128]{1,0:T(8,128)} custom-call(f32[768,128]{1,0:T(8,128)S(1)} %bitcast.35, s32[1,1,768]{2,1,0:T(1,128)S(1)} %copy-done.31, bf16[128,128]{1,0:T(8,128)(2,1)S(1)} %copy-done.22, bf16[256,256]{1,0:T(8,128)(2,1)S(1)} %copy-done.24, bf16[256,256]{1,0:T(8,128)(2,1)S(1)} %copy-done.25), custom_call_target="tpu_custom_call" | custom-call | tf_op jit(solution)/shard_map/project/pallas_call | solution.py:119
  39.0 4.5 %all-to-all-start.1 = ((f32[8,128,128]{2,1,0:T(8,128)}), f32[8,128,128]{2,1,0:T(8,128)S(1)}, u32[]{:S(2)}, u32[]{:S(2)}) async-start(f32[8,128,128]{2,1,0:T(8,128)} %bitcast.5), calls=%async_computation.1 | async-start | bytes 1048576 | tf_op jit(solution)/shard_map/all_to_all | solution.py:373
  43.5 1.1 fusion
  44.6 0.2 copy.48
  44.8 0.1 add_convert_fusion.refs_0_.flag_ref
  44.9 9.0 %all-to-all-done.1 = f32[8,128,128]{2,1,0:T(8,128)S(1)} async-done(((f32[8,128,128]{2,1,0:T(8,128)}), f32[8,128,128]{2,1,0:T(8,128)S(1)}, u32[]{:S(2)}, u32[]{:S(2)}) %all-to-all-start.1) | async-done | bytes 524320 | tf_op jit(solution)/shard_map/all_to_all | solution.py:373
  53.9 2.5 %y_forward.1 = f32[1024,128]{1,0:T(8,128)} custom-call(s32[2]{0:T(128)S(1)} %add_convert_fusion.refs_0_.flag_ref, f32[1024,128]{1,0:T(8,128)S(1)} %bitcast.40, bf16[512,512]{1,0:T(8,128)(2,1)S(1)} %copy-done.13, bf16[512,512]{1,0:T(8,128)(2,1)S(1)} %copy-done.14, bf16[512,512]{1,0:T(8,128)(2,1)S(1)} %copy-done.15, bf16[512,512]{1,0:T(8,128)(2,1)S(1)} %copy-done.16), custom_call_target="tpu_custom_call" | custom-call | tf_op jit(solution)/shard_map/y_forward/pallas_call | solution.py:119
  56.4 5.6 %all-to-all-start.2 = ((f32[32,32,128]{2,1,0:T(8,128)}), f32[32,32,128]{2,1,0:T(8,128)S(1)}, u32[]{:S(2)}, u32[]{:S(2)}) async-start(f32[32,32,128]{2,1,0:T(8,128)} %bitcast.7), calls=%async_computation.2 | async-start | bytes 1048576 | tf_op jit(solution)/shard_map/all_to_all | solution.py:373
  62.0 0.2 copy_select_fusion
  62.2 0.1 iota.27
  62.3 0.8 multiply_select_fusion
  63.1 0.1 broadcast_select_fusion.1
  63.2 1.3 reshape.59
  64.4 3.0 %copy.44 = f32[8,16,16,32]{1,2,0,3:T(8,128)S(1)} copy(f32[8,16,16,32]{3,2,0,1:T(8,128)} %reshape.59) | data formatting | bytes 524288 | tf_op jit(solution)/shard_map/reshape | solution.py:390
  67.5 0.9 reshape.60.green_ref
  68.4 0.1 broadcast_in_dim.34
  68.5 0.1 copy.45
  68.6 0.0 copy-start.1
  68.6 0.0 copy-start.3
  68.6 0.0 copy-start.4
  68.6 1.9 %broadcast_in_dim.36 = f32[32,8,16,16]{3,2,1,0:T(8,128)} broadcast(f32[32,8,16]{2,1,0:T(8,128)S(1)} %copy.45), dimensions={0,1,2} | broadcast | bytes 278528 | tf_op jit(solution)/shard_map/jit(_where)/broadcast_in_dim | solution.py:387
  70.6 3.1 %broadcast_in_dim.37 = f32[256,256]{1,0:T(8,128)} reshape(f32[32,8,16,16]{3,2,1,0:T(8,128)} %broadcast_in_dim.36) | data formatting | bytes 524288 | tf_op jit(solution)/shard_map/jit(_where)/broadcast_in_dim | solution.py:387
  73.6 1.0 broadcast_select_fusion.other_ref
  74.6 3.4 %all-to-all-done.2 = f32[32,32,128]{2,1,0:T(8,128)S(1)} async-done(((f32[32,32,128]{2,1,0:T(8,128)}), f32[32,32,128]{2,1,0:T(8,128)S(1)}, u32[]{:S(2)}, u32[]{:S(2)}) %all-to-all-start.2) | async-done | bytes 524320 | tf_op jit(solution)/shard_map/all_to_all | solution.py:373
  78.0 0.0 copy-start.5
  78.1 1.0 copy-done.5
  79.1 1.0 copy-done.6
  80.1 1.0 copy-done.7
  81.2 1.0 copy-done.8
  82.2 0.9 copy-done.17
  83.2 0.9 copy-done.18
  84.1 3.7 %x_stage.1 = f32[1024,128]{1,0:T(8,128)S(1)} custom-call(s32[2]{0:T(128)S(1)} %add_convert_fusion.refs_0_.flag_ref, f32[1024,128]{1,0:T(8,128)S(1)} %bitcast.37, bf16[512,512]{1,0:T(8,128)(2,1)S(1)} %copy-done.1, bf16[512,512]{1,0:T(8,128)(2,1)S(1)} %copy-done.2, bf16[512,512]{1,0:T(8,128)(2,1)S(1)} %copy-done.3, bf16[512,512]{1,0:T(8,128)(2,1)S(1)} %copy-done.4, ...), custom_call_target="tpu_custom_call" | custom-call | tf_op jit(solution)/shard_map/x_stage/pallas_call | solution.py:119
  87.8 21.7 %all_to_all.36 = f32[32,32,128]{2,1,0:T(8,128)S(1)} all-to-all(f32[32,32,128]{2,1,0:T(8,128)S(1)} %bitcast.38), channel_id=1, replica_groups=mesh['slab'=32,'pencil'=8] {'slab'}, dimensions={0} | all-to-all | bytes 1048576 | tf_op jit(solution)/shard_map/all_to_all | solution.py:373
  109.5 0.0 copy-start
  109.6 0.0 copy-start.20
  109.6 0.0 copy-start.21
  109.6 0.0 copy-start.23
  109.7 1.7 %y_backward.1 = f32[1024,128]{1,0:T(8,128)S(1)} custom-call(s32[2]{0:T(128)S(1)} %add_convert_fusion.refs_0_.flag_ref, f32[1024,128]{1,0:T(8,128)S(1)} %bitcast.41, bf16[512,512]{1,0:T(8,128)(2,1)S(1)} %copy-done.9, bf16[512,512]{1,0:T(8,128)(2,1)S(1)} %copy-done.10, bf16[512,512]{1,0:T(8,128)(2,1)S(1)} %copy-done.11, bf16[512,512]{1,0:T(8,128)(2,1)S(1)} %copy-done.12), custom_call_target="tpu_custom_call" | custom-call | tf_op jit(solution)/shard_map/y_backward/pallas_call | solution.py:119
  111.4 12.8 %all_to_all.37 = f32[8,128,128]{2,1,0:T(8,128)S(1)} all-to-all(f32[8,128,128]{2,1,0:T(8,128)S(1)} %bitcast.42), channel_id=1, replica_groups=mesh['slab'=32,'pencil'=8] {'pencil'}, dimensions={0} | all-to-all | bytes 1048576 | tf_op jit(solution)/shard_map/all_to_all | solution.py:373
  124.2 12.6 %sample.1 = f32[32,128]{1,0:T(8,128)} custom-call(f32[1024,128]{1,0:T(8,128)S(1)} %bitcast.39, f32[768,128]{1,0:T(8,128)S(1)} %bitcast.36, s32[1,1,768]{2,1,0:T(1,128)S(1)} %copy-done.32, bf16[128,128]{1,0:T(8,128)(2,1)S(1)} %copy-done.23, bf16[256,256]{1,0:T(8,128)(2,1)S(1)} %copy-done.20, bf16[256,256]{1,0:T(8,128)(2,1)S(1)} %copy-done.21, ...), custom_call_target="tpu_custom_call" | custom-call | tf_op jit(solution)/shard_map/sample/pallas_call | solution.py:119
  136.8 5.6 %all-to-all-start.5 = ((f32[32,1,128]{2,1,0:T(1,128)}), f32[32,1,128]{2,1,0:T(1,128)S(1)}, u32[]{:S(2)}, u32[]{:S(2)}) async-start(f32[32,1,128]{2,1,0:T(1,128)} %bitcast.18), calls=%async_computation.5 | async-start | bytes 32768 | tf_op jit(solution)/shard_map/all_to_all | solution.py:453
  142.4 1.5 %collective-permute-start.1 = (f32[1,256]{1,0:T(1,128)S(1)}, f32[1,256]{1,0:T(1,128)S(1)}, u32[]{:S(2)}, u32[]{:S(2)}) collective-permute-start(f32[1,256]{1,0:T(1,128)S(1)} %bitcast.45), channel_id=1, source_target_pairs={{0,8},{8,16},{16,24},{24,32},{32,40},{40,48},{48,56},{56,64},{64,7... | collective-permute-start | bytes 3080 | tf_op jit(solution)/shard_map/ppermute | solution.py:456
  144.0 0.6 collective-permute-start.2
  144.5 1.5 %collective-permute-done.1.low_ref = f32[1,256]{1,0:T(1,128)S(1)} collective-permute-done((f32[1,256]{1,0:T(1,128)S(1)}, f32[1,256]{1,0:T(1,128)S(1)}, u32[]{:S(2)}, u32[]{:S(2)}) %collective-permute-start.1) | collective-permute-done | bytes 1056 | tf_op jit(solution)/shard_map/ppermute | solution.py:456
  146.1 1.5 collective-permute-done.2.high_ref
  147.5 0.2 near.1.near_ref
  147.7 3.2 %all-to-all-done.5 = f32[32,1,128]{2,1,0:T(1,128)S(1)} async-done(((f32[32,1,128]{2,1,0:T(1,128)}), f32[32,1,128]{2,1,0:T(1,128)S(1)}, u32[]{:S(2)}, u32[]{:S(2)}) %all-to-all-start.5) | async-done | bytes 16416 | tf_op jit(solution)/shard_map/all_to_all | solution.py:453
  150.9 1.0 finish.1
  (50 shorter events, 0.1 us)
Async XLA Ops:
  0.0 0.8 copy-start.26
  0.8 0.7 copy-start.29
  1.5 0.7 copy-start.33
  3.4 25.6 %all-to-all-start = ((f32[32,24,128]{2,1,0:T(8,128)}), f32[32,24,128]{2,1,0:T(8,128)S(1)}, u32[]{:S(2)}, u32[]{:S(2)}) async-start(f32[32,24,128]{2,1,0:T(8,128)} %bitcast.3), calls=%async_computation | async-start | bytes 786432 | tf_op jit(solution)/shard_map/all_to_all | solution.py:373
  15.0 38.9 %copy-start.13 = (bf16[512,512]{1,0:T(8,128)(2,1)S(1)}, bf16[512,512]{1,0:T(8,128)(2,1)}, u32[]{:S(2)}) copy-start(bf16[512,512]{1,0:T(8,128)(2,1)} %constant.75.clone.refs_2_) | copy-start | bytes 1572868
  15.0 38.8 %copy-start.14 = (bf16[512,512]{1,0:T(8,128)(2,1)S(1)}, bf16[512,512]{1,0:T(8,128)(2,1)}, u32[]{:S(2)}) copy-start(bf16[512,512]{1,0:T(8,128)(2,1)} %constant.76.clone.refs_3_) | copy-start | bytes 1572868
  15.0 38.8 %copy-start.15 = (bf16[512,512]{1,0:T(8,128)(2,1)S(1)}, bf16[512,512]{1,0:T(8,128)(2,1)}, u32[]{:S(2)}) copy-start(bf16[512,512]{1,0:T(8,128)(2,1)} %constant.77.clone.refs_4_) | copy-start | bytes 1572868
  15.0 38.8 %copy-start.16 = (bf16[512,512]{1,0:T(8,128)(2,1)S(1)}, bf16[512,512]{1,0:T(8,128)(2,1)}, u32[]{:S(2)}) copy-start(bf16[512,512]{1,0:T(8,128)(2,1)} %constant.78.clone.refs_5_) | copy-start | bytes 1572868
  16.7 45.6 %collective-permute-start = (f32[8,512]{1,0:T(8,128)}, f32[8,512]{1,0:T(8,128)}, u32[]{:S(2)}, u32[]{:S(2)}) collective-permute-start(f32[8,512]{1,0:T(8,128)} %bitcast.34), channel_id=1, source_target_pairs={{4,0},{12,8},{20,16},{28,24},{36,32},{44,40},{52,48},{60,56},{68,6... | collective-permute-start | bytes 49160 | tf_op jit(solution)/shard_map/ppermute | solution.py:377
  29.0 0.8 copy-start.22
  29.8 0.9 copy-start.24
  30.7 0.9 copy-start.25
  31.6 0.7 copy-start.31
  39.0 14.8 %all-to-all-start.1 = ((f32[8,128,128]{2,1,0:T(8,128)}), f32[8,128,128]{2,1,0:T(8,128)S(1)}, u32[]{:S(2)}, u32[]{:S(2)}) async-start(f32[8,128,128]{2,1,0:T(8,128)} %bitcast.5), calls=%async_computation.1 | async-start | bytes 1048576 | tf_op jit(solution)/shard_map/all_to_all | solution.py:373
  56.4 21.6 %all-to-all-start.2 = ((f32[32,32,128]{2,1,0:T(8,128)}), f32[32,32,128]{2,1,0:T(8,128)S(1)}, u32[]{:S(2)}, u32[]{:S(2)}) async-start(f32[32,32,128]{2,1,0:T(8,128)} %bitcast.7), calls=%async_computation.2 | async-start | bytes 1048576 | tf_op jit(solution)/shard_map/all_to_all | solution.py:373
  68.6 9.4 %copy-start.1 = (bf16[512,512]{1,0:T(8,128)(2,1)S(1)}, bf16[512,512]{1,0:T(8,128)(2,1)}, u32[]{:S(2)}) copy-start(bf16[512,512]{1,0:T(8,128)(2,1)} %constant.83.clone.rh) | copy-start | bytes 1572868
  68.6 9.4 %copy-start.2 = (bf16[512,512]{1,0:T(8,128)(2,1)S(1)}, bf16[512,512]{1,0:T(8,128)(2,1)}, u32[]{:S(2)}) copy-start(bf16[512,512]{1,0:T(8,128)(2,1)} %constant.84.clone.rl) | copy-start | bytes 1572868
  68.6 9.4 %copy-start.3 = (bf16[512,512]{1,0:T(8,128)(2,1)S(1)}, bf16[512,512]{1,0:T(8,128)(2,1)}, u32[]{:S(2)}) copy-start(bf16[512,512]{1,0:T(8,128)(2,1)} %constant.85.clone.rbh) | copy-start | bytes 1572868
  68.6 9.4 %copy-start.4 = (bf16[512,512]{1,0:T(8,128)(2,1)S(1)}, bf16[512,512]{1,0:T(8,128)(2,1)}, u32[]{:S(2)}) copy-start(bf16[512,512]{1,0:T(8,128)(2,1)} %constant.86.clone.rbl) | copy-start | bytes 1572868
  78.0 1.0 copy-start.5
  79.1 1.0 copy-start.6
  80.1 1.0 copy-start.7
  81.2 1.0 copy-start.8
  82.2 0.9 copy-start.17
  83.2 0.9 copy-start.18
  84.1 25.4 %copy-start.9 = (bf16[512,512]{1,0:T(8,128)(2,1)S(1)}, bf16[512,512]{1,0:T(8,128)(2,1)}, u32[]{:S(2)}) copy-start(bf16[512,512]{1,0:T(8,128)(2,1)} %constant.79.clone.refs_2_) | copy-start | bytes 1572868
  84.1 25.4 %copy-start.10 = (bf16[512,512]{1,0:T(8,128)(2,1)S(1)}, bf16[512,512]{1,0:T(8,128)(2,1)}, u32[]{:S(2)}) copy-start(bf16[512,512]{1,0:T(8,128)(2,1)} %constant.80.clone.refs_3_) | copy-start | bytes 1572868
  84.1 25.4 %copy-start.11 = (bf16[512,512]{1,0:T(8,128)(2,1)S(1)}, bf16[512,512]{1,0:T(8,128)(2,1)}, u32[]{:S(2)}) copy-start(bf16[512,512]{1,0:T(8,128)(2,1)} %constant.81.clone.refs_4_) | copy-start | bytes 1572868
  84.1 25.4 %copy-start.12 = (bf16[512,512]{1,0:T(8,128)(2,1)S(1)}, bf16[512,512]{1,0:T(8,128)(2,1)}, u32[]{:S(2)}) copy-start(bf16[512,512]{1,0:T(8,128)(2,1)} %constant.82.clone.refs_5_) | copy-start | bytes 1572868
  109.5 14.7 %copy-start = (bf16[768,128]{1,0:T(8,128)(2,1)S(1)}, bf16[768,128]{1,0:T(8,128)(2,1)}, u32[]{:S(2)}) copy-start(bf16[768,128]{1,0:T(8,128)(2,1)} %constant.94.clone.spread_ref) | copy-start | bytes 589828
  109.6 14.7 %copy-start.20 = (bf16[256,256]{1,0:T(8,128)(2,1)S(1)}, bf16[256,256]{1,0:T(8,128)(2,1)}, u32[]{:S(2)}) copy-start(bf16[256,256]{1,0:T(8,128)(2,1)} %constant.73.clone.zh_ref) | copy-start | bytes 393220
  109.6 14.6 %copy-start.21 = (bf16[256,256]{1,0:T(8,128)(2,1)S(1)}, bf16[256,256]{1,0:T(8,128)(2,1)}, u32[]{:S(2)}) copy-start(bf16[256,256]{1,0:T(8,128)(2,1)} %constant.74.clone.zl_ref) | copy-start | bytes 393220
  109.6 14.6 %copy-start.23 = (bf16[128,128]{1,0:T(8,128)(2,1)S(1)}, bf16[128,128]{1,0:T(8,128)(2,1)}, u32[]{:S(2)}) copy-start(bf16[128,128]{1,0:T(8,128)(2,1)} %constant.93.clone.order_ref) | copy-start | bytes 98308
  109.6 14.6 %copy-start.32 = (s32[1,1,768]{2,1,0:T(1,128)S(1)}, s32[1,1,768]{2,1,0:T(1,128)}, u32[]{:S(2)}) copy-start(s32[1,1,768]{2,1,0:T(1,128)} %anchor_ref.3) | copy-start | bytes 9220
  109.6 32.8 %copy-start.34 = (f32[256]{0:T(256)S(1)}, f32[256]{0:T(256)}, u32[]{:S(2)}) copy-start(f32[256]{0:T(256)} %param.32) | copy-start | bytes 3076
  109.6 37.9 %copy-start.27 = (s32[32,256]{1,0:T(8,128)S(1)}, s32[32,256]{1,0:T(8,128)}, u32[]{:S(2)}) copy-start(s32[32,256]{1,0:T(8,128)} %index_ref.1) | copy-start | bytes 98308
  109.6 37.9 %copy-start.28 = (f32[32,256]{1,0:T(8,128)S(1)}, f32[32,256]{1,0:T(8,128)}, u32[]{:S(2)}) copy-start(f32[32,256]{1,0:T(8,128)} %factor_ref.1) | copy-start | bytes 98308
  109.6 41.3 %copy-start.19 = (bf16[768,32]{1,0:T(8,128)(2,1)S(1)}, bf16[768,32]{1,0:T(8,128)(2,1)}, u32[]{:S(2)}) copy-start(bf16[768,32]{1,0:T(8,128)(2,1)} %constant.95.clone.own_ref) | copy-start | bytes 147460
  109.7 41.3 %copy-start.30 = (s32[1,1,768]{2,1,0:T(1,128)S(1)}, s32[1,1,768]{2,1,0:T(1,128)}, u32[]{:S(2)}) copy-start(s32[1,1,768]{2,1,0:T(1,128)} %slot_ref.3) | copy-start | bytes 9220
  136.8 14.1 %all-to-all-start.5 = ((f32[32,1,128]{2,1,0:T(1,128)}), f32[32,1,128]{2,1,0:T(1,128)S(1)}, u32[]{:S(2)}, u32[]{:S(2)}) async-start(f32[32,1,128]{2,1,0:T(1,128)} %bitcast.18), calls=%async_computation.5 | async-start | bytes 32768 | tf_op jit(solution)/shard_map/all_to_all | solution.py:453
  142.4 3.6 %collective-permute-start.1 = (f32[1,256]{1,0:T(1,128)S(1)}, f32[1,256]{1,0:T(1,128)S(1)}, u32[]{:S(2)}, u32[]{:S(2)}) collective-permute-start(f32[1,256]{1,0:T(1,128)S(1)} %bitcast.45), channel_id=1, source_target_pairs={{0,8},{8,16},{16,24},{24,32},{32,40},{40,48},{48,56},{56,64},{64,7... | collective-permute-start | bytes 3080 | tf_op jit(solution)/shard_map/ppermute | solution.py:456
  144.0 3.6 %collective-permute-start.2 = (f32[1,256]{1,0:T(1,128)S(1)}, f32[1,256]{1,0:T(1,128)S(1)}, u32[]{:S(2)}, u32[]{:S(2)}) collective-permute-start(f32[1,256]{1,0:T(1,128)S(1)} %bitcast.46), channel_id=1, source_target_pairs={{8,0},{16,8},{24,16},{32,24},{40,32},{48,40},{56,48},{64,56},{72,6... | collective-permute-start | bytes 3080 | tf_op jit(solution)/shard_map/ppermute | solution.py:457

commit v2 on v1

v2 whole, which is shorter than its diff:
```python
import math

import jax
import jax.numpy as jnp
import numpy as np
from jax import lax
from jax.experimental import pallas as pl
from jax.experimental.pallas import tpu as pltpu
from jax.sharding import PartitionSpec as P

GX = 512
GY = 256
GZ = 256
EDGE = 4
PAN_DEV = 256
CAP = 24
N_SLAB = 32
N_PENCIL = 8
SLOTS = N_SLAB * CAP
SLAB_ROWS = 16
PENCIL_ROWS = 32
KZ = 16
ROWS = 13 * N_SLAB
F32 = jnp.float32
BF16 = jnp.bfloat16


def kz_of(pencil, place):
    return np.where(
        pencil < 4, 32 * pencil + place, -(32 * (7 - pencil) + 16 + place)
    )


def z_tables():
    pencil, ri, place = np.meshgrid(np.arange(8), np.arange(2), np.arange(KZ), indexing="ij")
    kz = kz_of(pencil, place).reshape(-1)
    ri = ri.reshape(-1)
    shared = (pencil.reshape(-1) == 0) & (place.reshape(-1) == 0)
    z = np.arange(GZ)
    theta = 2 * np.pi * ((z[:, None] * kz[None, :]) % GZ) / GZ
    sign = 1.0 - 2.0 * (z % 2)
    forward = np.where(ri == 0, np.cos(theta), -np.sin(theta))
    forward = np.where(shared & (ri == 1), sign[:, None], forward)
    scale = np.where(shared, 1.0, 2.0) / GZ
    backward = (forward * scale).T
    return forward, backward


def y_tables():
    slab, ro, k8 = (a.reshape(-1) for a in np.meshgrid(np.arange(32), np.arange(2), np.arange(8), indexing="ij"))
    pencil, ri, y32 = (a.reshape(-1) for a in np.meshgrid(np.arange(8), np.arange(2), np.arange(32), indexing="ij"))
    ky = (8 * slab + k8)[:, None]
    ro = ro[:, None]
    y = (32 * pencil + y32)[None, :]
    ri = ri[None, :]
    theta = 2 * np.pi * ((ky * y) % GY) / GY
    cosine, sine = np.cos(theta), np.sin(theta)
    forward = np.where(ro == ri, cosine, np.where(ro == 0, sine, -sine))
    backward = forward.T / GY
    low = (ky > 0) & (ky < 128)
    high = ky > 128
    ends = (ky == 0) | (ky == 128)
    part = np.where(ro == 0, cosine, -sine)
    shared = np.where(low & (ri == 0), part, 0.0)
    shared = np.where(high & (ri == 1), part, shared)
    shared = np.where(ends & (ro == ri), cosine, shared)
    shared_back = (shared * np.where(ends, 1.0, 2.0)).T / GY
    return forward, shared, backward, shared_back


def x_tables():
    k1, ro, ko = (a.reshape(-1)[:, None] for a in np.meshgrid(np.arange(32), np.arange(2), np.arange(8), indexing="ij"))
    slab, ri, ki = (a.reshape(-1)[None, :] for a in np.meshgrid(np.arange(32), np.arange(2), np.arange(8), indexing="ij"))
    theta = 2 * np.pi * ((k1 * slab) % 32) / 32
    rows = np.where(ro == ri, np.cos(theta), np.where(ro == 0, np.sin(theta), -np.sin(theta)))
    rows = rows * (ko == ki)
    rows_back = rows.T / GX
    x16 = np.arange(16)
    twist = 2 * np.pi * np.arange(32)[:, None] * x16[None, :] / GX
    twist = np.repeat(np.repeat(twist, 8, axis=0), KZ, axis=1)
    inner = 2 * np.pi * ((x16[:, None] * x16[None, :]) % 16) / 16
    eye = np.eye(KZ)
    cosine, sine = np.kron(np.cos(inner), eye), np.kron(np.sin(inner), eye)
    lanes = np.block([[cosine, -sine], [sine, cosine]])
    lanes_back = lanes.T
    ro, k1 = (a.reshape(-1)[:, None] for a in np.meshgrid(np.arange(2), np.arange(32), indexing="ij"))
    ri, slab = (a.reshape(-1)[None, :] for a in np.meshgrid(np.arange(2), np.arange(32), indexing="ij"))
    theta = 2 * np.pi * ((k1 * slab) % 32) / 32
    line = np.where(ro == ri, np.cos(theta), np.where(ro == 0, np.sin(theta), -np.sin(theta)))
    line = line * np.where(ri == 1, -1.0, 1.0)
    return rows, rows_back, np.cos(twist), np.sin(twist), lanes, lanes_back, line


def pair(table):
    high = np.asarray(table, np.float32).astype(jnp.bfloat16)
    low = (np.asarray(table, np.float64) - high.astype(np.float64)).astype(jnp.bfloat16)
    return jnp.asarray(high), jnp.asarray(low)


def split(value):
    high = value.astype(BF16)
    return high, (value - high.astype(F32)).astype(BF16)


def mm(left, right):
    return jnp.dot(left, right, preferred_element_type=F32)


def mm_nt(left, right):
    return lax.dot_general(left, right, (((1,), (1,)), ((), ())), preferred_element_type=F32)


def mm3(left, right):
    return mm(left[0], right[0]) + (mm(left[0], right[1]) + mm(left[1], right[0]))


class Late:
    def __init__(self, copy, buffer):
        self.copy, self.buffer, self.here = copy, buffer, False

    def __getitem__(self, index):
        if not self.here:
            self.copy.wait()
            self.here = True
        return self.buffer[index]


def call(kernel, out_shape, *args, scratch=(), smem=(), late=(), limit=20):
    spaces = {i: pltpu.SMEM for i in smem} | {i: pltpu.HBM for i in late}
    specs = [pl.BlockSpec(memory_space=spaces.get(i, pltpu.VMEM)) for i in range(len(args))]
    multi = isinstance(out_shape, list)
    out_spec = pl.BlockSpec(memory_space=pltpu.VMEM)
    buffers = [pltpu.VMEM(args[i].shape, args[i].dtype) for i in late]
    if late:
        buffers.append(pltpu.SemaphoreType.DMA((len(late),)))
    own = len(args) + (len(out_shape) if multi else 1) + len(scratch)

    def wrapped(*refs):
        ins = list(refs[: len(args)])
        for place, i in enumerate(late):
            copy = pltpu.make_async_copy(ins[i], refs[own + place], refs[-1].at[place])
            copy.start()
            ins[i] = Late(copy, refs[own + place])
        kernel(*ins, *refs[len(args) : own])

    return pl.pallas_call(
        wrapped,
        out_shape=out_shape,
        in_specs=specs,
        out_specs=[out_spec] * len(out_shape) if multi else out_spec,
        scratch_shapes=list(scratch) + buffers,
        compiler_params=pltpu.CompilerParams(vmem_limit_bytes=limit * 2**20),
        name=kernel.__name__,
    )(*args)


def swap_groups(tiles):
    tiles = list(tiles)
    group = lax.broadcasted_iota(jnp.int32, tiles[0].shape, 1) // 16
    for bit in range(3):
        step = 1 << bit
        upper = (group & step) != 0
        for i in range(8):
            if i & step:
                continue
            low, high = tiles[i], tiles[i + step]
            tiles[i] = jnp.where(upper, pltpu.roll(high, 16 * step, 1), low)
            tiles[i + step] = jnp.where(upper, high, pltpu.roll(low, 128 - 16 * step, 1))
    return tiles


def lookup(tables, index):
    inner, outer = index & 127, index >> 7
    found = jnp.zeros((8, 128), F32)
    for part, table in enumerate(tables):
        row = jnp.broadcast_to(table, (8, 128))
        value = jnp.take_along_axis(row, inner, axis=1, mode="promise_in_bounds")
        found = jnp.where(outer == part, value, found)
    return found


def own_slots():
    slab = lax.broadcasted_iota(jnp.int32, (N_SLAB, SLOTS), 0)
    slot = lax.broadcasted_iota(jnp.int32, (N_SLAB, SLOTS), 1)
    return (slot >= slab * CAP) & (slot < slab * CAP + CAP)


def pack(slot_ref, spread_ref, lines_ref, pick_ref, other_pick_ref, weight_ref, strength_ref, out_ref):
    slots = jnp.broadcast_to(slot_ref[0], (N_SLAB, SLOTS)).astype(F32)
    by_slab = mm(jnp.where(own_slots(), slots, 0.0).astype(BF16), spread_ref[...])
    lane = lax.broadcasted_iota(jnp.int32, by_slab.shape, 1)
    by_slab = jnp.where(lane < CAP, by_slab, float(PAN_DEV))
    lines = mm(lines_ref[...], by_slab.astype(BF16))
    ones = jnp.ones((128, 128), BF16)
    panel = lax.broadcasted_iota(jnp.int32, (ROWS, 128), 1).astype(F32)
    hot = []
    for pick in (pick_ref, other_pick_ref):
        chosen = mm((lines * pick[...].astype(F32)).astype(BF16), ones)
        hot += [chosen == panel, chosen == panel + 128.0]
    hot = jnp.where(jnp.concatenate(hot, axis=1), 1.0, 0.0).astype(BF16)
    weight = weight_ref[...]
    empty = jnp.zeros_like(weight)
    values = jnp.concatenate(
        [jnp.concatenate([weight, empty], axis=1), jnp.concatenate([empty, weight], axis=1)], axis=0
    )
    high, low = split(values)
    out_ref[...] = mm_nt(hot, high) + mm_nt(hot, low)
    strength = strength_ref[...]
    tables = [strength[:, :128], strength[:, 128:]]
    index = by_slab.astype(jnp.int32)
    sent = jnp.concatenate([lookup(tables, index[i * 8 : i * 8 + 8]) for i in range(4)], axis=0)
    out_ref[pl.ds(12, N_SLAB, stride=13), :] = sent


def anchor_parts(anchor):
    return anchor >> 13, (anchor >> 8) & 31, anchor & 255


def z_hot(third, dz):
    z = lax.broadcasted_iota(jnp.int32, (GZ, SLOTS), 0)
    return jnp.where(z - dz == third, 1.0, 0.0).astype(BF16)


def y_place(second, y_ref):
    rel = lax.broadcasted_iota(jnp.int32, (PENCIL_ROWS, SLOTS), 0) - second
    y_ref[...] = jnp.where((rel >= 0) & (rel < EDGE), rel, EDGE)


def stencil_row(x, first, weight_ref):
    total = jnp.zeros((32, SLOTS), F32)
    for dx in range(EDGE):
        total = jnp.where(first == x - dx, weight_ref[dx * 32 : dx * 32 + 32, :], total)
    return total


def place_rows(rows, y_ref):
    out = []
    for block in range(PENCIL_ROWS // 8):
        pieces = []
        for lane in range(SLOTS // 128):
            at = slice(lane * 128, lane * 128 + 128)
            index = y_ref[block * 8 : block * 8 + 8, at]
            pieces.append(jnp.take_along_axis(rows[:, at], index, axis=0, mode="promise_in_bounds"))
        out.append(jnp.concatenate(pieces, axis=1))
    return jnp.concatenate(out, axis=0)


def project(arrived_ref, select_ref, spread_ref, order_ref, anchor_ref, zh_ref, zl_ref, out_ref, weight_ref, scaled_ref, y_ref, high_ref, low_ref):
    arrived = jnp.concatenate(split(arrived_ref[...]), axis=0)
    select = select_ref[...]
    total = jnp.zeros((256, SLOTS), F32)
    for half in range(2):
        turned = mm_nt(order_ref[half * 128 : half * 128 + 128, :], arrived).astype(BF16)
        turned = jnp.concatenate([turned[:, :ROWS], turned[:, ROWS:]], axis=0)
        total += mm(turned, select[half * ROWS : half * ROWS + ROWS])
    weights = total[:128] + total[128:]
    weight_ref[...] = weights
    high, low = split(arrived_ref[pl.ds(12, N_SLAB, stride=13), :])
    spread = spread_ref[...]
    strength = jnp.where(own_slots(), mm_nt(high, spread) + mm_nt(low, spread), 0.0)
    scaled_ref[...] = weights * jnp.sum(strength, axis=0, keepdims=True)
    first, second, third = anchor_parts(anchor_ref[0])
    y_place(second, y_ref)

    def step(x, carry):
        rows = stencil_row(x, first, scaled_ref)
        for dz in range(EDGE):
            high, low = split(place_rows(rows[dz * 8 : dz * 8 + 8], y_ref))
            at = pl.ds(pl.multiple_of(dz * 512 + x * PENCIL_ROWS, PENCIL_ROWS), PENCIL_ROWS)
            high_ref[at, :] = high
            low_ref[at, :] = low
        return carry

    lax.fori_loop(0, SLAB_ROWS, step, 0)
    hot = z_hot(third, 0)
    charge = jnp.zeros((512, GZ), F32)
    for dz in range(EDGE):
        at = slice(dz * 512, dz * 512 + 512)
        part = mm_nt(high_ref[at, :], hot) + mm_nt(low_ref[at, :], hot)
        charge += pltpu.roll(part, dz, 1) if dz else part
    after = mm3(split(charge), (zh_ref[...], zl_ref[...]))
    for half in range(2):
        for quarter in range(2):
            tiles = [
                after[x * 32 : x * 32 + 32, quarter * 128 : quarter * 128 + 128]
                for x in range(half * 8, half * 8 + 8)
            ]
            for g, tile in enumerate(swap_groups(tiles)):
                pencil, ri = quarter * 4 + g // 2, g % 2
                start = pencil * 128 + half * 64 + ri * 32
                out_ref[start : start + 32, :] = tile


def gathered(ref, count, rows):
    block = ref[...].reshape(count, 2, rows, 128)
    return jnp.concatenate([block[:, half].reshape(count * rows, 128) for half in range(2)], axis=1)


def scattered(value, ref, count, rows):
    for half in range(2):
        part = value[:, half * 128 : half * 128 + 128].reshape(count, rows, 128)
        for i in range(count):
            ref[(i * 2 + half) * rows : (i * 2 + half + 1) * rows, :] = part[i]


def shared_lane(shape):
    return lax.broadcasted_iota(jnp.int32, shape, 1) % KZ == 0


def y_stage(source, target):
    def kernel(flag_ref, in_ref, th_ref, tl_ref, sh_ref, sl_ref, out_ref, work_ref):
        data = split(gathered(in_ref, *source))
        work_ref[...] = mm3((th_ref[...], tl_ref[...]), data)

        @pl.when(flag_ref[0] == 1)
        def _():
            other = mm3((sh_ref[...], sl_ref[...]), data)
            work_ref[...] = jnp.where(shared_lane(other.shape), other, work_ref[...])

        scattered(work_ref[...], out_ref, *target)

    return kernel


def y_forward(*refs):
    y_stage((8, 64), (32, 16))(*refs)


def y_backward(*refs):
    y_stage((32, 16), (8, 64))(*refs)


def x_stage(flag_ref, in_ref, rh, rl, green_ref, other_ref, cos_ref, sin_ref, lh, ll, mh, ml, lbh, lbl, rbh, rbl, out_ref, re_ref, im_ref):
    data = gathered(in_ref, 32, 16)
    rows = mm3((rh[...], rl[...]), split(data)).reshape(32, 2, 8, 256)
    cosine, sine = cos_ref[...], sin_ref[...]
    lane_tables = (lh[...], ll[...])
    line_tables = (mh[...], ml[...])

    def lanes_of(re, im, cosine, sine):
        turned = jnp.concatenate([re * cosine + im * sine, im * cosine - re * sine], axis=1)
        return mm3(split(turned), lane_tables)

    full = lanes_of(rows[:, 0].reshape(256, 256), rows[:, 1].reshape(256, 256), cosine, sine)
    green = green_ref[...]
    for half in range(2):
        at = slice(half * 128, half * 128 + 128)
        re_ref[half] = full[:, at] * green[:, at]
        im_ref[half] = full[:, 256 + half * 128 : 384 + half * 128] * green[:, at]

    @pl.when(flag_ref[1] == 1)
    def _():
        line = jnp.concatenate(
            [
                jnp.concatenate([in_ref[pl.ds(half * 16 + ri * 8, 32, stride=32), :] for half in range(2)], axis=1)
                for ri in range(2)
            ],
            axis=0,
        )
        turned = mm3(line_tables, split(line))
        few = (cosine.reshape(32, 8, 256)[:, 0], sine.reshape(32, 8, 256)[:, 0])
        mirror = lanes_of(turned[:32], turned[32:], *few)
        other = other_ref[...]
        rows_at = pl.ds(0, 32, stride=8)
        for half in range(2):
            at = slice(half * 128, half * 128 + 128)
            re_ref[half, rows_at, :] += mirror[:, at] * other[:, at]
            im_ref[half, rows_at, :] += mirror[:, 256 + half * 128 : 384 + half * 128] * other[:, at]

    product = jnp.concatenate([re_ref[0], re_ref[1], im_ref[0], im_ref[1]], axis=1)
    back = mm3(split(product), (lbh[...], lbl[...]))
    re, im = back[:, :256], back[:, 256:]
    re, im = re * cosine - im * sine, im * cosine + re * sine
    rows = jnp.stack([re.reshape(32, 8, 256), im.reshape(32, 8, 256)], axis=1).reshape(512, 256)
    scattered(mm3((rbh[...], rbl[...]), split(rows)), out_ref, 32, 16)


def sample(in_ref, weight_ref, anchor_ref, zh_ref, zl_ref, spread_ref, out_ref, y_ref, after_ref, rows_ref, grid_ref):
    for half in range(2):
        for quarter in range(2):
            tiles = []
            for g in range(8):
                pencil, ri = quarter * 4 + g // 2, g % 2
                start = pencil * 128 + half * 64 + ri * 32
                tiles.append(in_ref[start : start + 32, :])
            for i, tile in enumerate(swap_groups(tiles)):
                x = half * 8 + i
                after_ref[x * 32 : x * 32 + 32, quarter * 128 : quarter * 128 + 128] = tile
    high, low = split(mm3(split(after_ref[...]), (zh_ref[...], zl_ref[...])))
    first, second, third = anchor_parts(anchor_ref[0])
    y_place(second, y_ref)

    def fill(x, carry):
        rows_ref[pl.ds(pl.multiple_of(x * 32, 32), 32), :] = stencil_row(x, first, weight_ref)
        return carry

    lax.fori_loop(0, SLAB_ROWS, fill, 0)
    total = jnp.zeros((8, SLOTS), F32)
    for dz in range(EDGE):
        hot = z_hot(third, dz)
        grid_ref[...] = mm(high, hot) + mm(low, hot)

        def step(x, total, dz=dz):
            rows = rows_ref[pl.ds(pl.multiple_of(x * 32 + dz * 8, 8), 8), :]
            cells = grid_ref[pl.ds(pl.multiple_of(x * 32, 32), 32), :] * place_rows(rows, y_ref)
            return total + jnp.sum(cells.reshape(4, 8, SLOTS), axis=0)

        total = lax.fori_loop(0, SLAB_ROWS, step, total)
    far = jnp.sum(total, axis=0, keepdims=True)
    high, low = split(jnp.where(own_slots(), jnp.broadcast_to(far, (N_SLAB, SLOTS)), 0.0))
    out_ref[...] = mm(high, spread_ref[...]) + mm(low, spread_ref[...])


def near(low_ref, own_ref, high_ref, index_ref, factor_ref, out_ref):
    table = jnp.concatenate([low_ref[...], own_ref[...], high_ref[...]], axis=1)
    tables = [table[:, part * 128 : part * 128 + 128] for part in range(6)]
    for lane in range(2):
        total = jnp.zeros((8, 128), F32)
        for block in range(4):
            at = (slice(block * 8, block * 8 + 8), slice(lane * 128, lane * 128 + 128))
            total += lookup(tables, index_ref[at]) * factor_ref[at]
        out_ref[:, lane * 128 : lane * 128 + 128] = jnp.sum(total, axis=0, keepdims=True)


def finish(far_ref, spread_ref, own_ref, slot_ref, near_ref, out_ref):
    high, low = split(far_ref[...])
    own = own_ref[...]
    rows = (mm(own, high) + mm(own, low)) * spread_ref[...].astype(F32)
    column = jnp.sum(rows, axis=1, keepdims=True)
    slots = jnp.transpose(jnp.broadcast_to(slot_ref[0], (128, SLOTS)))
    panel = lax.broadcasted_iota(jnp.int32, (SLOTS, 128), 1)
    for lane in range(2):
        part = jnp.where(slots == panel + lane * 128, column, 0.0)
        at = slice(lane * 128, lane * 128 + 128)
        out_ref[:, at] = jnp.sum(part, axis=0, keepdims=True) + near_ref[:, at]


def swap(value, axis, count):
    rows = value.shape[0]
    return lax.all_to_all(value.reshape(count, rows // count, 128), axis, 0, 0, tiled=True).reshape(rows, 128)


def arrange_green(green, slab, pencil):
    plane = lax.ppermute(green[:, 0, :], "pencil", [(4, 0)])
    chosen = jnp.where(pencil < 4, green[:, :KZ], jnp.flip(green[:, 1 : KZ + 1], axis=1))
    zero = chosen[:, 0, :]
    line = lax.broadcasted_iota(jnp.int32, zero.shape, 0) == 0
    ends = line & ((slab == 0) | (slab == 16))
    both = jnp.where(ends, 0.5 * (zero + plane), jnp.where(slab >= 16, plane, zero))
    both = jnp.where(pencil == 0, both, zero)
    differ = jnp.where(ends & (pencil == 0), 0.5 * (zero - plane), 0.0)
    place = lax.broadcasted_iota(jnp.int32, chosen.shape, 1) == 0
    chosen = jnp.where(place, both[:, None, :], chosen)
    chosen = chosen.reshape(8, KZ, 16, 32).transpose(3, 0, 2, 1).reshape(256, 256)
    first = lax.broadcasted_iota(jnp.int32, (32, 16, KZ), 2) == 0
    other = jnp.where(first, differ[0].reshape(16, 32).T[:, :, None], 0.0).reshape(32, 256)
    return chosen, other


def slot_tables():
    order = np.zeros((256, 128))
    for half in range(2):
        for dx in range(4):
            for dy in range(4):
                for dz in range(4):
                    order[half * 128 + dx * 32 + dz * 8 + dy, half * 64 + dx * 16 + dy * 4 + dz] = 1.0
    index = np.arange(SLOTS)
    spread = (index % CAP)[:, None] == np.arange(128)[None, :]
    own = (index // CAP)[:, None] == np.arange(N_SLAB)[None, :]
    line = np.arange(ROWS)
    slab, place = line // 13, line % 13
    lines = slab[:, None] == np.arange(N_SLAB)[None, :]
    lane = np.arange(128)[None, :]
    pick = lane == np.where(place < 12, place, CAP)[:, None]
    other_pick = lane == np.where(place < 12, place + 12, CAP)[:, None]
    target = slab * CAP + place
    select = np.concatenate(
        [(place[:, None] < 12) & (index[None, :] == (target + shift)[:, None]) for shift in (0, 12)]
    )
    return [jnp.asarray(t, BF16) for t in (order, spread, own, lines, pick, other_pick, select)]


def per_device(strength, stencil_weight, slot_panel, slot_anchor, green_spectrum, near_index, near_factor):
    slab = lax.axis_index("slab")
    pencil = lax.axis_index("pencil")
    flags = jnp.stack([pencil == 0, (pencil == 0) & ((slab == 0) | (slab == 16))]).astype(jnp.int32)
    row = strength.reshape(1, PAN_DEV)

    z_fwd, z_bwd = (pair(t) for t in z_tables())
    y_fwd, y_fwd_shared, y_bwd, y_bwd_shared = (pair(t) for t in y_tables())
    rows, rows_back, cosine, sine, lanes, lanes_back, line = x_tables()
    rows, rows_back, lanes, lanes_back, line = (pair(t) for t in (rows, rows_back, lanes, lanes_back, line))
    cosine, sine = jnp.asarray(cosine, F32), jnp.asarray(sine, F32)
    order, spread, own, lines, pick, other_pick, select = slot_tables()

    shape = jax.ShapeDtypeStruct
    payload = call(
        pack, shape((ROWS, 128), F32), slot_panel, spread, lines, pick, other_pick, stencil_weight, row,
        late=range(7), limit=8,
    )
    arrived = lax.all_to_all(payload.reshape(N_SLAB, 1, 13 * 128), "slab", 0, 0, tiled=True).reshape(ROWS, 128)
    after_z, weights = call(
        project, [shape((1024, 128), F32), shape((128, SLOTS), F32)], arrived, select, spread, order, slot_anchor, *z_fwd,
        scratch=[pltpu.VMEM((128, SLOTS), F32), pltpu.VMEM((PENCIL_ROWS, SLOTS), jnp.int32)]
        + [pltpu.VMEM((EDGE * 512, SLOTS), BF16)] * 2,
        late=(4, 5, 6), limit=24,
    )
    by_y = swap(after_z, "pencil", N_PENCIL)
    after_y = call(
        y_forward, shape((1024, 128), F32), flags, by_y, *y_fwd, *y_fwd_shared,
        scratch=[pltpu.VMEM((512, 256), F32)], smem=(0,), limit=12,
    )
    by_x = swap(after_y, "slab", N_SLAB)
    green, other = arrange_green(green_spectrum, slab, pencil)
    after_x = call(
        x_stage, shape((1024, 128), F32), flags, by_x, *rows, green, other, cosine, sine, *lanes, *line, *lanes_back, *rows_back,
        scratch=[pltpu.VMEM((2, 256, 128), F32)] * 2, smem=(0,), late=range(6, 16), limit=16,
    )
    forward = [(i, (i + 1) % N_SLAB) for i in range(N_SLAB)]
    backward = [(target, source) for source, target in forward]
    low = lax.ppermute(row, "slab", forward)
    high = lax.ppermute(row, "slab", backward)
    near_field = call(near, shape((1, PAN_DEV), F32), low, row, high, near_index, near_factor, limit=4)
    back_x = swap(after_x, "slab", N_SLAB)
    back_y = call(
        y_backward, shape((1024, 128), F32), flags, back_x, *y_bwd, *y_bwd_shared,
        scratch=[pltpu.VMEM((512, 256), F32)], smem=(0,), limit=12,
    )
    back_y, near_field = lax.optimization_barrier((back_y, near_field))
    by_z = swap(back_y, "pencil", N_PENCIL)
    sampled = call(
        sample, shape((N_SLAB, 128), F32), by_z, weights, slot_anchor, *z_bwd, spread,
        scratch=[pltpu.VMEM((PENCIL_ROWS, SLOTS), jnp.int32), pltpu.VMEM((512, 256), F32)]
        + [pltpu.VMEM((512, SLOTS), F32)] * 2,
        limit=20,
    )
    far = lax.all_to_all(sampled, "slab", 0, 0, tiled=True)
    return call(finish, shape((1, PAN_DEV), F32), far, spread, own, slot_panel, near_field, limit=4).reshape(PAN_DEV)


def solution(mesh):
    in_specs = (
        P(("slab", "pencil")),
        P(None, ("slab", "pencil")),
        P("slab", "pencil", None),
        P("slab", "pencil", None),
        P("slab", "pencil", None),
        P(None, ("slab", "pencil")),
        P(None, ("slab", "pencil")),
    )
    out_specs = P(("slab", "pencil"))
    return jax.shard_map(
        per_device, mesh=mesh, in_specs=in_specs, out_specs=out_specs, check_vma=False
    )
```

time: 153 us -> 153 us (level)
  blocking collectives: 34.5 us -> 26.7 us
  waiting for transfers between devices: 29.6 us -> 33.9 us
  local copies, waits for them, and re-layouts: 25.1 us -> 27.7 us
  Pallas kernels: 29.6 us -> 27.2 us
  other arithmetic: 2.11 us -> 3.91 us
    all_to_all x2 -> x1, blocking collectives: 34.5 us -> 12.8 us  [swap(): lax.all_to_all(value.reshape(count, rows // count, 128), axis, 0, 0, tile...]
    all_to_all x0 -> x1, blocking collectives: none -> 13.9 us  [per_device(): far = lax.all_to_all(sampled, 'slab', 0, 0, tiled=True)]
    all_to_all x1, starting transfers between devices: 5.57 us -> 11.6 us  [per_device(): lax.all_to_all(payload.reshape(N_SLAB, 1, 13 * 128), 'slab', 0, 0, tiled=...]
    unnamed x72 -> x88, local copies, waits for them, and re-layouts: 12.4 us -> 18.2 us
    all_to_all x3, starting transfers between devices: 21.6 us -> 16.5 us  [swap(): lax.all_to_all(value.reshape(count, rows // count, 128), axis, 0, 0, tile...]
    broadcast_in_dim x4 -> x2, local copies, waits for them, and re-layouts: 5.19 us -> 0.08 us  [arrange_green(): jnp.where(first, differ[0].reshape(16, 32).T[:, :, None], 0.0)]
    all_to_all x3, waiting for transfers between devices: 23.4 us -> 26.3 us  [swap(): lax.all_to_all(value.reshape(count, rows // count, 128), axis, 0, 0, tile...]
    pallas_call x8, Pallas kernels: 29.6 us -> 27.2 us  [call(): pl.pallas_call(wrapped, out_shape=out_shape, in_specs=specs, out_specs=[o...]
where the time goes in v2:
time: 153 us; the launch traced here: 151 us
  waiting for transfers between devices  33.9 us (22%)
  starting transfers between devices  31.5 us (21%)
  local copies, waits for them, and re-layouts  27.7 us (18%)
  Pallas kernels  27.2 us (18%)
  blocking collectives  26.7 us (17%)
  other arithmetic  3.91 us (3%)
    pallas_call x8, Pallas kernels, call(): pl.pallas_call(wrapped, out_shape=out_shape, in_specs=specs, out_specs=[o...  27.2 us
    all_to_all x3, waiting for transfers between devices, swap(): lax.all_to_all(value.reshape(count, rows // count, 128), axis, 0, 0, tile...  26.3 us
    unnamed x88, local copies, waits for them, and re-layouts  18.2 us
    all_to_all x3, starting transfers between devices, swap(): lax.all_to_all(value.reshape(count, rows // count, 128), axis, 0, 0, tile...  16.5 us
    all_to_all x1, blocking collectives, per_device(): far = lax.all_to_all(sampled, 'slab', 0, 0, tiled=True)  13.9 us
    all_to_all x1, blocking collectives, swap(): lax.all_to_all(value.reshape(count, rows // count, 128), axis, 0, 0, tile...  12.8 us
    all_to_all x1, starting transfers between devices, per_device(): lax.all_to_all(payload.reshape(N_SLAB, 1, 13 * 128), 'slab', 0, 0, tiled=...  11.6 us
    reshape x3, local copies, waits for them, and re-layouts, arrange_green(): chosen.reshape(8, KZ, 16, 32).transpose(3, 0, 2, 1).reshape(256, 256)  5.82 us
  transfers between devices with their start and end apart: 7, of which 6 were waited for; matrix products, arithmetic and copies ran while one was open for 10% of the time, Pallas kernels for 6%

profile of v2, /device:TPU:2, one launch (start us, length us, event | category | flops | bytes accessed | tf_op | source)
XLA Modules:
  0.0 151.3 jit_solution(12020713721075544645)
XLA Ops:
  0.0 0.9 copy-done
  0.9 0.9 copy-done.28
  1.8 0.9 copy-done.29
  2.7 0.9 copy-done.30
  3.6 0.8 copy-done.31
  4.5 0.7 copy-done.38
  5.1 0.7 copy-done.40
  5.8 2.7 %pack.1 = f32[416,128]{1,0:T(8,128)} custom-call(s32[1,1,768]{2,1,0:T(1,128)S(1)} %copy-done.38, bf16[768,128]{1,0:T(8,128)(2,1)S(1)} %copy-done, bf16[416,32]{1,0:T(8,128)(2,1)S(1)} %copy-done.28, bf16[416,128]{1,0:T(8,128)(2,1)S(1)} %copy-done.29, bf16[416,128]{1,0:T(8,128)(2,1)S(1)} %copy-done.30, f32[64,256]{1,0:T(8,128)S(1)} %copy-done.31, ...), custom_call_target="tpu_custom_call" | custom-call | tf_op jit(solution)/shard_map/pack/pallas_call | solution.py:146
  8.6 11.6 %all-to-all-start = ((f32[32,1,1664]{2,1,0:T(1,128)}), f32[32,1,1664]{2,1,0:T(1,128)S(1)}, u32[]{:S(2)}, u32[]{:S(2)}) async-start(f32[32,1,1664]{2,1,0:T(1,128)} %bitcast.3), calls=%async_computation | async-start | bytes 425984 | tf_op jit(solution)/shard_map/all_to_all | solution.py:501
  20.2 0.9 slice.18
  21.1 0.6 copy.59
  21.7 1.3 collective-permute-start
  23.0 1.8 %fusion.2 = (f32[8,16,512]{2,1,0:T(8,128)S(1)}, f32[8,16,512]{2,1,0:T(8,128)}) fusion(f32[8,32,512]{2,1,0:T(8,128)} %param.42), kind=kLoop, calls=%fused_computation.14 | loop fusion | bytes 1048576 | tf_op jit(solution)/shard_map/slice | solution.py:445
  24.9 0.8 copy.55
  25.7 0.1 add_convert_fusion.refs_0_
  25.8 4.6 %all-to-all-done = f32[32,1,1664]{2,1,0:T(1,128)S(1)} async-done(((f32[32,1,1664]{2,1,0:T(1,128)}), f32[32,1,1664]{2,1,0:T(1,128)S(1)}, u32[]{:S(2)}, u32[]{:S(2)}) %all-to-all-start) | async-done | bytes 213024 | tf_op jit(solution)/shard_map/all_to_all | solution.py:501
  30.4 0.0 copy-start.32
  30.4 0.8 copy-done.32
  31.2 7.0 %project.1 = (f32[1024,128]{1,0:T(8,128)}, f32[128,768]{1,0:T(8,128)S(1)}) custom-call(f32[416,128]{1,0:T(8,128)S(1)} %bitcast.38, bf16[832,768]{1,0:T(8,128)(2,1)S(1)} %copy-done.2, bf16[768,128]{1,0:T(8,128)(2,1)S(1)} %copy-done.1, bf16[256,128]{1,0:T(8,128)(2,1)S(1)} %copy-done.32, s32[1,1,768]{2,1,0:T(1,128)S(1)} %copy-done.37, ...), custom_call_target="tpu_custom_call" | custom-call | tf_op jit(solution)/shard_map/project/pallas_call | solution.py:146
  38.2 0.7 copy-done.19
  39.0 4.6 %all-to-all-start.1 = ((f32[8,128,128]{2,1,0:T(8,128)}), f32[8,128,128]{2,1,0:T(8,128)S(1)}, u32[]{:S(2)}, u32[]{:S(2)}) async-start(f32[8,128,128]{2,1,0:T(8,128)} %bitcast.5), calls=%async_computation.1 | async-start | bytes 1048576 | tf_op jit(solution)/shard_map/all_to_all | solution.py:440
  43.6 1.2 copy_select_fusion
  44.8 0.7 slice_bitcast_fusion
  45.5 8.5 %all-to-all-done.1 = f32[8,128,128]{2,1,0:T(8,128)S(1)} async-done(((f32[8,128,128]{2,1,0:T(8,128)}), f32[8,128,128]{2,1,0:T(8,128)S(1)}, u32[]{:S(2)}, u32[]{:S(2)}) %all-to-all-start.1) | async-done | bytes 524320 | tf_op jit(solution)/shard_map/all_to_all | solution.py:440
  54.0 2.5 %y_forward.1 = f32[1024,128]{1,0:T(8,128)} custom-call(s32[2]{0:T(128)S(1)} %add_convert_fusion.refs_0_, f32[1024,128]{1,0:T(8,128)S(1)} %bitcast.36, bf16[512,512]{1,0:T(8,128)(2,1)S(1)} %copy-done.15, bf16[512,512]{1,0:T(8,128)(2,1)S(1)} %copy-done.16, bf16[512,512]{1,0:T(8,128)(2,1)S(1)} %copy-done.17, bf16[512,512]{1,0:T(8,128)(2,1)S(1)} %copy-done.18), custom_call_target="tpu_custom_call" | custom-call | tf_op jit(solution)/shard_map/y_forward/pallas_call | solution.py:146
  56.5 6.2 %all-to-all-start.2 = ((f32[32,32,128]{2,1,0:T(8,128)}), f32[32,32,128]{2,1,0:T(8,128)S(1)}, u32[]{:S(2)}, u32[]{:S(2)}) async-start(f32[32,32,128]{2,1,0:T(8,128)} %bitcast.7), calls=%async_computation.2 | async-start | bytes 1048576 | tf_op jit(solution)/shard_map/all_to_all | solution.py:440
  62.7 0.1 iota.29
  62.8 0.0 collective-permute-done
  62.8 0.8 select_select_fusion
  63.6 1.0 broadcast_select_fusion
  64.6 0.3 reshape.56
  64.9 2.9 %copy.51 = f32[8,16,16,32]{1,2,0,3:T(8,128)} copy(f32[8,16,16,32]{3,2,0,1:T(8,128)S(1)} %reshape.56) | data formatting | bytes 524288 | tf_op jit(solution)/shard_map/reshape | solution.py:454
  67.9 0.0 copy-start.21
  67.9 0.0 copy-start.35
  67.9 0.0 copy-start.36
  67.9 2.6 %reshape.57.refs_4_ = f32[256,256]{1,0:T(8,128)S(1)} reshape(f32[32,8,16,16]{3,2,1,0:T(8,128)} %bitcast.45) | data formatting | bytes 524288 | tf_op jit(solution)/shard_map/reshape | solution.py:454
  70.5 0.8 fusion
  71.3 0.1 reshape_squeeze.3
  71.4 0.1 copy.52
  71.5 7.2 %all-to-all-done.2 = f32[32,32,128]{2,1,0:T(8,128)S(1)} async-done(((f32[32,32,128]{2,1,0:T(8,128)}), f32[32,32,128]{2,1,0:T(8,128)S(1)}, u32[]{:S(2)}, u32[]{:S(2)}) %all-to-all-start.2) | async-done | bytes 524320 | tf_op jit(solution)/shard_map/all_to_all | solution.py:440
  78.8 0.0 copy-start.7
  78.8 1.0 copy-done.7
  79.8 1.0 copy-done.8
  80.9 1.0 copy-done.9
  81.9 1.0 copy-done.10
  82.9 0.9 copy-done.22
  83.9 5.1 %x_stage.1 = f32[1024,128]{1,0:T(8,128)} custom-call(s32[2]{0:T(128)S(1)} %add_convert_fusion.refs_0_, f32[1024,128]{1,0:T(8,128)S(1)} %bitcast.33, bf16[512,512]{1,0:T(8,128)(2,1)S(1)} %copy-done.7, bf16[512,512]{1,0:T(8,128)(2,1)S(1)} %copy-done.8, f32[256,256]{1,0:T(8,128)S(1)} %reshape.57.refs_4_, f32[32,256]{1,0:T(8,128)S(1)} %broadcast_select_fusion.1.refs_5_, ...), custom_call_target="tpu_custom_call" | custom-call | tf_op jit(solution)/shard_map/x_stage/pallas_call | solution.py:146
  89.0 5.8 %all-to-all-start.3 = ((f32[32,32,128]{2,1,0:T(8,128)}), f32[32,32,128]{2,1,0:T(8,128)S(1)}, u32[]{:S(2)}, u32[]{:S(2)}) async-start(f32[32,32,128]{2,1,0:T(8,128)} %bitcast.14), calls=%async_computation.3 | async-start | bytes 1048576 | tf_op jit(solution)/shard_map/all_to_all | solution.py:440
  94.8 1.5 %collective-permute-start.1 = (f32[1,256]{1,0:T(1,128)S(1)}, f32[1,256]{1,0:T(1,128)S(1)}, u32[]{:S(2)}, u32[]{:S(2)}) collective-permute-start(f32[1,256]{1,0:T(1,128)S(1)} %bitcast.42), channel_id=1, source_target_pairs={{0,8},{8,16},{16,24},{24,32},{32,40},{40,48},{48,56},{56,64},{64,7... | collective-permute-start | bytes 3080 | tf_op jit(solution)/shard_map/ppermute | solution.py:521
  96.3 0.6 collective-permute-start.2
  96.9 1.6 %collective-permute-done.1.refs_0_ = f32[1,256]{1,0:T(1,128)S(1)} collective-permute-done((f32[1,256]{1,0:T(1,128)S(1)}, f32[1,256]{1,0:T(1,128)S(1)}, u32[]{:S(2)}, u32[]{:S(2)}) %collective-permute-start.1) | collective-permute-done | bytes 1056 | tf_op jit(solution)/shard_map/ppermute | solution.py:521
  98.5 1.4 collective-permute-done.2.refs_2_
  99.9 0.2 near.1.refs_4_
  100.0 10.6 %all-to-all-done.3 = f32[32,32,128]{2,1,0:T(8,128)S(1)} async-done(((f32[32,32,128]{2,1,0:T(8,128)}), f32[32,32,128]{2,1,0:T(8,128)S(1)}, u32[]{:S(2)}, u32[]{:S(2)}) %all-to-all-start.3) | async-done | bytes 524320 | tf_op jit(solution)/shard_map/all_to_all | solution.py:440
  110.6 1.0 copy-done.11
  111.7 1.0 copy-done.12
  112.7 1.0 copy-done.13
  113.8 1.0 copy-done.14
  114.8 0.0 copy-start.39
  114.8 1.7 %y_backward.1 = f32[1024,128]{1,0:T(8,128)S(1)} custom-call(s32[2]{0:T(128)S(1)} %add_convert_fusion.refs_0_, f32[1024,128]{1,0:T(8,128)S(1)} %bitcast.35, bf16[512,512]{1,0:T(8,128)(2,1)S(1)} %copy-done.11, bf16[512,512]{1,0:T(8,128)(2,1)S(1)} %copy-done.12, bf16[512,512]{1,0:T(8,128)(2,1)S(1)} %copy-done.13, bf16[512,512]{1,0:T(8,128)(2,1)S(1)} %copy-done.14), custom_call_target="tpu_custom_call" | custom-call | tf_op jit(solution)/shard_map/y_backward/pallas_call | solution.py:146
  116.6 12.8 %all_to_all.36 = f32[8,128,128]{2,1,0:T(8,128)S(1)} all-to-all(f32[8,128,128]{2,1,0:T(8,128)S(1)} %bitcast.37), channel_id=1, replica_groups=mesh['slab'=32,'pencil'=8] {'pencil'}, dimensions={0} | all-to-all | bytes 1048576 | tf_op jit(solution)/shard_map/all_to_all | solution.py:440
  129.4 7.0 %sample.1 = f32[32,128]{1,0:T(8,128)S(1)} custom-call(f32[1024,128]{1,0:T(8,128)S(1)} %bitcast.34, f32[128,768]{1,0:T(8,128)S(1)} %copy-done.20, s32[1,1,768]{2,1,0:T(1,128)S(1)} %copy-done.37, bf16[256,256]{1,0:T(8,128)(2,1)S(1)} %copy-done.24, bf16[256,256]{1,0:T(8,128)(2,1)S(1)} %copy-done.25, bf16[768,128]{1,0:T(8,128)(2,1)S(1)} %copy-done.1), custom_call_target="tpu_custom_call" | custom-call | tf_op jit(solution)/shard_map/sample/pallas_call | solution.py:146
  136.4 13.9 %all_to_all.37 = f32[32,1,128]{2,1,0:T(1,128)S(1)} all-to-all(f32[32,1,128]{2,1,0:T(1,128)S(1)} %bitcast.39), channel_id=1, replica_groups=mesh['slab'=32,'pencil'=8] {'slab'}, dimensions={0} | all-to-all | bytes 32768 | tf_op jit(solution)/shard_map/all_to_all | solution.py:537
  150.3 1.0 finish.1
  (67 shorter events, 0.2 us)
Async XLA Ops:
  0.0 0.9 copy-start
  0.9 0.9 copy-start.28
  1.8 0.9 copy-start.29
  2.7 0.9 copy-start.30
  3.6 0.8 copy-start.31
  4.5 0.7 copy-start.38
  5.1 0.7 copy-start.40
  5.8 24.6 %copy-start.1 = (bf16[768,128]{1,0:T(8,128)(2,1)S(1)}, bf16[768,128]{1,0:T(8,128)(2,1)}, u32[]{:S(2)}) copy-start(bf16[768,128]{1,0:T(8,128)(2,1)} %constant.109.clone.refs_1_.refs_2_.refs_5_) | copy-start | bytes 589828
  5.8 24.6 %copy-start.2 = (bf16[832,768]{1,0:T(8,128)(2,1)S(1)}, bf16[832,768]{1,0:T(8,128)(2,1)}, u32[]{:S(2)}) copy-start(bf16[832,768]{1,0:T(8,128)(2,1)} %constant.114.clone.refs_1_) | copy-start | bytes 3833860
  5.8 24.6 %copy-start.26 = (bf16[256,256]{1,0:T(8,128)(2,1)S(1)}, bf16[256,256]{1,0:T(8,128)(2,1)}, u32[]{:S(2)}) copy-start(bf16[256,256]{1,0:T(8,128)(2,1)} %constant.84.clone.refs_5_) | copy-start | bytes 393220
  5.8 24.6 %copy-start.27 = (bf16[256,256]{1,0:T(8,128)(2,1)S(1)}, bf16[256,256]{1,0:T(8,128)(2,1)}, u32[]{:S(2)}) copy-start(bf16[256,256]{1,0:T(8,128)(2,1)} %constant.85.clone.refs_6_) | copy-start | bytes 393220
  5.8 24.6 %copy-start.37 = (s32[1,1,768]{2,1,0:T(1,128)S(1)}, s32[1,1,768]{2,1,0:T(1,128)}, u32[]{:S(2)}) copy-start(s32[1,1,768]{2,1,0:T(1,128)} %refs_2_.7) | copy-start | bytes 9220
  8.6 21.8 %all-to-all-start = ((f32[32,1,1664]{2,1,0:T(1,128)}), f32[32,1,1664]{2,1,0:T(1,128)S(1)}, u32[]{:S(2)}, u32[]{:S(2)}) async-start(f32[32,1,1664]{2,1,0:T(1,128)} %bitcast.3), calls=%async_computation | async-start | bytes 425984 | tf_op jit(solution)/shard_map/all_to_all | solution.py:501
  21.7 41.1 %collective-permute-start = (f32[8,512]{1,0:T(8,128)}, f32[8,512]{1,0:T(8,128)S(1)}, u32[]{:S(2)}, u32[]{:S(2)}) collective-permute-start(f32[8,512]{1,0:T(8,128)} %bitcast.31), channel_id=1, source_target_pairs={{4,0},{12,8},{20,16},{28,24},{36,32},{44,40},{52,48},{60,56},{68,6... | collective-permute-start | bytes 49160 | tf_op jit(solution)/shard_map/ppermute | solution.py:444
  24.9 29.1 %copy-start.15 = (bf16[512,512]{1,0:T(8,128)(2,1)S(1)}, bf16[512,512]{1,0:T(8,128)(2,1)}, u32[]{:S(2)}) copy-start(bf16[512,512]{1,0:T(8,128)(2,1)} %constant.88.clone.refs_2_) | copy-start | bytes 1572868
  24.9 29.1 %copy-start.16 = (bf16[512,512]{1,0:T(8,128)(2,1)S(1)}, bf16[512,512]{1,0:T(8,128)(2,1)}, u32[]{:S(2)}) copy-start(bf16[512,512]{1,0:T(8,128)(2,1)} %constant.89.clone.refs_3_) | copy-start | bytes 1572868
  24.9 29.1 %copy-start.17 = (bf16[512,512]{1,0:T(8,128)(2,1)S(1)}, bf16[512,512]{1,0:T(8,128)(2,1)}, u32[]{:S(2)}) copy-start(bf16[512,512]{1,0:T(8,128)(2,1)} %constant.90.clone.refs_4_) | copy-start | bytes 1572868
  30.4 0.8 copy-start.32
  38.2 0.8 copy-start.19
  39.0 15.0 %copy-start.18 = (bf16[512,512]{1,0:T(8,128)(2,1)S(1)}, bf16[512,512]{1,0:T(8,128)(2,1)}, u32[]{:S(2)}) copy-start(bf16[512,512]{1,0:T(8,128)(2,1)} %constant.91.clone.refs_5_) | copy-start | bytes 1572868
  39.0 14.9 %all-to-all-start.1 = ((f32[8,128,128]{2,1,0:T(8,128)}), f32[8,128,128]{2,1,0:T(8,128)S(1)}, u32[]{:S(2)}, u32[]{:S(2)}) async-start(f32[8,128,128]{2,1,0:T(8,128)} %bitcast.5), calls=%async_computation.1 | async-start | bytes 1048576 | tf_op jit(solution)/shard_map/all_to_all | solution.py:440
  44.8 9.1 %copy-start.42 = (f32[8,16,512]{2,0,1:T(8,128)}, f32[8,16,512]{2,0,1:T(8,128)S(1)}, u32[]{:S(2)}) copy-start(f32[8,16,512]{2,0,1:T(8,128)S(1)} %copy_select_fusion) | copy-start | bytes 786436
  56.5 22.2 %all-to-all-start.2 = ((f32[32,32,128]{2,1,0:T(8,128)}), f32[32,32,128]{2,1,0:T(8,128)S(1)}, u32[]{:S(2)}, u32[]{:S(2)}) async-start(f32[32,32,128]{2,1,0:T(8,128)} %bitcast.7), calls=%async_computation.2 | async-start | bytes 1048576 | tf_op jit(solution)/shard_map/all_to_all | solution.py:440
  67.9 10.9 %copy-start.3 = (bf16[512,512]{1,0:T(8,128)(2,1)S(1)}, bf16[512,512]{1,0:T(8,128)(2,1)}, u32[]{:S(2)}) copy-start(bf16[512,512]{1,0:T(8,128)(2,1)} %constant.100.clone.refs_8_) | copy-start | bytes 1572868
  67.9 10.9 %copy-start.4 = (bf16[512,512]{1,0:T(8,128)(2,1)S(1)}, bf16[512,512]{1,0:T(8,128)(2,1)}, u32[]{:S(2)}) copy-start(bf16[512,512]{1,0:T(8,128)(2,1)} %constant.101.clone.refs_9_) | copy-start | bytes 1572868
  67.9 10.9 %copy-start.5 = (bf16[512,512]{1,0:T(8,128)(2,1)S(1)}, bf16[512,512]{1,0:T(8,128)(2,1)}, u32[]{:S(2)}) copy-start(bf16[512,512]{1,0:T(8,128)(2,1)} %constant.102.clone.refs_12_) | copy-start | bytes 1572868
  67.9 10.9 %copy-start.6 = (bf16[512,512]{1,0:T(8,128)(2,1)S(1)}, bf16[512,512]{1,0:T(8,128)(2,1)}, u32[]{:S(2)}) copy-start(bf16[512,512]{1,0:T(8,128)(2,1)} %constant.103.clone.refs_13_) | copy-start | bytes 1572868
  67.9 10.9 %copy-start.21 = (f32[256,256]{1,0:T(8,128)S(1)}, f32[256,256]{1,0:T(8,128)}, u32[]{:S(2)}) copy-start(f32[256,256]{1,0:T(8,128)} %constant.106.clone.refs_6_) | copy-start | bytes 786436
  67.9 10.9 %copy-start.35 = (bf16[64,64]{1,0:T(8,128)(2,1)S(1)}, bf16[64,64]{1,0:T(8,128)(2,1)}, u32[]{:S(2)}) copy-start(bf16[64,64]{1,0:T(8,128)(2,1)} %constant.104.clone.refs_10_) | copy-start | bytes 24580
  67.9 10.9 %copy-start.36 = (bf16[64,64]{1,0:T(8,128)(2,1)S(1)}, bf16[64,64]{1,0:T(8,128)(2,1)}, u32[]{:S(2)}) copy-start(bf16[64,64]{1,0:T(8,128)(2,1)} %constant.105.clone.refs_11_) | copy-start | bytes 24580
  78.8 1.0 copy-start.7
  79.8 1.0 copy-start.8
  80.9 1.0 copy-start.9
  81.9 1.0 copy-start.10
  82.9 0.9 copy-start.22
  83.9 10.9 %copy-start.41 = (f32[256]{0:T(256)S(1)}, f32[256]{0:T(256)}, u32[]{:S(2)}) copy-start(f32[256]{0:T(256)} %param.38) | copy-start | bytes 3076
  83.9 16.0 %copy-start.33 = (s32[32,256]{1,0:T(8,128)S(1)}, s32[32,256]{1,0:T(8,128)}, u32[]{:S(2)}) copy-start(s32[32,256]{1,0:T(8,128)} %refs_3_.8) | copy-start | bytes 98308
  83.9 16.0 %copy-start.34 = (f32[32,256]{1,0:T(8,128)S(1)}, f32[32,256]{1,0:T(8,128)}, u32[]{:S(2)}) copy-start(f32[32,256]{1,0:T(8,128)} %refs_4_.7) | copy-start | bytes 98308
  89.0 21.7 %all-to-all-start.3 = ((f32[32,32,128]{2,1,0:T(8,128)}), f32[32,32,128]{2,1,0:T(8,128)S(1)}, u32[]{:S(2)}, u32[]{:S(2)}) async-start(f32[32,32,128]{2,1,0:T(8,128)} %bitcast.14), calls=%async_computation.3 | async-start | bytes 1048576 | tf_op jit(solution)/shard_map/all_to_all | solution.py:440
  94.8 3.8 %collective-permute-start.1 = (f32[1,256]{1,0:T(1,128)S(1)}, f32[1,256]{1,0:T(1,128)S(1)}, u32[]{:S(2)}, u32[]{:S(2)}) collective-permute-start(f32[1,256]{1,0:T(1,128)S(1)} %bitcast.42), channel_id=1, source_target_pairs={{0,8},{8,16},{16,24},{24,32},{32,40},{40,48},{48,56},{56,64},{64,7... | collective-permute-start | bytes 3080 | tf_op jit(solution)/shard_map/ppermute | solution.py:521
  96.3 3.6 %collective-permute-start.2 = (f32[1,256]{1,0:T(1,128)S(1)}, f32[1,256]{1,0:T(1,128)S(1)}, u32[]{:S(2)}, u32[]{:S(2)}) collective-permute-start(f32[1,256]{1,0:T(1,128)S(1)} %bitcast.43), channel_id=1, source_target_pairs={{8,0},{16,8},{24,16},{32,24},{40,32},{48,40},{56,48},{64,56},{72,6... | collective-permute-start | bytes 3080 | tf_op jit(solution)/shard_map/ppermute | solution.py:522
  110.6 1.0 copy-start.11
  111.7 1.0 copy-start.12
  112.7 1.0 copy-start.13
  113.8 1.0 copy-start.14
  114.8 14.6 %copy-start.20 = (f32[128,768]{1,0:T(8,128)S(1)}, f32[128,768]{1,0:T(8,128)}, u32[]{:S(2)}) copy-start(f32[128,768]{1,0:T(8,128)} %copy-done.19) | copy-start | bytes 1179652
  114.8 14.6 %copy-start.24 = (bf16[256,256]{1,0:T(8,128)(2,1)S(1)}, bf16[256,256]{1,0:T(8,128)(2,1)}, u32[]{:S(2)}) copy-start(bf16[256,256]{1,0:T(8,128)(2,1)} %constant.86.clone.refs_3_) | copy-start | bytes 393220
  114.8 14.6 %copy-start.25 = (bf16[256,256]{1,0:T(8,128)(2,1)S(1)}, bf16[256,256]{1,0:T(8,128)(2,1)}, u32[]{:S(2)}) copy-start(bf16[256,256]{1,0:T(8,128)(2,1)} %constant.87.clone.refs_4_) | copy-start | bytes 393220
  114.8 35.5 %copy-start.23 = (bf16[768,32]{1,0:T(8,128)(2,1)S(1)}, bf16[768,32]{1,0:T(8,128)(2,1)}, u32[]{:S(2)}) copy-start(bf16[768,32]{1,0:T(8,128)(2,1)} %constant.110.clone.refs_2_) | copy-start | bytes 147460
  114.8 35.5 %copy-start.39 = (s32[1,1,768]{2,1,0:T(1,128)S(1)}, s32[1,1,768]{2,1,0:T(1,128)}, u32[]{:S(2)}) copy-start(s32[1,1,768]{2,1,0:T(1,128)} %refs_3_.9) | copy-start | bytes 9220

commit v3 on v2

--- a/solution.py
+++ b/solution.py
@@ -74,7 +74,6 @@
     theta = 2 * np.pi * ((k1 * slab) % 32) / 32
     rows = np.where(ro == ri, np.cos(theta), np.where(ro == 0, np.sin(theta), -np.sin(theta)))
     rows = rows * (ko == ki)
-    rows_back = rows.T / GX
     x16 = np.arange(16)
     twist = 2 * np.pi * np.arange(32)[:, None] * x16[None, :] / GX
     twist = np.repeat(np.repeat(twist, 8, axis=0), KZ, axis=1)
@@ -82,19 +81,18 @@
     eye = np.eye(KZ)
     cosine, sine = np.kron(np.cos(inner), eye), np.kron(np.sin(inner), eye)
     lanes = np.block([[cosine, -sine], [sine, cosine]])
-    lanes_back = lanes.T
     ro, k1 = (a.reshape(-1)[:, None] for a in np.meshgrid(np.arange(2), np.arange(32), indexing="ij"))
     ri, slab = (a.reshape(-1)[None, :] for a in np.meshgrid(np.arange(2), np.arange(32), indexing="ij"))
     theta = 2 * np.pi * ((k1 * slab) % 32) / 32
     line = np.where(ro == ri, np.cos(theta), np.where(ro == 0, np.sin(theta), -np.sin(theta)))
     line = line * np.where(ri == 1, -1.0, 1.0)
-    return rows, rows_back, np.cos(twist), np.sin(twist), lanes, lanes_back, line
+    return rows, np.cos(twist), np.sin(twist), lanes, line
 
 
 def pair(table):
     high = np.asarray(table, np.float32).astype(jnp.bfloat16)
     low = (np.asarray(table, np.float64) - high.astype(np.float64)).astype(jnp.bfloat16)
-    return jnp.asarray(high), jnp.asarray(low)
+    return jnp.asarray(np.stack([high, low]))
 
 
 def split(value):
@@ -179,23 +177,36 @@
     return found
 
 
+def quotient(value, divisor):
+    return ((value.astype(F32) + 0.5) * (1.0 / divisor)).astype(jnp.int32)
+
+
 def own_slots():
     slab = lax.broadcasted_iota(jnp.int32, (N_SLAB, SLOTS), 0)
     slot = lax.broadcasted_iota(jnp.int32, (N_SLAB, SLOTS), 1)
     return (slot >= slab * CAP) & (slot < slab * CAP + CAP)
 
 
-def pack(slot_ref, spread_ref, lines_ref, pick_ref, other_pick_ref, weight_ref, strength_ref, out_ref):
+def pack(slot_ref, weight_ref, strength_ref, out_ref):
     slots = jnp.broadcast_to(slot_ref[0], (N_SLAB, SLOTS)).astype(F32)
-    by_slab = mm(jnp.where(own_slots(), slots, 0.0).astype(BF16), spread_ref[...])
+    index = lax.broadcasted_iota(jnp.int32, (SLOTS, 128), 0)
+    lane = lax.broadcasted_iota(jnp.int32, (SLOTS, 128), 1)
+    spread = jnp.where((lane < CAP) & (quotient(index, CAP) * CAP + lane == index), 1.0, 0.0)
+    by_slab = mm(jnp.where(own_slots(), slots, 0.0).astype(BF16), spread.astype(BF16))
     lane = lax.broadcasted_iota(jnp.int32, by_slab.shape, 1)
     by_slab = jnp.where(lane < CAP, by_slab, float(PAN_DEV))
-    lines = mm(lines_ref[...], by_slab.astype(BF16))
+    line = lax.broadcasted_iota(jnp.int32, (ROWS, 128), 0)
+    lane = lax.broadcasted_iota(jnp.int32, (ROWS, 128), 1)
+    slab = quotient(line, 13)
+    place = line - slab * 13
+    mine = jnp.where(lane == slab, 1.0, 0.0).astype(BF16)[:, :N_SLAB]
+    lines = mm(mine, by_slab.astype(BF16))
     ones = jnp.ones((128, 128), BF16)
-    panel = lax.broadcasted_iota(jnp.int32, (ROWS, 128), 1).astype(F32)
+    panel = lane.astype(F32)
     hot = []
-    for pick in (pick_ref, other_pick_ref):
-        chosen = mm((lines * pick[...].astype(F32)).astype(BF16), ones)
+    for shift in (0, 12):
+        pick = lane == jnp.where(place < 12, place + shift, CAP)
+        chosen = mm(jnp.where(pick, lines, 0.0).astype(BF16), ones)
         hot += [chosen == panel, chosen == panel + 128.0]
     hot = jnp.where(jnp.concatenate(hot, axis=1), 1.0, 0.0).astype(BF16)
     weight = weight_ref[...]
@@ -245,7 +256,7 @@
     return jnp.concatenate(out, axis=0)
 
 
-def project(arrived_ref, select_ref, spread_ref, order_ref, anchor_ref, zh_ref, zl_ref, out_ref, weight_ref, scaled_ref, y_ref, high_ref, low_ref):
+def project(arrived_ref, select_ref, spread_ref, order_ref, anchor_ref, z_ref, out_ref, weight_ref, scaled_ref, y_ref, high_ref, low_ref):
     arrived = jnp.concatenate(split(arrived_ref[...]), axis=0)
     select = select_ref[...]
     total = jnp.zeros((256, SLOTS), F32)
@@ -278,7 +289,7 @@
         at = slice(dz * 512, dz * 512 + 512)
         part = mm_nt(high_ref[at, :], hot) + mm_nt(low_ref[at, :], hot)
         charge += pltpu.roll(part, dz, 1) if dz else part
-    after = mm3(split(charge), (zh_ref[...], zl_ref[...]))
+    after = mm3(split(charge), z_ref[...])
     for half in range(2):
         for quarter in range(2):
             tiles = [
@@ -308,13 +319,13 @@
 
 
 def y_stage(source, target):
-    def kernel(flag_ref, in_ref, th_ref, tl_ref, sh_ref, sl_ref, out_ref, work_ref):
+    def kernel(flag_ref, in_ref, table_ref, shared_ref, out_ref, work_ref):
         data = split(gathered(in_ref, *source))
-        work_ref[...] = mm3((th_ref[...], tl_ref[...]), data)
+        work_ref[...] = mm3(table_ref[...], data)
 
         @pl.when(flag_ref[0] == 1)
         def _():
-            other = mm3((sh_ref[...], sl_ref[...]), data)
+            other = mm3(shared_ref[...], data)
             work_ref[...] = jnp.where(shared_lane(other.shape), other, work_ref[...])
 
         scattered(work_ref[...], out_ref, *target)
@@ -330,12 +341,12 @@
     y_stage((32, 16), (8, 64))(*refs)
 
 
-def x_stage(flag_ref, in_ref, rh, rl, green_ref, other_ref, cos_ref, sin_ref, lh, ll, mh, ml, lbh, lbl, rbh, rbl, out_ref, re_ref, im_ref):
-    data = gathered(in_ref, 32, 16)
-    rows = mm3((rh[...], rl[...]), split(data)).reshape(32, 2, 8, 256)
+def x_stage(flag_ref, in_ref, row_ref, green_ref, other_ref, cos_ref, sin_ref, lane_ref, line_ref, out_ref, re_ref, im_ref):
+    row_tables = row_ref[...]
+    rows = mm3(row_tables, split(gathered(in_ref, 32, 16))).reshape(32, 2, 8, 256)
     cosine, sine = cos_ref[...], sin_ref[...]
-    lane_tables = (lh[...], ll[...])
-    line_tables = (mh[...], ml[...])
+    lane_tables = lane_ref[...]
+    line_tables = line_ref[...]
 
     def lanes_of(re, im, cosine, sine):
         turned = jnp.concatenate([re * cosine + im * sine, im * cosine - re * sine], axis=1)
@@ -367,15 +378,17 @@
             re_ref[half, rows_at, :] += mirror[:, at] * other[:, at]
             im_ref[half, rows_at, :] += mirror[:, 256 + half * 128 : 384 + half * 128] * other[:, at]
 
-    product = jnp.concatenate([re_ref[0], re_ref[1], im_ref[0], im_ref[1]], axis=1)
-    back = mm3(split(product), (lbh[...], lbl[...]))
+    product = jnp.concatenate([re_ref[0], re_ref[1], -im_ref[0], -im_ref[1]], axis=1)
+    back = mm3(split(product), lane_tables)
     re, im = back[:, :256], back[:, 256:]
-    re, im = re * cosine - im * sine, im * cosine + re * sine
+    re, im = re * cosine + im * sine, im * cosine - re * sine
     rows = jnp.stack([re.reshape(32, 8, 256), im.reshape(32, 8, 256)], axis=1).reshape(512, 256)
-    scattered(mm3((rbh[...], rbl[...]), split(rows)), out_ref, 32, 16)
-
-
-def sample(in_ref, weight_ref, anchor_ref, zh_ref, zl_ref, spread_ref, out_ref, y_ref, after_ref, rows_ref, grid_ref):
+    rows = mm3(row_tables, split(rows)).reshape(32, 2, 8, 256) * (1.0 / GX)
+    rows = jnp.stack([rows[:, 0], -rows[:, 1]], axis=1).reshape(512, 256)
+    scattered(rows, out_ref, 32, 16)
+
+
+def sample(in_ref, weight_ref, anchor_ref, z_ref, spread_ref, out_ref, y_ref, after_ref, rows_ref, grid_ref):
     for half in range(2):
         for quarter in range(2):
             tiles = []
@@ -386,7 +399,7 @@
             for i, tile in enumerate(swap_groups(tiles)):
                 x = half * 8 + i
                 after_ref[x * 32 : x * 32 + 32, quarter * 128 : quarter * 128 + 128] = tile
-    high, low = split(mm3(split(after_ref[...]), (zh_ref[...], zl_ref[...])))
+    high, low = split(mm3(split(after_ref[...]), z_ref[...]))
     first, second, third = anchor_parts(anchor_ref[0])
     y_place(second, y_ref)
 
@@ -468,16 +481,11 @@
     spread = (index % CAP)[:, None] == np.arange(128)[None, :]
     own = (index // CAP)[:, None] == np.arange(N_SLAB)[None, :]
     line = np.arange(ROWS)
-    slab, place = line // 13, line % 13
-    lines = slab[:, None] == np.arange(N_SLAB)[None, :]
-    lane = np.arange(128)[None, :]
-    pick = lane == np.where(place < 12, place, CAP)[:, None]
-    other_pick = lane == np.where(place < 12, place + 12, CAP)[:, None]
-    target = slab * CAP + place
+    place, target = line % 13, line // 13 * CAP + line % 13
     select = np.concatenate(
         [(place[:, None] < 12) & (index[None, :] == (target + shift)[:, None]) for shift in (0, 12)]
     )
-    return [jnp.asarray(t, BF16) for t in (order, spread, own, lines, pick, other_pick, select)]
+    return [jnp.asarray(t, BF16) for t in (order, spread, own, select)]
 
 
 def per_device(strength, stencil_weight, slot_panel, slot_anchor, green_spectrum, near_index, near_factor):
@@ -488,54 +496,52 @@
 
     z_fwd, z_bwd = (pair(t) for t in z_tables())
     y_fwd, y_fwd_shared, y_bwd, y_bwd_shared = (pair(t) for t in y_tables())
-    rows, rows_back, cosine, sine, lanes, lanes_back, line = x_tables()
-    rows, rows_back, lanes, lanes_back, line = (pair(t) for t in (rows, rows_back, lanes, lanes_back, line))
+    rows, cosine, sine, lanes, line = x_tables()
+    rows, lanes, line = (pair(t) for t in (rows, lanes, line))
     cosine, sine = jnp.asarray(cosine, F32), jnp.asarray(sine, F32)
-    order, spread, own, lines, pick, other_pick, select = slot_tables()
+    order, spread, own, select = slot_tables()
 
     shape = jax.ShapeDtypeStruct
     payload = call(
-        pack, shape((ROWS, 128), F32), slot_panel, spread, lines, pick, other_pick, stencil_weight, row,
-        late=range(7), limit=8,
-    )
+        pack, shape((ROWS, 128), F32), slot_panel, stencil_weight, row, limit=56)
     arrived = lax.all_to_all(payload.reshape(N_SLAB, 1, 13 * 128), "slab", 0, 0, tiled=True).reshape(ROWS, 128)
     after_z, weights = call(
-        project, [shape((1024, 128), F32), shape((128, SLOTS), F32)], arrived, select, spread, order, slot_anchor, *z_fwd,
+        project, [shape((1024, 128), F32), shape((128, SLOTS), F32)], arrived, select, spread, order, slot_anchor, z_fwd,
         scratch=[pltpu.VMEM((128, SLOTS), F32), pltpu.VMEM((PENCIL_ROWS, SLOTS), jnp.int32)]
         + [pltpu.VMEM((EDGE * 512, SLOTS), BF16)] * 2,
-        late=(4, 5, 6), limit=24,
+        late=(5,), limit=54,
     )
     by_y = swap(after_z, "pencil", N_PENCIL)
     after_y = call(
-        y_forward, shape((1024, 128), F32), flags, by_y, *y_fwd, *y_fwd_shared,
-        scratch=[pltpu.VMEM((512, 256), F32)], smem=(0,), limit=12,
+        y_forward, shape((1024, 128), F32), flags, by_y, y_fwd, y_fwd_shared,
+        scratch=[pltpu.VMEM((512, 256), F32)], smem=(0,), limit=40,
     )
     by_x = swap(after_y, "slab", N_SLAB)
     green, other = arrange_green(green_spectrum, slab, pencil)
     after_x = call(
-        x_stage, shape((1024, 128), F32), flags, by_x, *rows, green, other, cosine, sine, *lanes, *line, *lanes_back, *rows_back,
-        scratch=[pltpu.VMEM((2, 256, 128), F32)] * 2, smem=(0,), late=range(6, 16), limit=16,
+        x_stage, shape((1024, 128), F32), flags, by_x, rows, green, other, cosine, sine, lanes, line,
+        scratch=[pltpu.VMEM((2, 256, 128), F32)] * 2, smem=(0,), late=range(5, 9), limit=56,
     )
     forward = [(i, (i + 1) % N_SLAB) for i in range(N_SLAB)]
     backward = [(target, source) for source, target in forward]
     low = lax.ppermute(row, "slab", forward)
     high = lax.ppermute(row, "slab", backward)
-    near_field = call(near, shape((1, PAN_DEV), F32), low, row, high, near_index, near_factor, limit=4)
+    near_field = call(near, shape((1, PAN_DEV), F32), low, row, high, near_index, near_factor, limit=40)
     back_x = swap(after_x, "slab", N_SLAB)
     back_y = call(
-        y_backward, shape((1024, 128), F32), flags, back_x, *y_bwd, *y_bwd_shared,
-        scratch=[pltpu.VMEM((512, 256), F32)], smem=(0,), limit=12,
+        y_backward, shape((1024, 128), F32), flags, back_x, y_bwd, y_bwd_shared,
+        scratch=[pltpu.VMEM((512, 256), F32)], smem=(0,), limit=40,
     )
     back_y, near_field = lax.optimization_barrier((back_y, near_field))
     by_z = swap(back_y, "pencil", N_PENCIL)
     sampled = call(
-        sample, shape((N_SLAB, 128), F32), by_z, weights, slot_anchor, *z_bwd, spread,
+        sample, shape((N_SLAB, 128), F32), by_z, weights, slot_anchor, z_bwd, spread,
         scratch=[pltpu.VMEM((PENCIL_ROWS, SLOTS), jnp.int32), pltpu.VMEM((512, 256), F32)]
         + [pltpu.VMEM((512, SLOTS), F32)] * 2,
-        limit=20,
+        limit=40,
     )
     far = lax.all_to_all(sampled, "slab", 0, 0, tiled=True)
-    return call(finish, shape((1, PAN_DEV), F32), far, spread, own, slot_panel, near_field, limit=4).reshape(PAN_DEV)
+    return call(finish, shape((1, PAN_DEV), F32), far, spread, own, slot_panel, near_field, limit=40).reshape(PAN_DEV)
 
 
 def solution(mesh):

time: 153 us -> 138 us (0.902)
  local copies, waits for them, and re-layouts: 27.7 us -> 6.79 us
  waiting for transfers between devices: 33.9 us -> 41.8 us
  other arithmetic: 3.91 us -> 1.1 us
  Pallas kernels: 27.2 us -> 28.9 us
    unnamed x88 -> x34, local copies, waits for them, and re-layouts: 18.2 us -> 0.92 us
    all_to_all x3, waiting for transfers between devices: 26.3 us -> 32.2 us  [swap(): lax.all_to_all(value.reshape(count, rows // count, 128), axis, 0, 0, tile...]
    reshape x3, local copies, waits for them, and re-layouts: 5.82 us -> 3.58 us  [arrange_green(): chosen.reshape(8, KZ, 16, 32).transpose(3, 0, 2, 1).reshape(256, 256)]
    all_to_all x1, waiting for transfers between devices: 4.58 us -> 6.51 us  [per_device(): lax.all_to_all(payload.reshape(N_SLAB, 1, 13 * 128), 'slab', 0, 0, tiled=...]
    pallas_call x8, Pallas kernels: 27.2 us -> 28.9 us  [call(): pl.pallas_call(wrapped, out_shape=out_shape, in_specs=specs, out_specs=[o...]
  transfers between devices with their start and end apart: 7 -> 7, of which waited for: 6 -> 6; matrix products, arithmetic and copies ran while one was open for 10% -> 5% of each run, Pallas kernels for 6% -> 8%
where the time goes in v3:
time: 138 us; the launch traced here: 137 us
  waiting for transfers between devices  41.8 us (30%)
  starting transfers between devices  31.5 us (23%)
  Pallas kernels  28.9 us (21%)
  blocking collectives  26.7 us (19%)
  local copies, waits for them, and re-layouts  6.79 us (5%)
    all_to_all x3, waiting for transfers between devices, swap(): lax.all_to_all(value.reshape(count, rows // count, 128), axis, 0, 0, tile...  32.2 us
    pallas_call x8, Pallas kernels, call(): pl.pallas_call(wrapped, out_shape=out_shape, in_specs=specs, out_specs=[o...  28.9 us
    all_to_all x3, starting transfers between devices, swap(): lax.all_to_all(value.reshape(count, rows // count, 128), axis, 0, 0, tile...  16.3 us
    all_to_all x1, blocking collectives, per_device(): far = lax.all_to_all(sampled, 'slab', 0, 0, tiled=True)  13.9 us
    all_to_all x1, blocking collectives, swap(): lax.all_to_all(value.reshape(count, rows // count, 128), axis, 0, 0, tile...  12.8 us
    all_to_all x1, starting transfers between devices, per_device(): lax.all_to_all(payload.reshape(N_SLAB, 1, 13 * 128), 'slab', 0, 0, tiled=...  11.6 us
    all_to_all x1, waiting for transfers between devices, per_device(): lax.all_to_all(payload.reshape(N_SLAB, 1, 13 * 128), 'slab', 0, 0, tiled=...  6.51 us
    reshape x3, local copies, waits for them, and re-layouts, arrange_green(): chosen.reshape(8, KZ, 16, 32).transpose(3, 0, 2, 1).reshape(256, 256)  3.58 us
  transfers between devices with their start and end apart: 7, of which 6 were waited for; matrix products, arithmetic and copies ran while one was open for 5% of the time, Pallas kernels for 8%

profile of v3, /device:TPU:2, one launch (start us, length us, event | category | flops | bytes accessed | tf_op | source)
XLA Modules:
  0.0 137.0 jit_solution(11181321146980580584)
XLA Ops:
  0.0 2.4 %pack.1 = f32[416,128]{1,0:T(8,128)} custom-call(s32[1,1,768]{2,1,0:T(1,128)} %refs_3_.7, f32[64,256]{1,0:T(8,128)} %refs_1_.3, f32[1,256]{1,0:T(1,128)} %bitcast.39), custom_call_target="tpu_custom_call" | custom-call | tf_op jit(solution)/shard_map/pack/pallas_call | solution.py:144
  2.4 11.6 %all-to-all-start = ((f32[32,1,1664]{2,1,0:T(1,128)}), f32[32,1,1664]{2,1,0:T(1,128)S(1)}, u32[]{:S(2)}, u32[]{:S(2)}) async-start(f32[32,1,1664]{2,1,0:T(1,128)} %bitcast.46), calls=%async_computation | async-start | bytes 425984 | tf_op jit(solution)/shard_map/all_to_all | solution.py:507
  14.1 0.9 slice.18
  15.0 1.3 collective-permute-start
  16.3 1.1 fusion.2
  17.4 0.0 copy-start.3
  17.5 0.0 copy-start.4
  17.5 0.2 copy.39
  17.6 0.1 add_convert_fusion.refs_0_
  17.7 6.5 %all-to-all-done = f32[32,1,1664]{2,1,0:T(1,128)S(1)} async-done(((f32[32,1,1664]{2,1,0:T(1,128)}), f32[32,1,1664]{2,1,0:T(1,128)S(1)}, u32[]{:S(2)}, u32[]{:S(2)}) %all-to-all-start) | async-done | bytes 213024 | tf_op jit(solution)/shard_map/all_to_all | solution.py:507
  24.2 0.7 copy-done.15
  24.9 8.0 %project.1 = (f32[1024,128]{1,0:T(8,128)}, f32[128,768]{1,0:T(8,128)}) custom-call(f32[416,128]{1,0:T(8,128)} %bitcast.45, bf16[832,768]{1,0:T(8,128)(2,1)} %constant.66.clone.refs_1_, bf16[768,128]{1,0:T(8,128)(2,1)} %constant.64.clone.refs_2_.refs_4_.refs_1_, bf16[256,128]{1,0:T(8,128)(2,1)} %constant.63.clone.refs_3_, s32[1,1,768]{2,1,0:T(1,128)} %refs_2_.6, ...), custom_call_target="tpu_custom_call" | custom-call | tf_op jit(solution)/shard_map/project/pallas_call | solution.py:144
  32.9 4.5 %all-to-all-start.1 = ((f32[8,128,128]{2,1,0:T(8,128)}), f32[8,128,128]{2,1,0:T(8,128)S(1)}, u32[]{:S(2)}, u32[]{:S(2)}) async-start(f32[8,128,128]{2,1,0:T(8,128)} %bitcast.48), calls=%async_computation.1 | async-start | bytes 1048576 | tf_op jit(solution)/shard_map/all_to_all | solution.py:453
  37.4 0.2 copy_select_fusion
  37.6 10.2 %all-to-all-done.1 = f32[8,128,128]{2,1,0:T(8,128)S(1)} async-done(((f32[8,128,128]{2,1,0:T(8,128)}), f32[8,128,128]{2,1,0:T(8,128)S(1)}, u32[]{:S(2)}, u32[]{:S(2)}) %all-to-all-start.1) | async-done | bytes 524320 | tf_op jit(solution)/shard_map/all_to_all | solution.py:453
  47.8 0.0 copy-done.3
  47.8 0.0 copy-done.4
  47.8 2.5 %y_forward.1 = f32[1024,128]{1,0:T(8,128)} custom-call(s32[2]{0:T(128)S(1)} %add_convert_fusion.refs_0_, f32[1024,128]{1,0:T(8,128)S(1)} %bitcast.35, bf16[2,512,512]{2,1,0:T(8,128)(2,1)S(1)} %copy-done.3, bf16[2,512,512]{2,1,0:T(8,128)(2,1)S(1)} %copy-done.4), custom_call_target="tpu_custom_call" | custom-call | tf_op jit(solution)/shard_map/y_forward/pallas_call | solution.py:144
  50.3 0.0 copy-done.12
  50.3 6.3 %all-to-all-start.2 = ((f32[32,32,128]{2,1,0:T(8,128)}), f32[32,32,128]{2,1,0:T(8,128)}, u32[]{:S(2)}, u32[]{:S(2)}) async-start(f32[32,32,128]{2,1,0:T(8,128)} %bitcast.7), calls=%async_computation.2 | async-start | bytes 1048576 | tf_op jit(solution)/shard_map/all_to_all | solution.py:453
  56.6 0.1 iota.29
  56.7 0.0 collective-permute-done
  56.7 0.1 select_select_fusion
  56.8 0.1 broadcast_select_fusion
  56.9 0.3 reshape.56
  57.2 1.8 %copy.35 = f32[8,16,16,32]{1,2,0,3:T(8,128)S(1)} copy(f32[8,16,16,32]{3,2,0,1:T(8,128)S(1)} %reshape.56) | data formatting | bytes 524288 | tf_op jit(solution)/shard_map/reshape | solution.py:467
  59.0 1.5 %reshape.57.refs_3_ = f32[256,256]{1,0:T(8,128)} reshape(f32[32,8,16,16]{3,2,1,0:T(8,128)S(1)} %bitcast.43) | data formatting | bytes 524288 | tf_op jit(solution)/shard_map/reshape | solution.py:467
  60.5 0.1 fusion
  60.6 0.1 reshape_squeeze.3
  60.7 0.1 copy.36
  60.7 0.6 broadcast_select_fusion.1.refs_4_
  61.3 11.7 %all-to-all-done.2 = f32[32,32,128]{2,1,0:T(8,128)} async-done(((f32[32,32,128]{2,1,0:T(8,128)}), f32[32,32,128]{2,1,0:T(8,128)}, u32[]{:S(2)}, u32[]{:S(2)}) %all-to-all-start.2) | async-done | bytes 524320 | tf_op jit(solution)/shard_map/all_to_all | solution.py:453
  73.1 0.0 copy-start.2
  73.1 0.0 copy-start.13
  73.1 6.0 %x_stage.1 = f32[1024,128]{1,0:T(8,128)} custom-call(s32[2]{0:T(128)} %copy-done.12, f32[1024,128]{1,0:T(8,128)} %bitcast.8.refs_1_, bf16[2,512,512]{2,1,0:T(8,128)(2,1)} %constant.58.clone.refs_2_, f32[256,256]{1,0:T(8,128)} %reshape.57.refs_3_, f32[32,256]{1,0:T(8,128)} %broadcast_select_fusion.1.refs_4_, f32[256,256]{1,0:T(8,128)} %constant.61.clone.refs_5_, ...), custom_call_target="tpu_custom_call" | custom-call | tf_op jit(solution)/shard_map/x_stage/pallas_call | solution.py:144
  79.1 5.6 %all-to-all-start.3 = ((f32[32,32,128]{2,1,0:T(8,128)}), f32[32,32,128]{2,1,0:T(8,128)S(1)}, u32[]{:S(2)}, u32[]{:S(2)}) async-start(f32[32,32,128]{2,1,0:T(8,128)} %bitcast.44), calls=%async_computation.3 | async-start | bytes 1048576 | tf_op jit(solution)/shard_map/all_to_all | solution.py:453
  84.7 0.0 copy-done.14
  84.7 1.7 %collective-permute-start.1 = (f32[1,256]{1,0:T(1,128)S(1)}, f32[1,256]{1,0:T(1,128)S(1)}, u32[]{:S(2)}, u32[]{:S(2)}) collective-permute-start(f32[1,256]{1,0:T(1,128)S(1)} %bitcast.40), channel_id=1, source_target_pairs={{0,8},{8,16},{16,24},{24,32},{32,40},{40,48},{48,56},{56,64},{64,7... | collective-permute-start | bytes 3080 | tf_op jit(solution)/shard_map/ppermute | solution.py:527
  86.4 0.6 collective-permute-start.2
  87.0 1.6 %collective-permute-done.1.refs_0_ = f32[1,256]{1,0:T(1,128)S(1)} collective-permute-done((f32[1,256]{1,0:T(1,128)S(1)}, f32[1,256]{1,0:T(1,128)S(1)}, u32[]{:S(2)}, u32[]{:S(2)}) %collective-permute-start.1) | collective-permute-done | bytes 1056 | tf_op jit(solution)/shard_map/ppermute | solution.py:527
  88.5 1.5 %collective-permute-done.2.refs_2_ = f32[1,256]{1,0:T(1,128)S(1)} collective-permute-done((f32[1,256]{1,0:T(1,128)S(1)}, f32[1,256]{1,0:T(1,128)S(1)}, u32[]{:S(2)}, u32[]{:S(2)}) %collective-permute-start.2) | collective-permute-done | bytes 1056 | tf_op jit(solution)/shard_map/ppermute | solution.py:528
  90.0 0.0 copy-done.8
  90.0 0.0 copy-done.9
  90.0 0.2 near.1.refs_4_
  90.2 10.4 %all-to-all-done.3 = f32[32,32,128]{2,1,0:T(8,128)S(1)} async-done(((f32[32,32,128]{2,1,0:T(8,128)}), f32[32,32,128]{2,1,0:T(8,128)S(1)}, u32[]{:S(2)}, u32[]{:S(2)}) %all-to-all-start.3) | async-done | bytes 524320 | tf_op jit(solution)/shard_map/all_to_all | solution.py:453
  100.5 0.0 copy-done.1
  100.5 0.0 copy-done.2
  100.5 0.0 copy-done.13
  100.5 0.0 copy-start
  100.5 0.0 copy-start.5
  100.6 0.0 copy-start.6
  100.6 0.0 copy-start.10
  100.6 0.0 copy-start.7
  100.6 0.0 copy-start.11
  100.6 1.7 %y_backward.1 = f32[1024,128]{1,0:T(8,128)S(1)} custom-call(s32[2]{0:T(128)S(1)} %copy-done.13, f32[1024,128]{1,0:T(8,128)S(1)} %bitcast.34, bf16[2,512,512]{2,1,0:T(8,128)(2,1)S(1)} %copy-done.1, bf16[2,512,512]{2,1,0:T(8,128)(2,1)S(1)} %copy-done.2), custom_call_target="tpu_custom_call" | custom-call | tf_op jit(solution)/shard_map/y_backward/pallas_call | solution.py:144
  102.4 12.8 %all_to_all.36 = f32[8,128,128]{2,1,0:T(8,128)S(1)} all-to-all(f32[8,128,128]{2,1,0:T(8,128)S(1)} %bitcast.36), channel_id=1, replica_groups=mesh['slab'=32,'pencil'=8] {'pencil'}, dimensions={0} | all-to-all | bytes 1048576 | tf_op jit(solution)/shard_map/all_to_all | solution.py:453
  115.2 0.0 copy-done
  115.2 0.0 copy-done.5
  115.2 0.0 copy-done.6
  115.2 0.0 copy-done.10
  115.2 7.0 %sample.1 = f32[32,128]{1,0:T(8,128)S(1)} custom-call(f32[1024,128]{1,0:T(8,128)S(1)} %bitcast.33, f32[128,768]{1,0:T(8,128)S(1)} %copy-done.5, s32[1,1,768]{2,1,0:T(1,128)S(1)} %copy-done.10, bf16[2,256,256]{2,1,0:T(8,128)(2,1)S(1)} %copy-done.6, bf16[768,128]{1,0:T(8,128)(2,1)S(1)} %copy-done), custom_call_target="tpu_custom_call" | custom-call | tf_op jit(solution)/shard_map/sample/pallas_call | solution.py:144
  122.2 13.9 %all_to_all.37 = f32[32,1,128]{2,1,0:T(1,128)S(1)} all-to-all(f32[32,1,128]{2,1,0:T(1,128)S(1)} %bitcast.37), channel_id=1, replica_groups=mesh['slab'=32,'pencil'=8] {'slab'}, dimensions={0} | all-to-all | bytes 32768 | tf_op jit(solution)/shard_map/all_to_all | solution.py:543
  136.1 0.0 copy-done.7
  136.1 1.0 finish.1
  (13 shorter events, 0.1 us)
Async XLA Ops:
  2.4 21.8 %all-to-all-start = ((f32[32,1,1664]{2,1,0:T(1,128)}), f32[32,1,1664]{2,1,0:T(1,128)S(1)}, u32[]{:S(2)}, u32[]{:S(2)}) async-start(f32[32,1,1664]{2,1,0:T(1,128)} %bitcast.46), calls=%async_computation | async-start | bytes 425984 | tf_op jit(solution)/shard_map/all_to_all | solution.py:507
  15.0 41.7 %collective-permute-start = (f32[8,512]{1,0:T(8,128)S(1)}, f32[8,512]{1,0:T(8,128)S(1)}, u32[]{:S(2)}, u32[]{:S(2)}) collective-permute-start(f32[8,512]{1,0:T(8,128)S(1)} %bitcast.50), channel_id=1, source_target_pairs={{4,0},{12,8},{20,16},{28,24},{36,32},{44,40},{52,48},{60,56},{68,6... | collective-permute-start | bytes 49160 | tf_op jit(solution)/shard_map/ppermute | solution.py:457
  17.4 30.3 %copy-start.3 = (bf16[2,512,512]{2,1,0:T(8,128)(2,1)S(1)}, bf16[2,512,512]{2,1,0:T(8,128)(2,1)}, u32[]{:S(2)}) copy-start(bf16[2,512,512]{2,1,0:T(8,128)(2,1)} %constant.54.clone.refs_2_) | copy-start | bytes 3145732
  17.5 30.3 %copy-start.4 = (bf16[2,512,512]{2,1,0:T(8,128)(2,1)S(1)}, bf16[2,512,512]{2,1,0:T(8,128)(2,1)}, u32[]{:S(2)}) copy-start(bf16[2,512,512]{2,1,0:T(8,128)(2,1)} %constant.55.clone.refs_3_) | copy-start | bytes 3145732
  17.7 32.6 %copy-start.12 = (s32[2]{0:T(128)}, s32[2]{0:T(128)S(1)}, u32[]{:S(2)}) copy-start(s32[2]{0:T(128)S(1)} %add_convert_fusion.refs_0_) | copy-start | bytes 28
  24.2 0.7 copy-start.15
  32.9 14.8 %all-to-all-start.1 = ((f32[8,128,128]{2,1,0:T(8,128)}), f32[8,128,128]{2,1,0:T(8,128)S(1)}, u32[]{:S(2)}, u32[]{:S(2)}) async-start(f32[8,128,128]{2,1,0:T(8,128)} %bitcast.48), calls=%async_computation.1 | async-start | bytes 1048576 | tf_op jit(solution)/shard_map/all_to_all | solution.py:453
  50.3 22.7 %all-to-all-start.2 = ((f32[32,32,128]{2,1,0:T(8,128)}), f32[32,32,128]{2,1,0:T(8,128)}, u32[]{:S(2)}, u32[]{:S(2)}) async-start(f32[32,32,128]{2,1,0:T(8,128)} %bitcast.7), calls=%async_computation.2 | async-start | bytes 1048576 | tf_op jit(solution)/shard_map/all_to_all | solution.py:453
  73.1 11.6 %copy-start.14 = (f32[256]{0:T(256)S(1)}, f32[256]{0:T(256)}, u32[]{:S(2)}) copy-start(f32[256]{0:T(256)} %param.22) | copy-start | bytes 3076
  73.1 16.9 %copy-start.8 = (s32[32,256]{1,0:T(8,128)S(1)}, s32[32,256]{1,0:T(8,128)}, u32[]{:S(2)}) copy-start(s32[32,256]{1,0:T(8,128)} %refs_3_.6) | copy-start | bytes 98308
  73.1 16.9 %copy-start.9 = (f32[32,256]{1,0:T(8,128)S(1)}, f32[32,256]{1,0:T(8,128)}, u32[]{:S(2)}) copy-start(f32[32,256]{1,0:T(8,128)} %refs_4_.4) | copy-start | bytes 98308
  73.1 27.5 %copy-start.1 = (bf16[2,512,512]{2,1,0:T(8,128)(2,1)S(1)}, bf16[2,512,512]{2,1,0:T(8,128)(2,1)}, u32[]{:S(2)}) copy-start(bf16[2,512,512]{2,1,0:T(8,128)(2,1)} %constant.56.clone.refs_2_) | copy-start | bytes 3145732
  73.1 27.4 %copy-start.2 = (bf16[2,512,512]{2,1,0:T(8,128)(2,1)S(1)}, bf16[2,512,512]{2,1,0:T(8,128)(2,1)}, u32[]{:S(2)}) copy-start(bf16[2,512,512]{2,1,0:T(8,128)(2,1)} %constant.57.clone.refs_3_) | copy-start | bytes 3145732
  73.1 27.4 %copy-start.13 = (s32[2]{0:T(128)S(1)}, s32[2]{0:T(128)}, u32[]{:S(2)}) copy-start(s32[2]{0:T(128)} %copy-done.12) | copy-start | bytes 28
  79.1 21.4 %all-to-all-start.3 = ((f32[32,32,128]{2,1,0:T(8,128)}), f32[32,32,128]{2,1,0:T(8,128)S(1)}, u32[]{:S(2)}, u32[]{:S(2)}) async-start(f32[32,32,128]{2,1,0:T(8,128)} %bitcast.44), calls=%async_computation.3 | async-start | bytes 1048576 | tf_op jit(solution)/shard_map/all_to_all | solution.py:453
  84.7 3.8 %collective-permute-start.1 = (f32[1,256]{1,0:T(1,128)S(1)}, f32[1,256]{1,0:T(1,128)S(1)}, u32[]{:S(2)}, u32[]{:S(2)}) collective-permute-start(f32[1,256]{1,0:T(1,128)S(1)} %bitcast.40), channel_id=1, source_target_pairs={{0,8},{8,16},{16,24},{24,32},{32,40},{40,48},{48,56},{56,64},{64,7... | collective-permute-start | bytes 3080 | tf_op jit(solution)/shard_map/ppermute | solution.py:527
  86.4 3.6 %collective-permute-start.2 = (f32[1,256]{1,0:T(1,128)S(1)}, f32[1,256]{1,0:T(1,128)S(1)}, u32[]{:S(2)}, u32[]{:S(2)}) collective-permute-start(f32[1,256]{1,0:T(1,128)S(1)} %bitcast.41), channel_id=1, source_target_pairs={{8,0},{16,8},{24,16},{32,24},{40,32},{48,40},{56,48},{64,56},{72,6... | collective-permute-start | bytes 3080 | tf_op jit(solution)/shard_map/ppermute | solution.py:528
  100.5 14.6 %copy-start = (bf16[768,128]{1,0:T(8,128)(2,1)S(1)}, bf16[768,128]{1,0:T(8,128)(2,1)}, u32[]{:S(2)}) copy-start(bf16[768,128]{1,0:T(8,128)(2,1)} %constant.64.clone.refs_2_.refs_4_.refs_1_) | copy-start | bytes 589828
  100.5 14.6 %copy-start.5 = (f32[128,768]{1,0:T(8,128)S(1)}, f32[128,768]{1,0:T(8,128)}, u32[]{:S(2)}) copy-start(f32[128,768]{1,0:T(8,128)} %get-tuple-element.11.refs_1_) | copy-start | bytes 1179652
  100.6 14.6 %copy-start.6 = (bf16[2,256,256]{2,1,0:T(8,128)(2,1)S(1)}, bf16[2,256,256]{2,1,0:T(8,128)(2,1)}, u32[]{:S(2)}) copy-start(bf16[2,256,256]{2,1,0:T(8,128)(2,1)} %constant.53.clone.refs_3_) | copy-start | bytes 786436
  100.6 14.6 %copy-start.10 = (s32[1,1,768]{2,1,0:T(1,128)S(1)}, s32[1,1,768]{2,1,0:T(1,128)}, u32[]{:S(2)}) copy-start(s32[1,1,768]{2,1,0:T(1,128)} %refs_2_.6) | copy-start | bytes 9220
  100.6 35.5 %copy-start.7 = (bf16[768,32]{1,0:T(8,128)(2,1)S(1)}, bf16[768,32]{1,0:T(8,128)(2,1)}, u32[]{:S(2)}) copy-start(bf16[768,32]{1,0:T(8,128)(2,1)} %constant.65.clone.refs_2_) | copy-start | bytes 147460
  100.6 35.5 %copy-start.11 = (s32[1,1,768]{2,1,0:T(1,128)S(1)}, s32[1,1,768]{2,1,0:T(1,128)}, u32[]{:S(2)}) copy-start(s32[1,1,768]{2,1,0:T(1,128)} %refs_3_.7) | copy-start | bytes 9220

commit v4 on v3

--- a/solution.py
+++ b/solution.py
@@ -21,6 +21,8 @@
 PENCIL_ROWS = 32
 KZ = 16
 ROWS = 13 * N_SLAB
+LIMIT_P, LIMIT_Y, LIMIT_X, LIMIT_S = 48, 40, 51, 40
+LIMIT_N = 40
 F32 = jnp.float32
 BF16 = jnp.bfloat16
 
@@ -76,7 +78,7 @@
     rows = rows * (ko == ki)
     x16 = np.arange(16)
     twist = 2 * np.pi * np.arange(32)[:, None] * x16[None, :] / GX
-    twist = np.repeat(np.repeat(twist, 8, axis=0), KZ, axis=1)
+    twist = np.repeat(twist, KZ, axis=1)
     inner = 2 * np.pi * ((x16[:, None] * x16[None, :]) % 16) / 16
     eye = np.eye(KZ)
     cosine, sine = np.kron(np.cos(inner), eye), np.kron(np.sin(inner), eye)
@@ -86,7 +88,7 @@
     theta = 2 * np.pi * ((k1 * slab) % 32) / 32
     line = np.where(ro == ri, np.cos(theta), np.where(ro == 0, np.sin(theta), -np.sin(theta)))
     line = line * np.where(ri == 1, -1.0, 1.0)
-    return rows, np.cos(twist), np.sin(twist), lanes, line
+    return rows, np.stack([np.cos(twist), np.sin(twist)]), lanes, line
 
 
 def pair(table):
@@ -181,10 +183,15 @@
     return ((value.astype(F32) + 0.5) * (1.0 / divisor)).astype(jnp.int32)
 
 
-def own_slots():
-    slab = lax.broadcasted_iota(jnp.int32, (N_SLAB, SLOTS), 0)
-    slot = lax.broadcasted_iota(jnp.int32, (N_SLAB, SLOTS), 1)
-    return (slot >= slab * CAP) & (slot < slab * CAP + CAP)
+def own_slots(width, slots):
+    slab = lax.broadcasted_iota(jnp.int32, (N_SLAB, slots), 0)
+    slot = lax.broadcasted_iota(jnp.int32, (N_SLAB, slots), 1)
+    return (slot >= slab * width) & (slot < slab * width + width)
+
+
+def received_slots():
+    own = own_slots(CAP // 2, SLOTS // 2)
+    return jnp.concatenate([own, own], axis=1)
 
 
 def pack(slot_ref, weight_ref, strength_ref, out_ref):
@@ -192,7 +199,7 @@
     index = lax.broadcasted_iota(jnp.int32, (SLOTS, 128), 0)
     lane = lax.broadcasted_iota(jnp.int32, (SLOTS, 128), 1)
     spread = jnp.where((lane < CAP) & (quotient(index, CAP) * CAP + lane == index), 1.0, 0.0)
-    by_slab = mm(jnp.where(own_slots(), slots, 0.0).astype(BF16), spread.astype(BF16))
+    by_slab = mm(jnp.where(own_slots(CAP, SLOTS), slots, 0.0).astype(BF16), spread.astype(BF16))
     lane = lax.broadcasted_iota(jnp.int32, by_slab.shape, 1)
     by_slab = jnp.where(lane < CAP, by_slab, float(PAN_DEV))
     line = lax.broadcasted_iota(jnp.int32, (ROWS, 128), 0)
@@ -256,38 +263,47 @@
     return jnp.concatenate(out, axis=0)
 
 
-def project(arrived_ref, select_ref, spread_ref, order_ref, anchor_ref, z_ref, out_ref, weight_ref, scaled_ref, y_ref, high_ref, low_ref):
-    arrived = jnp.concatenate(split(arrived_ref[...]), axis=0)
-    select = select_ref[...]
-    total = jnp.zeros((256, SLOTS), F32)
-    for half in range(2):
-        turned = mm_nt(order_ref[half * 128 : half * 128 + 128, :], arrived).astype(BF16)
-        turned = jnp.concatenate([turned[:, :ROWS], turned[:, ROWS:]], axis=0)
-        total += mm(turned, select[half * ROWS : half * ROWS + ROWS])
-    weights = total[:128] + total[128:]
+def fill_rows(rows_ref, first, weight_ref):
+    def step(x, carry):
+        rows_ref[pl.ds(pl.multiple_of(x * 32, 32), 32), :] = stencil_row(x, first, weight_ref)
+        return carry
+
+    lax.fori_loop(0, SLAB_ROWS, step, 0)
+
+
+def slot_order():
+    row = lax.broadcasted_iota(jnp.int32, (256, 128), 0)
+    lane = lax.broadcasted_iota(jnp.int32, (256, 128), 1)
+    dy = row & 7
+    picked = ((row >> 5) << 4) + (dy << 2) + ((row >> 3) & 3)
+    return jnp.where((lane == picked) & (dy < EDGE), 1.0, 0.0).astype(BF16)
+
+
+def project(arrived_ref, spread_ref, anchor_ref, z_ref, out_ref, weight_ref, scaled_ref, y_ref, rows_ref, packed_ref, high_ref, low_ref):
+    for s in range(N_SLAB):
+        packed_ref[s * 12 : s * 12 + 12, :] = arrived_ref[s * 13 : s * 13 + 12, :]
+    packed = jnp.concatenate(split(packed_ref[...]), axis=0)
+    order = slot_order()
+    turned = [mm_nt(order[half * 128 : half * 128 + 128, :], packed) for half in range(2)]
+    turned = [part[:, : SLOTS // 2] + part[:, SLOTS // 2 :] for part in turned]
+    weights = jnp.concatenate(turned, axis=1)
     weight_ref[...] = weights
     high, low = split(arrived_ref[pl.ds(12, N_SLAB, stride=13), :])
     spread = spread_ref[...]
-    strength = jnp.where(own_slots(), mm_nt(high, spread) + mm_nt(low, spread), 0.0)
+    strength = jnp.where(received_slots(), mm_nt(high, spread) + mm_nt(low, spread), 0.0)
     scaled_ref[...] = weights * jnp.sum(strength, axis=0, keepdims=True)
     first, second, third = anchor_parts(anchor_ref[0])
     y_place(second, y_ref)
-
-    def step(x, carry):
-        rows = stencil_row(x, first, scaled_ref)
-        for dz in range(EDGE):
-            high, low = split(place_rows(rows[dz * 8 : dz * 8 + 8], y_ref))
-            at = pl.ds(pl.multiple_of(dz * 512 + x * PENCIL_ROWS, PENCIL_ROWS), PENCIL_ROWS)
-            high_ref[at, :] = high
-            low_ref[at, :] = low
-        return carry
-
-    lax.fori_loop(0, SLAB_ROWS, step, 0)
+    fill_rows(rows_ref, first, scaled_ref)
     hot = z_hot(third, 0)
     charge = jnp.zeros((512, GZ), F32)
     for dz in range(EDGE):
-        at = slice(dz * 512, dz * 512 + 512)
-        part = mm_nt(high_ref[at, :], hot) + mm_nt(low_ref[at, :], hot)
+        for x in range(SLAB_ROWS):
+            at = slice(x * PENCIL_ROWS, x * PENCIL_ROWS + PENCIL_ROWS)
+            high, low = split(place_rows(rows_ref[x * 32 + dz * 8 : x * 32 + dz * 8 + 8, :], y_ref))
+            high_ref[dz, at, :] = high
+            low_ref[dz, at, :] = low
+        part = mm_nt(high_ref[dz], hot) + mm_nt(low_ref[dz], hot)
         charge += pltpu.roll(part, dz, 1) if dz else part
     after = mm3(split(charge), z_ref[...])
     for half in range(2):
@@ -341,10 +357,13 @@
     y_stage((32, 16), (8, 64))(*refs)
 
 
-def x_stage(flag_ref, in_ref, row_ref, green_ref, other_ref, cos_ref, sin_ref, lane_ref, line_ref, out_ref, re_ref, im_ref):
+def x_stage(flag_ref, in_ref, row_ref, green_ref, other_ref, twist_ref, lane_ref, line_ref, out_ref, re_ref, im_ref):
     row_tables = row_ref[...]
     rows = mm3(row_tables, split(gathered(in_ref, 32, 16))).reshape(32, 2, 8, 256)
-    cosine, sine = cos_ref[...], sin_ref[...]
+    few = twist_ref[0], twist_ref[1]
+    cosine, sine = (
+        jnp.concatenate([jnp.broadcast_to(part[k : k + 1], (8, 256)) for k in range(32)], axis=0) for part in few
+    )
     lane_tables = lane_ref[...]
     line_tables = line_ref[...]
 
@@ -369,7 +388,6 @@
             axis=0,
         )
         turned = mm3(line_tables, split(line))
-        few = (cosine.reshape(32, 8, 256)[:, 0], sine.reshape(32, 8, 256)[:, 0])
         mirror = lanes_of(turned[:32], turned[32:], *few)
         other = other_ref[...]
         rows_at = pl.ds(0, 32, stride=8)
@@ -403,24 +421,17 @@
     first, second, third = anchor_parts(anchor_ref[0])
     y_place(second, y_ref)
 
-    def fill(x, carry):
-        rows_ref[pl.ds(pl.multiple_of(x * 32, 32), 32), :] = stencil_row(x, first, weight_ref)
-        return carry
-
-    lax.fori_loop(0, SLAB_ROWS, fill, 0)
+    fill_rows(rows_ref, first, weight_ref)
     total = jnp.zeros((8, SLOTS), F32)
     for dz in range(EDGE):
         hot = z_hot(third, dz)
-        grid_ref[...] = mm(high, hot) + mm(low, hot)
-
-        def step(x, total, dz=dz):
-            rows = rows_ref[pl.ds(pl.multiple_of(x * 32 + dz * 8, 8), 8), :]
-            cells = grid_ref[pl.ds(pl.multiple_of(x * 32, 32), 32), :] * place_rows(rows, y_ref)
-            return total + jnp.sum(cells.reshape(4, 8, SLOTS), axis=0)
-
-        total = lax.fori_loop(0, SLAB_ROWS, step, total)
+        grid_ref[dz] = mm(high, hot) + mm(low, hot)
+        for x in range(SLAB_ROWS):
+            rows = rows_ref[x * 32 + dz * 8 : x * 32 + dz * 8 + 8, :]
+            cells = grid_ref[dz, x * 32 : x * 32 + 32, :] * place_rows(rows, y_ref)
+            total += jnp.sum(cells.reshape(4, 8, SLOTS), axis=0)
     far = jnp.sum(total, axis=0, keepdims=True)
-    high, low = split(jnp.where(own_slots(), jnp.broadcast_to(far, (N_SLAB, SLOTS)), 0.0))
+    high, low = split(jnp.where(received_slots(), jnp.broadcast_to(far, (N_SLAB, SLOTS)), 0.0))
     out_ref[...] = mm(high, spread_ref[...]) + mm(low, spread_ref[...])
 
 
@@ -453,39 +464,29 @@
     return lax.all_to_all(value.reshape(count, rows // count, 128), axis, 0, 0, tiled=True).reshape(rows, 128)
 
 
-def arrange_green(green, slab, pencil):
-    plane = lax.ppermute(green[:, 0, :], "pencil", [(4, 0)])
+def arrange_green(green, plane, slab, pencil):
     chosen = jnp.where(pencil < 4, green[:, :KZ], jnp.flip(green[:, 1 : KZ + 1], axis=1))
     zero = chosen[:, 0, :]
-    line = lax.broadcasted_iota(jnp.int32, zero.shape, 0) == 0
+    line = np.tile(np.arange(8)[:, None] == 0, (1, GX))
     ends = line & ((slab == 0) | (slab == 16))
     both = jnp.where(ends, 0.5 * (zero + plane), jnp.where(slab >= 16, plane, zero))
     both = jnp.where(pencil == 0, both, zero)
     differ = jnp.where(ends & (pencil == 0), 0.5 * (zero - plane), 0.0)
-    place = lax.broadcasted_iota(jnp.int32, chosen.shape, 1) == 0
+    place = np.tile(np.arange(KZ)[None, :, None] == 0, (8, 1, GX))
     chosen = jnp.where(place, both[:, None, :], chosen)
     chosen = chosen.reshape(8, KZ, 16, 32).transpose(3, 0, 2, 1).reshape(256, 256)
-    first = lax.broadcasted_iota(jnp.int32, (32, 16, KZ), 2) == 0
+    first = np.tile(np.arange(KZ)[None, None, :] == 0, (32, 16, 1))
     other = jnp.where(first, differ[0].reshape(16, 32).T[:, :, None], 0.0).reshape(32, 256)
     return chosen, other
 
 
 def slot_tables():
-    order = np.zeros((256, 128))
-    for half in range(2):
-        for dx in range(4):
-            for dy in range(4):
-                for dz in range(4):
-                    order[half * 128 + dx * 32 + dz * 8 + dy, half * 64 + dx * 16 + dy * 4 + dz] = 1.0
     index = np.arange(SLOTS)
-    spread = (index % CAP)[:, None] == np.arange(128)[None, :]
+    lane = np.arange(128)[None, :]
+    spread = (index % CAP)[:, None] == lane
     own = (index // CAP)[:, None] == np.arange(N_SLAB)[None, :]
-    line = np.arange(ROWS)
-    place, target = line % 13, line // 13 * CAP + line % 13
-    select = np.concatenate(
-        [(place[:, None] < 12) & (index[None, :] == (target + shift)[:, None]) for shift in (0, 12)]
-    )
-    return [jnp.asarray(t, BF16) for t in (order, spread, own, select)]
+    received = (index // (SLOTS // 2) * 12 + index % 12)[:, None] == lane
+    return [jnp.asarray(t, BF16) for t in (spread, own, received)]
 
 
 def per_device(strength, stencil_weight, slot_panel, slot_anchor, green_spectrum, near_index, near_factor):
@@ -496,49 +497,58 @@
 
     z_fwd, z_bwd = (pair(t) for t in z_tables())
     y_fwd, y_fwd_shared, y_bwd, y_bwd_shared = (pair(t) for t in y_tables())
-    rows, cosine, sine, lanes, line = x_tables()
+    rows, twist, lanes, line = x_tables()
     rows, lanes, line = (pair(t) for t in (rows, lanes, line))
-    cosine, sine = jnp.asarray(cosine, F32), jnp.asarray(sine, F32)
-    order, spread, own, select = slot_tables()
+    twist = jnp.asarray(twist, F32)
+    spread, own, received = slot_tables()
+
+    anchor = slot_anchor.reshape(N_SLAB, 2, 12).transpose(1, 0, 2).reshape(1, 1, SLOTS)
 
     shape = jax.ShapeDtypeStruct
     payload = call(
         pack, shape((ROWS, 128), F32), slot_panel, stencil_weight, row, limit=56)
+
+    payload, spectrum = lax.optimization_barrier((payload, green_spectrum))
+    plane = lax.ppermute(spectrum[:, 0, :], "pencil", [(4, 0)])
     arrived = lax.all_to_all(payload.reshape(N_SLAB, 1, 13 * 128), "slab", 0, 0, tiled=True).reshape(ROWS, 128)
+    arrived, plane, flags, anchor = lax.optimization_barrier((arrived, plane, flags, anchor))
     after_z, weights = call(
-        project, [shape((1024, 128), F32), shape((128, SLOTS), F32)], arrived, select, spread, order, slot_anchor, z_fwd,
+        project, [shape((1024, 128), F32), shape((128, SLOTS), F32)], arrived, received, anchor, z_fwd,
         scratch=[pltpu.VMEM((128, SLOTS), F32), pltpu.VMEM((PENCIL_ROWS, SLOTS), jnp.int32)]
-        + [pltpu.VMEM((EDGE * 512, SLOTS), BF16)] * 2,
-        late=(5,), limit=54,
+        + [pltpu.VMEM((512, SLOTS), F32), pltpu.VMEM((SLOTS // 2, 128), F32)]
+        + [pltpu.VMEM((EDGE, 512, SLOTS), BF16)] * 2,
+        late=(3,), limit=LIMIT_P,
     )
     by_y = swap(after_z, "pencil", N_PENCIL)
     after_y = call(
         y_forward, shape((1024, 128), F32), flags, by_y, y_fwd, y_fwd_shared,
-        scratch=[pltpu.VMEM((512, 256), F32)], smem=(0,), limit=40,
+        scratch=[pltpu.VMEM((512, 256), F32)], smem=(0,), limit=LIMIT_Y,
     )
     by_x = swap(after_y, "slab", N_SLAB)
-    green, other = arrange_green(green_spectrum, slab, pencil)
-    after_x = call(
-        x_stage, shape((1024, 128), F32), flags, by_x, rows, green, other, cosine, sine, lanes, line,
-        scratch=[pltpu.VMEM((2, 256, 128), F32)] * 2, smem=(0,), late=range(5, 9), limit=56,
-    )
+    after_y, green_spectrum, slab, pencil = lax.optimization_barrier((after_y, green_spectrum, slab, pencil))
+    green, other = arrange_green(green_spectrum, plane, slab, pencil)
+    green, strengths = lax.optimization_barrier((green, row))
     forward = [(i, (i + 1) % N_SLAB) for i in range(N_SLAB)]
     backward = [(target, source) for source, target in forward]
-    low = lax.ppermute(row, "slab", forward)
-    high = lax.ppermute(row, "slab", backward)
-    near_field = call(near, shape((1, PAN_DEV), F32), low, row, high, near_index, near_factor, limit=40)
+    low = lax.ppermute(strengths, "slab", forward)
+    high = lax.ppermute(strengths, "slab", backward)
+    near_field = call(near, shape((1, PAN_DEV), F32), low, row, high, near_index, near_factor, limit=LIMIT_N)
+    by_x, near_field = lax.optimization_barrier((by_x, near_field))
+    after_x = call(
+        x_stage, shape((1024, 128), F32), flags, by_x, rows, green, other, twist, lanes, line,
+        scratch=[pltpu.VMEM((2, 256, 128), F32)] * 2, smem=(0,), late=range(5, 8), limit=LIMIT_X,
+    )
     back_x = swap(after_x, "slab", N_SLAB)
     back_y = call(
         y_backward, shape((1024, 128), F32), flags, back_x, y_bwd, y_bwd_shared,
-        scratch=[pltpu.VMEM((512, 256), F32)], smem=(0,), limit=40,
-    )
-    back_y, near_field = lax.optimization_barrier((back_y, near_field))
+        scratch=[pltpu.VMEM((512, 256), F32)], smem=(0,), limit=LIMIT_Y,
+    )
     by_z = swap(back_y, "pencil", N_PENCIL)
     sampled = call(
-        sample, shape((N_SLAB, 128), F32), by_z, weights, slot_anchor, z_bwd, spread,
+        sample, shape((N_SLAB, 128), F32), by_z, weights, anchor, z_bwd, received,
         scratch=[pltpu.VMEM((PENCIL_ROWS, SLOTS), jnp.int32), pltpu.VMEM((512, 256), F32)]
-        + [pltpu.VMEM((512, SLOTS), F32)] * 2,
-        limit=40,
+        + [pltpu.VMEM((512, SLOTS), F32), pltpu.VMEM((EDGE, 512, SLOTS), F32)],
+        limit=LIMIT_S,
     )
     far = lax.all_to_all(sampled, "slab", 0, 0, tiled=True)
     return call(finish, shape((1, PAN_DEV), F32), far, spread, own, slot_panel, near_field, limit=40).reshape(PAN_DEV)

time: 138 us -> 127 us (0.920)
  blocking collectives: 26.7 us -> 62.8 us
  waiting for transfers between devices: 41.8 us -> 13.6 us
  starting transfers between devices: 31.5 us -> 21.4 us
  Pallas kernels: 28.9 us -> 19.5 us
    all_to_all x1 -> x3, blocking collectives: 12.8 us -> 49 us  [swap(): lax.all_to_all(value.reshape(count, rows // count, 128), axis, 0, 0, tile...]
    all_to_all x3 -> x1, waiting for transfers between devices: 32.2 us -> 2.38 us  [swap(): lax.all_to_all(value.reshape(count, rows // count, 128), axis, 0, 0, tile...]
    all_to_all x3 -> x1, starting transfers between devices: 16.3 us -> 6.39 us  [swap(): lax.all_to_all(value.reshape(count, rows // count, 128), axis, 0, 0, tile...]
    pallas_call x8, Pallas kernels: 28.9 us -> 19.5 us  [call(): pl.pallas_call(wrapped, out_shape=out_shape, in_specs=specs, out_specs=[o...]
    ppermute x3, waiting for transfers between devices: 3.01 us -> 9.56 us  [the longest x1 4.8 us: per_device(): plane = lax.ppermute(spectrum[:, 0, :], 'pencil', [(4, 0)])]
    all_to_all x1, waiting for transfers between devices: 6.51 us -> 1.66 us  [per_device(): lax.all_to_all(payload.reshape(N_SLAB, 1, 13 * 128), 'slab', 0, 0, tiled=...]
    reshape x3, local copies, waits for them, and re-layouts: 3.58 us -> 5.73 us  [arrange_green(): chosen.reshape(8, KZ, 16, 32).transpose(3, 0, 2, 1).reshape(256, 256)]
    optimization_barrier x0 -> x2, local copies, waits for them, and re-layouts: none -> 1.66 us  [the longest x1 1.35 us: per_device(): payload, spectrum = lax.optimization_barrier((payload, green_spectrum))]
  transfers between devices with their start and end apart: 7 -> 5, of which waited for: 6 -> 5; matrix products, arithmetic and copies ran while one was open for 5% -> 7% of each run, Pallas kernels for 8% -> 0%
where the time goes in v4:
time: 127 us; the launch traced here: 126 us
  blocking collectives  62.8 us (49%)
  starting transfers between devices  21.4 us (17%)
  Pallas kernels  19.5 us (15%)
  waiting for transfers between devices  13.6 us (11%)
  local copies, waits for them, and re-layouts  7.87 us (6%)
    all_to_all x3, blocking collectives, swap(): lax.all_to_all(value.reshape(count, rows // count, 128), axis, 0, 0, tile...  49 us
    pallas_call x8, Pallas kernels, call(): pl.pallas_call(wrapped, out_shape=out_shape, in_specs=specs, out_specs=[o...  19.5 us
    all_to_all x1, blocking collectives, per_device(): far = lax.all_to_all(sampled, 'slab', 0, 0, tiled=True)  13.9 us
    all_to_all x1, starting transfers between devices, per_device(): lax.all_to_all(payload.reshape(N_SLAB, 1, 13 * 128), 'slab', 0, 0, tiled=...  11.6 us
    all_to_all x1, starting transfers between devices, swap(): lax.all_to_all(value.reshape(count, rows // count, 128), axis, 0, 0, tile...  6.39 us
    reshape x3, local copies, waits for them, and re-layouts, arrange_green(): chosen.reshape(8, KZ, 16, 32).transpose(3, 0, 2, 1).reshape(256, 256)  5.73 us
    ppermute x1, waiting for transfers between devices, per_device(): plane = lax.ppermute(spectrum[:, 0, :], 'pencil', [(4, 0)])  4.8 us
    ppermute x1, waiting for transfers between devices, per_device(): low = lax.ppermute(strengths, 'slab', forward)  3.41 us
  transfers between devices with their start and end apart: 5, of which 5 were waited for; matrix products, arithmetic and copies ran while one was open for 7% of the time, Pallas kernels for 0%

profile of v4, /device:TPU:2, one launch (start us, length us, event | category | flops | bytes accessed | tf_op | source)
XLA Modules:
  0.0 126.4 jit_solution(2792077289310791649)
XLA Ops:
  0.0 0.0 copy-start.5
  0.0 0.0 copy-start.6
  0.0 0.0 copy-start.2
  0.0 0.0 copy-start.3
  0.0 2.6 %pack.1 = f32[416,128]{1,0:T(8,128)} custom-call(s32[1,1,768]{2,1,0:T(1,128)} %refs_3_.7, f32[64,256]{1,0:T(8,128)} %refs_1_.3, f32[1,256]{1,0:T(1,128)} %bitcast.42), custom_call_target="tpu_custom_call" | custom-call | tf_op jit(solution)/shard_map/pack/pallas_call | solution.py:146
  2.6 11.6 %all-to-all-start = ((f32[32,1,1664]{2,1,0:T(1,128)}), f32[32,1,1664]{2,1,0:T(1,128)S(1)}, u32[]{:S(2)}, u32[]{:S(2)}) async-start(f32[32,1,1664]{2,1,0:T(1,128)} %bitcast.47), calls=%async_computation | async-start | bytes 425984 | tf_op jit(solution)/shard_map/all_to_all | solution.py:513
  14.2 1.4 %copy.35 = f32[8,32,512]{2,0,1:T(8,128)S(1)} copy(f32[8,32,512]{2,1,0:T(8,128)} %param.27) | data formatting | bytes 1048576 | tf_op jit(solution)/shard_map/optimization_barrier | solution.py:511
  15.6 1.3 %collective-permute-start = (f32[8,512]{1,0:T(8,128)S(1)}, f32[8,512]{1,0:T(8,128)S(1)}, u32[]{:S(2)}, u32[]{:S(2)}) collective-permute-start(f32[8,512]{1,0:T(8,128)S(1)} %slice_bitcast_fusion.1), channel_id=1, source_target_pairs={{4,0},{12,8},{20,16},{28,24},{36,32},{44,40},{52,48},{60,56},{68,6... | collective-permute-start | bytes 49160 | tf_op jit(solution)/shard_map/ppermute | solution.py:512
  16.9 0.1 add_convert_fusion.refs_0_
  17.0 0.7 reduce
  17.7 0.1 reshape.58
  17.8 0.1 reshape.59.refs_2_
  17.9 4.8 %collective-permute-done = f32[8,512]{1,0:T(8,128)S(1)} collective-permute-done((f32[8,512]{1,0:T(8,128)S(1)}, f32[8,512]{1,0:T(8,128)S(1)}, u32[]{:S(2)}, u32[]{:S(2)}) %collective-permute-start) | collective-permute-done | bytes 16416 | tf_op jit(solution)/shard_map/ppermute | solution.py:512
  22.7 1.7 %all-to-all-done = f32[32,1,1664]{2,1,0:T(1,128)S(1)} async-done(((f32[32,1,1664]{2,1,0:T(1,128)}), f32[32,1,1664]{2,1,0:T(1,128)S(1)}, u32[]{:S(2)}, u32[]{:S(2)}) %all-to-all-start) | async-done | bytes 213024 | tf_op jit(solution)/shard_map/all_to_all | solution.py:513
  24.4 0.0 copy-done.5
  24.4 0.0 copy-done.6
  24.4 4.1 %project.1 = (f32[1024,128]{1,0:T(8,128)S(1)}, f32[128,768]{1,0:T(8,128)S(1)}) custom-call(f32[416,128]{1,0:T(8,128)S(1)} %bitcast.38, bf16[768,128]{1,0:T(8,128)(2,1)S(1)} %copy-done.5, s32[1,1,768]{2,1,0:T(1,128)S(1)} %reshape.59.refs_2_, bf16[2,256,256]{2,1,0:T(8,128)(2,1)S(1)} %copy-done.6), custom_call_target="tpu_custom_call" | custom-call | tf_op jit(solution)/shard_map/project/pallas_call | solution.py:146
  28.5 14.7 %all_to_all.36 = f32[8,128,128]{2,1,0:T(8,128)S(1)} all-to-all(f32[8,128,128]{2,1,0:T(8,128)S(1)} %bitcast.39), channel_id=1, replica_groups=mesh['slab'=32,'pencil'=8] {'pencil'}, dimensions={0} | all-to-all | bytes 1048576 | tf_op jit(solution)/shard_map/all_to_all | solution.py:464
  43.2 0.0 copy-done.2
  43.2 0.0 copy-done.3
  43.2 2.5 %y_forward.1 = f32[1024,128]{1,0:T(8,128)} custom-call(s32[2]{0:T(128)S(1)} %add_convert_fusion.refs_0_, f32[1024,128]{1,0:T(8,128)S(1)} %bitcast.35, bf16[2,512,512]{2,1,0:T(8,128)(2,1)S(1)} %copy-done.3, bf16[2,512,512]{2,1,0:T(8,128)(2,1)S(1)} %copy-done.2), custom_call_target="tpu_custom_call" | custom-call | tf_op jit(solution)/shard_map/y_forward/pallas_call | solution.py:146
  45.7 6.4 %all-to-all-start.2 = ((f32[32,32,128]{2,1,0:T(8,128)}), f32[32,32,128]{2,1,0:T(8,128)S(1)}, u32[]{:S(2)}, u32[]{:S(2)}) async-start(f32[32,32,128]{2,1,0:T(8,128)} %bitcast.9), calls=%async_computation.2 | async-start | bytes 1048576 | tf_op jit(solution)/shard_map/all_to_all | solution.py:464
  52.1 0.0 copy-done.16
  52.1 0.3 copy.37
  52.5 0.0 copy-done.19
  52.5 0.0 copy-done.17
  52.6 0.3 reshape.64
  52.9 0.0 copy-start.15
  52.9 0.0 copy-start.18
  52.9 2.9 %copy.39 = f32[8,16,16,32]{1,2,0,3:T(8,128)} copy(f32[8,16,16,32]{3,2,0,1:T(8,128)S(1)} %reshape.64) | data formatting | bytes 524288 | tf_op jit(solution)/shard_map/reshape | solution.py:477
  55.8 0.0 copy-start.13
  55.8 2.5 %reshape.65.refs_3_ = f32[256,256]{1,0:T(8,128)S(1)} reshape(f32[32,8,16,16]{3,2,1,0:T(8,128)} %bitcast.46) | data formatting | bytes 524288 | tf_op jit(solution)/shard_map/reshape | solution.py:477
  58.4 0.0 copy-done.15
  58.4 0.3 collective-permute-start.2
  58.7 1.8 %collective-permute-start.1 = (f32[1,256]{1,0:T(1,128)S(1)}, f32[1,256]{1,0:T(1,128)S(1)}, u32[]{:S(2)}, u32[]{:S(2)}) collective-permute-start(f32[1,256]{1,0:T(1,128)S(1)} %bitcast.44), channel_id=1, source_target_pairs={{0,8},{8,16},{16,24},{24,32},{32,40},{40,48},{48,56},{56,64},{64,7... | collective-permute-start | bytes 3080 | tf_op jit(solution)/shard_map/ppermute | solution.py:533
  60.5 0.1 reshape_squeeze.3
  60.6 0.0 copy-done.18
  60.6 0.1 copy.40.refs_4_
  60.7 1.3 %collective-permute-done.2.refs_2_ = f32[1,256]{1,0:T(1,128)S(1)} collective-permute-done((f32[1,256]{1,0:T(1,128)S(1)}, f32[1,256]{1,0:T(1,128)S(1)}, u32[]{:S(2)}, u32[]{:S(2)}) %collective-permute-start.2) | collective-permute-done | bytes 1056 | tf_op jit(solution)/shard_map/ppermute | solution.py:534
  62.0 3.4 %collective-permute-done.1.refs_0_ = f32[1,256]{1,0:T(1,128)S(1)} collective-permute-done((f32[1,256]{1,0:T(1,128)S(1)}, f32[1,256]{1,0:T(1,128)S(1)}, u32[]{:S(2)}, u32[]{:S(2)}) %collective-permute-start.1) | collective-permute-done | bytes 1056 | tf_op jit(solution)/shard_map/ppermute | solution.py:533
  65.4 0.0 copy-done.11
  65.4 0.0 copy-done.12
  65.4 0.2 near.1.refs_4_
  65.6 2.4 %all-to-all-done.2 = f32[32,32,128]{2,1,0:T(8,128)S(1)} async-done(((f32[32,32,128]{2,1,0:T(8,128)}), f32[32,32,128]{2,1,0:T(8,128)S(1)}, u32[]{:S(2)}, u32[]{:S(2)}) %all-to-all-start.2) | async-done | bytes 524320 | tf_op jit(solution)/shard_map/all_to_all | solution.py:464
  68.0 0.0 copy-done.4
  68.0 0.0 copy-done.10
  68.0 0.0 copy-done.13
  68.0 0.0 copy-start
  68.0 0.0 copy-start.1
  68.0 4.1 %x_stage.1 = f32[1024,128]{1,0:T(8,128)S(1)} custom-call(s32[2]{0:T(128)S(1)} %add_convert_fusion.refs_0_, f32[1024,128]{1,0:T(8,128)S(1)} %bitcast.36, bf16[2,512,512]{2,1,0:T(8,128)(2,1)S(1)} %copy-done.4, f32[256,256]{1,0:T(8,128)S(1)} %reshape.65.refs_3_, f32[32,256]{1,0:T(8,128)S(1)} %copy.40.refs_4_, f32[2,32,256]{2,1,0:T(8,128)S(1)} %copy-done.10, ...), custom_call_target="tpu_custom_call" | custom-call | tf_op jit(solution)/shard_map/x_stage/pallas_call | solution.py:146
  72.1 21.5 %all_to_all.37 = f32[32,32,128]{2,1,0:T(8,128)S(1)} all-to-all(f32[32,32,128]{2,1,0:T(8,128)S(1)} %bitcast.37), channel_id=1, replica_groups=mesh['slab'=32,'pencil'=8] {'slab'}, dimensions={0} | all-to-all | bytes 1048576 | tf_op jit(solution)/shard_map/all_to_all | solution.py:464
  93.6 0.0 copy-done
  93.6 0.0 copy-done.1
  93.6 0.0 copy-start.9
  93.6 0.0 copy-start.14
  93.6 1.7 %y_backward.1 = f32[1024,128]{1,0:T(8,128)S(1)} custom-call(s32[2]{0:T(128)S(1)} %add_convert_fusion.refs_0_, f32[1024,128]{1,0:T(8,128)S(1)} %bitcast.33, bf16[2,512,512]{2,1,0:T(8,128)(2,1)S(1)} %copy-done.1, bf16[2,512,512]{2,1,0:T(8,128)(2,1)S(1)} %copy-done), custom_call_target="tpu_custom_call" | custom-call | tf_op jit(solution)/shard_map/y_backward/pallas_call | solution.py:146
  95.3 12.8 %all_to_all.38 = f32[8,128,128]{2,1,0:T(8,128)S(1)} all-to-all(f32[8,128,128]{2,1,0:T(8,128)S(1)} %bitcast.34), channel_id=1, replica_groups=mesh['slab'=32,'pencil'=8] {'pencil'}, dimensions={0} | all-to-all | bytes 1048576 | tf_op jit(solution)/shard_map/all_to_all | solution.py:464
  108.1 0.0 copy-done.7
  108.2 3.4 %sample.1 = f32[32,128]{1,0:T(8,128)S(1)} custom-call(f32[1024,128]{1,0:T(8,128)S(1)} %bitcast.32, f32[128,768]{1,0:T(8,128)S(1)} %get-tuple-element.33.refs_1_, s32[1,1,768]{2,1,0:T(1,128)S(1)} %reshape.59.refs_2_, bf16[2,256,256]{2,1,0:T(8,128)(2,1)S(1)} %copy-done.7, bf16[768,128]{1,0:T(8,128)(2,1)S(1)} %copy-done.5), custom_call_target="tpu_custom_call" | custom-call | tf_op jit(solution)/shard_map/sample/pallas_call | solution.py:146
  111.6 13.9 %all_to_all.39 = f32[32,1,128]{2,1,0:T(1,128)S(1)} all-to-all(f32[32,1,128]{2,1,0:T(1,128)S(1)} %bitcast.40), channel_id=1, replica_groups=mesh['slab'=32,'pencil'=8] {'slab'}, dimensions={0} | all-to-all | bytes 32768 | tf_op jit(solution)/shard_map/all_to_all | solution.py:553
  125.5 0.0 copy-done.8
  125.5 0.0 copy-done.9
  125.5 0.0 copy-done.14
  125.5 1.0 finish.1
  (19 shorter events, 0.2 us)
Async XLA Ops:
  0.0 24.4 %copy-start.5 = (bf16[768,128]{1,0:T(8,128)(2,1)S(1)}, bf16[768,128]{1,0:T(8,128)(2,1)}, u32[]{:S(2)}) copy-start(bf16[768,128]{1,0:T(8,128)(2,1)} %constant.63.clone.refs_1_.refs_4_) | copy-start | bytes 589828
  0.0 24.4 %copy-start.6 = (bf16[2,256,256]{2,1,0:T(8,128)(2,1)S(1)}, bf16[2,256,256]{2,1,0:T(8,128)(2,1)}, u32[]{:S(2)}) copy-start(bf16[2,256,256]{2,1,0:T(8,128)(2,1)} %constant.51.clone.refs_3_) | copy-start | bytes 786436
  0.0 43.2 %copy-start.2 = (bf16[2,512,512]{2,1,0:T(8,128)(2,1)S(1)}, bf16[2,512,512]{2,1,0:T(8,128)(2,1)}, u32[]{:S(2)}) copy-start(bf16[2,512,512]{2,1,0:T(8,128)(2,1)} %constant.54.clone.refs_3_) | copy-start | bytes 3145732
  0.0 43.2 %copy-start.3 = (bf16[2,512,512]{2,1,0:T(8,128)(2,1)S(1)}, bf16[2,512,512]{2,1,0:T(8,128)(2,1)}, u32[]{:S(2)}) copy-start(bf16[2,512,512]{2,1,0:T(8,128)(2,1)} %constant.53.clone.refs_2_) | copy-start | bytes 3145732
  2.6 21.8 %all-to-all-start = ((f32[32,1,1664]{2,1,0:T(1,128)}), f32[32,1,1664]{2,1,0:T(1,128)S(1)}, u32[]{:S(2)}, u32[]{:S(2)}) async-start(f32[32,1,1664]{2,1,0:T(1,128)} %bitcast.47), calls=%async_computation | async-start | bytes 425984 | tf_op jit(solution)/shard_map/all_to_all | solution.py:513
  15.6 7.1 %collective-permute-start = (f32[8,512]{1,0:T(8,128)S(1)}, f32[8,512]{1,0:T(8,128)S(1)}, u32[]{:S(2)}, u32[]{:S(2)}) collective-permute-start(f32[8,512]{1,0:T(8,128)S(1)} %slice_bitcast_fusion.1), channel_id=1, source_target_pairs={{4,0},{12,8},{20,16},{28,24},{36,32},{44,40},{52,48},{60,56},{68,6... | collective-permute-start | bytes 49160 | tf_op jit(solution)/shard_map/ppermute | solution.py:512
  43.2 8.9 %copy-start.16 = (f32[8,32,512]{2,1,0:T(8,128)S(1)}, f32[8,32,512]{2,1,0:T(8,128)}, u32[]{:S(2)}) copy-start(f32[8,32,512]{2,1,0:T(8,128)} %param.27) | copy-start | bytes 1572868
  45.7 6.8 %copy-start.19 = (pred[8,512]{1,0:T(8,128)(4,1)S(1)}, pred[8,512]{1,0:T(8,128)(4,1)}, u32[]{:S(2)}) copy-start(pred[8,512]{1,0:T(8,128)(4,1)} %constant.64.clone) | copy-start | bytes 12292
  45.7 6.8 %copy-start.17 = (pred[8,16,512]{2,0,1:T(8,128)(4,1)S(1)}, pred[8,16,512]{2,0,1:T(8,128)(4,1)}, u32[]{:S(2)}) copy-start(pred[8,16,512]{2,0,1:T(8,128)(4,1)} %constant.65.clone) | copy-start | bytes 196612
  45.7 22.3 %all-to-all-start.2 = ((f32[32,32,128]{2,1,0:T(8,128)}), f32[32,32,128]{2,1,0:T(8,128)S(1)}, u32[]{:S(2)}, u32[]{:S(2)}) async-start(f32[32,32,128]{2,1,0:T(8,128)} %bitcast.9), calls=%async_computation.2 | async-start | bytes 1048576 | tf_op jit(solution)/shard_map/all_to_all | solution.py:464
  52.9 5.5 %copy-start.15 = (f32[256]{0:T(256)S(1)}, f32[256]{0:T(256)}, u32[]{:S(2)}) copy-start(f32[256]{0:T(256)} %param.23) | copy-start | bytes 3076
  52.9 7.7 %copy-start.18 = (pred[32,16,16]{0,2,1:T(8,128)(4,1)S(1)}, pred[32,16,16]{0,2,1:T(8,128)(4,1)}, u32[]{:S(2)}) copy-start(pred[32,16,16]{0,2,1:T(8,128)(4,1)} %constant.66.clone) | copy-start | bytes 24580
  55.8 9.6 %copy-start.11 = (s32[32,256]{1,0:T(8,128)S(1)}, s32[32,256]{1,0:T(8,128)}, u32[]{:S(2)}) copy-start(s32[32,256]{1,0:T(8,128)} %refs_3_.6) | copy-start | bytes 98308
  55.8 9.6 %copy-start.12 = (f32[32,256]{1,0:T(8,128)S(1)}, f32[32,256]{1,0:T(8,128)}, u32[]{:S(2)}) copy-start(f32[32,256]{1,0:T(8,128)} %refs_4_.2) | copy-start | bytes 98308
  55.8 12.2 %copy-start.4 = (bf16[2,512,512]{2,1,0:T(8,128)(2,1)S(1)}, bf16[2,512,512]{2,1,0:T(8,128)(2,1)}, u32[]{:S(2)}) copy-start(bf16[2,512,512]{2,1,0:T(8,128)(2,1)} %constant.57.clone.refs_2_) | copy-start | bytes 3145732
  55.8 12.2 %copy-start.10 = (f32[2,32,256]{2,1,0:T(8,128)S(1)}, f32[2,32,256]{2,1,0:T(8,128)}, u32[]{:S(2)}) copy-start(f32[2,32,256]{2,1,0:T(8,128)} %constant.60.clone.refs_5_) | copy-start | bytes 196612
  55.8 12.2 %copy-start.13 = (bf16[2,64,64]{2,1,0:T(8,128)(2,1)S(1)}, bf16[2,64,64]{2,1,0:T(8,128)(2,1)}, u32[]{:S(2)}) copy-start(bf16[2,64,64]{2,1,0:T(8,128)(2,1)} %constant.59.clone.refs_7_) | copy-start | bytes 49156
  58.4 3.7 %collective-permute-start.2 = (f32[1,256]{1,0:T(1,128)S(1)}, f32[1,256]{1,0:T(1,128)S(1)}, u32[]{:S(2)}, u32[]{:S(2)}) collective-permute-start(f32[1,256]{1,0:T(1,128)S(1)} %bitcast.43), channel_id=1, source_target_pairs={{8,0},{16,8},{24,16},{32,24},{40,32},{48,40},{56,48},{64,56},{72,6... | collective-permute-start | bytes 3080 | tf_op jit(solution)/shard_map/ppermute | solution.py:534
  58.7 6.7 %collective-permute-start.1 = (f32[1,256]{1,0:T(1,128)S(1)}, f32[1,256]{1,0:T(1,128)S(1)}, u32[]{:S(2)}, u32[]{:S(2)}) collective-permute-start(f32[1,256]{1,0:T(1,128)S(1)} %bitcast.44), channel_id=1, source_target_pairs={{0,8},{8,16},{16,24},{24,32},{32,40},{40,48},{48,56},{56,64},{64,7... | collective-permute-start | bytes 3080 | tf_op jit(solution)/shard_map/ppermute | solution.py:533
  68.0 25.6 %copy-start = (bf16[2,512,512]{2,1,0:T(8,128)(2,1)S(1)}, bf16[2,512,512]{2,1,0:T(8,128)(2,1)}, u32[]{:S(2)}) copy-start(bf16[2,512,512]{2,1,0:T(8,128)(2,1)} %constant.56.clone.refs_3_) | copy-start | bytes 3145732
  68.0 25.6 %copy-start.1 = (bf16[2,512,512]{2,1,0:T(8,128)(2,1)S(1)}, bf16[2,512,512]{2,1,0:T(8,128)(2,1)}, u32[]{:S(2)}) copy-start(bf16[2,512,512]{2,1,0:T(8,128)(2,1)} %constant.55.clone.refs_2_) | copy-start | bytes 3145732
  93.6 14.6 %copy-start.7 = (bf16[2,256,256]{2,1,0:T(8,128)(2,1)S(1)}, bf16[2,256,256]{2,1,0:T(8,128)(2,1)}, u32[]{:S(2)}) copy-start(bf16[2,256,256]{2,1,0:T(8,128)(2,1)} %constant.52.clone.refs_3_) | copy-start | bytes 786436
  93.6 31.9 %copy-start.8 = (bf16[768,32]{1,0:T(8,128)(2,1)S(1)}, bf16[768,32]{1,0:T(8,128)(2,1)}, u32[]{:S(2)}) copy-start(bf16[768,32]{1,0:T(8,128)(2,1)} %constant.62.clone.refs_2_) | copy-start | bytes 147460
  93.6 31.9 %copy-start.9 = (bf16[768,128]{1,0:T(8,128)(2,1)S(1)}, bf16[768,128]{1,0:T(8,128)(2,1)}, u32[]{:S(2)}) copy-start(bf16[768,128]{1,0:T(8,128)(2,1)} %constant.61.clone.refs_1_) | copy-start | bytes 589828
  93.6 31.9 %copy-start.14 = (s32[1,1,768]{2,1,0:T(1,128)S(1)}, s32[1,1,768]{2,1,0:T(1,128)}, u32[]{:S(2)}) copy-start(s32[1,1,768]{2,1,0:T(1,128)} %refs_3_.7) | copy-start | bytes 9220

commit v5 on v4

--- a/solution.py
+++ b/solution.py
@@ -20,7 +20,8 @@
 SLAB_ROWS = 16
 PENCIL_ROWS = 32
 KZ = 16
-ROWS = 13 * N_SLAB
+LINES = 15
+ROWS = LINES * N_SLAB
 LIMIT_P, LIMIT_Y, LIMIT_X, LIMIT_S = 48, 40, 51, 40
 LIMIT_N = 40
 F32 = jnp.float32
@@ -204,8 +205,8 @@
     by_slab = jnp.where(lane < CAP, by_slab, float(PAN_DEV))
     line = lax.broadcasted_iota(jnp.int32, (ROWS, 128), 0)
     lane = lax.broadcasted_iota(jnp.int32, (ROWS, 128), 1)
-    slab = quotient(line, 13)
-    place = line - slab * 13
+    slab = quotient(line, LINES)
+    place = line - slab * LINES
     mine = jnp.where(lane == slab, 1.0, 0.0).astype(BF16)[:, :N_SLAB]
     lines = mm(mine, by_slab.astype(BF16))
     ones = jnp.ones((128, 128), BF16)
@@ -227,7 +228,9 @@
     tables = [strength[:, :128], strength[:, 128:]]
     index = by_slab.astype(jnp.int32)
     sent = jnp.concatenate([lookup(tables, index[i * 8 : i * 8 + 8]) for i in range(4)], axis=0)
-    out_ref[pl.ds(12, N_SLAB, stride=13), :] = sent
+    out_ref[pl.ds(12, N_SLAB, stride=LINES), :] = sent
+    for half in range(2):
+        out_ref[pl.ds(13 + half, N_SLAB, stride=LINES), :] = jnp.broadcast_to(tables[half], (N_SLAB, 128))
 
 
 def anchor_parts(anchor):
@@ -281,14 +284,14 @@
 
 def project(arrived_ref, spread_ref, anchor_ref, z_ref, out_ref, weight_ref, scaled_ref, y_ref, rows_ref, packed_ref, high_ref, low_ref):
     for s in range(N_SLAB):
-        packed_ref[s * 12 : s * 12 + 12, :] = arrived_ref[s * 13 : s * 13 + 12, :]
+        packed_ref[s * 12 : s * 12 + 12, :] = arrived_ref[s * LINES : s * LINES + 12, :]
     packed = jnp.concatenate(split(packed_ref[...]), axis=0)
     order = slot_order()
     turned = [mm_nt(order[half * 128 : half * 128 + 128, :], packed) for half in range(2)]
     turned = [part[:, : SLOTS // 2] + part[:, SLOTS // 2 :] for part in turned]
     weights = jnp.concatenate(turned, axis=1)
     weight_ref[...] = weights
-    high, low = split(arrived_ref[pl.ds(12, N_SLAB, stride=13), :])
+    high, low = split(arrived_ref[pl.ds(12, N_SLAB, stride=LINES), :])
     spread = spread_ref[...]
     strength = jnp.where(received_slots(), mm_nt(high, spread) + mm_nt(low, spread), 0.0)
     scaled_ref[...] = weights * jnp.sum(strength, axis=0, keepdims=True)
@@ -372,11 +375,11 @@
         return mm3(split(turned), lane_tables)
 
     full = lanes_of(rows[:, 0].reshape(256, 256), rows[:, 1].reshape(256, 256), cosine, sine)
-    green = green_ref[...]
     for half in range(2):
         at = slice(half * 128, half * 128 + 128)
-        re_ref[half] = full[:, at] * green[:, at]
-        im_ref[half] = full[:, 256 + half * 128 : 384 + half * 128] * green[:, at]
+        green = green_ref[half]
+        re_ref[half] = full[:, at] * green
+        im_ref[half] = full[:, 256 + half * 128 : 384 + half * 128] * green
 
     @pl.when(flag_ref[1] == 1)
     def _():
@@ -435,9 +438,10 @@
     out_ref[...] = mm(high, spread_ref[...]) + mm(low, spread_ref[...])
 
 
-def near(low_ref, own_ref, high_ref, index_ref, factor_ref, out_ref):
-    table = jnp.concatenate([low_ref[...], own_ref[...], high_ref[...]], axis=1)
-    tables = [table[:, part * 128 : part * 128 + 128] for part in range(6)]
+def near(flag_ref, arrived_ref, own_ref, index_ref, factor_ref, out_ref):
+    before = [arrived_ref[pl.ds(flag_ref[4] + half, 1), :] for half in range(2)]
+    after = [arrived_ref[pl.ds(flag_ref[5] + half, 1), :] for half in range(2)]
+    tables = before + [own_ref[:, :128], own_ref[:, 128:]] + after
     for lane in range(2):
         total = jnp.zeros((8, 128), F32)
         for block in range(4):
@@ -464,20 +468,36 @@
     return lax.all_to_all(value.reshape(count, rows // count, 128), axis, 0, 0, tiled=True).reshape(rows, 128)
 
 
-def arrange_green(green, plane, slab, pencil):
-    chosen = jnp.where(pencil < 4, green[:, :KZ], jnp.flip(green[:, 1 : KZ + 1], axis=1))
-    zero = chosen[:, 0, :]
-    line = np.tile(np.arange(8)[:, None] == 0, (1, GX))
-    ends = line & ((slab == 0) | (slab == 16))
-    both = jnp.where(ends, 0.5 * (zero + plane), jnp.where(slab >= 16, plane, zero))
-    both = jnp.where(pencil == 0, both, zero)
-    differ = jnp.where(ends & (pencil == 0), 0.5 * (zero - plane), 0.0)
-    place = np.tile(np.arange(KZ)[None, :, None] == 0, (8, 1, GX))
-    chosen = jnp.where(place, both[:, None, :], chosen)
-    chosen = chosen.reshape(8, KZ, 16, 32).transpose(3, 0, 2, 1).reshape(256, 256)
-    first = np.tile(np.arange(KZ)[None, None, :] == 0, (32, 16, 1))
-    other = jnp.where(first, differ[0].reshape(16, 32).T[:, :, None], 0.0).reshape(32, 256)
-    return chosen, other
+def arrange_green(flag_ref, green_ref, plane_ref, out_ref, other_ref):
+    shared, ends, upper, straight = (flag_ref[i] == 1 for i in range(4))
+    place = lax.broadcasted_iota(jnp.int32, (KZ, GX), 0) == 0
+    group = lax.broadcasted_iota(jnp.int32, (32, 128), 1) // KZ
+
+    def lay(rows):
+        turned = jnp.transpose(jnp.concatenate([rows] * 8, axis=0))
+        halves = []
+        for half in range(2):
+            total = jnp.zeros((32, 128), F32)
+            for k2 in range(8):
+                start = (half * 8 + k2) * 32
+                total = jnp.where(group == k2, turned[start : start + 32], total)
+            halves.append(total)
+        return jnp.concatenate(halves, axis=1)
+
+    for k in range(8):
+        up = green_ref[k, :KZ, :]
+        down = jnp.concatenate([green_ref[k, KZ - i : KZ - i + 1, :] for i in range(KZ)], axis=0)
+        rows = jnp.where(straight, up, down)
+        zero, plane = rows[0:1], plane_ref[k : k + 1, :]
+        line = jnp.where(upper, plane, zero)
+        if k == 0:
+            line = jnp.where(ends, 0.5 * (zero + plane), line)
+            differ = jnp.where(ends, 0.5 * (zero - plane), 0.0)
+            other_ref[...] = lay(jnp.where(place, differ, 0.0))
+        rows = jnp.where(place & shared, line, rows)
+        laid = lay(rows)
+        for half in range(2):
+            out_ref[half, pl.ds(k, 32, stride=8), :] = laid[:, half * 128 : half * 128 + 128]
 
 
 def slot_tables():
@@ -492,7 +512,10 @@
 def per_device(strength, stencil_weight, slot_panel, slot_anchor, green_spectrum, near_index, near_factor):
     slab = lax.axis_index("slab")
     pencil = lax.axis_index("pencil")
-    flags = jnp.stack([pencil == 0, (pencil == 0) & ((slab == 0) | (slab == 16))]).astype(jnp.int32)
+    ends = (pencil == 0) & ((slab == 0) | (slab == 16))
+    flags = jnp.stack([pencil == 0, ends, slab >= 16, pencil < 4]).astype(jnp.int32)
+    around = jnp.stack([(slab + N_SLAB - 1) % N_SLAB, (slab + 1) % N_SLAB])
+    flags = jnp.concatenate([flags, around.astype(jnp.int32) * LINES + 13])
     row = strength.reshape(1, PAN_DEV)
 
     z_fwd, z_bwd = (pair(t) for t in z_tables())
@@ -510,8 +533,12 @@
 
     payload, spectrum = lax.optimization_barrier((payload, green_spectrum))
     plane = lax.ppermute(spectrum[:, 0, :], "pencil", [(4, 0)])
-    arrived = lax.all_to_all(payload.reshape(N_SLAB, 1, 13 * 128), "slab", 0, 0, tiled=True).reshape(ROWS, 128)
-    arrived, plane, flags, anchor = lax.optimization_barrier((arrived, plane, flags, anchor))
+    arrived = lax.all_to_all(payload.reshape(N_SLAB, 1, LINES * 128), "slab", 0, 0, tiled=True).reshape(ROWS, 128)
+    green, other = call(
+        arrange_green, [shape((2, 256, 128), F32), shape((32, 256), F32)], flags, spectrum, plane, smem=(0,), limit=LIMIT_N
+    )
+    arrived, green, other, flags, anchor = lax.optimization_barrier((arrived, green, other, flags, anchor))
+    near_field = call(near, shape((1, PAN_DEV), F32), flags, arrived, row, near_index, near_factor, smem=(0,), limit=LIMIT_N)
     after_z, weights = call(
         project, [shape((1024, 128), F32), shape((128, SLOTS), F32)], arrived, received, anchor, z_fwd,
         scratch=[pltpu.VMEM((128, SLOTS), F32), pltpu.VMEM((PENCIL_ROWS, SLOTS), jnp.int32)]
@@ -525,15 +552,6 @@
         scratch=[pltpu.VMEM((512, 256), F32)], smem=(0,), limit=LIMIT_Y,
     )
     by_x = swap(after_y, "slab", N_SLAB)
-    after_y, green_spectrum, slab, pencil = lax.optimization_barrier((after_y, green_spectrum, slab, pencil))
-    green, other = arrange_green(green_spectrum, plane, slab, pencil)
-    green, strengths = lax.optimization_barrier((green, row))
-    forward = [(i, (i + 1) % N_SLAB) for i in range(N_SLAB)]
-    backward = [(target, source) for source, target in forward]
-    low = lax.ppermute(strengths, "slab", forward)
-    high = lax.ppermute(strengths, "slab", backward)
-    near_field = call(near, shape((1, PAN_DEV), F32), low, row, high, near_index, near_factor, limit=LIMIT_N)
-    by_x, near_field = lax.optimization_barrier((by_x, near_field))
     after_x = call(
         x_stage, shape((1024, 128), F32), flags, by_x, rows, green, other, twist, lanes, line,
         scratch=[pltpu.VMEM((2, 256, 128), F32)] * 2, smem=(0,), late=range(5, 8), limit=LIMIT_X,

time: 127 us -> 128 us (level)
  blocking collectives: 62.8 us -> 71.4 us
  local copies, waits for them, and re-layouts: 7.87 us -> 1.35 us
  starting transfers between devices: 21.4 us -> 18.7 us
  Pallas kernels: 19.5 us -> 21 us
    all_to_all x3 -> x4, blocking collectives: 49 us -> 71.4 us  [swap(): lax.all_to_all(value.reshape(count, rows // count, 128), axis, 0, 0, tile...]
    all_to_all x1 -> x0, blocking collectives: 13.9 us -> none  [per_device(): far = lax.all_to_all(sampled, 'slab', 0, 0, tiled=True)]
    reshape x4 -> x0, local copies, waits for them, and re-layouts: 5.79 us -> none  [the longest x3 5.73 us: arrange_green(): chosen.reshape(8, KZ, 16, 32).transpose(3, 0, 2, 1).reshape(256, 256)]
    all_to_all x2, waiting for transfers between devices: 4.03 us -> 9.06 us  [the longest x1 7.77 us: per_device(): far = lax.all_to_all(sampled, 'slab', 0, 0, tiled=True)]
    ppermute x2 -> x0, waiting for transfers between devices: 4.75 us -> none  [the longest x1 3.41 us: per_device(): low = lax.ppermute(strengths, 'slab', forward)]
    ppermute x2 -> x0, starting transfers between devices: 2.1 us -> none  [the longest x1 1.79 us: per_device(): low = lax.ppermute(strengths, 'slab', forward)]
    pallas_call x8 -> x9, Pallas kernels: 19.5 us -> 21 us  [call(): pl.pallas_call(wrapped, out_shape=out_shape, in_specs=specs, out_specs=[o...]
  transfers between devices with their start and end apart: 5 -> 3, of which waited for: 5 -> 3; matrix products, arithmetic and copies ran while one was open for 7% -> 1% of each run, Pallas kernels for 0% -> 2%
where the time goes in v5:
time: 128 us; the launch traced here: 127 us
  blocking collectives  71.4 us (56%)
  Pallas kernels  21 us (16%)
  starting transfers between devices  18.7 us (15%)
  waiting for transfers between devices  14.3 us (11%)
  local copies, waits for them, and re-layouts  1.35 us (1%)
    all_to_all x4, blocking collectives, swap(): lax.all_to_all(value.reshape(count, rows // count, 128), axis, 0, 0, tile...  71.4 us
    pallas_call x9, Pallas kernels, call(): pl.pallas_call(wrapped, out_shape=out_shape, in_specs=specs, out_specs=[o...  21 us
    all_to_all x1, starting transfers between devices, per_device(): lax.all_to_all(payload.reshape(N_SLAB, 1, LINES * 128), 'slab', 0, 0, til...  11.6 us
    all_to_all x1, waiting for transfers between devices, per_device(): far = lax.all_to_all(sampled, 'slab', 0, 0, tiled=True)  7.77 us
    all_to_all x1, starting transfers between devices, per_device(): far = lax.all_to_all(sampled, 'slab', 0, 0, tiled=True)  5.7 us
    ppermute x1, waiting for transfers between devices, per_device(): plane = lax.ppermute(spectrum[:, 0, :], 'pencil', [(4, 0)])  5.27 us
  transfers between devices with their start and end apart: 3, of which 3 were waited for; matrix products, arithmetic and copies ran while one was open for 1% of the time, Pallas kernels for 2%

profile of v5, /device:TPU:2, one launch (start us, length us, event | category | flops | bytes accessed | tf_op | source)
XLA Modules:
  0.0 127.4 jit_solution(17475982926523628734)
XLA Ops:
  0.0 0.0 copy-start
  0.0 2.5 %pack.1 = f32[480,128]{1,0:T(8,128)} custom-call(s32[1,1,768]{2,1,0:T(1,128)} %refs_3_.7, f32[64,256]{1,0:T(8,128)} %refs_1_.3, f32[1,256]{1,0:T(1,128)} %bitcast.36), custom_call_target="tpu_custom_call" | custom-call | tf_op jit(solution)/shard_map/pack/pallas_call | solution.py:147
  2.6 11.6 %all-to-all-start = ((f32[32,1,1920]{2,1,0:T(1,128)}), f32[32,1,1920]{2,1,0:T(1,128)S(1)}, u32[]{:S(2)}, u32[]{:S(2)}) async-start(f32[32,1,1920]{2,1,0:T(1,128)} %bitcast.38), calls=%async_computation | async-start | bytes 491520 | tf_op jit(solution)/shard_map/all_to_all | solution.py:536
  14.2 0.0 copy-done
  14.2 0.0 copy-start.19
  14.2 0.3 copy.26
  14.5 0.0 copy-start.7
  14.5 1.4 %collective-permute-start = (f32[8,512]{1,0:T(8,128)S(1)}, f32[8,512]{1,0:T(8,128)S(1)}, u32[]{:S(2)}, u32[]{:S(2)}) collective-permute-start(f32[8,512]{1,0:T(8,128)S(1)} %slice_bitcast_fusion), channel_id=1, source_target_pairs={{4,0},{12,8},{20,16},{28,24},{36,32},{44,40},{52,48},{60,56},{68,6... | collective-permute-start | bytes 49160 | tf_op jit(solution)/shard_map/ppermute | solution.py:535
  16.0 0.1 fusion
  16.1 0.1 add_convert_fusion
  16.2 0.1 pad_add_fusion.refs_0_
  16.2 0.0 copy-done.19
  16.3 0.1 reshape.47
  16.4 0.0 copy-start.6
  16.4 0.1 reshape.48.refs_2_
  16.5 0.0 copy-start.3
  16.5 0.0 copy-start.4
  16.5 5.3 %collective-permute-done.refs_2_ = f32[8,512]{1,0:T(8,128)S(1)} collective-permute-done((f32[8,512]{1,0:T(8,128)S(1)}, f32[8,512]{1,0:T(8,128)S(1)}, u32[]{:S(2)}, u32[]{:S(2)}) %collective-permute-start) | collective-permute-done | bytes 16416 | tf_op jit(solution)/shard_map/ppermute | solution.py:535
  21.8 1.2 arrange_green.1
  23.0 0.0 copy-start.9
  23.0 0.7 copy-done.9
  23.7 1.3 %all-to-all-done = f32[32,1,1920]{2,1,0:T(1,128)S(1)} async-done(((f32[32,1,1920]{2,1,0:T(1,128)}), f32[32,1,1920]{2,1,0:T(1,128)S(1)}, u32[]{:S(2)}, u32[]{:S(2)}) %all-to-all-start) | async-done | bytes 245792 | tf_op jit(solution)/shard_map/all_to_all | solution.py:536
  25.0 0.0 copy-done.7
  25.0 0.0 copy-done.6
  25.0 4.1 %project.1 = (f32[1024,128]{1,0:T(8,128)S(1)}, f32[128,768]{1,0:T(8,128)S(1)}) custom-call(f32[480,128]{1,0:T(8,128)S(1)} %bitcast.25, bf16[768,128]{1,0:T(8,128)(2,1)S(1)} %copy-done.6, s32[1,1,768]{2,1,0:T(1,128)S(1)} %reshape.48.refs_2_, bf16[2,256,256]{2,1,0:T(8,128)(2,1)S(1)} %copy-done.7), custom_call_target="tpu_custom_call" | custom-call | tf_op jit(solution)/shard_map/project/pallas_call | solution.py:147
  29.1 14.7 %all_to_all.36 = f32[8,128,128]{2,1,0:T(8,128)S(1)} all-to-all(f32[8,128,128]{2,1,0:T(8,128)S(1)} %bitcast.34), channel_id=1, replica_groups=mesh['slab'=32,'pencil'=8] {'pencil'}, dimensions={0} | all-to-all | bytes 1048576 | tf_op jit(solution)/shard_map/all_to_all | solution.py:468
  43.8 0.0 copy-done.3
  43.8 0.0 copy-done.4
  43.8 0.0 copy-start.10
  43.8 0.0 copy-start.13
  43.8 0.0 copy-start.16
  43.8 1.7 %y_forward.1 = f32[1024,128]{1,0:T(8,128)S(1)} custom-call(s32[6]{0:T(128)S(1)} %pad_add_fusion.refs_0_, f32[1024,128]{1,0:T(8,128)S(1)} %bitcast.28, bf16[2,512,512]{2,1,0:T(8,128)(2,1)S(1)} %copy-done.4, bf16[2,512,512]{2,1,0:T(8,128)(2,1)S(1)} %copy-done.3), custom_call_target="tpu_custom_call" | custom-call | tf_op jit(solution)/shard_map/y_forward/pallas_call | solution.py:147
  45.6 0.0 copy-start.5
  45.6 22.5 %all_to_all.37 = f32[32,32,128]{2,1,0:T(8,128)S(1)} all-to-all(f32[32,32,128]{2,1,0:T(8,128)S(1)} %bitcast.29), channel_id=1, replica_groups=mesh['slab'=32,'pencil'=8] {'slab'}, dimensions={0} | all-to-all | bytes 1048576 | tf_op jit(solution)/shard_map/all_to_all | solution.py:468
  68.0 0.0 copy-done.10
  68.0 0.0 copy-done.13
  68.0 0.0 copy-done.16
  68.1 0.0 copy-done.5
  68.1 0.0 copy-start.2
  68.1 4.1 %x_stage.1 = f32[1024,128]{1,0:T(8,128)S(1)} custom-call(s32[6]{0:T(128)S(1)} %pad_add_fusion.refs_0_, f32[1024,128]{1,0:T(8,128)S(1)} %bitcast.32, bf16[2,512,512]{2,1,0:T(8,128)(2,1)S(1)} %copy-done.5, f32[2,256,128]{2,1,0:T(8,128)S(1)} %copy-done.10, f32[32,256]{1,0:T(8,128)S(1)} %get-tuple-element.25.refs_4_, f32[2,32,256]{2,1,0:T(8,128)S(1)} %copy-done.13, ...), custom_call_target="tpu_custom_call" | custom-call | tf_op jit(solution)/shard_map/x_stage/pallas_call | solution.py:147
  72.1 0.0 copy-start.1
  72.2 21.3 %all_to_all.38 = f32[32,32,128]{2,1,0:T(8,128)S(1)} all-to-all(f32[32,32,128]{2,1,0:T(8,128)S(1)} %bitcast.33), channel_id=1, replica_groups=mesh['slab'=32,'pencil'=8] {'slab'}, dimensions={0} | all-to-all | bytes 1048576 | tf_op jit(solution)/shard_map/all_to_all | solution.py:468
  93.5 0.0 copy-done.2
  93.5 0.0 copy-done.1
  93.5 1.7 %y_backward.1 = f32[1024,128]{1,0:T(8,128)S(1)} custom-call(s32[6]{0:T(128)S(1)} %pad_add_fusion.refs_0_, f32[1024,128]{1,0:T(8,128)S(1)} %bitcast.30, bf16[2,512,512]{2,1,0:T(8,128)(2,1)S(1)} %copy-done.2, bf16[2,512,512]{2,1,0:T(8,128)(2,1)S(1)} %copy-done.1), custom_call_target="tpu_custom_call" | custom-call | tf_op jit(solution)/shard_map/y_backward/pallas_call | solution.py:147
  95.2 0.0 copy-start.8
  95.2 12.9 %all_to_all.39 = f32[8,128,128]{2,1,0:T(8,128)S(1)} all-to-all(f32[8,128,128]{2,1,0:T(8,128)S(1)} %bitcast.31), channel_id=1, replica_groups=mesh['slab'=32,'pencil'=8] {'pencil'}, dimensions={0} | all-to-all | bytes 1048576 | tf_op jit(solution)/shard_map/all_to_all | solution.py:468
  108.2 0.0 copy-done.8
  108.2 0.0 copy-start.14
  108.2 0.0 copy-start.15
  108.2 0.0 copy-start.18
  108.2 0.0 copy-start.12
  108.2 4.0 %sample.1 = f32[32,128]{1,0:T(8,128)} custom-call(f32[1024,128]{1,0:T(8,128)S(1)} %bitcast.27, f32[128,768]{1,0:T(8,128)S(1)} %get-tuple-element.26.refs_1_, s32[1,1,768]{2,1,0:T(1,128)S(1)} %reshape.48.refs_2_, bf16[2,256,256]{2,1,0:T(8,128)(2,1)S(1)} %copy-done.8, bf16[768,128]{1,0:T(8,128)(2,1)S(1)} %copy-done.6), custom_call_target="tpu_custom_call" | custom-call | tf_op jit(solution)/shard_map/sample/pallas_call | solution.py:147
  112.2 5.7 %all-to-all-start.5 = ((f32[32,1,128]{2,1,0:T(1,128)}), f32[32,1,128]{2,1,0:T(1,128)S(1)}, u32[]{:S(2)}, u32[]{:S(2)}) async-start(f32[32,1,128]{2,1,0:T(1,128)} %bitcast.20), calls=%async_computation.5 | async-start | bytes 32768 | tf_op jit(solution)/shard_map/all_to_all | solution.py:571
  117.9 0.0 copy-done.14
  117.9 0.0 copy-done.15
  117.9 0.0 copy-done.18
  117.9 0.0 copy-start.17
  118.0 0.7 near.1.refs_4_
  118.7 7.8 %all-to-all-done.5 = f32[32,1,128]{2,1,0:T(1,128)S(1)} async-done(((f32[32,1,128]{2,1,0:T(1,128)}), f32[32,1,128]{2,1,0:T(1,128)S(1)}, u32[]{:S(2)}, u32[]{:S(2)}) %all-to-all-start.5) | async-done | bytes 16416 | tf_op jit(solution)/shard_map/all_to_all | solution.py:571
  126.4 0.0 copy-done.12
  126.4 0.0 copy-done.11
  126.4 0.0 copy-done.17
  126.4 1.0 finish.1
  (4 shorter events, 0.0 us)
Async XLA Ops:
  0.0 14.2 %copy-start = (f32[8,32,512]{2,1,0:T(8,128)S(1)}, f32[8,32,512]{2,1,0:T(8,128)}, u32[]{:S(2)}) copy-start(f32[8,32,512]{2,1,0:T(8,128)} %refs_1_.4) | copy-start | bytes 1572868
  2.6 22.5 %all-to-all-start = ((f32[32,1,1920]{2,1,0:T(1,128)}), f32[32,1,1920]{2,1,0:T(1,128)S(1)}, u32[]{:S(2)}, u32[]{:S(2)}) async-start(f32[32,1,1920]{2,1,0:T(1,128)} %bitcast.38), calls=%async_computation | async-start | bytes 491520 | tf_op jit(solution)/shard_map/all_to_all | solution.py:536
  14.2 2.1 %copy-start.19 = (s32[1,1,768]{2,1,0:T(1,128)S(1)}, s32[1,1,768]{2,1,0:T(1,128)}, u32[]{:S(2)}) copy-start(s32[1,1,768]{2,1,0:T(1,128)} %param.23) | copy-start | bytes 9220
  14.5 10.5 %copy-start.7 = (bf16[2,256,256]{2,1,0:T(8,128)(2,1)S(1)}, bf16[2,256,256]{2,1,0:T(8,128)(2,1)}, u32[]{:S(2)}) copy-start(bf16[2,256,256]{2,1,0:T(8,128)(2,1)} %constant.65.clone.refs_3_) | copy-start | bytes 786436
  14.5 7.3 %collective-permute-start = (f32[8,512]{1,0:T(8,128)S(1)}, f32[8,512]{1,0:T(8,128)S(1)}, u32[]{:S(2)}, u32[]{:S(2)}) collective-permute-start(f32[8,512]{1,0:T(8,128)S(1)} %slice_bitcast_fusion), channel_id=1, source_target_pairs={{4,0},{12,8},{20,16},{28,24},{36,32},{44,40},{52,48},{60,56},{68,6... | collective-permute-start | bytes 49160 | tf_op jit(solution)/shard_map/ppermute | solution.py:535
  16.4 8.7 %copy-start.6 = (bf16[768,128]{1,0:T(8,128)(2,1)S(1)}, bf16[768,128]{1,0:T(8,128)(2,1)}, u32[]{:S(2)}) copy-start(bf16[768,128]{1,0:T(8,128)(2,1)} %constant.77.clone.refs_1_.refs_4_) | copy-start | bytes 589828
  16.5 27.3 %copy-start.3 = (bf16[2,512,512]{2,1,0:T(8,128)(2,1)S(1)}, bf16[2,512,512]{2,1,0:T(8,128)(2,1)}, u32[]{:S(2)}) copy-start(bf16[2,512,512]{2,1,0:T(8,128)(2,1)} %constant.68.clone.refs_3_) | copy-start | bytes 3145732
  16.5 27.3 %copy-start.4 = (bf16[2,512,512]{2,1,0:T(8,128)(2,1)S(1)}, bf16[2,512,512]{2,1,0:T(8,128)(2,1)}, u32[]{:S(2)}) copy-start(bf16[2,512,512]{2,1,0:T(8,128)(2,1)} %constant.67.clone.refs_2_) | copy-start | bytes 3145732
  23.0 0.7 copy-start.9
  43.8 24.2 %copy-start.10 = (f32[2,256,128]{2,1,0:T(8,128)S(1)}, f32[2,256,128]{2,1,0:T(8,128)}, u32[]{:S(2)}) copy-start(f32[2,256,128]{2,1,0:T(8,128)} %copy-done.9) | copy-start | bytes 786436
  43.8 24.2 %copy-start.13 = (f32[2,32,256]{2,1,0:T(8,128)S(1)}, f32[2,32,256]{2,1,0:T(8,128)}, u32[]{:S(2)}) copy-start(f32[2,32,256]{2,1,0:T(8,128)} %constant.74.clone.refs_5_) | copy-start | bytes 196612
  43.8 24.2 %copy-start.16 = (bf16[2,64,64]{2,1,0:T(8,128)(2,1)S(1)}, bf16[2,64,64]{2,1,0:T(8,128)(2,1)}, u32[]{:S(2)}) copy-start(bf16[2,64,64]{2,1,0:T(8,128)(2,1)} %constant.73.clone.refs_7_) | copy-start | bytes 49156
  45.6 22.5 %copy-start.5 = (bf16[2,512,512]{2,1,0:T(8,128)(2,1)S(1)}, bf16[2,512,512]{2,1,0:T(8,128)(2,1)}, u32[]{:S(2)}) copy-start(bf16[2,512,512]{2,1,0:T(8,128)(2,1)} %constant.71.clone.refs_2_) | copy-start | bytes 3145732
  68.1 25.4 %copy-start.2 = (bf16[2,512,512]{2,1,0:T(8,128)(2,1)S(1)}, bf16[2,512,512]{2,1,0:T(8,128)(2,1)}, u32[]{:S(2)}) copy-start(bf16[2,512,512]{2,1,0:T(8,128)(2,1)} %constant.69.clone.refs_2_) | copy-start | bytes 3145732
  72.1 21.3 %copy-start.1 = (bf16[2,512,512]{2,1,0:T(8,128)(2,1)S(1)}, bf16[2,512,512]{2,1,0:T(8,128)(2,1)}, u32[]{:S(2)}) copy-start(bf16[2,512,512]{2,1,0:T(8,128)(2,1)} %constant.70.clone.refs_3_) | copy-start | bytes 3145732
  95.2 13.0 %copy-start.8 = (bf16[2,256,256]{2,1,0:T(8,128)(2,1)S(1)}, bf16[2,256,256]{2,1,0:T(8,128)(2,1)}, u32[]{:S(2)}) copy-start(bf16[2,256,256]{2,1,0:T(8,128)(2,1)} %constant.66.clone.refs_3_) | copy-start | bytes 786436
  108.2 9.7 %copy-start.14 = (s32[32,256]{1,0:T(8,128)S(1)}, s32[32,256]{1,0:T(8,128)}, u32[]{:S(2)}) copy-start(s32[32,256]{1,0:T(8,128)} %refs_3_.6) | copy-start | bytes 98308
  108.2 9.8 %copy-start.15 = (f32[32,256]{1,0:T(8,128)S(1)}, f32[32,256]{1,0:T(8,128)}, u32[]{:S(2)}) copy-start(f32[32,256]{1,0:T(8,128)} %refs_4_.2) | copy-start | bytes 98308
  108.2 9.8 %copy-start.18 = (f32[256]{0:T(256)S(1)}, f32[256]{0:T(256)}, u32[]{:S(2)}) copy-start(f32[256]{0:T(256)} %param.20) | copy-start | bytes 3076
  108.2 18.3 %copy-start.12 = (bf16[768,128]{1,0:T(8,128)(2,1)S(1)}, bf16[768,128]{1,0:T(8,128)(2,1)}, u32[]{:S(2)}) copy-start(bf16[768,128]{1,0:T(8,128)(2,1)} %constant.75.clone.refs_1_) | copy-start | bytes 589828
  112.2 14.2 %copy-start.11 = (bf16[768,32]{1,0:T(8,128)(2,1)S(1)}, bf16[768,32]{1,0:T(8,128)(2,1)}, u32[]{:S(2)}) copy-start(bf16[768,32]{1,0:T(8,128)(2,1)} %constant.76.clone.refs_2_) | copy-start | bytes 147460
  112.2 14.2 %all-to-all-start.5 = ((f32[32,1,128]{2,1,0:T(1,128)}), f32[32,1,128]{2,1,0:T(1,128)S(1)}, u32[]{:S(2)}, u32[]{:S(2)}) async-start(f32[32,1,128]{2,1,0:T(1,128)} %bitcast.20), calls=%async_computation.5 | async-start | bytes 32768 | tf_op jit(solution)/shard_map/all_to_all | solution.py:571
  117.9 8.5 %copy-start.17 = (s32[1,1,768]{2,1,0:T(1,128)S(1)}, s32[1,1,768]{2,1,0:T(1,128)}, u32[]{:S(2)}) copy-start(s32[1,1,768]{2,1,0:T(1,128)} %refs_3_.7) | copy-start | bytes 9220

commit v6 on v5

--- a/solution.py
+++ b/solution.py
@@ -115,41 +115,15 @@
     return mm(left[0], right[0]) + (mm(left[0], right[1]) + mm(left[1], right[0]))
 
 
-class Late:
-    def __init__(self, copy, buffer):
-        self.copy, self.buffer, self.here = copy, buffer, False
-
-    def __getitem__(self, index):
-        if not self.here:
-            self.copy.wait()
-            self.here = True
-        return self.buffer[index]
-
-
-def call(kernel, out_shape, *args, scratch=(), smem=(), late=(), limit=20):
-    spaces = {i: pltpu.SMEM for i in smem} | {i: pltpu.HBM for i in late}
-    specs = [pl.BlockSpec(memory_space=spaces.get(i, pltpu.VMEM)) for i in range(len(args))]
-    multi = isinstance(out_shape, list)
+def call(kernel, out_shape, *args, scratch=(), smem=(), limit):
+    space = {i: pltpu.SMEM for i in smem}
     out_spec = pl.BlockSpec(memory_space=pltpu.VMEM)
-    buffers = [pltpu.VMEM(args[i].shape, args[i].dtype) for i in late]
-    if late:
-        buffers.append(pltpu.SemaphoreType.DMA((len(late),)))
-    own = len(args) + (len(out_shape) if multi else 1) + len(scratch)
-
-    def wrapped(*refs):
-        ins = list(refs[: len(args)])
-        for place, i in enumerate(late):
-            copy = pltpu.make_async_copy(ins[i], refs[own + place], refs[-1].at[place])
-            copy.start()
-            ins[i] = Late(copy, refs[own + place])
-        kernel(*ins, *refs[len(args) : own])
-
     return pl.pallas_call(
-        wrapped,
+        kernel,
         out_shape=out_shape,
-        in_specs=specs,
-        out_specs=[out_spec] * len(out_shape) if multi else out_spec,
-        scratch_shapes=list(scratch) + buffers,
+        in_specs=[pl.BlockSpec(memory_space=space.get(i, pltpu.VMEM)) for i in range(len(args))],
+        out_specs=[out_spec] * len(out_shape) if isinstance(out_shape, list) else out_spec,
+        scratch_shapes=list(scratch),
         compiler_params=pltpu.CompilerParams(vmem_limit_bytes=limit * 2**20),
         name=kernel.__name__,
     )(*args)
@@ -190,32 +164,37 @@
     return (slot >= slab * width) & (slot < slab * width + width)
 
 
+def received_place():
+    slot = lax.broadcasted_iota(jnp.int32, (SLOTS, 128), 0)
+    lane = lax.broadcasted_iota(jnp.int32, (SLOTS, 128), 1)
+    twelfth = quotient(slot, 12)
+    place = slot - twelfth * 12 + jnp.where(slot >= SLOTS // 2, 12, 0)
+    return jnp.where(lane == place, 1.0, 0.0).astype(BF16)
+
+
 def received_slots():
     own = own_slots(CAP // 2, SLOTS // 2)
     return jnp.concatenate([own, own], axis=1)
 
 
 def pack(slot_ref, weight_ref, strength_ref, out_ref):
-    slots = jnp.broadcast_to(slot_ref[0], (N_SLAB, SLOTS)).astype(F32)
-    index = lax.broadcasted_iota(jnp.int32, (SLOTS, 128), 0)
-    lane = lax.broadcasted_iota(jnp.int32, (SLOTS, 128), 1)
-    spread = jnp.where((lane < CAP) & (quotient(index, CAP) * CAP + lane == index), 1.0, 0.0)
-    by_slab = mm(jnp.where(own_slots(CAP, SLOTS), slots, 0.0).astype(BF16), spread.astype(BF16))
-    lane = lax.broadcasted_iota(jnp.int32, by_slab.shape, 1)
-    by_slab = jnp.where(lane < CAP, by_slab, float(PAN_DEV))
     line = lax.broadcasted_iota(jnp.int32, (ROWS, 128), 0)
     lane = lax.broadcasted_iota(jnp.int32, (ROWS, 128), 1)
     slab = quotient(line, LINES)
     place = line - slab * LINES
-    mine = jnp.where(lane == slab, 1.0, 0.0).astype(BF16)[:, :N_SLAB]
-    lines = mm(mine, by_slab.astype(BF16))
-    ones = jnp.ones((128, 128), BF16)
-    panel = lane.astype(F32)
+    target = jnp.where(place < 12, slab * CAP + place, -CAP)
+    picks = []
+    for shift in (0, 12):
+        tiles = [jnp.where(lane + part * 128 == target + shift, 1.0, 0.0) for part in range(SLOTS // 128)]
+        picks.append(jnp.concatenate(tiles, axis=1).astype(BF16))
+    slots = (slot_ref[0].astype(F32) + 1.0) * jnp.where(slot_ref[0] < PAN_DEV, 1.0, 0.0)
+    rows = jnp.broadcast_to(slots, (128, SLOTS)).astype(BF16)
+    chosen = mm_nt(jnp.concatenate(picks, axis=0), rows)
+    panel = lane.astype(F32) + 1.0
     hot = []
-    for shift in (0, 12):
-        pick = lane == jnp.where(place < 12, place + shift, CAP)
-        chosen = mm(jnp.where(pick, lines, 0.0).astype(BF16), ones)
-        hot += [chosen == panel, chosen == panel + 128.0]
+    for half in range(2):
+        part = chosen[half * ROWS : half * ROWS + ROWS]
+        hot += [part == panel, part == panel + 128.0]
     hot = jnp.where(jnp.concatenate(hot, axis=1), 1.0, 0.0).astype(BF16)
     weight = weight_ref[...]
     empty = jnp.zeros_like(weight)
@@ -224,9 +203,15 @@
     )
     high, low = split(values)
     out_ref[...] = mm_nt(hot, high) + mm_nt(hot, low)
+    index = lax.broadcasted_iota(jnp.int32, (SLOTS, 128), 0)
+    lane = lax.broadcasted_iota(jnp.int32, (SLOTS, 128), 1)
+    spread = jnp.where((lane < CAP) & (quotient(index, CAP) * CAP + lane == index), 1.0, 0.0)
+    own = own_slots(CAP, SLOTS)
+    by_slab = mm(jnp.where(own, jnp.broadcast_to(slots, own.shape), 0.0).astype(BF16), spread.astype(BF16))
     strength = strength_ref[...]
     tables = [strength[:, :128], strength[:, 128:]]
     index = by_slab.astype(jnp.int32)
+    index = jnp.where(index > 0, index - 1, PAN_DEV)
     sent = jnp.concatenate([lookup(tables, index[i * 8 : i * 8 + 8]) for i in range(4)], axis=0)
     out_ref[pl.ds(12, N_SLAB, stride=LINES), :] = sent
     for half in range(2):
@@ -282,7 +267,7 @@
     return jnp.where((lane == picked) & (dy < EDGE), 1.0, 0.0).astype(BF16)
 
 
-def project(arrived_ref, spread_ref, anchor_ref, z_ref, out_ref, weight_ref, scaled_ref, y_ref, rows_ref, packed_ref, high_ref, low_ref):
+def project(arrived_ref, anchor_ref, z_ref, out_ref, weight_ref, scaled_ref, y_ref, rows_ref, packed_ref, high_ref, low_ref):
     for s in range(N_SLAB):
         packed_ref[s * 12 : s * 12 + 12, :] = arrived_ref[s * LINES : s * LINES + 12, :]
     packed = jnp.concatenate(split(packed_ref[...]), axis=0)
@@ -292,7 +277,7 @@
     weights = jnp.concatenate(turned, axis=1)
     weight_ref[...] = weights
     high, low = split(arrived_ref[pl.ds(12, N_SLAB, stride=LINES), :])
-    spread = spread_ref[...]
+    spread = received_place()
     strength = jnp.where(received_slots(), mm_nt(high, spread) + mm_nt(low, spread), 0.0)
     scaled_ref[...] = weights * jnp.sum(strength, axis=0, keepdims=True)
     first, second, third = anchor_parts(anchor_ref[0])
@@ -409,7 +394,7 @@
     scattered(rows, out_ref, 32, 16)
 
 
-def sample(in_ref, weight_ref, anchor_ref, z_ref, spread_ref, out_ref, y_ref, after_ref, rows_ref, grid_ref):
+def sample(in_ref, weight_ref, anchor_ref, z_ref, out_ref, y_ref, after_ref, rows_ref, grid_ref):
     for half in range(2):
         for quarter in range(2):
             tiles = []
@@ -435,10 +420,16 @@
             total += jnp.sum(cells.reshape(4, 8, SLOTS), axis=0)
     far = jnp.sum(total, axis=0, keepdims=True)
     high, low = split(jnp.where(received_slots(), jnp.broadcast_to(far, (N_SLAB, SLOTS)), 0.0))
-    out_ref[...] = mm(high, spread_ref[...]) + mm(low, spread_ref[...])
-
-
-def near(flag_ref, arrived_ref, own_ref, index_ref, factor_ref, out_ref):
+    spread = received_place()
+    out_ref[...] = mm(high, spread) + mm(low, spread)
+
+
+def near(flag_ref, arrived_ref, slot_ref, own_ref, index_ref, factor_ref, out_ref, hot_ref):
+    slots = jnp.transpose(jnp.broadcast_to(slot_ref[0], (128, SLOTS)))
+    panel = lax.broadcasted_iota(jnp.int32, (SLOTS, 128), 1)
+    for half in range(2):
+        hot = jnp.where(slots == panel + half * 128, 1.0, 0.0)
+        hot_ref[:, half * 128 : half * 128 + 128] = hot.astype(BF16)
     before = [arrived_ref[pl.ds(flag_ref[4] + half, 1), :] for half in range(2)]
     after = [arrived_ref[pl.ds(flag_ref[5] + half, 1), :] for half in range(2)]
     tables = before + [own_ref[:, :128], own_ref[:, 128:]] + after
@@ -450,17 +441,16 @@
         out_ref[:, lane * 128 : lane * 128 + 128] = jnp.sum(total, axis=0, keepdims=True)
 
 
-def finish(far_ref, spread_ref, own_ref, slot_ref, near_ref, out_ref):
-    high, low = split(far_ref[...])
-    own = own_ref[...]
-    rows = (mm(own, high) + mm(own, low)) * spread_ref[...].astype(F32)
-    column = jnp.sum(rows, axis=1, keepdims=True)
-    slots = jnp.transpose(jnp.broadcast_to(slot_ref[0], (128, SLOTS)))
-    panel = lax.broadcasted_iota(jnp.int32, (SLOTS, 128), 1)
-    for lane in range(2):
-        part = jnp.where(slots == panel + lane * 128, column, 0.0)
-        at = slice(lane * 128, lane * 128 + 128)
-        out_ref[:, at] = jnp.sum(part, axis=0, keepdims=True) + near_ref[:, at]
+def finish(far_ref, hot_ref, near_ref, out_ref):
+    index = lax.broadcasted_iota(jnp.int32, (SLOTS, 128), 0)
+    lane = lax.broadcasted_iota(jnp.int32, (SLOTS, 128), 1)
+    spread = jnp.where((lane < CAP) & (quotient(index, CAP) * CAP + lane == index), 1.0, 0.0)
+    by_slot = mm_nt(jnp.concatenate(split(far_ref[...]), axis=0), spread.astype(BF16))
+    by_slot = jnp.where(own_slots(CAP, SLOTS), by_slot[:N_SLAB] + by_slot[N_SLAB:], 0.0)
+    row = jnp.broadcast_to(jnp.sum(by_slot, axis=0, keepdims=True), (8, SLOTS))
+    high, low = split(row)
+    hot = hot_ref[...]
+    out_ref[...] = (mm(high, hot) + mm(low, hot))[:1] + near_ref[...]
 
 
 def swap(value, axis, count):
@@ -500,15 +490,6 @@
             out_ref[half, pl.ds(k, 32, stride=8), :] = laid[:, half * 128 : half * 128 + 128]
 
 
-def slot_tables():
-    index = np.arange(SLOTS)
-    lane = np.arange(128)[None, :]
-    spread = (index % CAP)[:, None] == lane
-    own = (index // CAP)[:, None] == np.arange(N_SLAB)[None, :]
-    received = (index // (SLOTS // 2) * 12 + index % 12)[:, None] == lane
-    return [jnp.asarray(t, BF16) for t in (spread, own, received)]
-
-
 def per_device(strength, stencil_weight, slot_panel, slot_anchor, green_spectrum, near_index, near_factor):
     slab = lax.axis_index("slab")
     pencil = lax.axis_index("pencil")
@@ -523,7 +504,6 @@
     rows, twist, lanes, line = x_tables()
     rows, lanes, line = (pair(t) for t in (rows, lanes, line))
     twist = jnp.asarray(twist, F32)
-    spread, own, received = slot_tables()
 
     anchor = slot_anchor.reshape(N_SLAB, 2, 12).transpose(1, 0, 2).reshape(1, 1, SLOTS)
 
@@ -538,13 +518,16 @@
         arrange_green, [shape((2, 256, 128), F32), shape((32, 256), F32)], flags, spectrum, plane, smem=(0,), limit=LIMIT_N
     )
     arrived, green, other, flags, anchor = lax.optimization_barrier((arrived, green, other, flags, anchor))
-    near_field = call(near, shape((1, PAN_DEV), F32), flags, arrived, row, near_index, near_factor, smem=(0,), limit=LIMIT_N)
+    near_field, hot = call(
+        near, [shape((1, PAN_DEV), F32), shape((SLOTS, PAN_DEV), BF16)], flags, arrived, slot_panel, row, near_index, near_factor,
+        smem=(0,), limit=LIMIT_N,
+    )
     after_z, weights = call(
-        project, [shape((1024, 128), F32), shape((128, SLOTS), F32)], arrived, received, anchor, z_fwd,
+        project, [shape((1024, 128), F32), shape((128, SLOTS), F32)], arrived, anchor, z_fwd,
         scratch=[pltpu.VMEM((128, SLOTS), F32), pltpu.VMEM((PENCIL_ROWS, SLOTS), jnp.int32)]
         + [pltpu.VMEM((512, SLOTS), F32), pltpu.VMEM((SLOTS // 2, 128), F32)]
         + [pltpu.VMEM((EDGE, 512, SLOTS), BF16)] * 2,
-        late=(3,), limit=LIMIT_P,
+        limit=LIMIT_P,
     )
     by_y = swap(after_z, "pencil", N_PENCIL)
     after_y = call(
@@ -554,7 +537,7 @@
     by_x = swap(after_y, "slab", N_SLAB)
     after_x = call(
         x_stage, shape((1024, 128), F32), flags, by_x, rows, green, other, twist, lanes, line,
-        scratch=[pltpu.VMEM((2, 256, 128), F32)] * 2, smem=(0,), late=range(5, 8), limit=LIMIT_X,
+        scratch=[pltpu.VMEM((2, 256, 128), F32)] * 2, smem=(0,), limit=LIMIT_X,
     )
     back_x = swap(after_x, "slab", N_SLAB)
     back_y = call(
@@ -563,13 +546,13 @@
     )
     by_z = swap(back_y, "pencil", N_PENCIL)
     sampled = call(
-        sample, shape((N_SLAB, 128), F32), by_z, weights, anchor, z_bwd, received,
+        sample, shape((N_SLAB, 128), F32), by_z, weights, anchor, z_bwd,
         scratch=[pltpu.VMEM((PENCIL_ROWS, SLOTS), jnp.int32), pltpu.VMEM((512, 256), F32)]
         + [pltpu.VMEM((512, SLOTS), F32), pltpu.VMEM((EDGE, 512, SLOTS), F32)],
         limit=LIMIT_S,
     )
     far = lax.all_to_all(sampled, "slab", 0, 0, tiled=True)
-    return call(finish, shape((1, PAN_DEV), F32), far, spread, own, slot_panel, near_field, limit=40).reshape(PAN_DEV)
+    return call(finish, shape((1, PAN_DEV), F32), far, hot, near_field, limit=40).reshape(PAN_DEV)
 
 
 def solution(mesh):

time: 128 us -> 128 us (level)
  no operation moved by 1% of the time
where the time goes in v6:
time: 128 us; the launch traced here: 127 us
  blocking collectives  70.7 us (55%)
  Pallas kernels  21.8 us (17%)
  starting transfers between devices  18.7 us (15%)
  waiting for transfers between devices  14.9 us (12%)
    all_to_all x4, blocking collectives, swap(): lax.all_to_all(value.reshape(count, rows // count, 128), axis, 0, 0, tile...  70.7 us
    pallas_call x9, Pallas kernels, call(): pl.pallas_call(kernel, out_shape=out_shape, in_specs=[pl.BlockSpec(memory...  21.8 us
    all_to_all x1, starting transfers between devices, per_device(): lax.all_to_all(payload.reshape(N_SLAB, 1, LINES * 128), 'slab', 0, 0, til...  11.6 us
    all_to_all x1, waiting for transfers between devices, per_device(): far = lax.all_to_all(sampled, 'slab', 0, 0, tiled=True)  7.66 us
    all_to_all x1, starting transfers between devices, per_device(): far = lax.all_to_all(sampled, 'slab', 0, 0, tiled=True)  5.7 us
    ppermute x1, waiting for transfers between devices, per_device(): plane = lax.ppermute(spectrum[:, 0, :], 'pencil', [(4, 0)])  5.28 us
  transfers between devices with their start and end apart: 3, of which 3 were waited for; matrix products, arithmetic and copies ran while one was open for 1% of the time, Pallas kernels for 2%

profile of v6, /device:TPU:2, one launch (start us, length us, event | category | flops | bytes accessed | tf_op | source)
XLA Modules:
  0.0 127.2 jit_solution(4269401691516617011)
XLA Ops:
  0.0 0.0 copy-start
  0.0 2.9 %pack.1 = f32[480,128]{1,0:T(8,128)} custom-call(s32[1,1,768]{2,1,0:T(1,128)} %slot_ref.3, f32[64,256]{1,0:T(8,128)} %weight_ref.1, f32[1,256]{1,0:T(1,128)} %bitcast.36), custom_call_target="tpu_custom_call" | custom-call | tf_op jit(solution)/shard_map/pack/pallas_call | solution.py:121
  2.9 11.6 %all-to-all-start = ((f32[32,1,1920]{2,1,0:T(1,128)}), f32[32,1,1920]{2,1,0:T(1,128)S(1)}, u32[]{:S(2)}, u32[]{:S(2)}) async-start(f32[32,1,1920]{2,1,0:T(1,128)} %bitcast.38), calls=%async_computation | async-start | bytes 491520 | tf_op jit(solution)/shard_map/all_to_all | solution.py:516
  14.5 0.0 copy-done
  14.5 0.0 copy-start.14
  14.5 0.3 copy.23
  14.9 0.0 copy-start.6
  14.9 1.4 %collective-permute-start = (f32[8,512]{1,0:T(8,128)S(1)}, f32[8,512]{1,0:T(8,128)S(1)}, u32[]{:S(2)}, u32[]{:S(2)}) collective-permute-start(f32[8,512]{1,0:T(8,128)S(1)} %slice_bitcast_fusion), channel_id=1, source_target_pairs={{4,0},{12,8},{20,16},{28,24},{36,32},{44,40},{52,48},{60,56},{68,6... | collective-permute-start | bytes 49160 | tf_op jit(solution)/shard_map/ppermute | solution.py:515
  16.4 0.1 fusion
  16.4 0.1 add_convert_fusion
  16.5 0.1 pad_add_fusion.flag_ref.refs_0_
  16.6 0.0 copy-done.14
  16.6 0.1 reshape.47
  16.7 0.1 reshape.48.anchor_ref
  16.8 0.0 copy-start.3
  16.9 0.0 copy-start.4
  16.9 5.3 %collective-permute-done.plane_ref = f32[8,512]{1,0:T(8,128)S(1)} collective-permute-done((f32[8,512]{1,0:T(8,128)S(1)}, f32[8,512]{1,0:T(8,128)S(1)}, u32[]{:S(2)}, u32[]{:S(2)}) %collective-permute-start) | collective-permute-done | bytes 16416 | tf_op jit(solution)/shard_map/ppermute | solution.py:515
  22.2 1.2 arrange_green.1
  23.4 2.0 %all-to-all-done = f32[32,1,1920]{2,1,0:T(1,128)S(1)} async-done(((f32[32,1,1920]{2,1,0:T(1,128)}), f32[32,1,1920]{2,1,0:T(1,128)S(1)}, u32[]{:S(2)}, u32[]{:S(2)}) %all-to-all-start) | async-done | bytes 245792 | tf_op jit(solution)/shard_map/all_to_all | solution.py:516
  25.4 0.0 copy-done.6
  25.4 3.9 %project.1 = (f32[1024,128]{1,0:T(8,128)S(1)}, f32[128,768]{1,0:T(8,128)S(1)}) custom-call(f32[480,128]{1,0:T(8,128)S(1)} %bitcast.25, s32[1,1,768]{2,1,0:T(1,128)S(1)} %reshape.48.anchor_ref, bf16[2,256,256]{2,1,0:T(8,128)(2,1)S(1)} %copy-done.6), custom_call_target="tpu_custom_call" | custom-call | tf_op jit(solution)/shard_map/project/pallas_call | solution.py:121
  29.3 14.7 %all_to_all.36 = f32[8,128,128]{2,1,0:T(8,128)S(1)} all-to-all(f32[8,128,128]{2,1,0:T(8,128)S(1)} %bitcast.34), channel_id=1, replica_groups=mesh['slab'=32,'pencil'=8] {'pencil'}, dimensions={0} | all-to-all | bytes 1048576 | tf_op jit(solution)/shard_map/all_to_all | solution.py:458
  44.0 0.0 copy-done.3
  44.0 0.0 copy-done.4
  44.0 0.0 copy-start.8
  44.0 0.0 copy-start.11
  44.0 1.7 %y_forward.1 = f32[1024,128]{1,0:T(8,128)S(1)} custom-call(s32[6]{0:T(128)S(1)} %pad_add_fusion.flag_ref.refs_0_, f32[1024,128]{1,0:T(8,128)S(1)} %bitcast.28, bf16[2,512,512]{2,1,0:T(8,128)(2,1)S(1)} %copy-done.3, bf16[2,512,512]{2,1,0:T(8,128)(2,1)S(1)} %copy-done.4), custom_call_target="tpu_custom_call" | custom-call | tf_op jit(solution)/shard_map/y_forward/pallas_call | solution.py:121
  45.7 0.0 copy-start.5
  45.8 21.8 %all_to_all.37 = f32[32,32,128]{2,1,0:T(8,128)S(1)} all-to-all(f32[32,32,128]{2,1,0:T(8,128)S(1)} %bitcast.29), channel_id=1, replica_groups=mesh['slab'=32,'pencil'=8] {'slab'}, dimensions={0} | all-to-all | bytes 1048576 | tf_op jit(solution)/shard_map/all_to_all | solution.py:458
  67.5 0.0 copy-done.8
  67.5 0.0 copy-done.11
  67.5 0.0 copy-done.5
  67.5 0.0 copy-start.2
  67.5 4.3 %x_stage.1 = f32[1024,128]{1,0:T(8,128)S(1)} custom-call(s32[6]{0:T(128)S(1)} %pad_add_fusion.flag_ref.refs_0_, f32[1024,128]{1,0:T(8,128)S(1)} %bitcast.32, bf16[2,512,512]{2,1,0:T(8,128)(2,1)S(1)} %copy-done.5, f32[2,256,128]{2,1,0:T(8,128)S(1)} %get-tuple-element.26.green_ref, f32[32,256]{1,0:T(8,128)S(1)} %get-tuple-element.27.other_ref, ...), custom_call_target="tpu_custom_call" | custom-call | tf_op jit(solution)/shard_map/x_stage/pallas_call | solution.py:121
  71.8 0.0 copy-start.1
  71.9 21.3 %all_to_all.38 = f32[32,32,128]{2,1,0:T(8,128)S(1)} all-to-all(f32[32,32,128]{2,1,0:T(8,128)S(1)} %bitcast.33), channel_id=1, replica_groups=mesh['slab'=32,'pencil'=8] {'slab'}, dimensions={0} | all-to-all | bytes 1048576 | tf_op jit(solution)/shard_map/all_to_all | solution.py:458
  93.2 0.0 copy-done.2
  93.2 0.0 copy-done.1
  93.2 1.7 %y_backward.1 = f32[1024,128]{1,0:T(8,128)S(1)} custom-call(s32[6]{0:T(128)S(1)} %pad_add_fusion.flag_ref.refs_0_, f32[1024,128]{1,0:T(8,128)S(1)} %bitcast.30, bf16[2,512,512]{2,1,0:T(8,128)(2,1)S(1)} %copy-done.1, bf16[2,512,512]{2,1,0:T(8,128)(2,1)S(1)} %copy-done.2), custom_call_target="tpu_custom_call" | custom-call | tf_op jit(solution)/shard_map/y_backward/pallas_call | solution.py:121
  94.9 0.0 copy-start.7
  94.9 12.9 %all_to_all.39 = f32[8,128,128]{2,1,0:T(8,128)S(1)} all-to-all(f32[8,128,128]{2,1,0:T(8,128)S(1)} %bitcast.31), channel_id=1, replica_groups=mesh['slab'=32,'pencil'=8] {'pencil'}, dimensions={0} | all-to-all | bytes 1048576 | tf_op jit(solution)/shard_map/all_to_all | solution.py:458
  107.9 0.0 copy-done.7
  107.9 0.0 copy-start.10
  107.9 0.0 copy-start.12
  107.9 4.1 %sample.1 = f32[32,128]{1,0:T(8,128)} custom-call(f32[1024,128]{1,0:T(8,128)S(1)} %bitcast.27, f32[128,768]{1,0:T(8,128)S(1)} %get-tuple-element.28.weight_ref, s32[1,1,768]{2,1,0:T(1,128)S(1)} %reshape.48.anchor_ref, bf16[2,256,256]{2,1,0:T(8,128)(2,1)S(1)} %copy-done.7), custom_call_target="tpu_custom_call" | custom-call | tf_op jit(solution)/shard_map/sample/pallas_call | solution.py:121
  112.0 0.0 copy-start.9
  112.0 0.0 copy-start.13
  112.0 5.7 %all-to-all-start.5 = ((f32[32,1,128]{2,1,0:T(1,128)}), f32[32,1,128]{2,1,0:T(1,128)S(1)}, u32[]{:S(2)}, u32[]{:S(2)}) async-start(f32[32,1,128]{2,1,0:T(1,128)} %bitcast.20), calls=%async_computation.5 | async-start | bytes 32768 | tf_op jit(solution)/shard_map/all_to_all | solution.py:554
  117.7 0.0 copy-done.10
  117.7 0.0 copy-done.12
  117.7 0.0 copy-done.9
  117.7 0.0 copy-done.13
  117.7 0.8 near.1
  118.5 7.7 %all-to-all-done.5 = f32[32,1,128]{2,1,0:T(1,128)S(1)} async-done(((f32[32,1,128]{2,1,0:T(1,128)}), f32[32,1,128]{2,1,0:T(1,128)S(1)}, u32[]{:S(2)}, u32[]{:S(2)}) %all-to-all-start.5) | async-done | bytes 16416 | tf_op jit(solution)/shard_map/all_to_all | solution.py:554
  126.2 1.0 finish.1
  (3 shorter events, 0.0 us)
Async XLA Ops:
  0.0 14.5 %copy-start = (f32[8,32,512]{2,1,0:T(8,128)S(1)}, f32[8,32,512]{2,1,0:T(8,128)}, u32[]{:S(2)}) copy-start(f32[8,32,512]{2,1,0:T(8,128)} %green_ref) | copy-start | bytes 1572868
  2.9 22.5 %all-to-all-start = ((f32[32,1,1920]{2,1,0:T(1,128)}), f32[32,1,1920]{2,1,0:T(1,128)S(1)}, u32[]{:S(2)}, u32[]{:S(2)}) async-start(f32[32,1,1920]{2,1,0:T(1,128)} %bitcast.38), calls=%async_computation | async-start | bytes 491520 | tf_op jit(solution)/shard_map/all_to_all | solution.py:516
  14.5 2.1 %copy-start.14 = (s32[1,1,768]{2,1,0:T(1,128)S(1)}, s32[1,1,768]{2,1,0:T(1,128)}, u32[]{:S(2)}) copy-start(s32[1,1,768]{2,1,0:T(1,128)} %param.20) | copy-start | bytes 9220
  14.9 10.5 %copy-start.6 = (bf16[2,256,256]{2,1,0:T(8,128)(2,1)S(1)}, bf16[2,256,256]{2,1,0:T(8,128)(2,1)}, u32[]{:S(2)}) copy-start(bf16[2,256,256]{2,1,0:T(8,128)(2,1)} %constant.59.clone.z_ref) | copy-start | bytes 786436
  14.9 7.3 %collective-permute-start = (f32[8,512]{1,0:T(8,128)S(1)}, f32[8,512]{1,0:T(8,128)S(1)}, u32[]{:S(2)}, u32[]{:S(2)}) collective-permute-start(f32[8,512]{1,0:T(8,128)S(1)} %slice_bitcast_fusion), channel_id=1, source_target_pairs={{4,0},{12,8},{20,16},{28,24},{36,32},{44,40},{52,48},{60,56},{68,6... | collective-permute-start | bytes 49160 | tf_op jit(solution)/shard_map/ppermute | solution.py:515
  16.8 27.1 %copy-start.3 = (bf16[2,512,512]{2,1,0:T(8,128)(2,1)S(1)}, bf16[2,512,512]{2,1,0:T(8,128)(2,1)}, u32[]{:S(2)}) copy-start(bf16[2,512,512]{2,1,0:T(8,128)(2,1)} %constant.61.clone.refs_2_) | copy-start | bytes 3145732
  16.9 27.1 %copy-start.4 = (bf16[2,512,512]{2,1,0:T(8,128)(2,1)S(1)}, bf16[2,512,512]{2,1,0:T(8,128)(2,1)}, u32[]{:S(2)}) copy-start(bf16[2,512,512]{2,1,0:T(8,128)(2,1)} %constant.62.clone.refs_3_) | copy-start | bytes 3145732
  44.0 23.5 %copy-start.8 = (f32[2,32,256]{2,1,0:T(8,128)S(1)}, f32[2,32,256]{2,1,0:T(8,128)}, u32[]{:S(2)}) copy-start(f32[2,32,256]{2,1,0:T(8,128)} %constant.68.clone.twist_ref) | copy-start | bytes 196612
  44.0 23.5 %copy-start.11 = (bf16[2,64,64]{2,1,0:T(8,128)(2,1)S(1)}, bf16[2,64,64]{2,1,0:T(8,128)(2,1)}, u32[]{:S(2)}) copy-start(bf16[2,64,64]{2,1,0:T(8,128)(2,1)} %constant.67.clone.line_ref) | copy-start | bytes 49156
  45.7 21.8 %copy-start.5 = (bf16[2,512,512]{2,1,0:T(8,128)(2,1)S(1)}, bf16[2,512,512]{2,1,0:T(8,128)(2,1)}, u32[]{:S(2)}) copy-start(bf16[2,512,512]{2,1,0:T(8,128)(2,1)} %constant.65.clone.row_ref) | copy-start | bytes 3145732
  67.5 25.7 %copy-start.2 = (bf16[2,512,512]{2,1,0:T(8,128)(2,1)S(1)}, bf16[2,512,512]{2,1,0:T(8,128)(2,1)}, u32[]{:S(2)}) copy-start(bf16[2,512,512]{2,1,0:T(8,128)(2,1)} %constant.64.clone.refs_3_) | copy-start | bytes 3145732
  71.8 21.3 %copy-start.1 = (bf16[2,512,512]{2,1,0:T(8,128)(2,1)S(1)}, bf16[2,512,512]{2,1,0:T(8,128)(2,1)}, u32[]{:S(2)}) copy-start(bf16[2,512,512]{2,1,0:T(8,128)(2,1)} %constant.63.clone.refs_2_) | copy-start | bytes 3145732
  94.9 13.0 %copy-start.7 = (bf16[2,256,256]{2,1,0:T(8,128)(2,1)S(1)}, bf16[2,256,256]{2,1,0:T(8,128)(2,1)}, u32[]{:S(2)}) copy-start(bf16[2,256,256]{2,1,0:T(8,128)(2,1)} %constant.60.clone.z_ref) | copy-start | bytes 786436
  107.9 9.8 %copy-start.10 = (f32[32,256]{1,0:T(8,128)S(1)}, f32[32,256]{1,0:T(8,128)}, u32[]{:S(2)}) copy-start(f32[32,256]{1,0:T(8,128)} %factor_ref.1) | copy-start | bytes 98308
  107.9 9.8 %copy-start.12 = (s32[1,1,768]{2,1,0:T(1,128)S(1)}, s32[1,1,768]{2,1,0:T(1,128)}, u32[]{:S(2)}) copy-start(s32[1,1,768]{2,1,0:T(1,128)} %slot_ref.3) | copy-start | bytes 9220
  112.0 5.7 %copy-start.9 = (s32[32,256]{1,0:T(8,128)S(1)}, s32[32,256]{1,0:T(8,128)}, u32[]{:S(2)}) copy-start(s32[32,256]{1,0:T(8,128)} %index_ref.1) | copy-start | bytes 98308
  112.0 5.7 %copy-start.13 = (f32[256]{0:T(256)S(1)}, f32[256]{0:T(256)}, u32[]{:S(2)}) copy-start(f32[256]{0:T(256)} %param.17) | copy-start | bytes 3076
  112.0 14.2 %all-to-all-start.5 = ((f32[32,1,128]{2,1,0:T(1,128)}), f32[32,1,128]{2,1,0:T(1,128)S(1)}, u32[]{:S(2)}, u32[]{:S(2)}) async-start(f32[32,1,128]{2,1,0:T(1,128)} %bitcast.20), calls=%async_computation.5 | async-start | bytes 32768 | tf_op jit(solution)/shard_map/all_to_all | solution.py:554

commit v7 on v6

--- a/solution.py
+++ b/solution.py
@@ -19,6 +19,7 @@
 SLOTS = N_SLAB * CAP
 SLAB_ROWS = 16
 PENCIL_ROWS = 32
+STENCIL = 64
 KZ = 16
 LINES = 15
 ROWS = LINES * N_SLAB
@@ -72,11 +73,10 @@
 
 
 def x_tables():
-    k1, ro, ko = (a.reshape(-1)[:, None] for a in np.meshgrid(np.arange(32), np.arange(2), np.arange(8), indexing="ij"))
-    slab, ri, ki = (a.reshape(-1)[None, :] for a in np.meshgrid(np.arange(32), np.arange(2), np.arange(8), indexing="ij"))
+    ro, k1 = (a.reshape(-1)[:, None] for a in np.meshgrid(np.arange(2), np.arange(32), indexing="ij"))
+    ri, slab = (a.reshape(-1)[None, :] for a in np.meshgrid(np.arange(2), np.arange(32), indexing="ij"))
     theta = 2 * np.pi * ((k1 * slab) % 32) / 32
     rows = np.where(ro == ri, np.cos(theta), np.where(ro == 0, np.sin(theta), -np.sin(theta)))
-    rows = rows * (ko == ki)
     x16 = np.arange(16)
     twist = 2 * np.pi * np.arange(32)[:, None] * x16[None, :] / GX
     twist = np.repeat(twist, KZ, axis=1)
@@ -84,12 +84,7 @@
     eye = np.eye(KZ)
     cosine, sine = np.kron(np.cos(inner), eye), np.kron(np.sin(inner), eye)
     lanes = np.block([[cosine, -sine], [sine, cosine]])
-    ro, k1 = (a.reshape(-1)[:, None] for a in np.meshgrid(np.arange(2), np.arange(32), indexing="ij"))
-    ri, slab = (a.reshape(-1)[None, :] for a in np.meshgrid(np.arange(2), np.arange(32), indexing="ij"))
-    theta = 2 * np.pi * ((k1 * slab) % 32) / 32
-    line = np.where(ro == ri, np.cos(theta), np.where(ro == 0, np.sin(theta), -np.sin(theta)))
-    line = line * np.where(ri == 1, -1.0, 1.0)
-    return rows, np.stack([np.cos(twist), np.sin(twist)]), lanes, line
+    return rows, np.stack([np.cos(twist), np.sin(twist)]), lanes
 
 
 def pair(table):
@@ -158,64 +153,50 @@
     return ((value.astype(F32) + 0.5) * (1.0 / divisor)).astype(jnp.int32)
 
 
-def own_slots(width, slots):
-    slab = lax.broadcasted_iota(jnp.int32, (N_SLAB, slots), 0)
-    slot = lax.broadcasted_iota(jnp.int32, (N_SLAB, slots), 1)
-    return (slot >= slab * width) & (slot < slab * width + width)
-
-
-def received_place():
-    slot = lax.broadcasted_iota(jnp.int32, (SLOTS, 128), 0)
-    lane = lax.broadcasted_iota(jnp.int32, (SLOTS, 128), 1)
-    twelfth = quotient(slot, 12)
-    place = slot - twelfth * 12 + jnp.where(slot >= SLOTS // 2, 12, 0)
-    return jnp.where(lane == place, 1.0, 0.0).astype(BF16)
-
-
-def received_slots():
-    own = own_slots(CAP // 2, SLOTS // 2)
-    return jnp.concatenate([own, own], axis=1)
-
-
-def pack(slot_ref, weight_ref, strength_ref, out_ref):
-    line = lax.broadcasted_iota(jnp.int32, (ROWS, 128), 0)
-    lane = lax.broadcasted_iota(jnp.int32, (ROWS, 128), 1)
-    slab = quotient(line, LINES)
-    place = line - slab * LINES
-    target = jnp.where(place < 12, slab * CAP + place, -CAP)
-    picks = []
-    for shift in (0, 12):
-        tiles = [jnp.where(lane + part * 128 == target + shift, 1.0, 0.0) for part in range(SLOTS // 128)]
-        picks.append(jnp.concatenate(tiles, axis=1).astype(BF16))
-    slots = (slot_ref[0].astype(F32) + 1.0) * jnp.where(slot_ref[0] < PAN_DEV, 1.0, 0.0)
-    rows = jnp.broadcast_to(slots, (128, SLOTS)).astype(BF16)
-    chosen = mm_nt(jnp.concatenate(picks, axis=0), rows)
-    panel = lane.astype(F32) + 1.0
-    hot = []
-    for half in range(2):
-        part = chosen[half * ROWS : half * ROWS + ROWS]
-        hot += [part == panel, part == panel + 128.0]
-    hot = jnp.where(jnp.concatenate(hot, axis=1), 1.0, 0.0).astype(BF16)
-    weight = weight_ref[...]
-    empty = jnp.zeros_like(weight)
-    values = jnp.concatenate(
-        [jnp.concatenate([weight, empty], axis=1), jnp.concatenate([empty, weight], axis=1)], axis=0
-    )
-    high, low = split(values)
-    out_ref[...] = mm_nt(hot, high) + mm_nt(hot, low)
-    index = lax.broadcasted_iota(jnp.int32, (SLOTS, 128), 0)
-    lane = lax.broadcasted_iota(jnp.int32, (SLOTS, 128), 1)
-    spread = jnp.where((lane < CAP) & (quotient(index, CAP) * CAP + lane == index), 1.0, 0.0)
-    own = own_slots(CAP, SLOTS)
-    by_slab = mm(jnp.where(own, jnp.broadcast_to(slots, own.shape), 0.0).astype(BF16), spread.astype(BF16))
+def pick(table, slab, place):
+    sublane = lax.broadcasted_iota(jnp.int32, (8, 128), 0)
+    total = jnp.zeros((8, 128), F32)
+    for block in range(N_SLAB // 8):
+        value = jnp.take_along_axis(table[block * 8 : block * 8 + 8], place, axis=1, mode="promise_in_bounds")
+        total = jnp.where(slab == sublane + block * 8, value, total)
+    return jnp.sum(total, axis=0, keepdims=True)
+
+
+def pack(slot_ref, weight_ref, strength_ref, out_ref, by_slot_ref):
     strength = strength_ref[...]
-    tables = [strength[:, :128], strength[:, 128:]]
-    index = by_slab.astype(jnp.int32)
-    index = jnp.where(index > 0, index - 1, PAN_DEV)
-    sent = jnp.concatenate([lookup(tables, index[i * 8 : i * 8 + 8]) for i in range(4)], axis=0)
-    out_ref[pl.ds(12, N_SLAB, stride=LINES), :] = sent
-    for half in range(2):
-        out_ref[pl.ds(13 + half, N_SLAB, stride=LINES), :] = jnp.broadcast_to(tables[half], (N_SLAB, 128))
+    halves = [strength[:, :128], strength[:, 128:]]
+    tables = []
+    for tile in range(SLOTS // 128):
+        at = slice(tile * 128, tile * 128 + 128)
+        index = jnp.broadcast_to(slot_ref[0, :, at], (8, 128))
+        inner, outer = index & 127, index >> 7
+        tables.append(lookup(halves, index)[:1])
+        found = []
+        for block in range(8):
+            low, high = (
+                jnp.take_along_axis(
+                    weight_ref[block * 8 : block * 8 + 8, half * 128 : half * 128 + 128],
+                    inner,
+                    axis=1,
+                    mode="promise_in_bounds",
+                )
+                for half in range(2)
+            )
+            found.append(jnp.where(outer == 0, low, jnp.where(outer == 1, high, 0.0)))
+        by_slot_ref[at, :] = jnp.transpose(jnp.concatenate(found * 2, axis=0))
+    first = lax.broadcasted_iota(jnp.int32, (12, 128), 1) < STENCIL
+    for d in range(N_SLAB):
+        out_ref[d * LINES : d * LINES + 12, :] = jnp.where(
+            first, by_slot_ref[d * CAP : d * CAP + 12, :], by_slot_ref[d * CAP + 12 : d * CAP + 24, :]
+        )
+    sent = []
+    for block in range(N_SLAB // 8):
+        slab = lax.broadcasted_iota(jnp.int32, (8, 128), 0) + block * 8
+        place = lax.broadcasted_iota(jnp.int32, (8, 128), 1)
+        sent.append(lookup(tables, jnp.where(place < CAP, slab * CAP + place, SLOTS)))
+    out_ref[pl.ds(12, N_SLAB, stride=LINES), :] = jnp.concatenate(sent, axis=0)
+    for half in range(2):
+        out_ref[pl.ds(13 + half, N_SLAB, stride=LINES), :] = jnp.broadcast_to(halves[half], (N_SLAB, 128))
 
 
 def anchor_parts(anchor):
@@ -276,10 +257,13 @@
     turned = [part[:, : SLOTS // 2] + part[:, SLOTS // 2 :] for part in turned]
     weights = jnp.concatenate(turned, axis=1)
     weight_ref[...] = weights
-    high, low = split(arrived_ref[pl.ds(12, N_SLAB, stride=LINES), :])
-    spread = received_place()
-    strength = jnp.where(received_slots(), mm_nt(high, spread) + mm_nt(low, spread), 0.0)
-    scaled_ref[...] = weights * jnp.sum(strength, axis=0, keepdims=True)
+    sent = arrived_ref[pl.ds(12, N_SLAB, stride=LINES), :]
+    strength = []
+    for tile in range(SLOTS // 128):
+        slot = lax.broadcasted_iota(jnp.int32, (8, 128), 1) + tile % 3 * 128
+        slab = quotient(slot, 12)
+        strength.append(pick(sent, slab, slot - slab * 12 + tile // 3 * 12))
+    scaled_ref[...] = weights * jnp.concatenate(strength, axis=1)
     first, second, third = anchor_parts(anchor_ref[0])
     y_place(second, y_ref)
     fill_rows(rows_ref, first, scaled_ref)
@@ -345,53 +329,46 @@
     y_stage((32, 16), (8, 64))(*refs)
 
 
-def x_stage(flag_ref, in_ref, row_ref, green_ref, other_ref, twist_ref, lane_ref, line_ref, out_ref, re_ref, im_ref):
-    row_tables = row_ref[...]
-    rows = mm3(row_tables, split(gathered(in_ref, 32, 16))).reshape(32, 2, 8, 256)
-    few = twist_ref[0], twist_ref[1]
-    cosine, sine = (
-        jnp.concatenate([jnp.broadcast_to(part[k : k + 1], (8, 256)) for k in range(32)], axis=0) for part in few
-    )
-    lane_tables = lane_ref[...]
-    line_tables = line_ref[...]
-
-    def lanes_of(re, im, cosine, sine):
-        turned = jnp.concatenate([re * cosine + im * sine, im * cosine - re * sine], axis=1)
-        return mm3(split(turned), lane_tables)
-
-    full = lanes_of(rows[:, 0].reshape(256, 256), rows[:, 1].reshape(256, 256), cosine, sine)
+def x_stage(flag_ref, in_ref, green_ref, other_ref, twist_ref, row_ref, lane_ref, out_ref, re_ref, im_ref):
+    row_tables, lane_tables = row_ref[...], lane_ref[...]
+    cosine, sine = twist_ref[0], twist_ref[1]
+
+    def line(k, ri):
+        return [in_ref[pl.ds(half * 16 + ri * 8 + k, 32, stride=32), :] for half in range(2)]
+
+    def turn(re, im):
+        return jnp.concatenate([re * cosine + im * sine, im * cosine - re * sine], axis=1)
+
+    data = [jnp.concatenate(sum((line(k, ri) for k in range(8)), []), axis=1) for ri in range(2)]
+    rows = mm3(row_tables, split(jnp.concatenate(data, axis=0)))
+    columns = [slice(k * 256, k * 256 + 256) for k in range(8)]
+    full = mm3(split(jnp.concatenate([turn(rows[:32, at], rows[32:, at]) for at in columns], axis=0)), lane_tables)
     for half in range(2):
         at = slice(half * 128, half * 128 + 128)
-        green = green_ref[half]
-        re_ref[half] = full[:, at] * green
-        im_ref[half] = full[:, 256 + half * 128 : 384 + half * 128] * green
+        re_ref[half] = full[:, at] * green_ref[half]
+        im_ref[half] = full[:, 256 + half * 128 : 384 + half * 128] * green_ref[half]
 
     @pl.when(flag_ref[1] == 1)
     def _():
-        line = jnp.concatenate(
-            [
-                jnp.concatenate([in_ref[pl.ds(half * 16 + ri * 8, 32, stride=32), :] for half in range(2)], axis=1)
-                for ri in range(2)
-            ],
-            axis=0,
-        )
-        turned = mm3(line_tables, split(line))
-        mirror = lanes_of(turned[:32], turned[32:], *few)
-        other = other_ref[...]
-        rows_at = pl.ds(0, 32, stride=8)
+        conjugate = jnp.concatenate([data[0][:, :256], -data[1][:, :256]], axis=0)
+        rows = mm3(row_tables, split(conjugate))
+        mirror = mm3(split(turn(rows[:32], rows[32:])), lane_tables)
         for half in range(2):
             at = slice(half * 128, half * 128 + 128)
-            re_ref[half, rows_at, :] += mirror[:, at] * other[:, at]
-            im_ref[half, rows_at, :] += mirror[:, 256 + half * 128 : 384 + half * 128] * other[:, at]
+            other = other_ref[:, at]
+            re_ref[half, :32, :] += mirror[:, at] * other
+            im_ref[half, :32, :] += mirror[:, 256 + half * 128 : 384 + half * 128] * other
 
     product = jnp.concatenate([re_ref[0], re_ref[1], -im_ref[0], -im_ref[1]], axis=1)
     back = mm3(split(product), lane_tables)
-    re, im = back[:, :256], back[:, 256:]
-    re, im = re * cosine + im * sine, im * cosine - re * sine
-    rows = jnp.stack([re.reshape(32, 8, 256), im.reshape(32, 8, 256)], axis=1).reshape(512, 256)
-    rows = mm3(row_tables, split(rows)).reshape(32, 2, 8, 256) * (1.0 / GX)
-    rows = jnp.stack([rows[:, 0], -rows[:, 1]], axis=1).reshape(512, 256)
-    scattered(rows, out_ref, 32, 16)
+    back = [turn(back[k * 32 : k * 32 + 32, :256], back[k * 32 : k * 32 + 32, 256:]) for k in range(8)]
+    data = [jnp.concatenate([part[:, ri * 256 : ri * 256 + 256] for part in back], axis=1) for ri in range(2)]
+    rows = mm3(row_tables, split(jnp.concatenate(data, axis=0)))
+    for k in range(8):
+        for ri in range(2):
+            for half in range(2):
+                part = rows[ri * 32 : ri * 32 + 32, k * 256 + half * 128 : k * 256 + half * 128 + 128]
+                out_ref[pl.ds(half * 16 + ri * 8 + k, 32, stride=32), :] = part * ((1 - 2 * ri) / GX)
 
 
 def sample(in_ref, weight_ref, anchor_ref, z_ref, out_ref, y_ref, after_ref, rows_ref, grid_ref):
@@ -419,17 +396,25 @@
             cells = grid_ref[dz, x * 32 : x * 32 + 32, :] * place_rows(rows, y_ref)
             total += jnp.sum(cells.reshape(4, 8, SLOTS), axis=0)
     far = jnp.sum(total, axis=0, keepdims=True)
-    high, low = split(jnp.where(received_slots(), jnp.broadcast_to(far, (N_SLAB, SLOTS)), 0.0))
-    spread = received_place()
-    out_ref[...] = mm(high, spread) + mm(low, spread)
-
-
-def near(flag_ref, arrived_ref, slot_ref, own_ref, index_ref, factor_ref, out_ref, hot_ref):
+    tables = [far[:, tile * 128 : tile * 128 + 128] for tile in range(SLOTS // 128)]
+    for block in range(N_SLAB // 8):
+        slab = lax.broadcasted_iota(jnp.int32, (8, 128), 0) + block * 8
+        place = lax.broadcasted_iota(jnp.int32, (8, 128), 1)
+        index = slab * 12 + place + jnp.where(place < 12, 0, SLOTS // 2 - 12)
+        out_ref[block * 8 : block * 8 + 8, :] = lookup(tables, jnp.where(place < CAP, index, SLOTS))
+
+
+def near(flag_ref, arrived_ref, slot_ref, own_ref, index_ref, factor_ref, out_ref, slab_ref, place_ref):
     slots = jnp.transpose(jnp.broadcast_to(slot_ref[0], (128, SLOTS)))
     panel = lax.broadcasted_iota(jnp.int32, (SLOTS, 128), 1)
-    for half in range(2):
-        hot = jnp.where(slots == panel + half * 128, 1.0, 0.0)
-        hot_ref[:, half * 128 : half * 128 + 128] = hot.astype(BF16)
+    slot = lax.broadcasted_iota(jnp.int32, (SLOTS, 128), 0).astype(F32)
+    for half in range(2):
+        at = slice(half * 128, half * 128 + 128)
+        own = jnp.sum(jnp.where(slots == panel + half * 128, slot, 0.0), axis=0, keepdims=True)
+        own = jnp.broadcast_to(own, (8, 128)).astype(jnp.int32)
+        slab = quotient(own, CAP)
+        slab_ref[:, at] = slab
+        place_ref[:, at] = own - slab * CAP
     before = [arrived_ref[pl.ds(flag_ref[4] + half, 1), :] for half in range(2)]
     after = [arrived_ref[pl.ds(flag_ref[5] + half, 1), :] for half in range(2)]
     tables = before + [own_ref[:, :128], own_ref[:, 128:]] + after
@@ -441,16 +426,11 @@
         out_ref[:, lane * 128 : lane * 128 + 128] = jnp.sum(total, axis=0, keepdims=True)
 
 
-def finish(far_ref, hot_ref, near_ref, out_ref):
-    index = lax.broadcasted_iota(jnp.int32, (SLOTS, 128), 0)
-    lane = lax.broadcasted_iota(jnp.int32, (SLOTS, 128), 1)
-    spread = jnp.where((lane < CAP) & (quotient(index, CAP) * CAP + lane == index), 1.0, 0.0)
-    by_slot = mm_nt(jnp.concatenate(split(far_ref[...]), axis=0), spread.astype(BF16))
-    by_slot = jnp.where(own_slots(CAP, SLOTS), by_slot[:N_SLAB] + by_slot[N_SLAB:], 0.0)
-    row = jnp.broadcast_to(jnp.sum(by_slot, axis=0, keepdims=True), (8, SLOTS))
-    high, low = split(row)
-    hot = hot_ref[...]
-    out_ref[...] = (mm(high, hot) + mm(low, hot))[:1] + near_ref[...]
+def finish(far_ref, slab_ref, place_ref, near_ref, out_ref):
+    far = far_ref[...]
+    for half in range(2):
+        at = slice(half * 128, half * 128 + 128)
+        out_ref[:, at] = pick(far, slab_ref[:, at], place_ref[:, at]) + near_ref[:, at]
 
 
 def swap(value, axis, count):
@@ -487,7 +467,7 @@
         rows = jnp.where(place & shared, line, rows)
         laid = lay(rows)
         for half in range(2):
-            out_ref[half, pl.ds(k, 32, stride=8), :] = laid[:, half * 128 : half * 128 + 128]
+            out_ref[half, k * 32 : k * 32 + 32, :] = laid[:, half * 128 : half * 128 + 128]
 
 
 def per_device(strength, stencil_weight, slot_panel, slot_anchor, green_spectrum, near_index, near_factor):
@@ -501,15 +481,17 @@
 
     z_fwd, z_bwd = (pair(t) for t in z_tables())
     y_fwd, y_fwd_shared, y_bwd, y_bwd_shared = (pair(t) for t in y_tables())
-    rows, twist, lanes, line = x_tables()
-    rows, lanes, line = (pair(t) for t in (rows, lanes, line))
+    rows, twist, lanes = x_tables()
+    rows, lanes = pair(rows), pair(lanes)
     twist = jnp.asarray(twist, F32)
 
     anchor = slot_anchor.reshape(N_SLAB, 2, 12).transpose(1, 0, 2).reshape(1, 1, SLOTS)
 
     shape = jax.ShapeDtypeStruct
     payload = call(
-        pack, shape((ROWS, 128), F32), slot_panel, stencil_weight, row, limit=56)
+        pack, shape((ROWS, 128), F32), slot_panel, stencil_weight, row,
+        scratch=[pltpu.VMEM((SLOTS, 128), F32)], limit=56,
+    )
 
     payload, spectrum = lax.optimization_barrier((payload, green_spectrum))
     plane = lax.ppermute(spectrum[:, 0, :], "pencil", [(4, 0)])
@@ -518,8 +500,8 @@
         arrange_green, [shape((2, 256, 128), F32), shape((32, 256), F32)], flags, spectrum, plane, smem=(0,), limit=LIMIT_N
     )
     arrived, green, other, flags, anchor = lax.optimization_barrier((arrived, green, other, flags, anchor))
-    near_field, hot = call(
-        near, [shape((1, PAN_DEV), F32), shape((SLOTS, PAN_DEV), BF16)], flags, arrived, slot_panel, row, near_index, near_factor,
+    near_field, *home = call(
+        near, [shape((1, PAN_DEV), F32)] + [shape((8, PAN_DEV), jnp.int32)] * 2, flags, arrived, slot_panel, row, near_index, near_factor,
         smem=(0,), limit=LIMIT_N,
     )
     after_z, weights = call(
@@ -536,7 +518,7 @@
     )
     by_x = swap(after_y, "slab", N_SLAB)
     after_x = call(
-        x_stage, shape((1024, 128), F32), flags, by_x, rows, green, other, twist, lanes, line,
+        x_stage, shape((1024, 128), F32), flags, by_x, green, other, twist, rows, lanes,
         scratch=[pltpu.VMEM((2, 256, 128), F32)] * 2, smem=(0,), limit=LIMIT_X,
     )
     back_x = swap(after_x, "slab", N_SLAB)
@@ -552,7 +534,7 @@
         limit=LIMIT_S,
     )
     far = lax.all_to_all(sampled, "slab", 0, 0, tiled=True)
-    return call(finish, shape((1, PAN_DEV), F32), far, hot, near_field, limit=40).reshape(PAN_DEV)
+    return call(finish, shape((1, PAN_DEV), F32), far, *home, near_field, limit=40).reshape(PAN_DEV)
 
 
 def solution(mesh):

time: 128 us -> 125 us (0.977)
  Pallas kernels: 21.8 us -> 18.6 us
    pallas_call x9, Pallas kernels: 21.8 us -> 18.6 us  [call(): pl.pallas_call(kernel, out_shape=out_shape, in_specs=[pl.BlockSpec(memory...]
where the time goes in v7:
time: 125 us; the launch traced here: 124 us
  blocking collectives  70.7 us (57%)
  starting transfers between devices  18.7 us (15%)
  Pallas kernels  18.6 us (15%)
  waiting for transfers between devices  14.9 us (12%)
    all_to_all x4, blocking collectives, swap(): lax.all_to_all(value.reshape(count, rows // count, 128), axis, 0, 0, tile...  70.7 us
    pallas_call x9, Pallas kernels, call(): pl.pallas_call(kernel, out_shape=out_shape, in_specs=[pl.BlockSpec(memory...  18.6 us
    all_to_all x1, starting transfers between devices, per_device(): lax.all_to_all(payload.reshape(N_SLAB, 1, LINES * 128), 'slab', 0, 0, til...  11.6 us
    all_to_all x1, waiting for transfers between devices, per_device(): far = lax.all_to_all(sampled, 'slab', 0, 0, tiled=True)  7.66 us
    all_to_all x1, starting transfers between devices, per_device(): far = lax.all_to_all(sampled, 'slab', 0, 0, tiled=True)  5.7 us
    ppermute x1, waiting for transfers between devices, per_device(): plane = lax.ppermute(spectrum[:, 0, :], 'pencil', [(4, 0)])  5.28 us
  transfers between devices with their start and end apart: 3, of which 3 were waited for; matrix products, arithmetic and copies ran while one was open for 1% of the time, Pallas kernels for 2%

profile of v7, /device:TPU:2, one launch (start us, length us, event | category | flops | bytes accessed | tf_op | source)
XLA Modules:
  0.0 124.0 jit_solution(3692749792396030001)
XLA Ops:
  0.0 0.0 copy-start
  0.0 2.0 %pack.1 = f32[480,128]{1,0:T(8,128)} custom-call(s32[1,1,768]{2,1,0:T(1,128)} %slot_ref.3, f32[64,256]{1,0:T(8,128)} %weight_ref.1, f32[1,256]{1,0:T(1,128)} %bitcast.36), custom_call_target="tpu_custom_call" | custom-call | tf_op jit(solution)/shard_map/pack/pallas_call | solution.py:116
  2.0 11.6 %all-to-all-start = ((f32[32,1,1920]{2,1,0:T(1,128)}), f32[32,1,1920]{2,1,0:T(1,128)S(1)}, u32[]{:S(2)}, u32[]{:S(2)}) async-start(f32[32,1,1920]{2,1,0:T(1,128)} %bitcast.38), calls=%async_computation | async-start | bytes 491520 | tf_op jit(solution)/shard_map/all_to_all | solution.py:498
  13.6 0.0 copy-done
  13.6 0.0 copy-start.14
  13.6 0.3 copy.22
  14.0 0.0 copy-start.6
  14.0 1.4 %collective-permute-start = (f32[8,512]{1,0:T(8,128)S(1)}, f32[8,512]{1,0:T(8,128)S(1)}, u32[]{:S(2)}, u32[]{:S(2)}) collective-permute-start(f32[8,512]{1,0:T(8,128)S(1)} %slice_bitcast_fusion), channel_id=1, source_target_pairs={{4,0},{12,8},{20,16},{28,24},{36,32},{44,40},{52,48},{60,56},{68,6... | collective-permute-start | bytes 49160 | tf_op jit(solution)/shard_map/ppermute | solution.py:497
  15.4 0.1 fusion
  15.5 0.1 add_convert_fusion
  15.6 0.1 pad_add_fusion.flag_ref.refs_0_
  15.7 0.0 copy-done.14
  15.7 0.1 reshape.47
  15.8 0.1 reshape.48.anchor_ref
  15.9 0.0 copy-start.4
  16.0 0.0 copy-start.5
  16.0 5.3 %collective-permute-done.plane_ref = f32[8,512]{1,0:T(8,128)S(1)} collective-permute-done((f32[8,512]{1,0:T(8,128)S(1)}, f32[8,512]{1,0:T(8,128)S(1)}, u32[]{:S(2)}, u32[]{:S(2)}) %collective-permute-start) | collective-permute-done | bytes 16416 | tf_op jit(solution)/shard_map/ppermute | solution.py:497
  21.2 1.2 arrange_green.1
  22.5 2.0 %all-to-all-done = f32[32,1,1920]{2,1,0:T(1,128)S(1)} async-done(((f32[32,1,1920]{2,1,0:T(1,128)}), f32[32,1,1920]{2,1,0:T(1,128)S(1)}, u32[]{:S(2)}, u32[]{:S(2)}) %all-to-all-start) | async-done | bytes 245792 | tf_op jit(solution)/shard_map/all_to_all | solution.py:498
  24.5 0.0 copy-done.6
  24.5 3.8 %project.1 = (f32[1024,128]{1,0:T(8,128)S(1)}, f32[128,768]{1,0:T(8,128)S(1)}) custom-call(f32[480,128]{1,0:T(8,128)S(1)} %bitcast.25, s32[1,1,768]{2,1,0:T(1,128)S(1)} %reshape.48.anchor_ref, bf16[2,256,256]{2,1,0:T(8,128)(2,1)S(1)} %copy-done.6), custom_call_target="tpu_custom_call" | custom-call | tf_op jit(solution)/shard_map/project/pallas_call | solution.py:116
  28.3 14.7 %all_to_all.36 = f32[8,128,128]{2,1,0:T(8,128)S(1)} all-to-all(f32[8,128,128]{2,1,0:T(8,128)S(1)} %bitcast.34), channel_id=1, replica_groups=mesh['slab'=32,'pencil'=8] {'pencil'}, dimensions={0} | all-to-all | bytes 1048576 | tf_op jit(solution)/shard_map/all_to_all | solution.py:438
  42.9 0.0 copy-done.4
  42.9 0.0 copy-done.5
  42.9 0.0 copy-start.8
  42.9 0.0 copy-start.9
  42.9 1.7 %y_forward.1 = f32[1024,128]{1,0:T(8,128)S(1)} custom-call(s32[6]{0:T(128)S(1)} %pad_add_fusion.flag_ref.refs_0_, f32[1024,128]{1,0:T(8,128)S(1)} %bitcast.30, bf16[2,512,512]{2,1,0:T(8,128)(2,1)S(1)} %copy-done.5, bf16[2,512,512]{2,1,0:T(8,128)(2,1)S(1)} %copy-done.4), custom_call_target="tpu_custom_call" | custom-call | tf_op jit(solution)/shard_map/y_forward/pallas_call | solution.py:116
  44.7 0.0 copy-start.3
  44.7 21.8 %all_to_all.37 = f32[32,32,128]{2,1,0:T(8,128)S(1)} all-to-all(f32[32,32,128]{2,1,0:T(8,128)S(1)} %bitcast.31), channel_id=1, replica_groups=mesh['slab'=32,'pencil'=8] {'slab'}, dimensions={0} | all-to-all | bytes 1048576 | tf_op jit(solution)/shard_map/all_to_all | solution.py:438
  66.5 0.0 copy-done.8
  66.5 0.0 copy-done.9
  66.5 0.0 copy-done.3
  66.5 0.0 copy-start.2
  66.5 2.8 %x_stage.1 = f32[1024,128]{1,0:T(8,128)S(1)} custom-call(s32[6]{0:T(128)S(1)} %pad_add_fusion.flag_ref.refs_0_, f32[1024,128]{1,0:T(8,128)S(1)} %bitcast.28, f32[2,256,128]{2,1,0:T(8,128)S(1)} %get-tuple-element.27.green_ref, f32[32,256]{1,0:T(8,128)S(1)} %get-tuple-element.28.other_ref, f32[2,32,256]{2,1,0:T(8,128)S(1)} %copy-done.8, ...), custom_call_target="tpu_custom_call" | custom-call | tf_op jit(solution)/shard_map/x_stage/pallas_call | solution.py:116
  69.3 0.0 copy-start.1
  69.3 21.3 %all_to_all.38 = f32[32,32,128]{2,1,0:T(8,128)S(1)} all-to-all(f32[32,32,128]{2,1,0:T(8,128)S(1)} %bitcast.29), channel_id=1, replica_groups=mesh['slab'=32,'pencil'=8] {'slab'}, dimensions={0} | all-to-all | bytes 1048576 | tf_op jit(solution)/shard_map/all_to_all | solution.py:438
  90.6 0.0 copy-done.2
  90.6 0.0 copy-done.1
  90.6 1.7 %y_backward.1 = f32[1024,128]{1,0:T(8,128)S(1)} custom-call(s32[6]{0:T(128)S(1)} %pad_add_fusion.flag_ref.refs_0_, f32[1024,128]{1,0:T(8,128)S(1)} %bitcast.32, bf16[2,512,512]{2,1,0:T(8,128)(2,1)S(1)} %copy-done.2, bf16[2,512,512]{2,1,0:T(8,128)(2,1)S(1)} %copy-done.1), custom_call_target="tpu_custom_call" | custom-call | tf_op jit(solution)/shard_map/y_backward/pallas_call | solution.py:116
  92.4 0.0 copy-start.7
  92.4 12.9 %all_to_all.39 = f32[8,128,128]{2,1,0:T(8,128)S(1)} all-to-all(f32[8,128,128]{2,1,0:T(8,128)S(1)} %bitcast.33), channel_id=1, replica_groups=mesh['slab'=32,'pencil'=8] {'pencil'}, dimensions={0} | all-to-all | bytes 1048576 | tf_op jit(solution)/shard_map/all_to_all | solution.py:438
  105.3 0.0 copy-done.7
  105.3 0.0 copy-start.11
  105.3 0.0 copy-start.12
  105.3 3.8 %sample.1 = f32[32,128]{1,0:T(8,128)} custom-call(f32[1024,128]{1,0:T(8,128)S(1)} %bitcast.27, f32[128,768]{1,0:T(8,128)S(1)} %get-tuple-element.29.weight_ref, s32[1,1,768]{2,1,0:T(1,128)S(1)} %reshape.48.anchor_ref, bf16[2,256,256]{2,1,0:T(8,128)(2,1)S(1)} %copy-done.7), custom_call_target="tpu_custom_call" | custom-call | tf_op jit(solution)/shard_map/sample/pallas_call | solution.py:116
  109.2 0.0 copy-start.10
  109.2 0.0 copy-start.13
  109.2 5.7 %all-to-all-start.5 = ((f32[32,1,128]{2,1,0:T(1,128)}), f32[32,1,128]{2,1,0:T(1,128)S(1)}, u32[]{:S(2)}, u32[]{:S(2)}) async-start(f32[32,1,128]{2,1,0:T(1,128)} %bitcast.20), calls=%async_computation.5 | async-start | bytes 32768 | tf_op jit(solution)/shard_map/all_to_all | solution.py:536
  114.9 0.0 copy-done.11
  114.9 0.0 copy-done.12
  114.9 0.0 copy-done.10
  114.9 0.0 copy-done.13
  114.9 0.8 near.1
  115.7 7.7 %all-to-all-done.5 = f32[32,1,128]{2,1,0:T(1,128)S(1)} async-done(((f32[32,1,128]{2,1,0:T(1,128)}), f32[32,1,128]{2,1,0:T(1,128)S(1)}, u32[]{:S(2)}, u32[]{:S(2)}) %all-to-all-start.5) | async-done | bytes 16416 | tf_op jit(solution)/shard_map/all_to_all | solution.py:536
  123.4 0.7 finish.1
  (3 shorter events, 0.0 us)
Async XLA Ops:
  0.0 13.6 %copy-start = (f32[8,32,512]{2,1,0:T(8,128)S(1)}, f32[8,32,512]{2,1,0:T(8,128)}, u32[]{:S(2)}) copy-start(f32[8,32,512]{2,1,0:T(8,128)} %green_ref) | copy-start | bytes 1572868
  2.0 22.5 %all-to-all-start = ((f32[32,1,1920]{2,1,0:T(1,128)}), f32[32,1,1920]{2,1,0:T(1,128)S(1)}, u32[]{:S(2)}, u32[]{:S(2)}) async-start(f32[32,1,1920]{2,1,0:T(1,128)} %bitcast.38), calls=%async_computation | async-start | bytes 491520 | tf_op jit(solution)/shard_map/all_to_all | solution.py:498
  13.6 2.1 %copy-start.14 = (s32[1,1,768]{2,1,0:T(1,128)S(1)}, s32[1,1,768]{2,1,0:T(1,128)}, u32[]{:S(2)}) copy-start(s32[1,1,768]{2,1,0:T(1,128)} %param.19) | copy-start | bytes 9220
  14.0 10.5 %copy-start.6 = (bf16[2,256,256]{2,1,0:T(8,128)(2,1)S(1)}, bf16[2,256,256]{2,1,0:T(8,128)(2,1)}, u32[]{:S(2)}) copy-start(bf16[2,256,256]{2,1,0:T(8,128)(2,1)} %constant.57.clone.z_ref) | copy-start | bytes 786436
  14.0 7.3 %collective-permute-start = (f32[8,512]{1,0:T(8,128)S(1)}, f32[8,512]{1,0:T(8,128)S(1)}, u32[]{:S(2)}, u32[]{:S(2)}) collective-permute-start(f32[8,512]{1,0:T(8,128)S(1)} %slice_bitcast_fusion), channel_id=1, source_target_pairs={{4,0},{12,8},{20,16},{28,24},{36,32},{44,40},{52,48},{60,56},{68,6... | collective-permute-start | bytes 49160 | tf_op jit(solution)/shard_map/ppermute | solution.py:497
  15.9 27.0 %copy-start.4 = (bf16[2,512,512]{2,1,0:T(8,128)(2,1)S(1)}, bf16[2,512,512]{2,1,0:T(8,128)(2,1)}, u32[]{:S(2)}) copy-start(bf16[2,512,512]{2,1,0:T(8,128)(2,1)} %constant.60.clone.refs_3_) | copy-start | bytes 3145732
  16.0 27.0 %copy-start.5 = (bf16[2,512,512]{2,1,0:T(8,128)(2,1)S(1)}, bf16[2,512,512]{2,1,0:T(8,128)(2,1)}, u32[]{:S(2)}) copy-start(bf16[2,512,512]{2,1,0:T(8,128)(2,1)} %constant.59.clone.refs_2_) | copy-start | bytes 3145732
  42.9 23.5 %copy-start.8 = (f32[2,32,256]{2,1,0:T(8,128)S(1)}, f32[2,32,256]{2,1,0:T(8,128)}, u32[]{:S(2)}) copy-start(f32[2,32,256]{2,1,0:T(8,128)} %constant.65.clone.twist_ref) | copy-start | bytes 196612
  42.9 23.5 %copy-start.9 = (bf16[2,64,64]{2,1,0:T(8,128)(2,1)S(1)}, bf16[2,64,64]{2,1,0:T(8,128)(2,1)}, u32[]{:S(2)}) copy-start(bf16[2,64,64]{2,1,0:T(8,128)(2,1)} %constant.63.clone.row_ref) | copy-start | bytes 49156
  44.7 21.8 %copy-start.3 = (bf16[2,512,512]{2,1,0:T(8,128)(2,1)S(1)}, bf16[2,512,512]{2,1,0:T(8,128)(2,1)}, u32[]{:S(2)}) copy-start(bf16[2,512,512]{2,1,0:T(8,128)(2,1)} %constant.64.clone.lane_ref) | copy-start | bytes 3145732
  66.5 24.2 %copy-start.2 = (bf16[2,512,512]{2,1,0:T(8,128)(2,1)S(1)}, bf16[2,512,512]{2,1,0:T(8,128)(2,1)}, u32[]{:S(2)}) copy-start(bf16[2,512,512]{2,1,0:T(8,128)(2,1)} %constant.61.clone.refs_2_) | copy-start | bytes 3145732
  69.3 21.3 %copy-start.1 = (bf16[2,512,512]{2,1,0:T(8,128)(2,1)S(1)}, bf16[2,512,512]{2,1,0:T(8,128)(2,1)}, u32[]{:S(2)}) copy-start(bf16[2,512,512]{2,1,0:T(8,128)(2,1)} %constant.62.clone.refs_3_) | copy-start | bytes 3145732
  92.4 13.0 %copy-start.7 = (bf16[2,256,256]{2,1,0:T(8,128)(2,1)S(1)}, bf16[2,256,256]{2,1,0:T(8,128)(2,1)}, u32[]{:S(2)}) copy-start(bf16[2,256,256]{2,1,0:T(8,128)(2,1)} %constant.58.clone.z_ref) | copy-start | bytes 786436
  105.3 9.5 %copy-start.11 = (f32[32,256]{1,0:T(8,128)S(1)}, f32[32,256]{1,0:T(8,128)}, u32[]{:S(2)}) copy-start(f32[32,256]{1,0:T(8,128)} %factor_ref.1) | copy-start | bytes 98308
  105.3 9.6 %copy-start.12 = (s32[1,1,768]{2,1,0:T(1,128)S(1)}, s32[1,1,768]{2,1,0:T(1,128)}, u32[]{:S(2)}) copy-start(s32[1,1,768]{2,1,0:T(1,128)} %slot_ref.3) | copy-start | bytes 9220
  109.2 5.7 %copy-start.10 = (s32[32,256]{1,0:T(8,128)S(1)}, s32[32,256]{1,0:T(8,128)}, u32[]{:S(2)}) copy-start(s32[32,256]{1,0:T(8,128)} %index_ref.1) | copy-start | bytes 98308
  109.2 5.7 %copy-start.13 = (f32[256]{0:T(256)S(1)}, f32[256]{0:T(256)}, u32[]{:S(2)}) copy-start(f32[256]{0:T(256)} %param.16) | copy-start | bytes 3076
  109.2 14.2 %all-to-all-start.5 = ((f32[32,1,128]{2,1,0:T(1,128)}), f32[32,1,128]{2,1,0:T(1,128)S(1)}, u32[]{:S(2)}, u32[]{:S(2)}) async-start(f32[32,1,128]{2,1,0:T(1,128)} %bitcast.20), calls=%async_computation.5 | async-start | bytes 32768 | tf_op jit(solution)/shard_map/all_to_all | solution.py:536

commit v8 on v7

--- a/solution.py
+++ b/solution.py
@@ -61,14 +61,13 @@
     cosine, sine = np.cos(theta), np.sin(theta)
     forward = np.where(ro == ri, cosine, np.where(ro == 0, sine, -sine))
     backward = forward.T / GY
-    low = (ky > 0) & (ky < 128)
-    high = ky > 128
+    part = np.where(ro == 0, cosine, -sine)
     ends = (ky == 0) | (ky == 128)
-    part = np.where(ro == 0, cosine, -sine)
-    shared = np.where(low & (ri == 0), part, 0.0)
-    shared = np.where(high & (ri == 1), part, shared)
-    shared = np.where(ends & (ro == ri), cosine, shared)
-    shared_back = (shared * np.where(ends, 1.0, 2.0)).T / GY
+    part = np.where(ends, np.where(ro == 0, 1.0, 1.0 - 2.0 * (y % 2)), part)
+    first = part[:, np.broadcast_to(ri == 0, y.shape)[0]]
+    shared = np.stack([first[:256], first[256:]])
+    scale = (np.where(ends, 1.0, 2.0) / GY).reshape(2, 256, 1)
+    shared_back = (shared * scale).transpose(0, 2, 1)
     return forward, shared, backward, shared_back
 
 
@@ -213,10 +212,11 @@
     y_ref[...] = jnp.where((rel >= 0) & (rel < EDGE), rel, EDGE)
 
 
-def stencil_row(x, first, weight_ref):
-    total = jnp.zeros((32, SLOTS), F32)
+def stencil_row(x, dz, first, weight_ref):
+    total = jnp.zeros((8, SLOTS), F32)
     for dx in range(EDGE):
-        total = jnp.where(first == x - dx, weight_ref[dx * 32 : dx * 32 + 32, :], total)
+        start = dx * 32 + dz * 8
+        total = jnp.where(first == x - dx, weight_ref[start : start + 8, :], total)
     return total
 
 
@@ -232,14 +232,6 @@
     return jnp.concatenate(out, axis=0)
 
 
-def fill_rows(rows_ref, first, weight_ref):
-    def step(x, carry):
-        rows_ref[pl.ds(pl.multiple_of(x * 32, 32), 32), :] = stencil_row(x, first, weight_ref)
-        return carry
-
-    lax.fori_loop(0, SLAB_ROWS, step, 0)
-
-
 def slot_order():
     row = lax.broadcasted_iota(jnp.int32, (256, 128), 0)
     lane = lax.broadcasted_iota(jnp.int32, (256, 128), 1)
@@ -248,7 +240,8 @@
     return jnp.where((lane == picked) & (dy < EDGE), 1.0, 0.0).astype(BF16)
 
 
-def project(arrived_ref, anchor_ref, z_ref, out_ref, weight_ref, scaled_ref, y_ref, rows_ref, packed_ref, high_ref, low_ref):
+def project(flag_ref, arrived_ref, anchor_ref, z_ref, own_ref, index_ref, factor_ref, out_ref, weight_ref, near_ref, scaled_ref, y_ref, packed_ref, high_ref, low_ref):
+    near(flag_ref, arrived_ref, own_ref, index_ref, factor_ref, near_ref)
     for s in range(N_SLAB):
         packed_ref[s * 12 : s * 12 + 12, :] = arrived_ref[s * LINES : s * LINES + 12, :]
     packed = jnp.concatenate(split(packed_ref[...]), axis=0)
@@ -266,13 +259,12 @@
     scaled_ref[...] = weights * jnp.concatenate(strength, axis=1)
     first, second, third = anchor_parts(anchor_ref[0])
     y_place(second, y_ref)
-    fill_rows(rows_ref, first, scaled_ref)
     hot = z_hot(third, 0)
     charge = jnp.zeros((512, GZ), F32)
     for dz in range(EDGE):
         for x in range(SLAB_ROWS):
             at = slice(x * PENCIL_ROWS, x * PENCIL_ROWS + PENCIL_ROWS)
-            high, low = split(place_rows(rows_ref[x * 32 + dz * 8 : x * 32 + dz * 8 + 8, :], y_ref))
+            high, low = split(place_rows(stencil_row(x, dz, first, scaled_ref), y_ref))
             high_ref[dz, at, :] = high
             low_ref[dz, at, :] = low
         part = mm_nt(high_ref[dz], hot) + mm_nt(low_ref[dz], hot)
@@ -306,14 +298,23 @@
     return lax.broadcasted_iota(jnp.int32, shape, 1) % KZ == 0
 
 
-def y_stage(source, target):
+def halves_of(value, group):
+    return value[group * 256 : group * 256 + 256]
+
+
+def planes_of(value, plane):
+    return value.reshape(8, 2, 32, 256)[:, plane].reshape(256, 256)
+
+
+def y_stage(source, target, join, fuse):
     def kernel(flag_ref, in_ref, table_ref, shared_ref, out_ref, work_ref):
         data = split(gathered(in_ref, *source))
         work_ref[...] = mm3(table_ref[...], data)
 
         @pl.when(flag_ref[0] == 1)
         def _():
-            other = mm3(shared_ref[...], data)
+            parts = [[join(part, group) for part in data] for group in range(2)]
+            other = fuse([mm3(shared_ref[:, group], parts[group]) for group in range(2)])
             work_ref[...] = jnp.where(shared_lane(other.shape), other, work_ref[...])
 
         scattered(work_ref[...], out_ref, *target)
@@ -322,11 +323,14 @@
 
 
 def y_forward(*refs):
-    y_stage((8, 64), (32, 16))(*refs)
+    y_stage((8, 64), (32, 16), planes_of, lambda parts: jnp.concatenate(parts, axis=0))(*refs)
 
 
 def y_backward(*refs):
-    y_stage((32, 16), (8, 64))(*refs)
+    def fuse(parts):
+        return jnp.stack([part.reshape(8, 32, 256) for part in parts], axis=1).reshape(512, 256)
+
+    y_stage((32, 16), (8, 64), halves_of, fuse)(*refs)
 
 
 def x_stage(flag_ref, in_ref, green_ref, other_ref, twist_ref, row_ref, lane_ref, out_ref, re_ref, im_ref):
@@ -371,7 +375,7 @@
                 out_ref[pl.ds(half * 16 + ri * 8 + k, 32, stride=32), :] = part * ((1 - 2 * ri) / GX)
 
 
-def sample(in_ref, weight_ref, anchor_ref, z_ref, out_ref, y_ref, after_ref, rows_ref, grid_ref):
+def sample(in_ref, weight_ref, anchor_ref, z_ref, out_ref, y_ref, after_ref, grid_ref):
     for half in range(2):
         for quarter in range(2):
             tiles = []
@@ -386,14 +390,13 @@
     first, second, third = anchor_parts(anchor_ref[0])
     y_place(second, y_ref)
 
-    fill_rows(rows_ref, first, weight_ref)
     total = jnp.zeros((8, SLOTS), F32)
     for dz in range(EDGE):
         hot = z_hot(third, dz)
         grid_ref[dz] = mm(high, hot) + mm(low, hot)
         for x in range(SLAB_ROWS):
-            rows = rows_ref[x * 32 + dz * 8 : x * 32 + dz * 8 + 8, :]
-            cells = grid_ref[dz, x * 32 : x * 32 + 32, :] * place_rows(rows, y_ref)
+            rows = place_rows(stencil_row(x, dz, first, weight_ref), y_ref)
+            cells = grid_ref[dz, x * 32 : x * 32 + 32, :] * rows
             total += jnp.sum(cells.reshape(4, 8, SLOTS), axis=0)
     far = jnp.sum(total, axis=0, keepdims=True)
     tables = [far[:, tile * 128 : tile * 128 + 128] for tile in range(SLOTS // 128)]
@@ -404,7 +407,7 @@
         out_ref[block * 8 : block * 8 + 8, :] = lookup(tables, jnp.where(place < CAP, index, SLOTS))
 
 
-def near(flag_ref, arrived_ref, slot_ref, own_ref, index_ref, factor_ref, out_ref, slab_ref, place_ref):
+def home(slot_ref, slab_ref, place_ref):
     slots = jnp.transpose(jnp.broadcast_to(slot_ref[0], (128, SLOTS)))
     panel = lax.broadcasted_iota(jnp.int32, (SLOTS, 128), 1)
     slot = lax.broadcasted_iota(jnp.int32, (SLOTS, 128), 0).astype(F32)
@@ -415,6 +418,9 @@
         slab = quotient(own, CAP)
         slab_ref[:, at] = slab
         place_ref[:, at] = own - slab * CAP
+
+
+def near(flag_ref, arrived_ref, own_ref, index_ref, factor_ref, out_ref):
     before = [arrived_ref[pl.ds(flag_ref[4] + half, 1), :] for half in range(2)]
     after = [arrived_ref[pl.ds(flag_ref[5] + half, 1), :] for half in range(2)]
     tables = before + [own_ref[:, :128], own_ref[:, 128:]] + after
@@ -438,7 +444,7 @@
     return lax.all_to_all(value.reshape(count, rows // count, 128), axis, 0, 0, tiled=True).reshape(rows, 128)
 
 
-def arrange_green(flag_ref, green_ref, plane_ref, out_ref, other_ref):
+def arrange_green(flag_ref, green_ref, plane_ref, across_ref, out_ref, other_ref):
     shared, ends, upper, straight = (flag_ref[i] == 1 for i in range(4))
     place = lax.broadcasted_iota(jnp.int32, (KZ, GX), 0) == 0
     group = lax.broadcasted_iota(jnp.int32, (32, 128), 1) // KZ
@@ -461,8 +467,10 @@
         zero, plane = rows[0:1], plane_ref[k : k + 1, :]
         line = jnp.where(upper, plane, zero)
         if k == 0:
-            line = jnp.where(ends, 0.5 * (zero + plane), line)
-            differ = jnp.where(ends, 0.5 * (zero - plane), 0.0)
+            across = across_ref[...]
+            re, im = jnp.where(upper, across, zero), jnp.where(upper, plane, across)
+            line = jnp.where(ends, 0.5 * (re + im), line)
+            differ = jnp.where(ends, 0.5 * (re - im), 0.0)
             other_ref[...] = lay(jnp.where(place, differ, 0.0))
         rows = jnp.where(place & shared, line, rows)
         laid = lay(rows)
@@ -493,23 +501,28 @@
         scratch=[pltpu.VMEM((SLOTS, 128), F32)], limit=56,
     )
 
-    payload, spectrum = lax.optimization_barrier((payload, green_spectrum))
-    plane = lax.ppermute(spectrum[:, 0, :], "pencil", [(4, 0)])
+    payload, spectrum, own_slots = lax.optimization_barrier((payload, green_spectrum, slot_panel))
+    sent = spectrum[:, 0, :]
+    plane = lax.ppermute(sent, "pencil", [(4, 0)])
+    across = lax.ppermute(
+        sent[:1], ("slab", "pencil"), [(16 * N_PENCIL, 0), (4, 16 * N_PENCIL)]
+    )
     arrived = lax.all_to_all(payload.reshape(N_SLAB, 1, LINES * 128), "slab", 0, 0, tiled=True).reshape(ROWS, 128)
     green, other = call(
-        arrange_green, [shape((2, 256, 128), F32), shape((32, 256), F32)], flags, spectrum, plane, smem=(0,), limit=LIMIT_N
-    )
-    arrived, green, other, flags, anchor = lax.optimization_barrier((arrived, green, other, flags, anchor))
-    near_field, *home = call(
-        near, [shape((1, PAN_DEV), F32)] + [shape((8, PAN_DEV), jnp.int32)] * 2, flags, arrived, slot_panel, row, near_index, near_factor,
-        smem=(0,), limit=LIMIT_N,
-    )
-    after_z, weights = call(
-        project, [shape((1024, 128), F32), shape((128, SLOTS), F32)], arrived, anchor, z_fwd,
+        arrange_green, [shape((2, 256, 128), F32), shape((32, 256), F32)], flags, spectrum, plane, across, smem=(0,), limit=LIMIT_N
+    )
+    homes = call(home, [shape((8, PAN_DEV), jnp.int32)] * 2, own_slots, limit=LIMIT_N)
+    arrived, green, other, flags, anchor, homes = lax.optimization_barrier(
+        (arrived, green, other, flags, anchor, homes)
+    )
+    after_z, weights, near_field = call(
+        project,
+        [shape((1024, 128), F32), shape((128, SLOTS), F32), shape((1, PAN_DEV), F32)],
+        flags, arrived, anchor, z_fwd, row, near_index, near_factor,
         scratch=[pltpu.VMEM((128, SLOTS), F32), pltpu.VMEM((PENCIL_ROWS, SLOTS), jnp.int32)]
-        + [pltpu.VMEM((512, SLOTS), F32), pltpu.VMEM((SLOTS // 2, 128), F32)]
+        + [pltpu.VMEM((SLOTS // 2, 128), F32)]
         + [pltpu.VMEM((EDGE, 512, SLOTS), BF16)] * 2,
-        limit=LIMIT_P,
+        smem=(0,), limit=LIMIT_P,
     )
     by_y = swap(after_z, "pencil", N_PENCIL)
     after_y = call(
@@ -530,11 +543,11 @@
     sampled = call(
         sample, shape((N_SLAB, 128), F32), by_z, weights, anchor, z_bwd,
         scratch=[pltpu.VMEM((PENCIL_ROWS, SLOTS), jnp.int32), pltpu.VMEM((512, 256), F32)]
-        + [pltpu.VMEM((512, SLOTS), F32), pltpu.VMEM((EDGE, 512, SLOTS), F32)],
+        + [pltpu.VMEM((EDGE, 512, SLOTS), F32)],
         limit=LIMIT_S,
     )
     far = lax.all_to_all(sampled, "slab", 0, 0, tiled=True)
-    return call(finish, shape((1, PAN_DEV), F32), far, *home, near_field, limit=40).reshape(PAN_DEV)
+    return call(finish, shape((1, PAN_DEV), F32), far, *homes, near_field, limit=40).reshape(PAN_DEV)
 
 
 def solution(mesh):

time: 125 us -> 125 us (level)
  blocking collectives: 70.7 us -> 86.8 us
  waiting for transfers between devices: 14.9 us -> 5.44 us
  starting transfers between devices: 18.7 us -> 13.6 us
  Pallas kernels: 18.6 us -> 16.4 us
    all_to_all x0 -> x1, blocking collectives: none -> 13.9 us  [per_device(): far = lax.all_to_all(sampled, 'slab', 0, 0, tiled=True)]
    all_to_all x1 -> x0, waiting for transfers between devices: 7.66 us -> none  [per_device(): far = lax.all_to_all(sampled, 'slab', 0, 0, tiled=True)]
    all_to_all x1 -> x0, starting transfers between devices: 5.7 us -> none  [per_device(): far = lax.all_to_all(sampled, 'slab', 0, 0, tiled=True)]
    all_to_all x4, blocking collectives: 70.7 us -> 72.9 us  [swap(): lax.all_to_all(value.reshape(count, rows // count, 128), axis, 0, 0, tile...]
    pallas_call x9, Pallas kernels: 18.6 us -> 16.4 us  [call(): pl.pallas_call(kernel, out_shape=out_shape, in_specs=[pl.BlockSpec(memory...]
    ppermute x1 -> x2, waiting for transfers between devices: 5.28 us -> 3.97 us  [the longest x1 3.97 us: per_device(): plane = lax.ppermute(sent, 'pencil', [(4, 0)])]
  transfers between devices with their start and end apart: 3 -> 3, of which waited for: 3 -> 2; matrix products, arithmetic and copies ran while one was open for 1% -> 1% of each run, Pallas kernels for 2% -> 1%
where the time goes in v8:
time: 125 us; the launch traced here: 124 us
  blocking collectives  86.8 us (69%)
  Pallas kernels  16.4 us (13%)
  starting transfers between devices  13.6 us (11%)
  waiting for transfers between devices  5.44 us (4%)
  local copies, waits for them, and re-layouts  1.69 us (1%)
    all_to_all x4, blocking collectives, swap(): lax.all_to_all(value.reshape(count, rows // count, 128), axis, 0, 0, tile...  72.9 us
    pallas_call x9, Pallas kernels, call(): pl.pallas_call(kernel, out_shape=out_shape, in_specs=[pl.BlockSpec(memory...  16.4 us
    all_to_all x1, blocking collectives, per_device(): far = lax.all_to_all(sampled, 'slab', 0, 0, tiled=True)  13.9 us
    all_to_all x1, starting transfers between devices, per_device(): lax.all_to_all(payload.reshape(N_SLAB, 1, LINES * 128), 'slab', 0, 0, til...  11.6 us
    ppermute x1, waiting for transfers between devices, per_device(): plane = lax.ppermute(sent, 'pencil', [(4, 0)])  3.97 us
  transfers between devices with their start and end apart: 3, of which 2 were waited for; matrix products, arithmetic and copies ran while one was open for 1% of the time, Pallas kernels for 1%

profile of v8, /device:TPU:2, one launch (start us, length us, event | category | flops | bytes accessed | tf_op | source)
XLA Modules:
  0.0 124.4 jit_solution(17453318232143409264)
XLA Ops:
  0.0 0.0 copy-start
  0.0 2.0 %pack.1 = f32[480,128]{1,0:T(8,128)} custom-call(s32[1,1,768]{2,1,0:T(1,128)} %slot_ref.2, f32[64,256]{1,0:T(8,128)} %weight_ref.1, f32[1,256]{1,0:T(1,128)} %bitcast.38), custom_call_target="tpu_custom_call" | custom-call | tf_op jit(solution)/shard_map/pack/pallas_call | solution.py:115
  2.0 11.6 %all-to-all-start = ((f32[32,1,1920]{2,1,0:T(1,128)}), f32[32,1,1920]{2,1,0:T(1,128)S(1)}, u32[]{:S(2)}, u32[]{:S(2)}) async-start(f32[32,1,1920]{2,1,0:T(1,128)} %bitcast.40), calls=%async_computation | async-start | bytes 491520 | tf_op jit(solution)/shard_map/all_to_all | solution.py:510
  13.6 0.0 copy-done
  13.6 0.7 collective-permute-start.1
  14.3 0.3 copy.22
  14.6 1.3 %collective-permute-start = (f32[8,512]{1,0:T(8,128)S(1)}, f32[8,512]{1,0:T(8,128)S(1)}, u32[]{:S(2)}, u32[]{:S(2)}) collective-permute-start(f32[8,512]{1,0:T(8,128)S(1)} %slice_bitcast_fusion), channel_id=1, source_target_pairs={{4,0},{12,8},{20,16},{28,24},{36,32},{44,40},{52,48},{60,56},{68,6... | collective-permute-start | bytes 49160 | tf_op jit(solution)/shard_map/ppermute | solution.py:506
  16.0 0.1 fusion
  16.1 0.0 copy-start.14
  16.1 0.1 add_convert_fusion
  16.1 0.1 pad_add_fusion.flag_ref.refs_0_
  16.2 0.5 copy-done.14
  16.8 0.1 reshape.48
  16.9 0.0 copy-start.12
  16.9 0.0 copy-start.13
  16.9 0.1 reshape.49.anchor_ref
  17.0 0.6 copy-done.12
  17.6 0.0 copy-start.6
  17.6 0.0 copy-start.10
  17.6 0.0 copy-start.11
  17.6 0.2 home.1
  17.8 0.0 copy-start.3
  17.8 0.0 collective-permute-done.1.across_ref
  17.8 4.0 %collective-permute-done.plane_ref = f32[8,512]{1,0:T(8,128)S(1)} collective-permute-done((f32[8,512]{1,0:T(8,128)S(1)}, f32[8,512]{1,0:T(8,128)S(1)}, u32[]{:S(2)}, u32[]{:S(2)}) %collective-permute-start) | collective-permute-done | bytes 16416 | tf_op jit(solution)/shard_map/ppermute | solution.py:506
  21.8 1.2 arrange_green.1
  23.0 1.5 %all-to-all-done = f32[32,1,1920]{2,1,0:T(1,128)S(1)} async-done(((f32[32,1,1920]{2,1,0:T(1,128)}), f32[32,1,1920]{2,1,0:T(1,128)S(1)}, u32[]{:S(2)}, u32[]{:S(2)}) %all-to-all-start) | async-done | bytes 245792 | tf_op jit(solution)/shard_map/all_to_all | solution.py:510
  24.5 0.0 copy-done.13
  24.5 0.0 copy-done.6
  24.5 0.0 copy-done.10
  24.5 0.0 copy-done.11
  24.5 3.7 %project.1 = (f32[1024,128]{1,0:T(8,128)S(1)}, f32[128,768]{1,0:T(8,128)S(1)}, f32[1,256]{1,0:T(1,128)S(1)}) custom-call(s32[6]{0:T(128)S(1)} %pad_add_fusion.flag_ref.refs_0_, f32[480,128]{1,0:T(8,128)S(1)} %bitcast.34, s32[1,1,768]{2,1,0:T(1,128)S(1)} %reshape.49.anchor_ref, bf16[2,256,256]{2,1,0:T(8,128)(2,1)S(1)} %copy-done.6, f32[1,256]{1,0:T(1,128)S(1)} %bitcast.39, ...), custom_call_target="tpu_custom_call" | custom-call | tf_op jit(solution)/shard_map/project/pallas_call | solution.py:115
  28.3 0.0 copy-start.5
  28.3 14.8 %all_to_all.36 = f32[8,128,128]{2,1,0:T(8,128)S(1)} all-to-all(f32[8,128,128]{2,1,0:T(8,128)S(1)} %bitcast.35), channel_id=1, replica_groups=mesh['slab'=32,'pencil'=8] {'pencil'}, dimensions={0} | all-to-all | bytes 1048576 | tf_op jit(solution)/shard_map/all_to_all | solution.py:444
  43.1 0.0 copy-done.3
  43.1 0.0 copy-done.5
  43.1 0.0 copy-start.8
  43.1 0.0 copy-start.9
  43.1 1.5 %y_forward.1 = f32[1024,128]{1,0:T(8,128)S(1)} custom-call(s32[6]{0:T(128)S(1)} %pad_add_fusion.flag_ref.refs_0_, f32[1024,128]{1,0:T(8,128)S(1)} %bitcast.32, bf16[2,512,512]{2,1,0:T(8,128)(2,1)S(1)} %copy-done.3, bf16[2,2,256,256]{3,2,1,0:T(8,128)(2,1)S(1)} %copy-done.5), custom_call_target="tpu_custom_call" | custom-call | tf_op jit(solution)/shard_map/y_forward/pallas_call | solution.py:115
  44.6 0.0 copy-start.2
  44.6 23.8 %all_to_all.37 = f32[32,32,128]{2,1,0:T(8,128)S(1)} all-to-all(f32[32,32,128]{2,1,0:T(8,128)S(1)} %bitcast.33), channel_id=1, replica_groups=mesh['slab'=32,'pencil'=8] {'slab'}, dimensions={0} | all-to-all | bytes 1048576 | tf_op jit(solution)/shard_map/all_to_all | solution.py:444
  68.4 0.0 copy-done.8
  68.4 0.0 copy-done.9
  68.4 0.0 copy-done.2
  68.4 0.0 copy-start.4
  68.4 2.8 %x_stage.1 = f32[1024,128]{1,0:T(8,128)S(1)} custom-call(s32[6]{0:T(128)S(1)} %pad_add_fusion.flag_ref.refs_0_, f32[1024,128]{1,0:T(8,128)S(1)} %bitcast.28, f32[2,256,128]{2,1,0:T(8,128)S(1)} %get-tuple-element.33.green_ref, f32[32,256]{1,0:T(8,128)S(1)} %get-tuple-element.34.other_ref, f32[2,32,256]{2,1,0:T(8,128)S(1)} %copy-done.8, ...), custom_call_target="tpu_custom_call" | custom-call | tf_op jit(solution)/shard_map/x_stage/pallas_call | solution.py:115
  71.2 0.0 copy-start.1
  71.3 21.4 %all_to_all.38 = f32[32,32,128]{2,1,0:T(8,128)S(1)} all-to-all(f32[32,32,128]{2,1,0:T(8,128)S(1)} %bitcast.29), channel_id=1, replica_groups=mesh['slab'=32,'pencil'=8] {'slab'}, dimensions={0} | all-to-all | bytes 1048576 | tf_op jit(solution)/shard_map/all_to_all | solution.py:444
  92.7 0.0 copy-done.4
  92.7 0.0 copy-done.1
  92.7 1.5 %y_backward.1 = f32[1024,128]{1,0:T(8,128)S(1)} custom-call(s32[6]{0:T(128)S(1)} %pad_add_fusion.flag_ref.refs_0_, f32[1024,128]{1,0:T(8,128)S(1)} %bitcast.30, bf16[2,512,512]{2,1,0:T(8,128)(2,1)S(1)} %copy-done.1, bf16[2,2,256,256]{3,2,1,0:T(8,128)(2,1)S(1)} %copy-done.4), custom_call_target="tpu_custom_call" | custom-call | tf_op jit(solution)/shard_map/y_backward/pallas_call | solution.py:115
  94.2 0.0 copy-start.7
  94.2 12.9 %all_to_all.39 = f32[8,128,128]{2,1,0:T(8,128)S(1)} all-to-all(f32[8,128,128]{2,1,0:T(8,128)S(1)} %bitcast.31), channel_id=1, replica_groups=mesh['slab'=32,'pencil'=8] {'pencil'}, dimensions={0} | all-to-all | bytes 1048576 | tf_op jit(solution)/shard_map/all_to_all | solution.py:444
  107.1 0.0 copy-done.7
  107.1 2.8 %sample.1 = f32[32,128]{1,0:T(8,128)S(1)} custom-call(f32[1024,128]{1,0:T(8,128)S(1)} %bitcast.27, f32[128,768]{1,0:T(8,128)S(1)} %get-tuple-element.35.weight_ref, s32[1,1,768]{2,1,0:T(1,128)S(1)} %reshape.49.anchor_ref, bf16[2,256,256]{2,1,0:T(8,128)(2,1)S(1)} %copy-done.7), custom_call_target="tpu_custom_call" | custom-call | tf_op jit(solution)/shard_map/sample/pallas_call | solution.py:115
  109.9 13.9 %all_to_all.40 = f32[32,1,128]{2,1,0:T(1,128)S(1)} all-to-all(f32[32,1,128]{2,1,0:T(1,128)S(1)} %bitcast.36), channel_id=1, replica_groups=mesh['slab'=32,'pencil'=8] {'slab'}, dimensions={0} | all-to-all | bytes 32768 | tf_op jit(solution)/shard_map/all_to_all | solution.py:549
  123.8 0.7 finish.1
  (4 shorter events, 0.0 us)
Async XLA Ops:
  0.0 13.6 %copy-start = (f32[8,32,512]{2,1,0:T(8,128)S(1)}, f32[8,32,512]{2,1,0:T(8,128)}, u32[]{:S(2)}) copy-start(f32[8,32,512]{2,1,0:T(8,128)} %green_ref) | copy-start | bytes 1572868
  2.0 22.5 %all-to-all-start = ((f32[32,1,1920]{2,1,0:T(1,128)}), f32[32,1,1920]{2,1,0:T(1,128)S(1)}, u32[]{:S(2)}, u32[]{:S(2)}) async-start(f32[32,1,1920]{2,1,0:T(1,128)} %bitcast.40), calls=%async_computation | async-start | bytes 491520 | tf_op jit(solution)/shard_map/all_to_all | solution.py:510
  13.6 4.2 %collective-permute-start.1 = (f32[1,512]{1,0:T(1,128)S(1)}, f32[1,512]{1,0:T(1,128)S(1)}, u32[]{:S(2)}, u32[]{:S(2)}) collective-permute-start(f32[1,512]{1,0:T(1,128)S(1)} %slice_bitcast_fusion.1), channel_id=1, source_target_pairs={{128,0},{4,128}} | collective-permute-start | bytes 6152 | tf_op jit(solution)/shard_map/ppermute | solution.py:507
  14.6 7.1 %collective-permute-start = (f32[8,512]{1,0:T(8,128)S(1)}, f32[8,512]{1,0:T(8,128)S(1)}, u32[]{:S(2)}, u32[]{:S(2)}) collective-permute-start(f32[8,512]{1,0:T(8,128)S(1)} %slice_bitcast_fusion), channel_id=1, source_target_pairs={{4,0},{12,8},{20,16},{28,24},{36,32},{44,40},{52,48},{60,56},{68,6... | collective-permute-start | bytes 49160 | tf_op jit(solution)/shard_map/ppermute | solution.py:506
  16.1 0.7 copy-start.14
  16.9 0.7 copy-start.12
  16.9 7.6 %copy-start.13 = (f32[256]{0:T(256)S(1)}, f32[256]{0:T(256)}, u32[]{:S(2)}) copy-start(f32[256]{0:T(256)} %param.16) | copy-start | bytes 3076
  17.6 6.9 %copy-start.6 = (bf16[2,256,256]{2,1,0:T(8,128)(2,1)S(1)}, bf16[2,256,256]{2,1,0:T(8,128)(2,1)}, u32[]{:S(2)}) copy-start(bf16[2,256,256]{2,1,0:T(8,128)(2,1)} %constant.57.clone.z_ref) | copy-start | bytes 786436
  17.6 6.9 %copy-start.10 = (s32[32,256]{1,0:T(8,128)S(1)}, s32[32,256]{1,0:T(8,128)}, u32[]{:S(2)}) copy-start(s32[32,256]{1,0:T(8,128)} %index_ref.1) | copy-start | bytes 98308
  17.6 6.9 %copy-start.11 = (f32[32,256]{1,0:T(8,128)S(1)}, f32[32,256]{1,0:T(8,128)}, u32[]{:S(2)}) copy-start(f32[32,256]{1,0:T(8,128)} %factor_ref.1) | copy-start | bytes 98308
  17.8 25.3 %copy-start.3 = (bf16[2,512,512]{2,1,0:T(8,128)(2,1)S(1)}, bf16[2,512,512]{2,1,0:T(8,128)(2,1)}, u32[]{:S(2)}) copy-start(bf16[2,512,512]{2,1,0:T(8,128)(2,1)} %constant.59.clone.refs_2_) | copy-start | bytes 3145732
  28.3 14.8 %copy-start.5 = (bf16[2,2,256,256]{3,2,1,0:T(8,128)(2,1)S(1)}, bf16[2,2,256,256]{3,2,1,0:T(8,128)(2,1)}, u32[]{:S(2)}) copy-start(bf16[2,2,256,256]{3,2,1,0:T(8,128)(2,1)} %constant.60.clone.refs_3_) | copy-start | bytes 1572868
  43.1 25.3 %copy-start.8 = (f32[2,32,256]{2,1,0:T(8,128)S(1)}, f32[2,32,256]{2,1,0:T(8,128)}, u32[]{:S(2)}) copy-start(f32[2,32,256]{2,1,0:T(8,128)} %constant.65.clone.twist_ref) | copy-start | bytes 196612
  43.1 25.3 %copy-start.9 = (bf16[2,64,64]{2,1,0:T(8,128)(2,1)S(1)}, bf16[2,64,64]{2,1,0:T(8,128)(2,1)}, u32[]{:S(2)}) copy-start(bf16[2,64,64]{2,1,0:T(8,128)(2,1)} %constant.63.clone.row_ref) | copy-start | bytes 49156
  44.6 23.8 %copy-start.2 = (bf16[2,512,512]{2,1,0:T(8,128)(2,1)S(1)}, bf16[2,512,512]{2,1,0:T(8,128)(2,1)}, u32[]{:S(2)}) copy-start(bf16[2,512,512]{2,1,0:T(8,128)(2,1)} %constant.64.clone.lane_ref) | copy-start | bytes 3145732
  68.4 24.2 %copy-start.4 = (bf16[2,2,256,256]{3,2,1,0:T(8,128)(2,1)S(1)}, bf16[2,2,256,256]{3,2,1,0:T(8,128)(2,1)}, u32[]{:S(2)}) copy-start(bf16[2,2,256,256]{3,2,1,0:T(8,128)(2,1)} %constant.62.clone.refs_3_) | copy-start | bytes 1572868
  71.2 21.4 %copy-start.1 = (bf16[2,512,512]{2,1,0:T(8,128)(2,1)S(1)}, bf16[2,512,512]{2,1,0:T(8,128)(2,1)}, u32[]{:S(2)}) copy-start(bf16[2,512,512]{2,1,0:T(8,128)(2,1)} %constant.61.clone.refs_2_) | copy-start | bytes 3145732
  94.2 13.0 %copy-start.7 = (bf16[2,256,256]{2,1,0:T(8,128)(2,1)S(1)}, bf16[2,256,256]{2,1,0:T(8,128)(2,1)}, u32[]{:S(2)}) copy-start(bf16[2,256,256]{2,1,0:T(8,128)(2,1)} %constant.58.clone.z_ref) | copy-start | bytes 786436

commit v9 on v8

--- a/solution.py
+++ b/solution.py
@@ -63,7 +63,7 @@
     backward = forward.T / GY
     part = np.where(ro == 0, cosine, -sine)
     ends = (ky == 0) | (ky == 128)
-    part = np.where(ends, np.where(ro == 0, 1.0, 1.0 - 2.0 * (y % 2)), part)
+    part = np.where(ends, np.where(ro == (ky == 128), cosine, 0.0), part)
     first = part[:, np.broadcast_to(ri == 0, y.shape)[0]]
     shared = np.stack([first[:256], first[256:]])
     scale = (np.where(ends, 1.0, 2.0) / GY).reshape(2, 256, 1)
@@ -109,13 +109,12 @@
     return mm(left[0], right[0]) + (mm(left[0], right[1]) + mm(left[1], right[0]))
 
 
-def call(kernel, out_shape, *args, scratch=(), smem=(), limit):
-    space = {i: pltpu.SMEM for i in smem}
+def call(kernel, out_shape, *args, scratch=(), limit):
     out_spec = pl.BlockSpec(memory_space=pltpu.VMEM)
     return pl.pallas_call(
         kernel,
         out_shape=out_shape,
-        in_specs=[pl.BlockSpec(memory_space=space.get(i, pltpu.VMEM)) for i in range(len(args))],
+        in_specs=[pl.BlockSpec(memory_space=pltpu.VMEM)] * len(args),
         out_specs=[out_spec] * len(out_shape) if isinstance(out_shape, list) else out_spec,
         scratch_shapes=list(scratch),
         compiler_params=pltpu.CompilerParams(vmem_limit_bytes=limit * 2**20),
@@ -136,6 +135,11 @@
             tiles[i] = jnp.where(upper, pltpu.roll(high, 16 * step, 1), low)
             tiles[i + step] = jnp.where(upper, high, pltpu.roll(low, 128 - 16 * step, 1))
     return tiles
+
+
+def position():
+    slab, pencil = lax.axis_index("slab"), lax.axis_index("pencil")
+    return slab, pencil, (pencil == 0) & ((slab == 0) | (slab == 16))
 
 
 def lookup(tables, index):
@@ -240,8 +244,7 @@
     return jnp.where((lane == picked) & (dy < EDGE), 1.0, 0.0).astype(BF16)
 
 
-def project(flag_ref, arrived_ref, anchor_ref, z_ref, own_ref, index_ref, factor_ref, out_ref, weight_ref, near_ref, scaled_ref, y_ref, packed_ref, high_ref, low_ref):
-    near(flag_ref, arrived_ref, own_ref, index_ref, factor_ref, near_ref)
+def project(arrived_ref, anchor_ref, z_ref, out_ref, weight_ref, scaled_ref, y_ref, packed_ref, high_ref, low_ref):
     for s in range(N_SLAB):
         packed_ref[s * 12 : s * 12 + 12, :] = arrived_ref[s * LINES : s * LINES + 12, :]
     packed = jnp.concatenate(split(packed_ref[...]), axis=0)
@@ -298,23 +301,37 @@
     return lax.broadcasted_iota(jnp.int32, shape, 1) % KZ == 0
 
 
-def halves_of(value, group):
-    return value[group * 256 : group * 256 + 256]
-
-
-def planes_of(value, plane):
-    return value.reshape(8, 2, 32, 256)[:, plane].reshape(256, 256)
-
-
-def y_stage(source, target, join, fuse):
-    def kernel(flag_ref, in_ref, table_ref, shared_ref, out_ref, work_ref):
-        data = split(gathered(in_ref, *source))
+def sign_of_y():
+    return (1 - 2 * (lax.broadcasted_iota(jnp.int32, (256, 256), 0) % 2)).astype(F32)
+
+
+def shared_forward(value, data, table_ref):
+    def plane(part, index):
+        return part.reshape(8, 2, 32, 256)[:, index].reshape(256, 256)
+
+    parts = [mm3(table_ref[:, i], [plane(part, i) for part in data]) for i in range(2)]
+    row = lax.broadcasted_iota(jnp.int32, (256, 256), 0)
+    second = jnp.sum(plane(value, 1), axis=0, keepdims=True)
+    first = jnp.sum(plane(value, 0) * sign_of_y(), axis=0, keepdims=True)
+    return jnp.concatenate([jnp.where(row == 8, second, parts[0]), jnp.where(row == 0, first, parts[1])], axis=0)
+
+
+def shared_backward(value, data, table_ref):
+    parts = [mm3(table_ref[:, i], [part[i * 256 : i * 256 + 256] for part in data]) for i in range(2)]
+    parts[0] += value[256:257] * (sign_of_y() * (1.0 / GY))
+    parts[1] += value[8:9] * (1.0 / GY)
+    return jnp.stack([part.reshape(8, 32, 256) for part in parts], axis=1).reshape(512, 256)
+
+
+def y_stage(source, target, shared):
+    def kernel(in_ref, table_ref, shared_ref, out_ref, work_ref):
+        value = gathered(in_ref, *source)
+        data = split(value)
         work_ref[...] = mm3(table_ref[...], data)
 
-        @pl.when(flag_ref[0] == 1)
+        @pl.when(lax.axis_index("pencil") == 0)
         def _():
-            parts = [[join(part, group) for part in data] for group in range(2)]
-            other = fuse([mm3(shared_ref[:, group], parts[group]) for group in range(2)])
+            other = shared(value, data, shared_ref)
             work_ref[...] = jnp.where(shared_lane(other.shape), other, work_ref[...])
 
         scattered(work_ref[...], out_ref, *target)
@@ -323,17 +340,14 @@
 
 
 def y_forward(*refs):
-    y_stage((8, 64), (32, 16), planes_of, lambda parts: jnp.concatenate(parts, axis=0))(*refs)
+    y_stage((8, 64), (32, 16), shared_forward)(*refs)
 
 
 def y_backward(*refs):
-    def fuse(parts):
-        return jnp.stack([part.reshape(8, 32, 256) for part in parts], axis=1).reshape(512, 256)
-
-    y_stage((32, 16), (8, 64), halves_of, fuse)(*refs)
-
-
-def x_stage(flag_ref, in_ref, green_ref, other_ref, twist_ref, row_ref, lane_ref, out_ref, re_ref, im_ref):
+    y_stage((32, 16), (8, 64), shared_backward)(*refs)
+
+
+def x_stage(in_ref, green_ref, other_ref, twist_ref, row_ref, lane_ref, out_ref, re_ref, im_ref):
     row_tables, lane_tables = row_ref[...], lane_ref[...]
     cosine, sine = twist_ref[0], twist_ref[1]
 
@@ -352,7 +366,7 @@
         re_ref[half] = full[:, at] * green_ref[half]
         im_ref[half] = full[:, 256 + half * 128 : 384 + half * 128] * green_ref[half]
 
-    @pl.when(flag_ref[1] == 1)
+    @pl.when(position()[2])
     def _():
         conjugate = jnp.concatenate([data[0][:, :256], -data[1][:, :256]], axis=0)
         rows = mm3(row_tables, split(conjugate))
@@ -420,9 +434,12 @@
         place_ref[:, at] = own - slab * CAP
 
 
-def near(flag_ref, arrived_ref, own_ref, index_ref, factor_ref, out_ref):
-    before = [arrived_ref[pl.ds(flag_ref[4] + half, 1), :] for half in range(2)]
-    after = [arrived_ref[pl.ds(flag_ref[5] + half, 1), :] for half in range(2)]
+def near(arrived_ref, own_ref, index_ref, factor_ref, out_ref):
+    slab = lax.axis_index("slab")
+    before, after = (
+        [arrived_ref[pl.ds(lax.rem(slab + shift, N_SLAB) * LINES + 13 + half, 1), :] for half in range(2)]
+        for shift in (N_SLAB - 1, 1)
+    )
     tables = before + [own_ref[:, :128], own_ref[:, 128:]] + after
     for lane in range(2):
         total = jnp.zeros((8, 128), F32)
@@ -444,8 +461,9 @@
     return lax.all_to_all(value.reshape(count, rows // count, 128), axis, 0, 0, tiled=True).reshape(rows, 128)
 
 
-def arrange_green(flag_ref, green_ref, plane_ref, across_ref, out_ref, other_ref):
-    shared, ends, upper, straight = (flag_ref[i] == 1 for i in range(4))
+def arrange_green(green_ref, plane_ref, out_ref, other_ref):
+    slab, pencil, ends = position()
+    shared, upper, straight = pencil == 0, slab >= 16, pencil < 4
     place = lax.broadcasted_iota(jnp.int32, (KZ, GX), 0) == 0
     group = lax.broadcasted_iota(jnp.int32, (32, 128), 1) // KZ
 
@@ -467,10 +485,8 @@
         zero, plane = rows[0:1], plane_ref[k : k + 1, :]
         line = jnp.where(upper, plane, zero)
         if k == 0:
-            across = across_ref[...]
-            re, im = jnp.where(upper, across, zero), jnp.where(upper, plane, across)
-            line = jnp.where(ends, 0.5 * (re + im), line)
-            differ = jnp.where(ends, 0.5 * (re - im), 0.0)
+            line = jnp.where(ends, 0.5 * (zero + plane), line)
+            differ = jnp.where(ends, 0.5 * (zero - plane), 0.0)
             other_ref[...] = lay(jnp.where(place, differ, 0.0))
         rows = jnp.where(place & shared, line, rows)
         laid = lay(rows)
@@ -479,12 +495,6 @@
 
 
 def per_device(strength, stencil_weight, slot_panel, slot_anchor, green_spectrum, near_index, near_factor):
-    slab = lax.axis_index("slab")
-    pencil = lax.axis_index("pencil")
-    ends = (pencil == 0) & ((slab == 0) | (slab == 16))
-    flags = jnp.stack([pencil == 0, ends, slab >= 16, pencil < 4]).astype(jnp.int32)
-    around = jnp.stack([(slab + N_SLAB - 1) % N_SLAB, (slab + 1) % N_SLAB])
-    flags = jnp.concatenate([flags, around.astype(jnp.int32) * LINES + 13])
     row = strength.reshape(1, PAN_DEV)
 
     z_fwd, z_bwd = (pair(t) for t in z_tables())
@@ -502,42 +512,38 @@
     )
 
     payload, spectrum, own_slots = lax.optimization_barrier((payload, green_spectrum, slot_panel))
-    sent = spectrum[:, 0, :]
-    plane = lax.ppermute(sent, "pencil", [(4, 0)])
-    across = lax.ppermute(
-        sent[:1], ("slab", "pencil"), [(16 * N_PENCIL, 0), (4, 16 * N_PENCIL)]
-    )
+    plane = lax.ppermute(spectrum[:, 0, :], "pencil", [(4, 0)])
     arrived = lax.all_to_all(payload.reshape(N_SLAB, 1, LINES * 128), "slab", 0, 0, tiled=True).reshape(ROWS, 128)
     green, other = call(
-        arrange_green, [shape((2, 256, 128), F32), shape((32, 256), F32)], flags, spectrum, plane, across, smem=(0,), limit=LIMIT_N
+        arrange_green, [shape((2, 256, 128), F32), shape((32, 256), F32)], spectrum, plane, limit=LIMIT_N
     )
     homes = call(home, [shape((8, PAN_DEV), jnp.int32)] * 2, own_slots, limit=LIMIT_N)
-    arrived, green, other, flags, anchor, homes = lax.optimization_barrier(
-        (arrived, green, other, flags, anchor, homes)
-    )
-    after_z, weights, near_field = call(
-        project,
-        [shape((1024, 128), F32), shape((128, SLOTS), F32), shape((1, PAN_DEV), F32)],
-        flags, arrived, anchor, z_fwd, row, near_index, near_factor,
+    arrived, green, other, anchor, homes = lax.optimization_barrier((arrived, green, other, anchor, homes))
+    near_field = call(
+        near, shape((1, PAN_DEV), F32), arrived, row, near_index, near_factor, limit=LIMIT_N
+    )
+    after_z, weights = call(
+        project, [shape((1024, 128), F32), shape((128, SLOTS), F32)], arrived, anchor, z_fwd,
         scratch=[pltpu.VMEM((128, SLOTS), F32), pltpu.VMEM((PENCIL_ROWS, SLOTS), jnp.int32)]
         + [pltpu.VMEM((SLOTS // 2, 128), F32)]
         + [pltpu.VMEM((EDGE, 512, SLOTS), BF16)] * 2,
-        smem=(0,), limit=LIMIT_P,
-    )
+        limit=LIMIT_P,
+    )
+    after_z, near_field = lax.optimization_barrier((after_z, near_field))
     by_y = swap(after_z, "pencil", N_PENCIL)
     after_y = call(
-        y_forward, shape((1024, 128), F32), flags, by_y, y_fwd, y_fwd_shared,
-        scratch=[pltpu.VMEM((512, 256), F32)], smem=(0,), limit=LIMIT_Y,
+        y_forward, shape((1024, 128), F32), by_y, y_fwd, y_fwd_shared,
+        scratch=[pltpu.VMEM((512, 256), F32)], limit=LIMIT_Y,
     )
     by_x = swap(after_y, "slab", N_SLAB)
     after_x = call(
-        x_stage, shape((1024, 128), F32), flags, by_x, green, other, twist, rows, lanes,
-        scratch=[pltpu.VMEM((2, 256, 128), F32)] * 2, smem=(0,), limit=LIMIT_X,
+        x_stage, shape((1024, 128), F32), by_x, green, other, twist, rows, lanes,
+        scratch=[pltpu.VMEM((2, 256, 128), F32)] * 2, limit=LIMIT_X,
     )
     back_x = swap(after_x, "slab", N_SLAB)
     back_y = call(
-        y_backward, shape((1024, 128), F32), flags, back_x, y_bwd, y_bwd_shared,
-        scratch=[pltpu.VMEM((512, 256), F32)], smem=(0,), limit=LIMIT_Y,
+        y_backward, shape((1024, 128), F32), back_x, y_bwd, y_bwd_shared,
+        scratch=[pltpu.VMEM((512, 256), F32)], limit=LIMIT_Y,
     )
     by_z = swap(back_y, "pencil", N_PENCIL)
     sampled = call(

time: 125 us -> 121 us (0.968)
  Pallas kernels: 16.4 us -> 13.9 us
  blocking collectives: 86.8 us -> 84.6 us
  waiting for transfers between devices: 5.44 us -> 7.42 us
    pallas_call x9 -> x10, Pallas kernels: 16.4 us -> 13.9 us  [call(): pl.pallas_call(kernel, out_shape=out_shape, in_specs=[pl.BlockSpec(memory...]
    all_to_all x4, blocking collectives: 72.9 us -> 70.8 us  [swap(): lax.all_to_all(value.reshape(count, rows // count, 128), axis, 0, 0, tile...]
    ppermute x2 -> x1, waiting for transfers between devices: 3.97 us -> 4.76 us  [per_device(): plane = lax.ppermute(spectrum[:, 0, :], 'pencil', [(4, 0)])]
  transfers between devices with their start and end apart: 3 -> 2, of which waited for: 2 -> 2; matrix products, arithmetic and copies ran while one was open for 1% -> 0% of each run, Pallas kernels for 1% -> 1%
where the time goes in v9:
time: 121 us; the launch traced here: 120 us
  blocking collectives  84.6 us (70%)
  Pallas kernels  13.9 us (11%)
  starting transfers between devices  12.9 us (11%)
  waiting for transfers between devices  7.42 us (6%)
    all_to_all x4, blocking collectives, swap(): lax.all_to_all(value.reshape(count, rows // count, 128), axis, 0, 0, tile...  70.8 us
    pallas_call x10, Pallas kernels, call(): pl.pallas_call(kernel, out_shape=out_shape, in_specs=[pl.BlockSpec(memory...  13.9 us
    all_to_all x1, blocking collectives, per_device(): far = lax.all_to_all(sampled, 'slab', 0, 0, tiled=True)  13.9 us
    all_to_all x1, starting transfers between devices, per_device(): lax.all_to_all(payload.reshape(N_SLAB, 1, LINES * 128), 'slab', 0, 0, til...  11.6 us
    ppermute x1, waiting for transfers between devices, per_device(): plane = lax.ppermute(spectrum[:, 0, :], 'pencil', [(4, 0)])  4.76 us
    all_to_all x1, waiting for transfers between devices, per_device(): lax.all_to_all(payload.reshape(N_SLAB, 1, LINES * 128), 'slab', 0, 0, til...  2.66 us
  transfers between devices with their start and end apart: 2, of which 2 were waited for; matrix products, arithmetic and copies ran while one was open for 0% of the time, Pallas kernels for 1%

profile of v9, /device:TPU:2, one launch (start us, length us, event | category | flops | bytes accessed | tf_op | source)
XLA Modules:
  0.0 120.3 jit_solution(15102663204880243309)
XLA Ops:
  0.0 0.0 copy-start
  0.0 2.0 %pack.1 = f32[480,128]{1,0:T(8,128)} custom-call(s32[1,1,768]{2,1,0:T(1,128)} %slot_ref.2, f32[64,256]{1,0:T(8,128)} %weight_ref.1, f32[1,256]{1,0:T(1,128)} %bitcast.31), custom_call_target="tpu_custom_call" | custom-call | tf_op jit(solution)/shard_map/pack/pallas_call | solution.py:114
  2.0 11.6 %all-to-all-start = ((f32[32,1,1920]{2,1,0:T(1,128)}), f32[32,1,1920]{2,1,0:T(1,128)S(1)}, u32[]{:S(2)}, u32[]{:S(2)}) async-start(f32[32,1,1920]{2,1,0:T(1,128)} %bitcast.33), calls=%async_computation | async-start | bytes 491520 | tf_op jit(solution)/shard_map/all_to_all | solution.py:516
  13.6 0.0 copy-done
  13.6 0.3 copy.22
  13.9 0.0 copy-start.14
  14.0 1.3 %collective-permute-start = (f32[8,512]{1,0:T(8,128)S(1)}, f32[8,512]{1,0:T(8,128)S(1)}, u32[]{:S(2)}, u32[]{:S(2)}) collective-permute-start(f32[8,512]{1,0:T(8,128)S(1)} %slice_bitcast_fusion), channel_id=1, source_target_pairs={{4,0},{12,8},{20,16},{28,24},{36,32},{44,40},{52,48},{60,56},{68,6... | collective-permute-start | bytes 49160 | tf_op jit(solution)/shard_map/ppermute | solution.py:515
  15.3 0.0 copy-done.14
  15.3 0.1 reshape.47
  15.4 0.0 copy-start.12
  15.4 0.1 reshape.48.anchor_ref
  15.6 0.6 copy-done.12
  16.1 0.2 home.1
  16.3 0.0 copy-start.10
  16.3 0.0 copy-start.11
  16.3 4.8 %collective-permute-done.plane_ref = f32[8,512]{1,0:T(8,128)S(1)} collective-permute-done((f32[8,512]{1,0:T(8,128)S(1)}, f32[8,512]{1,0:T(8,128)S(1)}, u32[]{:S(2)}, u32[]{:S(2)}) %collective-permute-start) | collective-permute-done | bytes 16416 | tf_op jit(solution)/shard_map/ppermute | solution.py:515
  21.1 0.0 copy-start.13
  21.1 0.0 copy-start.6
  21.1 0.7 arrange_green.1
  21.8 0.0 copy-start.3
  21.8 2.7 %all-to-all-done = f32[32,1,1920]{2,1,0:T(1,128)S(1)} async-done(((f32[32,1,1920]{2,1,0:T(1,128)}), f32[32,1,1920]{2,1,0:T(1,128)S(1)}, u32[]{:S(2)}, u32[]{:S(2)}) %all-to-all-start) | async-done | bytes 245792 | tf_op jit(solution)/shard_map/all_to_all | solution.py:516
  24.5 0.0 copy-done.10
  24.5 0.0 copy-done.11
  24.5 0.0 copy-done.13
  24.5 0.2 near.1.near_ref
  24.7 0.0 copy-done.6
  24.7 3.2 %project.1 = (f32[1024,128]{1,0:T(8,128)S(1)}, f32[128,768]{1,0:T(8,128)S(1)}) custom-call(f32[480,128]{1,0:T(8,128)S(1)} %bitcast.20, s32[1,1,768]{2,1,0:T(1,128)S(1)} %reshape.48.anchor_ref, bf16[2,256,256]{2,1,0:T(8,128)(2,1)S(1)} %copy-done.6), custom_call_target="tpu_custom_call" | custom-call | tf_op jit(solution)/shard_map/project/pallas_call | solution.py:114
  27.9 0.0 copy-start.5
  27.9 14.8 %all_to_all.36 = f32[8,128,128]{2,1,0:T(8,128)S(1)} all-to-all(f32[8,128,128]{2,1,0:T(8,128)S(1)} %bitcast.28), channel_id=1, replica_groups=mesh['slab'=32,'pencil'=8] {'pencil'}, dimensions={0} | all-to-all | bytes 1048576 | tf_op jit(solution)/shard_map/all_to_all | solution.py:461
  42.7 0.0 copy-done.3
  42.7 0.0 copy-done.5
  42.7 0.0 copy-start.8
  42.7 0.0 copy-start.9
  42.7 1.0 y_forward.1
  43.7 0.0 copy-start.2
  43.8 21.6 %all_to_all.37 = f32[32,32,128]{2,1,0:T(8,128)S(1)} all-to-all(f32[32,32,128]{2,1,0:T(8,128)S(1)} %bitcast.24), channel_id=1, replica_groups=mesh['slab'=32,'pencil'=8] {'slab'}, dimensions={0} | all-to-all | bytes 1048576 | tf_op jit(solution)/shard_map/all_to_all | solution.py:461
  65.4 0.0 copy-done.8
  65.4 0.0 copy-done.9
  65.4 0.0 copy-done.2
  65.4 0.0 copy-start.4
  65.4 2.3 %x_stage.1 = f32[1024,128]{1,0:T(8,128)S(1)} custom-call(f32[1024,128]{1,0:T(8,128)S(1)} %bitcast.21, f32[2,256,128]{2,1,0:T(8,128)S(1)} %get-tuple-element.33.green_ref, f32[32,256]{1,0:T(8,128)S(1)} %get-tuple-element.34.other_ref, f32[2,32,256]{2,1,0:T(8,128)S(1)} %copy-done.8, bf16[2,64,64]{2,1,0:T(8,128)(2,1)S(1)} %copy-done.9, ...), custom_call_target="tpu_custom_call" | custom-call | tf_op jit(solution)/shard_map/x_stage/pallas_call | solution.py:114
  67.7 0.0 copy-start.1
  67.7 21.4 %all_to_all.38 = f32[32,32,128]{2,1,0:T(8,128)S(1)} all-to-all(f32[32,32,128]{2,1,0:T(8,128)S(1)} %bitcast.22), channel_id=1, replica_groups=mesh['slab'=32,'pencil'=8] {'slab'}, dimensions={0} | all-to-all | bytes 1048576 | tf_op jit(solution)/shard_map/all_to_all | solution.py:461
  89.1 0.0 copy-done.4
  89.1 0.0 copy-done.1
  89.1 1.0 y_backward.1
  90.1 0.0 copy-start.7
  90.1 12.9 %all_to_all.39 = f32[8,128,128]{2,1,0:T(8,128)S(1)} all-to-all(f32[8,128,128]{2,1,0:T(8,128)S(1)} %bitcast.26), channel_id=1, replica_groups=mesh['slab'=32,'pencil'=8] {'pencil'}, dimensions={0} | all-to-all | bytes 1048576 | tf_op jit(solution)/shard_map/all_to_all | solution.py:461
  103.0 0.0 copy-done.7
  103.0 2.8 %sample.1 = f32[32,128]{1,0:T(8,128)S(1)} custom-call(f32[1024,128]{1,0:T(8,128)S(1)} %bitcast.27, f32[128,768]{1,0:T(8,128)S(1)} %get-tuple-element.35.weight_ref, s32[1,1,768]{2,1,0:T(1,128)S(1)} %reshape.48.anchor_ref, bf16[2,256,256]{2,1,0:T(8,128)(2,1)S(1)} %copy-done.7), custom_call_target="tpu_custom_call" | custom-call | tf_op jit(solution)/shard_map/sample/pallas_call | solution.py:114
  105.8 13.9 %all_to_all.40 = f32[32,1,128]{2,1,0:T(1,128)S(1)} all-to-all(f32[32,1,128]{2,1,0:T(1,128)S(1)} %bitcast.29), channel_id=1, replica_groups=mesh['slab'=32,'pencil'=8] {'slab'}, dimensions={0} | all-to-all | bytes 32768 | tf_op jit(solution)/shard_map/all_to_all | solution.py:555
  119.7 0.7 finish.1
  (3 shorter events, 0.0 us)
Async XLA Ops:
  0.0 13.6 %copy-start = (f32[8,32,512]{2,1,0:T(8,128)S(1)}, f32[8,32,512]{2,1,0:T(8,128)}, u32[]{:S(2)}) copy-start(f32[8,32,512]{2,1,0:T(8,128)} %green_ref) | copy-start | bytes 1572868
  2.0 22.5 %all-to-all-start = ((f32[32,1,1920]{2,1,0:T(1,128)}), f32[32,1,1920]{2,1,0:T(1,128)S(1)}, u32[]{:S(2)}, u32[]{:S(2)}) async-start(f32[32,1,1920]{2,1,0:T(1,128)} %bitcast.33), calls=%async_computation | async-start | bytes 491520 | tf_op jit(solution)/shard_map/all_to_all | solution.py:516
  13.9 1.3 %copy-start.14 = (s32[1,1,768]{2,1,0:T(1,128)S(1)}, s32[1,1,768]{2,1,0:T(1,128)}, u32[]{:S(2)}) copy-start(s32[1,1,768]{2,1,0:T(1,128)} %param.19) | copy-start | bytes 9220
  14.0 7.1 %collective-permute-start = (f32[8,512]{1,0:T(8,128)S(1)}, f32[8,512]{1,0:T(8,128)S(1)}, u32[]{:S(2)}, u32[]{:S(2)}) collective-permute-start(f32[8,512]{1,0:T(8,128)S(1)} %slice_bitcast_fusion), channel_id=1, source_target_pairs={{4,0},{12,8},{20,16},{28,24},{36,32},{44,40},{52,48},{60,56},{68,6... | collective-permute-start | bytes 49160 | tf_op jit(solution)/shard_map/ppermute | solution.py:515
  15.4 0.7 copy-start.12
  16.3 8.2 %copy-start.10 = (s32[32,256]{1,0:T(8,128)S(1)}, s32[32,256]{1,0:T(8,128)}, u32[]{:S(2)}) copy-start(s32[32,256]{1,0:T(8,128)} %index_ref.1) | copy-start | bytes 98308
  16.3 8.2 %copy-start.11 = (f32[32,256]{1,0:T(8,128)S(1)}, f32[32,256]{1,0:T(8,128)}, u32[]{:S(2)}) copy-start(f32[32,256]{1,0:T(8,128)} %factor_ref.1) | copy-start | bytes 98308
  21.1 3.4 %copy-start.13 = (f32[256]{0:T(256)S(1)}, f32[256]{0:T(256)}, u32[]{:S(2)}) copy-start(f32[256]{0:T(256)} %param.16) | copy-start | bytes 3076
  21.1 3.6 %copy-start.6 = (bf16[2,256,256]{2,1,0:T(8,128)(2,1)S(1)}, bf16[2,256,256]{2,1,0:T(8,128)(2,1)}, u32[]{:S(2)}) copy-start(bf16[2,256,256]{2,1,0:T(8,128)(2,1)} %constant.18.clone.z_ref) | copy-start | bytes 786436
  21.8 20.9 %copy-start.3 = (bf16[2,512,512]{2,1,0:T(8,128)(2,1)S(1)}, bf16[2,512,512]{2,1,0:T(8,128)(2,1)}, u32[]{:S(2)}) copy-start(bf16[2,512,512]{2,1,0:T(8,128)(2,1)} %constant.20.clone.refs_1_) | copy-start | bytes 3145732
  27.9 14.8 %copy-start.5 = (bf16[2,2,256,256]{3,2,1,0:T(8,128)(2,1)S(1)}, bf16[2,2,256,256]{3,2,1,0:T(8,128)(2,1)}, u32[]{:S(2)}) copy-start(bf16[2,2,256,256]{3,2,1,0:T(8,128)(2,1)} %constant.21.clone.refs_2_) | copy-start | bytes 1572868
  42.7 22.6 %copy-start.8 = (f32[2,32,256]{2,1,0:T(8,128)S(1)}, f32[2,32,256]{2,1,0:T(8,128)}, u32[]{:S(2)}) copy-start(f32[2,32,256]{2,1,0:T(8,128)} %constant.26.clone.twist_ref) | copy-start | bytes 196612
  42.7 22.6 %copy-start.9 = (bf16[2,64,64]{2,1,0:T(8,128)(2,1)S(1)}, bf16[2,64,64]{2,1,0:T(8,128)(2,1)}, u32[]{:S(2)}) copy-start(bf16[2,64,64]{2,1,0:T(8,128)(2,1)} %constant.24.clone.row_ref) | copy-start | bytes 49156
  43.7 21.6 %copy-start.2 = (bf16[2,512,512]{2,1,0:T(8,128)(2,1)S(1)}, bf16[2,512,512]{2,1,0:T(8,128)(2,1)}, u32[]{:S(2)}) copy-start(bf16[2,512,512]{2,1,0:T(8,128)(2,1)} %constant.25.clone.lane_ref) | copy-start | bytes 3145732
  65.4 23.7 %copy-start.4 = (bf16[2,2,256,256]{3,2,1,0:T(8,128)(2,1)S(1)}, bf16[2,2,256,256]{3,2,1,0:T(8,128)(2,1)}, u32[]{:S(2)}) copy-start(bf16[2,2,256,256]{3,2,1,0:T(8,128)(2,1)} %constant.23.clone.refs_2_) | copy-start | bytes 1572868
  67.7 21.4 %copy-start.1 = (bf16[2,512,512]{2,1,0:T(8,128)(2,1)S(1)}, bf16[2,512,512]{2,1,0:T(8,128)(2,1)}, u32[]{:S(2)}) copy-start(bf16[2,512,512]{2,1,0:T(8,128)(2,1)} %constant.22.clone.refs_1_) | copy-start | bytes 3145732
  90.1 13.0 %copy-start.7 = (bf16[2,256,256]{2,1,0:T(8,128)(2,1)S(1)}, bf16[2,256,256]{2,1,0:T(8,128)(2,1)}, u32[]{:S(2)}) copy-start(bf16[2,256,256]{2,1,0:T(8,128)(2,1)} %constant.19.clone.z_ref) | copy-start | bytes 786436

commit v10 on v9

--- a/solution.py
+++ b/solution.py
@@ -324,17 +324,12 @@
 
 
 def y_stage(source, target, shared):
-    def kernel(in_ref, table_ref, shared_ref, out_ref, work_ref):
+    def kernel(in_ref, table_ref, shared_ref, out_ref):
         value = gathered(in_ref, *source)
         data = split(value)
-        work_ref[...] = mm3(table_ref[...], data)
-
-        @pl.when(lax.axis_index("pencil") == 0)
-        def _():
-            other = shared(value, data, shared_ref)
-            work_ref[...] = jnp.where(shared_lane(other.shape), other, work_ref[...])
-
-        scattered(work_ref[...], out_ref, *target)
+        out = mm3(table_ref[...], data)
+        lone = shared_lane(out.shape) & (lax.axis_index("pencil") == 0)
+        scattered(jnp.where(lone, shared(value, data, shared_ref), out), out_ref, *target)
 
     return kernel
 
@@ -347,7 +342,7 @@
     y_stage((32, 16), (8, 64), shared_backward)(*refs)
 
 
-def x_stage(in_ref, green_ref, other_ref, twist_ref, row_ref, lane_ref, out_ref, re_ref, im_ref):
+def x_stage(in_ref, green_ref, other_ref, twist_ref, row_ref, lane_ref, out_ref):
     row_tables, lane_tables = row_ref[...], lane_ref[...]
     cosine, sine = twist_ref[0], twist_ref[1]
 
@@ -357,28 +352,20 @@
     def turn(re, im):
         return jnp.concatenate([re * cosine + im * sine, im * cosine - re * sine], axis=1)
 
-    data = [jnp.concatenate(sum((line(k, ri) for k in range(8)), []), axis=1) for ri in range(2)]
+    lines = [[jnp.concatenate(line(k, ri), axis=1) for k in range(8)] for ri in range(2)]
+    data = [jnp.concatenate(lines[0] + [lines[0][0]], axis=1), jnp.concatenate(lines[1] + [-lines[1][0]], axis=1)]
     rows = mm3(row_tables, split(jnp.concatenate(data, axis=0)))
-    columns = [slice(k * 256, k * 256 + 256) for k in range(8)]
+    columns = [slice(k * 256, k * 256 + 256) for k in range(9)]
     full = mm3(split(jnp.concatenate([turn(rows[:32, at], rows[32:, at]) for at in columns], axis=0)), lane_tables)
-    for half in range(2):
-        at = slice(half * 128, half * 128 + 128)
-        re_ref[half] = full[:, at] * green_ref[half]
-        im_ref[half] = full[:, 256 + half * 128 : 384 + half * 128] * green_ref[half]
-
-    @pl.when(position()[2])
-    def _():
-        conjugate = jnp.concatenate([data[0][:, :256], -data[1][:, :256]], axis=0)
-        rows = mm3(row_tables, split(conjugate))
-        mirror = mm3(split(turn(rows[:32], rows[32:])), lane_tables)
-        for half in range(2):
-            at = slice(half * 128, half * 128 + 128)
-            other = other_ref[:, at]
-            re_ref[half, :32, :] += mirror[:, at] * other
-            im_ref[half, :32, :] += mirror[:, 256 + half * 128 : 384 + half * 128] * other
-
-    product = jnp.concatenate([re_ref[0], re_ref[1], -im_ref[0], -im_ref[1]], axis=1)
-    back = mm3(split(product), lane_tables)
+    product = []
+    for part in range(4):
+        at = slice(part * 128, part * 128 + 128)
+        other = other_ref[:, part % 2 * 128 : part % 2 * 128 + 128]
+        value = full[:256, at] * green_ref[part % 2]
+        value = jnp.concatenate([value[:32] + full[256:, at] * other, value[32:]], axis=0)
+        product.append(value if part < 2 else -value)
+
+    back = mm3(split(jnp.concatenate(product, axis=1)), lane_tables)
     back = [turn(back[k * 32 : k * 32 + 32, :256], back[k * 32 : k * 32 + 32, 256:]) for k in range(8)]
     data = [jnp.concatenate([part[:, ri * 256 : ri * 256 + 256] for part in back], axis=1) for ri in range(2)]
     rows = mm3(row_tables, split(jnp.concatenate(data, axis=0)))
@@ -533,17 +520,17 @@
     by_y = swap(after_z, "pencil", N_PENCIL)
     after_y = call(
         y_forward, shape((1024, 128), F32), by_y, y_fwd, y_fwd_shared,
-        scratch=[pltpu.VMEM((512, 256), F32)], limit=LIMIT_Y,
+        limit=LIMIT_Y,
     )
     by_x = swap(after_y, "slab", N_SLAB)
     after_x = call(
         x_stage, shape((1024, 128), F32), by_x, green, other, twist, rows, lanes,
-        scratch=[pltpu.VMEM((2, 256, 128), F32)] * 2, limit=LIMIT_X,
+        limit=LIMIT_X,
     )
     back_x = swap(after_x, "slab", N_SLAB)
     back_y = call(
         y_backward, shape((1024, 128), F32), back_x, y_bwd, y_bwd_shared,
-        scratch=[pltpu.VMEM((512, 256), F32)], limit=LIMIT_Y,
+        limit=LIMIT_Y,
     )
     by_z = swap(back_y, "pencil", N_PENCIL)
     sampled = call(

time: 121 us -> 121 us (level)
  no operation moved by 1% of the time
where the time goes in v10:
time: 121 us; the launch traced here: 120 us
  blocking collectives  85 us (70%)
  Pallas kernels  13.6 us (11%)
  starting transfers between devices  12.9 us (11%)
  waiting for transfers between devices  7.42 us (6%)
    all_to_all x4, blocking collectives, swap(): lax.all_to_all(value.reshape(count, rows // count, 128), axis, 0, 0, tile...  71.1 us
    all_to_all x1, blocking collectives, per_device(): far = lax.all_to_all(sampled, 'slab', 0, 0, tiled=True)  13.9 us
    pallas_call x10, Pallas kernels, call(): pl.pallas_call(kernel, out_shape=out_shape, in_specs=[pl.BlockSpec(memory...  13.6 us
    all_to_all x1, starting transfers between devices, per_device(): lax.all_to_all(payload.reshape(N_SLAB, 1, LINES * 128), 'slab', 0, 0, til...  11.6 us
    ppermute x1, waiting for transfers between devices, per_device(): plane = lax.ppermute(spectrum[:, 0, :], 'pencil', [(4, 0)])  4.76 us
    all_to_all x1, waiting for transfers between devices, per_device(): lax.all_to_all(payload.reshape(N_SLAB, 1, LINES * 128), 'slab', 0, 0, til...  2.66 us
  transfers between devices with their start and end apart: 2, of which 2 were waited for; matrix products, arithmetic and copies ran while one was open for 0% of the time, Pallas kernels for 1%

profile of v10, /device:TPU:2, one launch (start us, length us, event | category | flops | bytes accessed | tf_op | source)
XLA Modules:
  0.0 120.3 jit_solution(16193622490139941497)
XLA Ops:
  0.0 0.0 copy-start
  0.0 2.0 %pack.1 = f32[480,128]{1,0:T(8,128)} custom-call(s32[1,1,768]{2,1,0:T(1,128)} %slot_ref.2, f32[64,256]{1,0:T(8,128)} %weight_ref.1, f32[1,256]{1,0:T(1,128)} %bitcast.31), custom_call_target="tpu_custom_call" | custom-call | tf_op jit(solution)/shard_map/pack/pallas_call | solution.py:114
  2.0 11.6 %all-to-all-start = ((f32[32,1,1920]{2,1,0:T(1,128)}), f32[32,1,1920]{2,1,0:T(1,128)S(1)}, u32[]{:S(2)}, u32[]{:S(2)}) async-start(f32[32,1,1920]{2,1,0:T(1,128)} %bitcast.33), calls=%async_computation | async-start | bytes 491520 | tf_op jit(solution)/shard_map/all_to_all | solution.py:503
  13.6 0.0 copy-done
  13.6 0.3 copy.22
  13.9 0.0 copy-start.14
  14.0 1.3 %collective-permute-start = (f32[8,512]{1,0:T(8,128)S(1)}, f32[8,512]{1,0:T(8,128)S(1)}, u32[]{:S(2)}, u32[]{:S(2)}) collective-permute-start(f32[8,512]{1,0:T(8,128)S(1)} %slice_bitcast_fusion), channel_id=1, source_target_pairs={{4,0},{12,8},{20,16},{28,24},{36,32},{44,40},{52,48},{60,56},{68,6... | collective-permute-start | bytes 49160 | tf_op jit(solution)/shard_map/ppermute | solution.py:502
  15.3 0.0 copy-done.14
  15.3 0.1 reshape.47
  15.4 0.0 copy-start.12
  15.4 0.1 reshape.48.anchor_ref
  15.6 0.6 copy-done.12
  16.1 0.2 home.1
  16.3 0.0 copy-start.10
  16.3 0.0 copy-start.11
  16.3 4.8 %collective-permute-done.plane_ref = f32[8,512]{1,0:T(8,128)S(1)} collective-permute-done((f32[8,512]{1,0:T(8,128)S(1)}, f32[8,512]{1,0:T(8,128)S(1)}, u32[]{:S(2)}, u32[]{:S(2)}) %collective-permute-start) | collective-permute-done | bytes 16416 | tf_op jit(solution)/shard_map/ppermute | solution.py:502
  21.1 0.0 copy-start.13
  21.1 0.0 copy-start.6
  21.1 0.7 arrange_green.1
  21.8 0.0 copy-start.3
  21.8 2.7 %all-to-all-done = f32[32,1,1920]{2,1,0:T(1,128)S(1)} async-done(((f32[32,1,1920]{2,1,0:T(1,128)}), f32[32,1,1920]{2,1,0:T(1,128)S(1)}, u32[]{:S(2)}, u32[]{:S(2)}) %all-to-all-start) | async-done | bytes 245792 | tf_op jit(solution)/shard_map/all_to_all | solution.py:503
  24.5 0.0 copy-done.10
  24.5 0.0 copy-done.11
  24.5 0.0 copy-done.13
  24.5 0.2 near.1.near_ref
  24.7 0.0 copy-done.6
  24.7 3.2 %project.1 = (f32[1024,128]{1,0:T(8,128)S(1)}, f32[128,768]{1,0:T(8,128)S(1)}) custom-call(f32[480,128]{1,0:T(8,128)S(1)} %bitcast.20, s32[1,1,768]{2,1,0:T(1,128)S(1)} %reshape.48.anchor_ref, bf16[2,256,256]{2,1,0:T(8,128)(2,1)S(1)} %copy-done.6), custom_call_target="tpu_custom_call" | custom-call | tf_op jit(solution)/shard_map/project/pallas_call | solution.py:114
  27.9 0.0 copy-start.5
  27.9 14.8 %all_to_all.36 = f32[8,128,128]{2,1,0:T(8,128)S(1)} all-to-all(f32[8,128,128]{2,1,0:T(8,128)S(1)} %bitcast.28), channel_id=1, replica_groups=mesh['slab'=32,'pencil'=8] {'pencil'}, dimensions={0} | all-to-all | bytes 1048576 | tf_op jit(solution)/shard_map/all_to_all | solution.py:448
  42.7 0.0 copy-done.3
  42.7 0.0 copy-done.5
  42.7 0.0 copy-start.8
  42.7 0.0 copy-start.9
  42.7 0.8 y_forward.1
  43.5 0.0 copy-start.2
  43.5 22.0 %all_to_all.37 = f32[32,32,128]{2,1,0:T(8,128)S(1)} all-to-all(f32[32,32,128]{2,1,0:T(8,128)S(1)} %bitcast.24), channel_id=1, replica_groups=mesh['slab'=32,'pencil'=8] {'slab'}, dimensions={0} | all-to-all | bytes 1048576 | tf_op jit(solution)/shard_map/all_to_all | solution.py:448
  65.5 0.0 copy-done.8
  65.5 0.0 copy-done.9
  65.5 0.0 copy-done.2
  65.5 0.0 copy-start.4
  65.5 2.3 %x_stage.1 = f32[1024,128]{1,0:T(8,128)S(1)} custom-call(f32[1024,128]{1,0:T(8,128)S(1)} %bitcast.21, f32[2,256,128]{2,1,0:T(8,128)S(1)} %get-tuple-element.33.green_ref, f32[32,256]{1,0:T(8,128)S(1)} %get-tuple-element.34.other_ref, f32[2,32,256]{2,1,0:T(8,128)S(1)} %copy-done.8, bf16[2,64,64]{2,1,0:T(8,128)(2,1)S(1)} %copy-done.9, ...), custom_call_target="tpu_custom_call" | custom-call | tf_op jit(solution)/shard_map/x_stage/pallas_call | solution.py:114
  67.9 0.0 copy-start.1
  67.9 21.4 %all_to_all.38 = f32[32,32,128]{2,1,0:T(8,128)S(1)} all-to-all(f32[32,32,128]{2,1,0:T(8,128)S(1)} %bitcast.22), channel_id=1, replica_groups=mesh['slab'=32,'pencil'=8] {'slab'}, dimensions={0} | all-to-all | bytes 1048576 | tf_op jit(solution)/shard_map/all_to_all | solution.py:448
  89.3 0.0 copy-done.4
  89.3 0.0 copy-done.1
  89.3 0.8 y_backward.1
  90.1 0.0 copy-start.7
  90.1 12.9 %all_to_all.39 = f32[8,128,128]{2,1,0:T(8,128)S(1)} all-to-all(f32[8,128,128]{2,1,0:T(8,128)S(1)} %bitcast.26), channel_id=1, replica_groups=mesh['slab'=32,'pencil'=8] {'pencil'}, dimensions={0} | all-to-all | bytes 1048576 | tf_op jit(solution)/shard_map/all_to_all | solution.py:448
  103.0 0.0 copy-done.7
  103.0 2.8 %sample.1 = f32[32,128]{1,0:T(8,128)S(1)} custom-call(f32[1024,128]{1,0:T(8,128)S(1)} %bitcast.27, f32[128,768]{1,0:T(8,128)S(1)} %get-tuple-element.35.weight_ref, s32[1,1,768]{2,1,0:T(1,128)S(1)} %reshape.48.anchor_ref, bf16[2,256,256]{2,1,0:T(8,128)(2,1)S(1)} %copy-done.7), custom_call_target="tpu_custom_call" | custom-call | tf_op jit(solution)/shard_map/sample/pallas_call | solution.py:114
  105.8 13.9 %all_to_all.40 = f32[32,1,128]{2,1,0:T(1,128)S(1)} all-to-all(f32[32,1,128]{2,1,0:T(1,128)S(1)} %bitcast.29), channel_id=1, replica_groups=mesh['slab'=32,'pencil'=8] {'slab'}, dimensions={0} | all-to-all | bytes 32768 | tf_op jit(solution)/shard_map/all_to_all | solution.py:542
  119.7 0.7 finish.1
  (3 shorter events, 0.0 us)
Async XLA Ops:
  0.0 13.6 %copy-start = (f32[8,32,512]{2,1,0:T(8,128)S(1)}, f32[8,32,512]{2,1,0:T(8,128)}, u32[]{:S(2)}) copy-start(f32[8,32,512]{2,1,0:T(8,128)} %green_ref) | copy-start | bytes 1572868
  2.0 22.5 %all-to-all-start = ((f32[32,1,1920]{2,1,0:T(1,128)}), f32[32,1,1920]{2,1,0:T(1,128)S(1)}, u32[]{:S(2)}, u32[]{:S(2)}) async-start(f32[32,1,1920]{2,1,0:T(1,128)} %bitcast.33), calls=%async_computation | async-start | bytes 491520 | tf_op jit(solution)/shard_map/all_to_all | solution.py:503
  13.9 1.3 %copy-start.14 = (s32[1,1,768]{2,1,0:T(1,128)S(1)}, s32[1,1,768]{2,1,0:T(1,128)}, u32[]{:S(2)}) copy-start(s32[1,1,768]{2,1,0:T(1,128)} %param.19) | copy-start | bytes 9220
  14.0 7.1 %collective-permute-start = (f32[8,512]{1,0:T(8,128)S(1)}, f32[8,512]{1,0:T(8,128)S(1)}, u32[]{:S(2)}, u32[]{:S(2)}) collective-permute-start(f32[8,512]{1,0:T(8,128)S(1)} %slice_bitcast_fusion), channel_id=1, source_target_pairs={{4,0},{12,8},{20,16},{28,24},{36,32},{44,40},{52,48},{60,56},{68,6... | collective-permute-start | bytes 49160 | tf_op jit(solution)/shard_map/ppermute | solution.py:502
  15.4 0.7 copy-start.12
  16.3 8.2 %copy-start.10 = (s32[32,256]{1,0:T(8,128)S(1)}, s32[32,256]{1,0:T(8,128)}, u32[]{:S(2)}) copy-start(s32[32,256]{1,0:T(8,128)} %index_ref.1) | copy-start | bytes 98308
  16.3 8.2 %copy-start.11 = (f32[32,256]{1,0:T(8,128)S(1)}, f32[32,256]{1,0:T(8,128)}, u32[]{:S(2)}) copy-start(f32[32,256]{1,0:T(8,128)} %factor_ref.1) | copy-start | bytes 98308
  21.1 3.4 %copy-start.13 = (f32[256]{0:T(256)S(1)}, f32[256]{0:T(256)}, u32[]{:S(2)}) copy-start(f32[256]{0:T(256)} %param.16) | copy-start | bytes 3076
  21.1 3.6 %copy-start.6 = (bf16[2,256,256]{2,1,0:T(8,128)(2,1)S(1)}, bf16[2,256,256]{2,1,0:T(8,128)(2,1)}, u32[]{:S(2)}) copy-start(bf16[2,256,256]{2,1,0:T(8,128)(2,1)} %constant.18.clone.z_ref) | copy-start | bytes 786436
  21.8 20.9 %copy-start.3 = (bf16[2,512,512]{2,1,0:T(8,128)(2,1)S(1)}, bf16[2,512,512]{2,1,0:T(8,128)(2,1)}, u32[]{:S(2)}) copy-start(bf16[2,512,512]{2,1,0:T(8,128)(2,1)} %constant.20.clone.refs_1_) | copy-start | bytes 3145732
  27.9 14.8 %copy-start.5 = (bf16[2,2,256,256]{3,2,1,0:T(8,128)(2,1)S(1)}, bf16[2,2,256,256]{3,2,1,0:T(8,128)(2,1)}, u32[]{:S(2)}) copy-start(bf16[2,2,256,256]{3,2,1,0:T(8,128)(2,1)} %constant.21.clone.refs_2_) | copy-start | bytes 1572868
  42.7 22.8 %copy-start.8 = (f32[2,32,256]{2,1,0:T(8,128)S(1)}, f32[2,32,256]{2,1,0:T(8,128)}, u32[]{:S(2)}) copy-start(f32[2,32,256]{2,1,0:T(8,128)} %constant.26.clone.twist_ref) | copy-start | bytes 196612
  42.7 22.8 %copy-start.9 = (bf16[2,64,64]{2,1,0:T(8,128)(2,1)S(1)}, bf16[2,64,64]{2,1,0:T(8,128)(2,1)}, u32[]{:S(2)}) copy-start(bf16[2,64,64]{2,1,0:T(8,128)(2,1)} %constant.24.clone.row_ref) | copy-start | bytes 49156
  43.5 22.0 %copy-start.2 = (bf16[2,512,512]{2,1,0:T(8,128)(2,1)S(1)}, bf16[2,512,512]{2,1,0:T(8,128)(2,1)}, u32[]{:S(2)}) copy-start(bf16[2,512,512]{2,1,0:T(8,128)(2,1)} %constant.25.clone.lane_ref) | copy-start | bytes 3145732
  65.5 23.8 %copy-start.4 = (bf16[2,2,256,256]{3,2,1,0:T(8,128)(2,1)S(1)}, bf16[2,2,256,256]{3,2,1,0:T(8,128)(2,1)}, u32[]{:S(2)}) copy-start(bf16[2,2,256,256]{3,2,1,0:T(8,128)(2,1)} %constant.23.clone.refs_2_) | copy-start | bytes 1572868
  67.9 21.4 %copy-start.1 = (bf16[2,512,512]{2,1,0:T(8,128)(2,1)S(1)}, bf16[2,512,512]{2,1,0:T(8,128)(2,1)}, u32[]{:S(2)}) copy-start(bf16[2,512,512]{2,1,0:T(8,128)(2,1)} %constant.22.clone.refs_1_) | copy-start | bytes 3145732
  90.1 13.0 %copy-start.7 = (bf16[2,256,256]{2,1,0:T(8,128)(2,1)S(1)}, bf16[2,256,256]{2,1,0:T(8,128)(2,1)}, u32[]{:S(2)}) copy-start(bf16[2,256,256]{2,1,0:T(8,128)(2,1)} %constant.19.clone.z_ref) | copy-start | bytes 786436

commit v11 on v10

--- a/solution.py
+++ b/solution.py
@@ -324,12 +324,17 @@
 
 
 def y_stage(source, target, shared):
-    def kernel(in_ref, table_ref, shared_ref, out_ref):
+    def kernel(in_ref, table_ref, shared_ref, out_ref, work_ref):
         value = gathered(in_ref, *source)
         data = split(value)
-        out = mm3(table_ref[...], data)
-        lone = shared_lane(out.shape) & (lax.axis_index("pencil") == 0)
-        scattered(jnp.where(lone, shared(value, data, shared_ref), out), out_ref, *target)
+        work_ref[...] = mm3(table_ref[...], data)
+
+        @pl.when(lax.axis_index("pencil") == 0)
+        def _():
+            other = shared(value, data, shared_ref)
+            work_ref[...] = jnp.where(shared_lane(other.shape), other, work_ref[...])
+
+        scattered(work_ref[...], out_ref, *target)
 
     return kernel
 
@@ -520,7 +525,7 @@
     by_y = swap(after_z, "pencil", N_PENCIL)
     after_y = call(
         y_forward, shape((1024, 128), F32), by_y, y_fwd, y_fwd_shared,
-        limit=LIMIT_Y,
+        scratch=[pltpu.VMEM((512, 256), F32)], limit=LIMIT_Y,
     )
     by_x = swap(after_y, "slab", N_SLAB)
     after_x = call(
@@ -530,7 +535,7 @@
     back_x = swap(after_x, "slab", N_SLAB)
     back_y = call(
         y_backward, shape((1024, 128), F32), back_x, y_bwd, y_bwd_shared,
-        limit=LIMIT_Y,
+        scratch=[pltpu.VMEM((512, 256), F32)], limit=LIMIT_Y,
     )
     by_z = swap(back_y, "pencil", N_PENCIL)
     sampled = call(

time: 121 us -> 121 us (level)
  no operation moved by 1% of the time
where the time goes in v11:
time: 121 us; the launch traced here: 120 us
  blocking collectives  84.6 us (70%)
  Pallas kernels  14 us (12%)
  starting transfers between devices  12.9 us (11%)
  waiting for transfers between devices  7.42 us (6%)
    all_to_all x4, blocking collectives, swap(): lax.all_to_all(value.reshape(count, rows // count, 128), axis, 0, 0, tile...  70.7 us
    pallas_call x10, Pallas kernels, call(): pl.pallas_call(kernel, out_shape=out_shape, in_specs=[pl.BlockSpec(memory...  14 us
    all_to_all x1, blocking collectives, per_device(): far = lax.all_to_all(sampled, 'slab', 0, 0, tiled=True)  13.9 us
    all_to_all x1, starting transfers between devices, per_device(): lax.all_to_all(payload.reshape(N_SLAB, 1, LINES * 128), 'slab', 0, 0, til...  11.6 us
    ppermute x1, waiting for transfers between devices, per_device(): plane = lax.ppermute(spectrum[:, 0, :], 'pencil', [(4, 0)])  4.76 us
    all_to_all x1, waiting for transfers between devices, per_device(): lax.all_to_all(payload.reshape(N_SLAB, 1, LINES * 128), 'slab', 0, 0, til...  2.66 us
  transfers between devices with their start and end apart: 2, of which 2 were waited for; matrix products, arithmetic and copies ran while one was open for 0% of the time, Pallas kernels for 1%

profile of v11, /device:TPU:2, one launch (start us, length us, event | category | flops | bytes accessed | tf_op | source)
XLA Modules:
  0.0 120.4 jit_solution(13122619709532471281)
XLA Ops:
  0.0 0.0 copy-start
  0.0 2.0 %pack.1 = f32[480,128]{1,0:T(8,128)} custom-call(s32[1,1,768]{2,1,0:T(1,128)} %slot_ref.2, f32[64,256]{1,0:T(8,128)} %weight_ref.1, f32[1,256]{1,0:T(1,128)} %bitcast.31), custom_call_target="tpu_custom_call" | custom-call | tf_op jit(solution)/shard_map/pack/pallas_call | solution.py:114
  2.0 11.6 %all-to-all-start = ((f32[32,1,1920]{2,1,0:T(1,128)}), f32[32,1,1920]{2,1,0:T(1,128)S(1)}, u32[]{:S(2)}, u32[]{:S(2)}) async-start(f32[32,1,1920]{2,1,0:T(1,128)} %bitcast.33), calls=%async_computation | async-start | bytes 491520 | tf_op jit(solution)/shard_map/all_to_all | solution.py:508
  13.6 0.0 copy-done
  13.6 0.3 copy.22
  13.9 0.0 copy-start.14
  14.0 1.3 %collective-permute-start = (f32[8,512]{1,0:T(8,128)S(1)}, f32[8,512]{1,0:T(8,128)S(1)}, u32[]{:S(2)}, u32[]{:S(2)}) collective-permute-start(f32[8,512]{1,0:T(8,128)S(1)} %slice_bitcast_fusion), channel_id=1, source_target_pairs={{4,0},{12,8},{20,16},{28,24},{36,32},{44,40},{52,48},{60,56},{68,6... | collective-permute-start | bytes 49160 | tf_op jit(solution)/shard_map/ppermute | solution.py:507
  15.3 0.0 copy-done.14
  15.3 0.1 reshape.47
  15.4 0.0 copy-start.12
  15.4 0.1 reshape.48.anchor_ref
  15.6 0.6 copy-done.12
  16.1 0.2 home.1
  16.3 0.0 copy-start.10
  16.3 0.0 copy-start.11
  16.3 4.8 %collective-permute-done.plane_ref = f32[8,512]{1,0:T(8,128)S(1)} collective-permute-done((f32[8,512]{1,0:T(8,128)S(1)}, f32[8,512]{1,0:T(8,128)S(1)}, u32[]{:S(2)}, u32[]{:S(2)}) %collective-permute-start) | collective-permute-done | bytes 16416 | tf_op jit(solution)/shard_map/ppermute | solution.py:507
  21.1 0.0 copy-start.13
  21.1 0.0 copy-start.6
  21.1 0.7 arrange_green.1
  21.8 0.0 copy-start.3
  21.8 2.7 %all-to-all-done = f32[32,1,1920]{2,1,0:T(1,128)S(1)} async-done(((f32[32,1,1920]{2,1,0:T(1,128)}), f32[32,1,1920]{2,1,0:T(1,128)S(1)}, u32[]{:S(2)}, u32[]{:S(2)}) %all-to-all-start) | async-done | bytes 245792 | tf_op jit(solution)/shard_map/all_to_all | solution.py:508
  24.5 0.0 copy-done.10
  24.5 0.0 copy-done.11
  24.5 0.0 copy-done.13
  24.5 0.2 near.1.near_ref
  24.7 0.0 copy-done.6
  24.7 3.2 %project.1 = (f32[1024,128]{1,0:T(8,128)S(1)}, f32[128,768]{1,0:T(8,128)S(1)}) custom-call(f32[480,128]{1,0:T(8,128)S(1)} %bitcast.20, s32[1,1,768]{2,1,0:T(1,128)S(1)} %reshape.48.anchor_ref, bf16[2,256,256]{2,1,0:T(8,128)(2,1)S(1)} %copy-done.6), custom_call_target="tpu_custom_call" | custom-call | tf_op jit(solution)/shard_map/project/pallas_call | solution.py:114
  27.9 0.0 copy-start.5
  27.9 14.8 %all_to_all.36 = f32[8,128,128]{2,1,0:T(8,128)S(1)} all-to-all(f32[8,128,128]{2,1,0:T(8,128)S(1)} %bitcast.28), channel_id=1, replica_groups=mesh['slab'=32,'pencil'=8] {'pencil'}, dimensions={0} | all-to-all | bytes 1048576 | tf_op jit(solution)/shard_map/all_to_all | solution.py:453
  42.7 0.0 copy-done.3
  42.7 0.0 copy-done.5
  42.7 0.0 copy-start.8
  42.7 0.0 copy-start.9
  42.7 1.0 y_forward.1
  43.7 0.0 copy-start.2
  43.8 21.6 %all_to_all.37 = f32[32,32,128]{2,1,0:T(8,128)S(1)} all-to-all(f32[32,32,128]{2,1,0:T(8,128)S(1)} %bitcast.24), channel_id=1, replica_groups=mesh['slab'=32,'pencil'=8] {'slab'}, dimensions={0} | all-to-all | bytes 1048576 | tf_op jit(solution)/shard_map/all_to_all | solution.py:453
  65.4 0.0 copy-done.8
  65.4 0.0 copy-done.9
  65.4 0.0 copy-done.2
  65.4 0.0 copy-start.4
  65.4 2.3 %x_stage.1 = f32[1024,128]{1,0:T(8,128)S(1)} custom-call(f32[1024,128]{1,0:T(8,128)S(1)} %bitcast.21, f32[2,256,128]{2,1,0:T(8,128)S(1)} %get-tuple-element.33.green_ref, f32[32,256]{1,0:T(8,128)S(1)} %get-tuple-element.34.other_ref, f32[2,32,256]{2,1,0:T(8,128)S(1)} %copy-done.8, bf16[2,64,64]{2,1,0:T(8,128)(2,1)S(1)} %copy-done.9, ...), custom_call_target="tpu_custom_call" | custom-call | tf_op jit(solution)/shard_map/x_stage/pallas_call | solution.py:114
  67.7 0.0 copy-start.1
  67.7 21.4 %all_to_all.38 = f32[32,32,128]{2,1,0:T(8,128)S(1)} all-to-all(f32[32,32,128]{2,1,0:T(8,128)S(1)} %bitcast.22), channel_id=1, replica_groups=mesh['slab'=32,'pencil'=8] {'slab'}, dimensions={0} | all-to-all | bytes 1048576 | tf_op jit(solution)/shard_map/all_to_all | solution.py:453
  89.1 0.0 copy-done.4
  89.1 0.0 copy-done.1
  89.1 1.0 y_backward.1
  90.1 0.0 copy-start.7
  90.1 12.9 %all_to_all.39 = f32[8,128,128]{2,1,0:T(8,128)S(1)} all-to-all(f32[8,128,128]{2,1,0:T(8,128)S(1)} %bitcast.26), channel_id=1, replica_groups=mesh['slab'=32,'pencil'=8] {'pencil'}, dimensions={0} | all-to-all | bytes 1048576 | tf_op jit(solution)/shard_map/all_to_all | solution.py:453
  103.1 0.0 copy-done.7
  103.1 2.8 %sample.1 = f32[32,128]{1,0:T(8,128)S(1)} custom-call(f32[1024,128]{1,0:T(8,128)S(1)} %bitcast.27, f32[128,768]{1,0:T(8,128)S(1)} %get-tuple-element.35.weight_ref, s32[1,1,768]{2,1,0:T(1,128)S(1)} %reshape.48.anchor_ref, bf16[2,256,256]{2,1,0:T(8,128)(2,1)S(1)} %copy-done.7), custom_call_target="tpu_custom_call" | custom-call | tf_op jit(solution)/shard_map/sample/pallas_call | solution.py:114
  105.8 13.9 %all_to_all.40 = f32[32,1,128]{2,1,0:T(1,128)S(1)} all-to-all(f32[32,1,128]{2,1,0:T(1,128)S(1)} %bitcast.29), channel_id=1, replica_groups=mesh['slab'=32,'pencil'=8] {'slab'}, dimensions={0} | all-to-all | bytes 32768 | tf_op jit(solution)/shard_map/all_to_all | solution.py:547
  119.7 0.7 finish.1
  (3 shorter events, 0.0 us)
Async XLA Ops:
  0.0 13.6 %copy-start = (f32[8,32,512]{2,1,0:T(8,128)S(1)}, f32[8,32,512]{2,1,0:T(8,128)}, u32[]{:S(2)}) copy-start(f32[8,32,512]{2,1,0:T(8,128)} %green_ref) | copy-start | bytes 1572868
  2.0 22.5 %all-to-all-start = ((f32[32,1,1920]{2,1,0:T(1,128)}), f32[32,1,1920]{2,1,0:T(1,128)S(1)}, u32[]{:S(2)}, u32[]{:S(2)}) async-start(f32[32,1,1920]{2,1,0:T(1,128)} %bitcast.33), calls=%async_computation | async-start | bytes 491520 | tf_op jit(solution)/shard_map/all_to_all | solution.py:508
  13.9 1.3 %copy-start.14 = (s32[1,1,768]{2,1,0:T(1,128)S(1)}, s32[1,1,768]{2,1,0:T(1,128)}, u32[]{:S(2)}) copy-start(s32[1,1,768]{2,1,0:T(1,128)} %param.19) | copy-start | bytes 9220
  14.0 7.1 %collective-permute-start = (f32[8,512]{1,0:T(8,128)S(1)}, f32[8,512]{1,0:T(8,128)S(1)}, u32[]{:S(2)}, u32[]{:S(2)}) collective-permute-start(f32[8,512]{1,0:T(8,128)S(1)} %slice_bitcast_fusion), channel_id=1, source_target_pairs={{4,0},{12,8},{20,16},{28,24},{36,32},{44,40},{52,48},{60,56},{68,6... | collective-permute-start | bytes 49160 | tf_op jit(solution)/shard_map/ppermute | solution.py:507
  15.4 0.7 copy-start.12
  16.3 8.2 %copy-start.10 = (s32[32,256]{1,0:T(8,128)S(1)}, s32[32,256]{1,0:T(8,128)}, u32[]{:S(2)}) copy-start(s32[32,256]{1,0:T(8,128)} %index_ref.1) | copy-start | bytes 98308
  16.3 8.2 %copy-start.11 = (f32[32,256]{1,0:T(8,128)S(1)}, f32[32,256]{1,0:T(8,128)}, u32[]{:S(2)}) copy-start(f32[32,256]{1,0:T(8,128)} %factor_ref.1) | copy-start | bytes 98308
  21.1 3.4 %copy-start.13 = (f32[256]{0:T(256)S(1)}, f32[256]{0:T(256)}, u32[]{:S(2)}) copy-start(f32[256]{0:T(256)} %param.16) | copy-start | bytes 3076
  21.1 3.6 %copy-start.6 = (bf16[2,256,256]{2,1,0:T(8,128)(2,1)S(1)}, bf16[2,256,256]{2,1,0:T(8,128)(2,1)}, u32[]{:S(2)}) copy-start(bf16[2,256,256]{2,1,0:T(8,128)(2,1)} %constant.18.clone.z_ref) | copy-start | bytes 786436
  21.8 20.9 %copy-start.3 = (bf16[2,512,512]{2,1,0:T(8,128)(2,1)S(1)}, bf16[2,512,512]{2,1,0:T(8,128)(2,1)}, u32[]{:S(2)}) copy-start(bf16[2,512,512]{2,1,0:T(8,128)(2,1)} %constant.20.clone.refs_1_) | copy-start | bytes 3145732
  27.9 14.8 %copy-start.5 = (bf16[2,2,256,256]{3,2,1,0:T(8,128)(2,1)S(1)}, bf16[2,2,256,256]{3,2,1,0:T(8,128)(2,1)}, u32[]{:S(2)}) copy-start(bf16[2,2,256,256]{3,2,1,0:T(8,128)(2,1)} %constant.21.clone.refs_2_) | copy-start | bytes 1572868
  42.7 22.6 %copy-start.8 = (f32[2,32,256]{2,1,0:T(8,128)S(1)}, f32[2,32,256]{2,1,0:T(8,128)}, u32[]{:S(2)}) copy-start(f32[2,32,256]{2,1,0:T(8,128)} %constant.26.clone.twist_ref) | copy-start | bytes 196612
  42.7 22.6 %copy-start.9 = (bf16[2,64,64]{2,1,0:T(8,128)(2,1)S(1)}, bf16[2,64,64]{2,1,0:T(8,128)(2,1)}, u32[]{:S(2)}) copy-start(bf16[2,64,64]{2,1,0:T(8,128)(2,1)} %constant.24.clone.row_ref) | copy-start | bytes 49156
  43.7 21.6 %copy-start.2 = (bf16[2,512,512]{2,1,0:T(8,128)(2,1)S(1)}, bf16[2,512,512]{2,1,0:T(8,128)(2,1)}, u32[]{:S(2)}) copy-start(bf16[2,512,512]{2,1,0:T(8,128)(2,1)} %constant.25.clone.lane_ref) | copy-start | bytes 3145732
  65.4 23.8 %copy-start.4 = (bf16[2,2,256,256]{3,2,1,0:T(8,128)(2,1)S(1)}, bf16[2,2,256,256]{3,2,1,0:T(8,128)(2,1)}, u32[]{:S(2)}) copy-start(bf16[2,2,256,256]{3,2,1,0:T(8,128)(2,1)} %constant.23.clone.refs_2_) | copy-start | bytes 1572868
  67.7 21.4 %copy-start.1 = (bf16[2,512,512]{2,1,0:T(8,128)(2,1)S(1)}, bf16[2,512,512]{2,1,0:T(8,128)(2,1)}, u32[]{:S(2)}) copy-start(bf16[2,512,512]{2,1,0:T(8,128)(2,1)} %constant.22.clone.refs_1_) | copy-start | bytes 3145732
  90.1 13.0 %copy-start.7 = (bf16[2,256,256]{2,1,0:T(8,128)(2,1)S(1)}, bf16[2,256,256]{2,1,0:T(8,128)(2,1)}, u32[]{:S(2)}) copy-start(bf16[2,256,256]{2,1,0:T(8,128)(2,1)} %constant.19.clone.z_ref) | copy-start | bytes 786436
